TPU v7x, 32 devices: a whole 2x2x4 slice. The times are simulated.
32 devices in a mesh: section: 2 (over x), dp: 16 (over z, y, core).
Axes of the slice: x: 2, y: 2, z: 4, core: 2. Of those that a mesh axis runs over, the one named last changes fastest.
Arguments:
- inputs: bfloat16 [2, 4096, 512], P('section', 'dp'), may hold values from -6 to 6
- lengths: int32 [32, 2, 16], P('dp'), may hold values from 0 to 128, as said below
- w_qkv: bfloat16 [2, 512, 1536], P('section'), may hold values from -0.25 to 0.25
- w_attn_out: bfloat16 [2, 512, 512], P('section'), may hold values from -0.5 to 0.5
- w_cross: bfloat16 [2, 512, 1024], P('section'), may hold values from -0.25 to 0.25
- w_up: bfloat16 [2, 512, 2048], P('section'), may hold values from -0.25 to 0.25
- w_down: bfloat16 [2, 2048, 512], P('section'), may hold values from -0.125 to 0.125
- cotangent: bfloat16 [2, 4096, 512], P('section', 'dp'), may hold values from -6 to 6
Outputs:
- outputs: bfloat16 [2, 4096, 512], P('section', 'dp')
- input_grad: bfloat16 [2, 4096, 512], P('section', 'dp')
- grad_qkv: float32 [2, 512, 1536], P('section')
- grad_attn_out: float32 [2, 512, 512], P('section')
- grad_cross: float32 [2, 512, 1024], P('section')
- grad_up: float32 [2, 512, 2048], P('section')
- grad_down: float32 [2, 2048, 512], P('section')
Inputs may be any that keep to these rules, and one draw needn't show every extreme that they name: For each micro-batch g, lengths[g, 0, :] and lengths[g, 1, :] each sum to 128; a slot's source length is 0 exactly when its target length is 0; some micro-batch holds a single pair of 128 source and 128 target tokens.
All inputs are finite; a program needn't handle non-finite values.
Results may differ from a plain program's by a relative error of at most 0.018.
Values may be sent and summed in bfloat16 or wider, within the bound.
No kernel may reach another device: no remote copies, remote signals or barrier semaphores. Data moves between devices by JAX's collectives and lax.ppermute only.
A program may use at most 256 MiB of HBM per device.

v0:
```python
import jax
import jax.numpy as jnp
from jax import lax
from jax.sharding import PartitionSpec as P

D = 512
HEADS = 8
HEAD_DIM = 64
ROWS = 128
MB = 2


def from_behind(block, axis, distance):
    devices = range(lax.axis_size(axis))
    route = [(i - distance, i) for i in devices if i - distance in devices]
    return lax.ppermute(block, axis, route)


def segments(pair_lengths, position):
    pair_ends = jnp.cumsum(pair_lengths)
    return jnp.sum((position[:, None] >= pair_ends[None, :]).astype(jnp.int32), axis=1)


def forward_dot(values_in, weight):
    return jnp.dot(values_in, weight, preferred_element_type=jnp.float32)


def back_dot(grad_in, weight):
    return lax.dot_general(
        grad_in, weight, (((1,), (1,)), ((), ())), preferred_element_type=jnp.float32
    )


def weight_dot(values_in, grad_in):
    return lax.dot_general(
        values_in, grad_in, (((0,), (0,)), ((), ())), preferred_element_type=jnp.float32
    )


def split_heads(values_in):
    return values_in.reshape(values_in.shape[0], HEADS, HEAD_DIM)


def scores_of(query_in, keys_in, mask_in):
    scores = jnp.einsum(
        "qhd,khd->hqk",
        split_heads(query_in),
        split_heads(keys_in),
        preferred_element_type=jnp.float32,
    )
    return jnp.where(mask_in[None], scores * HEAD_DIM ** (-0.5), -1e30)


def attend(query_in, keys_in, values_in, mask_in):
    scores = scores_of(query_in, keys_in, mask_in)
    highest = jnp.max(scores, axis=-1, keepdims=True)
    weights_raw = jnp.exp(scores - highest)
    row_total = jnp.sum(weights_raw, axis=-1, keepdims=True)
    weights_soft = (weights_raw / row_total).astype(jnp.bfloat16)
    mixed_heads = jnp.einsum(
        "hqk,khd->qhd", weights_soft, split_heads(values_in), preferred_element_type=jnp.float32
    )
    return (
        mixed_heads.reshape(query_in.shape[0], D).astype(jnp.bfloat16),
        highest + jnp.log(row_total),
    )


def attend_back(query_in, keys_in, values_in, mask_in, log_total, grad_mixed):
    weights_soft = jnp.exp(scores_of(query_in, keys_in, mask_in) - log_total)
    grad_heads = split_heads(grad_mixed)
    grad_values = jnp.einsum(
        "hqk,qhd->khd",
        weights_soft.astype(jnp.bfloat16),
        grad_heads,
        preferred_element_type=jnp.float32,
    )
    grad_weights = jnp.einsum(
        "qhd,khd->hqk", grad_heads, split_heads(values_in), preferred_element_type=jnp.float32
    )
    row_terms = jnp.sum(weights_soft * grad_weights, axis=-1, keepdims=True)
    grad_scores = (weights_soft * (grad_weights - row_terms)).astype(jnp.bfloat16)
    score_scale = HEAD_DIM ** (-0.5)
    grad_query = (
        jnp.einsum(
            "hqk,khd->qhd", grad_scores, split_heads(keys_in), preferred_element_type=jnp.float32
        )
        * score_scale
    )
    grad_keys = (
        jnp.einsum(
            "hqk,qhd->khd", grad_scores, split_heads(query_in), preferred_element_type=jnp.float32
        )
        * score_scale
    )
    rows_query = query_in.shape[0]
    rows_keys = keys_in.shape[0]
    return (
        grad_query.reshape(rows_query, D),
        grad_keys.reshape(rows_keys, D),
        grad_values.reshape(rows_keys, D),
    )


def feed_forward(residual, w_grow, w_shrink):
    residual_low = residual.astype(jnp.bfloat16)
    hidden = forward_dot(residual_low, w_grow)
    active = jax.nn.gelu(hidden).astype(jnp.bfloat16)
    return (forward_dot(active, w_shrink), residual_low, hidden, active)


def feed_backward(grad_out, residual_low, hidden, active, w_grow, w_shrink):
    grad_low = grad_out.astype(jnp.bfloat16)
    grad_shrink = weight_dot(active, grad_low)
    grad_active = back_dot(grad_low, w_shrink)
    unused, pullback = jax.vjp(jax.nn.gelu, hidden)
    grad_hidden = pullback(grad_active)[0].astype(jnp.bfloat16)
    grad_grow = weight_dot(residual_low, grad_hidden)
    return (grad_out + back_dot(grad_hidden, w_grow), grad_grow, grad_shrink)


def silenced(function):

    def silent(packed):
        return jax.tree.map(jnp.zeros_like, function(packed))

    return silent


def on_device(inputs, lengths, w_qkv, w_attn_out, w_cross, w_up, w_down, cotangent):
    w_in = w_qkv[0]
    w_mix = w_attn_out[0]
    w_link = w_cross[0]
    w_grow = w_up[0]
    w_shrink = w_down[0]
    is_first = lax.axis_index("section") == 0
    position = jnp.arange(ROWS)

    def encode(packed):
        tokens_now, seg_src = packed
        projected = forward_dot(tokens_now, w_in).astype(jnp.bfloat16)
        own_mask = seg_src[:, None] == seg_src[None, :]
        mixed_heads, log_total = attend(
            projected[:, :D], projected[:, D : 2 * D], projected[:, 2 * D :], own_mask
        )
        after_attn = tokens_now.astype(jnp.float32) + forward_dot(mixed_heads, w_mix)
        branch_out, after_low, hidden, active = feed_forward(after_attn, w_grow, w_shrink)
        memory_low = (after_attn + branch_out).astype(jnp.bfloat16)
        link_keys = forward_dot(memory_low, w_link).astype(jnp.bfloat16)
        return (
            link_keys,
            (projected, log_total, mixed_heads, after_low, hidden, active, memory_low),
        )

    def encode_back(packed):
        tokens_now, later_grad, link_grad, seg_src, stored = packed
        projected, log_total, mixed_heads, after_low, hidden, active, memory_low = stored
        grad_link = weight_dot(memory_low, link_grad)
        grad_memory = later_grad.astype(jnp.float32) + back_dot(link_grad, w_link)
        grad_after, grad_grow, grad_shrink = feed_backward(
            grad_memory, after_low, hidden, active, w_grow, w_shrink
        )
        grad_branch = grad_after.astype(jnp.bfloat16)
        grad_mix = weight_dot(mixed_heads, grad_branch)
        grad_mixed = back_dot(grad_branch, w_mix).astype(jnp.bfloat16)
        own_mask = seg_src[:, None] == seg_src[None, :]
        grad_query, grad_keys, grad_values = attend_back(
            projected[:, :D],
            projected[:, D : 2 * D],
            projected[:, 2 * D :],
            own_mask,
            log_total,
            grad_mixed,
        )
        grad_proj = jnp.concatenate([grad_query, grad_keys, grad_values], axis=1).astype(
            jnp.bfloat16
        )
        grad_in = weight_dot(tokens_now, grad_proj)
        grad_tokens = grad_after + back_dot(grad_proj, w_in)
        return (
            grad_tokens.astype(jnp.bfloat16),
            (grad_in, grad_mix, grad_link, grad_grow, grad_shrink),
        )

    def decode(packed):
        tokens_now, final_grad, link_keys, seg_src, seg_tgt = packed
        projected = forward_dot(tokens_now, w_in).astype(jnp.bfloat16)
        own_mask = (seg_tgt[:, None] == seg_tgt[None, :]) & (position[:, None] >= position[None, :])
        mixed_heads, log_total = attend(
            projected[:, :D], projected[:, D : 2 * D], projected[:, 2 * D :], own_mask
        )
        after_self = tokens_now.astype(jnp.float32) + forward_dot(mixed_heads, w_mix)
        self_low = after_self.astype(jnp.bfloat16)
        query_low = forward_dot(self_low, w_link[:, :D]).astype(jnp.bfloat16)
        across = seg_tgt[:, None] == seg_src[None, :]
        cross_keys = link_keys[:, :D]
        cross_values = link_keys[:, D:]
        cross_mixed, cross_total = attend(query_low, cross_keys, cross_values, across)
        after_cross = after_self + forward_dot(cross_mixed, w_link[:, D:])
        branch_out, cross_low, hidden, active = feed_forward(after_cross, w_grow, w_shrink)
        decoded = after_cross + branch_out
        grad_cross, grad_grow, grad_shrink = feed_backward(
            final_grad.astype(jnp.float32), cross_low, hidden, active, w_grow, w_shrink
        )
        grad_branch = grad_cross.astype(jnp.bfloat16)
        grad_cross_out = weight_dot(cross_mixed, grad_branch)
        grad_cross_mixed = back_dot(grad_branch, w_link[:, D:]).astype(jnp.bfloat16)
        grad_cq, grad_ck, grad_cv = attend_back(
            query_low, cross_keys, cross_values, across, cross_total, grad_cross_mixed
        )
        query_grad = grad_cq.astype(jnp.bfloat16)
        link_grad = jnp.concatenate([grad_ck, grad_cv], axis=1).astype(jnp.bfloat16)
        grad_query_weight = weight_dot(self_low, query_grad)
        grad_self = grad_cross + back_dot(query_grad, w_link[:, :D])
        grad_attn = grad_self.astype(jnp.bfloat16)
        grad_mix = weight_dot(mixed_heads, grad_attn)
        grad_mixed = back_dot(grad_attn, w_mix).astype(jnp.bfloat16)
        grad_query, grad_keys, grad_values = attend_back(
            projected[:, :D],
            projected[:, D : 2 * D],
            projected[:, 2 * D :],
            own_mask,
            log_total,
            grad_mixed,
        )
        grad_proj = jnp.concatenate([grad_query, grad_keys, grad_values], axis=1).astype(
            jnp.bfloat16
        )
        grad_in = weight_dot(tokens_now, grad_proj)
        grad_tokens = grad_self + back_dot(grad_proj, w_in)
        grad_link = jnp.concatenate([grad_query_weight, grad_cross_out], axis=1)
        return (
            decoded.astype(jnp.bfloat16),
            grad_tokens.astype(jnp.bfloat16),
            link_grad,
            (grad_in, grad_mix, grad_link, grad_grow, grad_shrink),
        )

    def pick_section(first_value, second_value):
        return jnp.where(is_first, first_value, second_value)

    results = []
    grads_rows = []
    running = None
    for micro_step in range(MB):
        tokens_now = inputs[0, micro_step * ROWS : (micro_step + 1) * ROWS]
        upstream = cotangent[0, micro_step * ROWS : (micro_step + 1) * ROWS]
        seg_src = segments(lengths[micro_step, 0], position)
        seg_tgt = segments(lengths[micro_step, 1], position)
        link_keys, stored = lax.cond(is_first, encode, silenced(encode), (tokens_now, seg_src))
        arrived = from_behind(link_keys, "section", 1)
        decoded, grad_target, link_grad, decoder_grads = lax.cond(
            is_first, silenced(decode), decode, (tokens_now, upstream, arrived, seg_src, seg_tgt)
        )
        returned = from_behind(link_grad, "section", -1)
        grad_source, encoder_grads = lax.cond(
            is_first,
            encode_back,
            silenced(encode_back),
            (tokens_now, upstream, returned, seg_src, stored),
        )
        results.append(pick_section(stored[6], decoded))
        grads_rows.append(pick_section(grad_source, grad_target))
        current = jax.tree.map(pick_section, encoder_grads, decoder_grads)
        running = current if running is None else jax.tree.map(jnp.add, running, current)
    running = lax.psum((running[0], running[1], running[2], running[3], running[4]), "dp")
    outputs = jnp.concatenate(results, axis=0)[None]
    input_grad = jnp.concatenate(grads_rows, axis=0)[None]
    return (
        outputs,
        input_grad,
        running[0][None],
        running[1][None],
        running[2][None],
        running[3][None],
        running[4][None],
    )


def solution(mesh):
    return jax.shard_map(
        on_device,
        mesh=mesh,
        in_specs=(
            P("section", "dp", None),
            P("dp", None, None),
            P("section", None, None),
            P("section", None, None),
            P("section", None, None),
            P("section", None, None),
            P("section", None, None),
            P("section", "dp", None),
        ),
        out_specs=(
            P("section", "dp", None),
            P("section", "dp", None),
            P("section", None, None),
            P("section", None, None),
            P("section", None, None),
            P("section", None, None),
            P("section", None, None),
        ),
        check_vma=False,
    )
```

profile of v0, /device:TPU:0, one launch (start us, length us, event | category | flops | bytes accessed | tf_op | source)
XLA Modules:
  0.0 500.3 jit_solution(2599317343951684615)
XLA Ops:
  9.8 11.0 %conditional.8 = (bf16[128,1024]{1,0:T(8,128)(2,1)S(1)}, bf16[128,1536]{1,0:T(8,128)(2,1)S(1)}, f32[8,128,1]{1,0,2:T(8,128)S(1)}, bf16[128,512]{0,1:T(8,128)(2,1...) conditional(s32[]{:T(128)} %convert_element_type.310, () %tuple.60, ...), branch_computations={%region_18.19_spmd, %region_19.22_spmd} | conditional | flops 977222656 | bytes 42009348 | solution.py:250
  10.6 1.8 convolution_convert_fusion.11
  14.8 2.5 fusion.63
  17.4 2.3 fusion.55
  19.6 1.2 convolution_convert_fusion.12
  21.9 2.0 collective-permute-start.1
  24.8 11.1 %conditional.6 = (bf16[128,1024]{1,0:T(8,128)(2,1)S(1)}, bf16[128,1536]{1,0:T(8,128)(2,1)S(1)}, f32[8,128,1]{1,0,2:T(8,128)S(1)}, bf16[128,512]{0,1:T(8,128)(2,1...) conditional(s32[]{:T(128)} %convert_element_type.310, () %tuple.56, ...), branch_computations={%region_2.3_spmd, %region_3.0_spmd} | conditional | flops 977222656 | bytes 42009348 | solution.py:250
  25.7 1.8 convolution_convert_fusion
  29.9 2.5 fusion.9
  32.4 2.3 fusion.1
  34.7 1.2 convolution_convert_fusion.1
  36.7 1.3 collective-permute-start
  39.8 4.6 collective-permute-done
  44.5 12.4 %conditional.7 = (bf16[128,512]{1,0:T(8,128)(2,1)}, bf16[128,512]{1,0:T(8,128)(2,1)}, bf16[128,1024]{0,1:T(8,128)(2,1)}, f32[512,512]{1,0:T(8,128)}, f32[512,204...) conditional(s32[]{:T(128)} %convert_element_type.310, ...), branch_computations={%region_7.15_spmd, %region_15.16_spmd} | conditional | flops 3040147456 | bytes 124963768 | solution.py:252
  48.2 1.6 broadcast.405.clone
  49.8 2.0 broadcast.403.clone
  51.8 2.6 broadcast.407
  54.3 2.5 broadcast.406
  56.8 1.8 copy.227
  58.6 1.3 collective-permute-start.2
  60.7 12.1 %conditional.9 = (bf16[128,512]{1,0:T(8,128)(2,1)}, bf16[128,512]{1,0:T(8,128)(2,1)}, bf16[128,1024]{0,1:T(8,128)(2,1)}, f32[512,512]{1,0:T(8,128)}, f32[512,204...) conditional(s32[]{:T(128)} %convert_element_type.310, ...), branch_computations={%region_23.31_spmd, %region_31.32_spmd} | conditional | flops 3040147456 | bytes 124963768 | solution.py:252
  64.0 1.6 broadcast.431.clone
  65.6 2.0 broadcast.429.clone
  67.7 2.5 broadcast.433
  70.2 2.5 broadcast.432
  72.7 1.8 copy.230
  74.5 1.3 collective-permute-start.3
  75.8 22.4 %collective-permute-done.2 = bf16[128,1024]{1,0:T(8,128)(2,1)} collective-permute-done((bf16[128,1024]{1,0:T(8,128)(2,1)}, bf16[128,1024]{1,0:T(8,128)(2,1)}, u32[]{:S(2)}, u32[]{:S(2)}) %collective-permute-start.2) | collective-permute-done | bytes 262176 | tf_op jit(solution)/shard_map/ppermute | solution.py:16
  98.2 37.8 %conditional.10 = (bf16[128,512]{1,0:T(8,128)(2,1)S(1)}, f32[512,1024]{1,0:T(8,128)}, f32[512,1536]{1,0:T(8,128)}, f32[512,512]{1,0:T(8,128)}, f32[512,2048]{1,0:T(8,128)}, /*index=5*/f32[2048,512]{1,0:T(8,128)}) conditional(s32[]{:T(128)} %convert_element_type.310, () %tuple.64, (bf16[128,512]{1,0:T(8,128)(2,1)}, bf16[128,1024]{1,0:T(8,128)(2,1)}, ...), branch_computations={%region_32.33_spmd, %region_33.35_spmd} | conditional | flops 1972714496 | bytes 89060312 | solution.py:256
  99.2 1.8 convolution_add_fusion.18
  101.0 3.1 fusion.120
  107.8 1.3 fusion.113
  109.5 1.3 copy.282
  110.8 2.8 fusion.175
  113.6 1.5 convolution_bitcast_fusion.2
  115.1 2.3 copy.280
  117.4 3.9 convolution_bitcast_fusion.3
  121.3 5.5 %copy.286 = f32[2048,512]{1,0:T(8,128)} copy(f32[2048,512]{0,1:T(8,128)} %convolution_bitcast_fusion.3) | data formatting | bytes 8388608 | tf_op jit(solution)/shard_map/cond | solution.py:256
  126.8 3.7 convolution_bitcast_fusion.4
  130.5 5.4 %copy.284 = f32[512,2048]{1,0:T(8,128)} copy(f32[512,2048]{0,1:T(8,128)} %convolution_bitcast_fusion.4) | data formatting | bytes 8388608 | tf_op jit(solution)/shard_map/cond | solution.py:256
  136.0 7.4 %collective-permute-done.3 = bf16[128,1024]{1,0:T(8,128)(2,1)} collective-permute-done((bf16[128,1024]{1,0:T(8,128)(2,1)}, bf16[128,1024]{1,0:T(8,128)(2,1)}, u32[]{:S(2)}, u32[]{:S(2)}) %collective-permute-start.3) | collective-permute-done | bytes 262176 | tf_op jit(solution)/shard_map/ppermute | solution.py:16
  143.3 36.9 %conditional.11 = (bf16[128,512]{1,0:T(8,128)(2,1)}, f32[512,1024]{1,0:T(8,128)}, f32[512,1536]{1,0:T(8,128)}, f32[512,512]{1,0:T(8,128)}, f32[512,2048]{1,0:T(8,128)}, /*index=5*/f32[2048,512]{1,0:T(8,128)}) conditional(s32[]{:T(128)} %convert_element_type.310, () %tuple.66, (bf16[128,512]{1,0:T(8,128)(2,1)S(1)}, bf16[128,1024]{1,0:T(8,128)(2,1)}, ...), branch_computations={%region_35.36_spmd, %region_36.38_spmd} | conditional | flops 1972714496 | bytes 89043864 | solution.py:256
  144.3 1.8 convolution_add_fusion.21
  146.2 3.1 fusion.143
  152.9 1.3 fusion.136
  154.6 1.3 copy.290
  155.9 2.9 fusion.177
  159.3 2.3 copy.288
  161.7 3.8 convolution_bitcast_fusion.7
  165.5 5.4 %copy.294 = f32[2048,512]{1,0:T(8,128)} copy(f32[2048,512]{0,1:T(8,128)} %convolution_bitcast_fusion.7) | data formatting | bytes 8388608 | tf_op jit(solution)/shard_map/cond | solution.py:256
  170.9 3.7 convolution_bitcast_fusion.8
  174.6 5.4 %copy.292 = f32[512,2048]{1,0:T(8,128)} copy(f32[512,2048]{0,1:T(8,128)} %convolution_bitcast_fusion.8) | data formatting | bytes 8388608 | tf_op jit(solution)/shard_map/cond | solution.py:256
  180.3 7.6 %add_bitcast_fusion.2 = f32[1,2048,512]{2,1,0:T(8,128)} fusion(f32[2048,512]{1,0:T(8,128)} %get-tuple-element.458, f32[2048,512]{1,0:T(8,128)} %get-tuple-element.302, f32[2048,512]{1,0:T(8,128)} %get-tuple-element.454, f32[2048,512]{1,0:T(8,128)} %get-tuple-element.300, pred[]{:T(512)S(6)} %eq.135), kind=kLoop, calls=%fused_computation.286 | loop fusion | flops 3145728 | bytes 20971520 | tf_op jit(solution)/shard_map/broadcast_in_dim | solution.py:276
  187.9 7.8 %add_bitcast_fusion.3 = f32[1,512,2048]{2,1,0:T(8,128)} fusion(f32[512,2048]{1,0:T(8,128)} %get-tuple-element.457, f32[512,2048]{1,0:T(8,128)} %get-tuple-element.298, f32[512,2048]{1,0:T(8,128)} %get-tuple-element.453, f32[512,2048]{1,0:T(8,128)} %get-tuple-element.296, pred[]{:T(512)S(6)} %eq.135), kind=kLoop, calls=%fused_computation.287 | loop fusion | flops 3145728 | bytes 20971520 | tf_op jit(solution)/shard_map/broadcast_in_dim | solution.py:275
  195.7 4.7 add_bitcast_fusion.5
  200.4 3.0 add_bitcast_fusion.6
  203.4 5.9 %add_bitcast_fusion.4 = f32[1,512,1536]{2,1,0:T(8,128)} fusion(f32[512,1536]{1,0:T(8,128)} %get-tuple-element.455, f32[512,1536]{1,0:T(8,128)} %get-tuple-element.449, f32[512,1536]{1,0:T(8,128)} %get-tuple-element.451, f32[512,1536]{1,0:T(8,128)} %get-tuple-element.447, pred[]{:T(512)S(6)} %eq.135), kind=kLoop, calls=%fused_computation.288 | loop fusion | flops 2359296 | bytes 15728641 | tf_op jit(solution)/shard_map/broadcast_in_dim | solution.py:272
  213.6 264.9 %all-reduce.3.cloned.1.call-done = (f32[1,512,1536]{2,1,0:T(8,128)}, f32[1,512,512]{2,1,0:T(8,128)}, f32[1,512,1024]{2,1,0:T(8,128)}, f32[1,512,2048]{2,1,0:T(8,128)}, f32[1,2048,512]{2,1,0:T(8,128)}) async-done(((f32[1,512,1536]{2,1,0:T(8,128)}, f32[1,512,512]{2,1,0:T(8,128)}, f32[1,512,1024]{2,1,0:T(8,128)}, f32[1,512,2048]{2,1,0:T(8,128)}, f32[1,2048,512]{2,1,0:T(8,128)}), (f32[1,512,1536]{2,1,0:T(8,128)}, ...) | async-done | bytes 14680080 | tf_op jit(solution)/shard_map/psum | solution.py:266
  478.5 3.8 copy.388
  484.3 1.3 copy.390
  485.7 1.6 copy-done.25
  487.3 2.1 copy.391
  489.4 1.6 copy-done.24
  491.0 2.0 copy.392
  (197 shorter events, 36.7 us)
Async XLA Ops:
  7.2 471.4 %all-reduce.3.cloned.1.call-start = ((), (), s32[]{:S(2)}) async-start(), calls=%async_computation | async-start | bytes 29360128 | tf_op jit(solution)/shard_map/psum | solution.py:266
  12.4 1.1 copy-start.26
  12.5 1.2 copy-start.4
  13.1 1.7 copy-start.10
  13.5 3.9 copy-start.62
  14.5 2.8 copy-start.16
  17.4 2.3 copy-start
  17.4 3.5 copy-start.27
  20.9 3.9 copy-start.110
  20.9 3.9 copy-start.71
  20.9 3.9 copy-start.28
  21.9 38.8 %collective-permute-start.1 = (bf16[128,1024]{0,1:T(8,128)(2,1)}, bf16[128,1024]{0,1:T(8,128)(2,1)}, u32[]{:S(2)}, u32[]{:S(2)}) collective-permute-start(bf16[128,1024]{0,1:T(8,128)(2,1)} %copy.226), channel_id=1, source_target_pairs={{0,16},{1,17},{2,18},{3,19},{4,20},{5,21},{6,22},{7,23},{8,24},{9,... | collective-permute-start | bytes 786440 | tf_op jit(solution)/shard_map/ppermute | solution.py:16
  24.8 13.2 %copy-start.109 = (bf16[1,256,512]{2,1,0:T(8,128)(2,1)S(1)}, bf16[1,256,512]{2,1,0:T(8,128)(2,1)}, u32[]{:S(2)}) copy-start(bf16[1,256,512]{2,1,0:T(8,128)(2,1)} %param.27) | copy-start | bytes 786436
  27.5 1.1 copy-start.30
  27.5 1.2 copy-start.5
  28.2 1.7 copy-start.11
  28.6 3.9 copy-start.64
  29.6 2.8 copy-start.17
  32.4 2.3 copy-start.1
  32.4 3.5 copy-start.31
  35.9 0.6 copy-start.112
  36.5 7.9 %copy-start.72 = (f32[128,2048]{1,0:T(8,128)}, f32[128,2048]{1,0:T(8,128)S(1)}, u32[]{:S(2)}) copy-start(f32[128,2048]{1,0:T(8,128)S(1)} %get-tuple-element.266) | copy-start | bytes 3145732
  36.5 7.9 %copy-start.32 = (bf16[128,1536]{1,0:T(8,128)(2,1)}, bf16[128,1536]{1,0:T(8,128)(2,1)S(1)}, u32[]{:S(2)}) copy-start(bf16[128,1536]{1,0:T(8,128)(2,1)S(1)} %get-tuple-element.267) | copy-start | bytes 1179652
  36.7 7.8 %collective-permute-start = (bf16[128,1024]{0,1:T(8,128)(2,1)S(1)}, bf16[128,1024]{0,1:T(8,128)(2,1)S(1)}, u32[]{:S(2)}, u32[]{:S(2)}) collective-permute-start(bf16[128,1024]{0,1:T(8,128)(2,1)S(1)} %copy.223), channel_id=1, source_target_pairs={{0,16},{1,17},{2,18},{3,19},{4,20},{5,21},{6,22},{7,23},{8,24},{9,... | collective-permute-start | bytes 786440 | tf_op jit(solution)/shard_map/ppermute | solution.py:16
  58.6 39.6 %collective-permute-start.2 = (bf16[128,1024]{1,0:T(8,128)(2,1)}, bf16[128,1024]{1,0:T(8,128)(2,1)}, u32[]{:S(2)}, u32[]{:S(2)}) collective-permute-start(bf16[128,1024]{1,0:T(8,128)(2,1)} %copy.227), channel_id=1, source_target_pairs={{16,0},{17,1},{18,2},{19,3},{20,4},{21,5},{22,6},{23,7},{24,8},{25... | collective-permute-start | bytes 786440 | tf_op jit(solution)/shard_map/ppermute | solution.py:16
  74.5 68.8 %collective-permute-start.3 = (bf16[128,1024]{1,0:T(8,128)(2,1)}, bf16[128,1024]{1,0:T(8,128)(2,1)}, u32[]{:S(2)}, u32[]{:S(2)}) collective-permute-start(bf16[128,1024]{1,0:T(8,128)(2,1)} %copy.230), channel_id=1, source_target_pairs={{16,0},{17,1},{18,2},{19,3},{20,4},{21,5},{22,6},{23,7},{24,8},{25... | collective-permute-start | bytes 786440 | tf_op jit(solution)/shard_map/ppermute | solution.py:16
  98.2 45.1 %copy-start.111 = (f32[8,128,1]{1,0,2:T(8,128)S(1)}, f32[8,128,1]{1,0,2:T(8,128)}, u32[]{:S(2)}) copy-start(f32[8,128,1]{1,0,2:T(8,128)} %copy-done.110) | copy-start | bytes 12292
  101.0 3.1 copy-start.34
  101.0 3.1 copy-start.14
  104.1 1.7 copy-start.42
  104.1 1.2 copy-start.8
  104.1 1.7 copy-start.33
  105.4 1.0 copy-start.113
  106.4 1.4 copy-start.22
  106.8 2.3 copy-start.65
  107.1 2.3 copy-start.89
  107.4 2.0 copy-start.93
  107.6 3.2 copy-start.97
  110.8 2.8 copy-start.90
  110.8 2.8 copy-start.94
  121.3 5.5 %copy-start.43 = (bf16[128,2048]{1,0:T(8,128)(2,1)S(1)}, bf16[128,2048]{1,0:T(8,128)(2,1)}, u32[]{:S(2)}) copy-start(bf16[128,2048]{1,0:T(8,128)(2,1)} %copy-done.42) | copy-start | bytes 1572868 | tf_op jit(solution)/shard_map/cond
  130.5 5.4 %copy-start.98 = (bf16[128,512]{1,0:T(8,128)(2,1)S(1)}, bf16[128,512]{1,0:T(8,128)(2,1)}, u32[]{:S(2)}) copy-start(bf16[128,512]{1,0:T(8,128)(2,1)} %fusion.113) | copy-start | bytes 393220 | tf_op jit(solution)/shard_map/cond
  136.0 7.4 %copy-start.99 = (bf16[128,512]{1,0:T(8,128)(2,1)}, bf16[128,512]{1,0:T(8,128)(2,1)S(1)}, u32[]{:S(2)}) copy-start(bf16[128,512]{1,0:T(8,128)(2,1)S(1)} %get-tuple-element.272) | copy-start | bytes 393220
  146.1 3.1 copy-start.35
  146.2 3.1 copy-start.15
  149.2 1.7 copy-start.44
  149.3 1.2 copy-start.9
  149.3 1.7 copy-start.29
  151.5 1.4 copy-start.23
  151.9 2.3 copy-start.63
  152.2 2.3 copy-start.91
  152.5 2.1 copy-start.95
  155.9 2.9 copy-start.92
  155.9 2.9 copy-start.96
  159.3 2.3 copy-start.36
  165.5 5.4 %copy-start.45 = (bf16[128,2048]{1,0:T(8,128)(2,1)S(1)}, bf16[128,2048]{1,0:T(8,128)(2,1)}, u32[]{:S(2)}) copy-start(bf16[128,2048]{1,0:T(8,128)(2,1)} %copy-done.44) | copy-start | bytes 1572868 | tf_op jit(solution)/shard_map/cond
  209.3 2.7 copy-start.100
  478.5 3.8 copy-start.70
  482.4 2.0 copy-start.37
  484.3 2.9 copy-start.25
  487.3 3.7 copy-start.24
Sparse Core Ops, SparseCore 0:
  209.5 269.0 all-reduce.2
where the time goes:
time: 506 us; the launch traced here: 500 us
  waiting for transfers between devices  299 us (59%)
  local copies, waits for them, and re-layouts  78.9 us (16%)
  matrix products  59.3 us (12%)
  other arithmetic  40.1 us (8%)
  between operations  14.7 us (3%)
  starting transfers between devices  5.91 us (1%)
    psum x1, waiting for transfers between devices, on_device(): lax.psum((running[0], running[1], running[2], running[3], running[4]), 'dp')  265 us
    ppermute x4, waiting for transfers between devices, from_behind(): return lax.ppermute(block, axis, route)  34.4 us
    cond x8, local copies, waits for them, and re-layouts, on_device(): lax.cond(is_first, encode_back, silenced(encode_back), (tokens_now, upstr...  29 us
    another operation x23, local copies, waits for them, and re-layouts  25.2 us
    dot_general x10, matrix products, weight_dot(): lax.dot_general(values_in, grad_in, (((0,), (0,)), ((), ())), preferred_e...  23.5 us
    dot_general x10, matrix products, forward_dot(): return jnp.dot(values_in, weight, preferred_element_type=jnp.float32)  17.4 us
    unnamed x33, local copies, waits for them, and re-layouts  15.1 us
    dot_general x10, matrix products, back_dot(): lax.dot_general(grad_in, weight, (((1,), (1,)), ((), ())), preferred_elem...  14.7 us
  transfers between devices with their start and end apart: 5, of which 4 were waited for; matrix products, arithmetic and copies ran while one was open for 16% of the time, Pallas kernels for 0%

commit v1 on v0

v1 whole, which is shorter than its diff:
```python
import functools

import jax
import jax.numpy as jnp
from jax import lax
from jax.experimental import pallas as pl
from jax.experimental.pallas import tpu as pltpu
from jax.sharding import PartitionSpec as P

D = 512
HEADS = 8
HEAD_DIM = 64
FF = 2048
ROWS = 128
SLOTS = 16
MB = 2
PAIRS = HEADS // 2
LANES = 2 * HEAD_DIM
HALF = D // 2
SCALE = HEAD_DIM ** (-0.5)
GELU_IN = 0.7978845608028654
GELU_CUBE = 0.044715
LOW = jnp.bfloat16
F32 = jnp.float32
VMEM_LIMIT = 48 * 1024 * 1024

CROSS_AT, UP_AT, DOWN_AT, OUT_AT, QKV_AT = 0, 2, 6, 10, 11
BLOCKS = 14
EARLY = 10
LATE = BLOCKS - EARLY


def mm(left, right):
    return jnp.dot(left, right, preferred_element_type=F32)


def mm_nt(left, right):
    return lax.dot_general(left, right, (((1,), (1,)), ((), ())), preferred_element_type=F32)


def mm_tn(left, right):
    return lax.dot_general(left, right, (((0,), (0,)), ((), ())), preferred_element_type=F32)


def gelu(hidden):
    inner = GELU_IN * (hidden + GELU_CUBE * (hidden * hidden * hidden))
    return hidden * (0.5 * (1.0 + jnp.tanh(inner)))


def gelu_slope(hidden):
    square = hidden * hidden
    inner = GELU_IN * (hidden + GELU_CUBE * (square * hidden))
    bent = jnp.tanh(inner)
    inner_slope = GELU_IN * (1.0 + (3.0 * GELU_CUBE) * square)
    return 0.5 * (1.0 + bent) + 0.5 * hidden * (1.0 - bent * bent) * inner_slope


def segments(lengths_ref, micro, which, dim):
    position = lax.broadcasted_iota(jnp.int32, (ROWS, ROWS), dim)
    end = jnp.int32(0)
    seg = jnp.zeros((ROWS, ROWS), jnp.int32)
    for slot in range(SLOTS):
        end = end + lengths_ref[micro, which, slot]
        seg = seg + (position >= end).astype(jnp.int32)
    return seg


def low_lanes():
    return lax.broadcasted_iota(jnp.int32, (ROWS, LANES), 1) < HEAD_DIM


def two_heads(pair, lanes):
    nothing = jnp.zeros_like(pair)
    return jnp.concatenate(
        [jnp.where(lanes, pair, nothing), jnp.where(lanes, nothing, pair)], axis=0
    )


def softmax(scores):
    highest = jnp.max(scores, axis=1, keepdims=True)
    raised = jnp.exp(scores - highest)
    return raised * (1.0 / jnp.sum(raised, axis=1, keepdims=True))


def attend(read_q, read_k, read_v, mask, write_probs, write_mix):
    lanes = low_lanes()
    for pair in range(PAIRS):
        query = (read_q(pair).astype(F32) * SCALE).astype(LOW)
        scores = mm_nt(query, two_heads(read_k(pair), lanes))
        probs = jnp.concatenate(
            [
                softmax(jnp.where(mask, scores[:, :ROWS], -1e30)),
                softmax(jnp.where(mask, scores[:, ROWS:], -1e30)),
            ],
            axis=1,
        )
        write_probs(pair, probs)
        write_mix(pair, mm(probs.astype(LOW), two_heads(read_v(pair), lanes)).astype(LOW))


def attend_back(read_q, read_k, read_v, read_probs, read_grad, write):
    lanes = low_lanes()
    for pair in range(PAIRS):
        query = (read_q(pair).astype(F32) * SCALE).astype(LOW)
        probs = read_probs(pair)
        grad = read_grad(pair)
        grad_probs = mm_nt(grad, two_heads(read_v(pair), lanes))
        product = probs * grad_probs
        slopes = []
        for head in range(2):
            cut = slice(head * ROWS, (head + 1) * ROWS)
            total = jnp.sum(product[:, cut], axis=1, keepdims=True)
            slopes.append((probs[:, cut] * (grad_probs[:, cut] - total)).astype(LOW))
        probs_low = probs.astype(LOW)
        grad_q = mm(jnp.concatenate(slopes, axis=1), two_heads(read_k(pair), lanes)) * SCALE
        grad_k = mm_tn(jnp.concatenate(slopes, axis=0), two_heads(query, lanes))
        grad_v = mm_tn(
            jnp.concatenate([probs_low[:, :ROWS], probs_low[:, ROWS:]], axis=0),
            two_heads(grad, lanes),
        )
        write(pair, grad_q.astype(LOW), grad_k.astype(LOW), grad_v.astype(LOW))


def columns(ref, start):
    def read(pair):
        return ref[:, start + pair * LANES : start + (pair + 1) * LANES]

    return read


def fetch(source, target, sem):
    copy = pltpu.make_async_copy(source, target, sem)
    copy.start()
    return copy


def forward_kernel(
    micro,
    section_ref,
    lengths_ref,
    tokens_ref,
    w_qkv,
    w_out,
    w_cross,
    w_up,
    w_down,
    proj,
    mix,
    mid_low,
    wide,
    act,
    memory,
    link,
    probs,
    qkv_v,
    out_v,
    cross_v,
    up_v,
    down_v,
    sems,
):
    first = section_ref[0] == 0
    get_qkv = fetch(w_qkv.at[0], qkv_v, sems.at[0])
    get_out = fetch(w_out.at[0], out_v, sems.at[1])
    get_cross = pltpu.make_async_copy(w_cross.at[0], cross_v, sems.at[2])
    get_up = pltpu.make_async_copy(w_up.at[0], up_v, sems.at[3])
    get_down = pltpu.make_async_copy(w_down.at[0], down_v, sems.at[4])

    @pl.when(first)
    def _():
        get_up.start()
        get_down.start()

    get_cross.start()

    tokens = tokens_ref[0, micro * ROWS : (micro + 1) * ROWS, :]
    seg_q_src = segments(lengths_ref, micro, 0, 0)
    seg_k_src = segments(lengths_ref, micro, 0, 1)
    seg_q_tgt = segments(lengths_ref, micro, 1, 0)
    seg_k_tgt = segments(lengths_ref, micro, 1, 1)
    later = lax.broadcasted_iota(jnp.int32, (ROWS, ROWS), 0) >= lax.broadcasted_iota(
        jnp.int32, (ROWS, ROWS), 1
    )
    source_mask = (seg_q_src == seg_k_src).astype(jnp.int32)
    target_mask = ((seg_q_tgt == seg_k_tgt) & later).astype(jnp.int32)
    mask = jnp.where(first, source_mask, target_mask) != 0

    get_qkv.wait()
    for part in range(3):
        cut = slice(part * D, (part + 1) * D)
        proj[:, cut] = mm(tokens, qkv_v[:, cut]).astype(LOW)

    def write_probs(pair, value):
        probs[pair] = value

    def write_mix(pair, value):
        mix[:, pair * LANES : (pair + 1) * LANES] = value

    attend(columns(proj, 0), columns(proj, D), columns(proj, 2 * D), mask, write_probs, write_mix)
    get_out.wait()
    mid = tokens.astype(F32) + mm(mix[...], out_v[...])
    mid_low[...] = mid.astype(LOW)

    @pl.when(first)
    def _():
        get_up.wait()
        get_down.wait()
        total = mid
        for part in range(4):
            cut = slice(part * D, (part + 1) * D)
            hidden = mm(mid_low[...], up_v[:, cut])
            wide[:, cut] = hidden
            act[:, cut] = gelu(hidden).astype(LOW)
            total = total + mm(act[:, cut], down_v[cut, :])
        memory[...] = total.astype(LOW)
        get_cross.wait()
        for part in range(2):
            cut = slice(part * D, (part + 1) * D)
            link[:, cut] = mm(memory[...], cross_v[:, cut]).astype(LOW)

    @pl.when(jnp.logical_not(first))
    def _():
        wide[:, :D] = mid
        get_cross.wait()
        link[:, :D] = mm(mid_low[...], cross_v[:, :D]).astype(LOW)


def whole():
    return pl.BlockSpec(memory_space=pltpu.VMEM)


def in_smem():
    return pl.BlockSpec(memory_space=pltpu.SMEM)


def anywhere():
    return pl.BlockSpec(memory_space=pl.ANY)


def forward_stage(micro, section, lengths, tokens, weights):
    shapes = (
        ((ROWS, 3 * D), LOW),
        ((ROWS, D), LOW),
        ((ROWS, D), LOW),
        ((ROWS, FF), F32),
        ((ROWS, FF), LOW),
        ((ROWS, D), LOW),
        ((ROWS, 2 * D), LOW),
        ((PAIRS, ROWS, 2 * ROWS), F32),
    )
    return pl.pallas_call(
        functools.partial(forward_kernel, micro),
        out_shape=[jax.ShapeDtypeStruct(s, t) for s, t in shapes],
        in_specs=[in_smem(), in_smem(), whole()] + [anywhere()] * 5,
        out_specs=[pl.BlockSpec(memory_space=pltpu.VMEM)] * len(shapes),
        scratch_shapes=[
            pltpu.VMEM((D, 3 * D), LOW),
            pltpu.VMEM((D, D), LOW),
            pltpu.VMEM((D, 2 * D), LOW),
            pltpu.VMEM((D, FF), LOW),
            pltpu.VMEM((FF, D), LOW),
            pltpu.SemaphoreType.DMA((5,)),
        ],
        compiler_params=pltpu.CompilerParams(vmem_limit_bytes=VMEM_LIMIT),
        cost_estimate=pl.CostEstimate(
            flops=2 * ROWS * D * 7168, bytes_accessed=10_000_000, transcendentals=400_000
        ),
        name="forward_stage",
    )(section, lengths, tokens, *weights)


def middle_kernel(
    micro,
    section_ref,
    lengths_ref,
    mid_ref,
    query_ref,
    link_ref,
    cotangent_ref,
    w_cross,
    w_up,
    w_down,
    decoded,
    link_grad,
    cross_low,
    cross_mix,
    act,
    grad_hidden,
    cross_grad_low,
    query_grad,
    cross_grad,
    cross_v,
    up_v,
    down_v,
    hidden_v,
    probs_v,
    mixed_v,
    mid_v,
    query_v,
    sems,
):
    @pl.when(section_ref[0] != 0)
    def _():
        get_query = fetch(query_ref.at[:, pl.ds(0, D)], query_v, sems.at[3])
        get_mid = fetch(mid_ref.at[:, pl.ds(0, D)], mid_v, sems.at[4])
        get_cross = fetch(w_cross.at[0], cross_v, sems.at[0])
        get_up = fetch(w_up.at[0], up_v, sems.at[1])
        get_down = fetch(w_down.at[0], down_v, sems.at[2])
        mask = segments(lengths_ref, micro, 1, 0) == segments(lengths_ref, micro, 0, 1)

        def write_probs(pair, value):
            probs_v[pair] = value

        def write_mix(pair, value):
            cross_mix[:, pair * LANES : (pair + 1) * LANES] = value

        read_q, read_k, read_v = columns(query_v, 0), columns(link_ref, 0), columns(link_ref, D)
        get_query.wait()
        attend(read_q, read_k, read_v, mask, write_probs, write_mix)
        get_mid.wait()
        get_cross.wait()
        after = mid_v[...] + mm(cross_mix[...], cross_v[:, D:])
        cross_low[...] = after.astype(LOW)
        get_up.wait()
        get_down.wait()
        total = after
        for part in range(4):
            cut = slice(part * D, (part + 1) * D)
            hidden = mm(cross_low[...], up_v[:, cut])
            hidden_v[:, cut] = hidden
            act[:, cut] = gelu(hidden).astype(LOW)
            total = total + mm(act[:, cut], down_v[cut, :])
        decoded[...] = total.astype(LOW)
        grad_low = cotangent_ref[0, micro * ROWS : (micro + 1) * ROWS, :]
        grad = grad_low.astype(F32)
        for part in range(4):
            cut = slice(part * D, (part + 1) * D)
            grad_act = mm_nt(grad_low, down_v[cut, :])
            grad_hidden[:, cut] = (gelu_slope(hidden_v[:, cut]) * grad_act).astype(LOW)
            grad = grad + mm_nt(grad_hidden[:, cut], up_v[:, cut])
        cross_grad[...] = grad
        cross_grad_low[...] = grad.astype(LOW)
        mixed_v[...] = mm_nt(cross_grad_low[...], cross_v[:, D:]).astype(LOW)

        def write(pair, grad_q, grad_k, grad_v):
            query_grad[:, pair * LANES : (pair + 1) * LANES] = grad_q
            link_grad[:, pair * LANES : (pair + 1) * LANES] = grad_k
            link_grad[:, D + pair * LANES : D + (pair + 1) * LANES] = grad_v

        attend_back(read_q, read_k, read_v, lambda pair: probs_v[pair], columns(mixed_v, 0), write)


def middle_stage(micro, section, lengths, mid, query, link, cotangent, w_cross, w_up, w_down):
    shapes = (
        ((ROWS, D), LOW),
        ((ROWS, 2 * D), LOW),
        ((ROWS, D), LOW),
        ((ROWS, D), LOW),
        ((ROWS, FF), LOW),
        ((ROWS, FF), LOW),
        ((ROWS, D), LOW),
        ((ROWS, D), LOW),
        ((ROWS, D), F32),
    )
    return pl.pallas_call(
        functools.partial(middle_kernel, micro),
        out_shape=[jax.ShapeDtypeStruct(s, t) for s, t in shapes],
        in_specs=[
            in_smem(),
            in_smem(),
            anywhere(),
            anywhere(),
            whole(),
            whole(),
            anywhere(),
            anywhere(),
            anywhere(),
        ],
        out_specs=[pl.BlockSpec(memory_space=pltpu.VMEM)] * len(shapes),
        scratch_shapes=[
            pltpu.VMEM((D, 2 * D), LOW),
            pltpu.VMEM((D, FF), LOW),
            pltpu.VMEM((FF, D), LOW),
            pltpu.VMEM((ROWS, FF), F32),
            pltpu.VMEM((PAIRS, ROWS, 2 * ROWS), F32),
            pltpu.VMEM((ROWS, D), LOW),
            pltpu.VMEM((ROWS, D), F32),
            pltpu.VMEM((ROWS, D), LOW),
            pltpu.SemaphoreType.DMA((5,)),
        ],
        compiler_params=pltpu.CompilerParams(vmem_limit_bytes=VMEM_LIMIT),
        cost_estimate=pl.CostEstimate(
            flops=2 * ROWS * D * 10000, bytes_accessed=8_000_000, transcendentals=600_000
        ),
        name="middle_stage",
    )(section, lengths, mid, query, link, cotangent, w_cross, w_up, w_down)


def put_block(core, keep, send, at, left_ref, left_at, right):
    own = pl.ds(pl.multiple_of(left_at + core * HALF, HALF), HALF)
    other = pl.ds(pl.multiple_of(left_at + (1 - core) * HALF, HALF), HALF)
    send[at] = mm_tn(left_ref[:, other], right).astype(LOW)
    keep[at] = mm_tn(left_ref[:, own], right)


def early_kernel(
    section_ref,
    core_ref,
    cotangent_ref,
    memory0,
    memory1,
    lg0,
    lg1,
    mid0,
    mid1,
    wide0,
    wide1,
    act0,
    act1,
    cl0,
    cl1,
    cm0,
    cm1,
    dact0,
    dact1,
    gh0,
    gh1,
    cgl0,
    cgl1,
    qg0,
    qg1,
    cg0,
    cg1,
    w_cross,
    w_up,
    w_down,
    keep,
    send,
    residual,
    a_v,
    b_v,
    z_v,
    g_v,
    act_v,
    gh_v,
    wide_v,
    lg_v,
    cross_v,
    up_v,
    down_v,
    sems,
):
    core = core_ref[0]
    first = section_ref[0] == 0
    get_cross = fetch(w_cross.at[0], cross_v, sems.at[0])

    def both(pair_refs, target, at):
        return [
            fetch(ref, target.at[pl.ds(i * ROWS, ROWS)], sems.at[at + i])
            for i, ref in enumerate(pair_refs)
        ]

    @pl.when(first)
    def _():
        gets_lg = both((lg0, lg1), lg_v, 1)
        gets_mem = both((memory0, memory1), a_v, 3)
        get_down = fetch(w_down.at[0], down_v, sems.at[5])
        gets_wide = both((wide0, wide1), wide_v, 6)
        gets_act = both((act0, act1), act_v, 8)
        get_up = fetch(w_up.at[0], up_v, sems.at[10])
        gets_z = both((mid0, mid1), z_v, 11)
        for copy in gets_lg:
            copy.wait()
        get_cross.wait()
        grad = cotangent_ref[0].astype(F32) + mm_nt(lg_v[...], cross_v[...])
        g_v[...] = grad.astype(LOW)
        for copy in gets_mem:
            copy.wait()
        for part in range(2):
            put_block(core, keep, send, CROSS_AT + part, a_v, 0, lg_v[:, part * D : (part + 1) * D])
        get_down.wait()
        for copy in gets_wide + gets_act + gets_z:
            copy.wait()
        get_up.wait()
        for part in range(4):
            cut = slice(part * D, (part + 1) * D)
            grad_act = mm_nt(g_v[...], down_v[cut, :])
            gh_v[:, cut] = (gelu_slope(wide_v[:, cut]) * grad_act).astype(LOW)
            grad = grad + mm_nt(gh_v[:, cut], up_v[:, cut])
            put_block(core, keep, send, UP_AT + part, z_v, 0, gh_v[:, cut])
            put_block(core, keep, send, DOWN_AT + part, act_v, part * D, g_v[...])
        residual[...] = grad

    @pl.when(jnp.logical_not(first))
    def _():
        gets = both((dact0, dact1), act_v, 1) + both((gh0, gh1), gh_v, 3)
        gets_z = both((cl0, cl1), z_v, 5)
        gets_q = both((qg0, qg1), lg_v.at[:, :D], 7) + both((cgl0, cgl1), lg_v.at[:, D:], 9)
        gets_a = both((mid0, mid1), a_v, 11) + both((cm0, cm1), b_v, 13)
        gets_c = both((cg0, cg1), wide_v.at[:, :D], 15)
        for copy in gets_q + gets_a + gets_c:
            copy.wait()
        get_cross.wait()
        put_block(core, keep, send, CROSS_AT, a_v, 0, lg_v[:, :D])
        put_block(core, keep, send, CROSS_AT + 1, b_v, 0, lg_v[:, D:])
        residual[...] = wide_v[:, :D] + mm_nt(lg_v[:, :D], cross_v[:, :D])
        for copy in gets + gets_z:
            copy.wait()
        for part in range(4):
            cut = slice(part * D, (part + 1) * D)
            put_block(core, keep, send, UP_AT + part, z_v, 0, gh_v[:, cut])
            put_block(core, keep, send, DOWN_AT + part, act_v, part * D, cotangent_ref[0])


def early_stage(section, core, cotangent, ones, twos, weights):
    operands = [section, core, cotangent]
    for name in ("memory", "lg", "mid_low", "wide", "act"):
        operands += [one[name] for one in ones]
    for name in (
        "cross_low",
        "cross_mix",
        "act",
        "grad_hidden",
        "cross_grad_low",
        "query_grad",
        "cross_grad",
    ):
        operands += [two[name] for two in twos]
    operands += list(weights)
    return pl.pallas_call(
        early_kernel,
        out_shape=[
            jax.ShapeDtypeStruct((EARLY, HALF, D), F32),
            jax.ShapeDtypeStruct((EARLY, HALF, D), LOW),
            jax.ShapeDtypeStruct((MB * ROWS, D), F32),
        ],
        in_specs=[in_smem(), in_smem(), whole()] + [anywhere()] * (len(operands) - 3),
        out_specs=[pl.BlockSpec(memory_space=pltpu.VMEM)] * 3,
        scratch_shapes=[
            pltpu.VMEM((MB * ROWS, D), LOW),
            pltpu.VMEM((MB * ROWS, D), LOW),
            pltpu.VMEM((MB * ROWS, D), LOW),
            pltpu.VMEM((MB * ROWS, D), LOW),
            pltpu.VMEM((MB * ROWS, FF), LOW),
            pltpu.VMEM((MB * ROWS, FF), LOW),
            pltpu.VMEM((MB * ROWS, FF), F32),
            pltpu.VMEM((MB * ROWS, 2 * D), LOW),
            pltpu.VMEM((D, 2 * D), LOW),
            pltpu.VMEM((D, FF), LOW),
            pltpu.VMEM((FF, D), LOW),
            pltpu.SemaphoreType.DMA((17,)),
        ],
        compiler_params=pltpu.CompilerParams(vmem_limit_bytes=VMEM_LIMIT),
        cost_estimate=pl.CostEstimate(
            flops=2 * 256 * D * 10000, bytes_accessed=20_000_000, transcendentals=500_000
        ),
        name="early_stage",
    )(*operands)


def late_kernel(
    section_ref,
    core_ref,
    tokens_ref,
    residual_ref,
    mix0,
    mix1,
    proj0,
    proj1,
    probs0,
    probs1,
    memory0,
    memory1,
    decoded0,
    decoded1,
    w_qkv,
    w_out,
    keep,
    send,
    outputs,
    input_grad,
    mix_v,
    proj_v,
    probs_v,
    final_v,
    g_v,
    mixed_v,
    gp_v,
    qkv_v,
    out_v,
    sems,
):
    core = core_ref[0]
    first = section_ref[0] == 0
    get_out = fetch(w_out.at[0], out_v, sems.at[0])
    gets_probs = [fetch(r, probs_v.at[i], sems.at[1 + i]) for i, r in enumerate((probs0, probs1))]
    gets_proj = [fetch(r, proj_v.at[i], sems.at[3 + i]) for i, r in enumerate((proj0, proj1))]

    def both(pair_refs, target, at):
        return [
            fetch(ref, target.at[pl.ds(i * ROWS, ROWS)], sems.at[at + i])
            for i, ref in enumerate(pair_refs)
        ]

    gets_mix = both((mix0, mix1), mix_v, 5)
    get_qkv = fetch(w_qkv.at[0], qkv_v, sems.at[7])

    @pl.when(first)
    def _():
        for copy in both((memory0, memory1), final_v, 8):
            copy.wait()

    @pl.when(jnp.logical_not(first))
    def _():
        for copy in both((decoded0, decoded1), final_v, 8):
            copy.wait()

    outputs[0] = final_v[...]
    g_v[...] = residual_ref[...].astype(LOW)
    get_out.wait()
    mixed_v[...] = mm_nt(g_v[...], out_v[...]).astype(LOW)
    for copy in gets_probs + gets_proj:
        copy.wait()
    for micro in range(MB):
        rows = slice(micro * ROWS, (micro + 1) * ROWS)

        def write(pair, grad_q, grad_k, grad_v, rows=rows):
            for part, value in enumerate((grad_q, grad_k, grad_v)):
                at = part * D + pair * LANES
                gp_v[rows, at : at + LANES] = value

        attend_back(
            columns(proj_v.at[micro], 0),
            columns(proj_v.at[micro], D),
            columns(proj_v.at[micro], 2 * D),
            lambda pair, micro=micro: probs_v[micro, pair],
            columns(mixed_v.at[pl.ds(micro * ROWS, ROWS)], 0),
            write,
        )
    for copy in gets_mix:
        copy.wait()
    put_block(core, keep, send, 0, mix_v, 0, g_v[...])
    for part in range(3):
        put_block(core, keep, send, 1 + part, tokens_ref.at[0], 0, gp_v[:, part * D : (part + 1) * D])
    get_qkv.wait()
    input_grad[0] = (residual_ref[...] + mm_nt(gp_v[...], qkv_v[...])).astype(LOW)


def late_stage(section, core, tokens, residual, ones, twos, w_qkv, w_out):
    operands = [section, core, tokens, residual]
    for name in ("mix", "proj", "probs", "memory"):
        operands += [one[name] for one in ones]
    operands += [two["decoded"] for two in twos]
    operands += [w_qkv, w_out]
    return pl.pallas_call(
        late_kernel,
        out_shape=[
            jax.ShapeDtypeStruct((LATE, HALF, D), F32),
            jax.ShapeDtypeStruct((LATE, HALF, D), LOW),
            jax.ShapeDtypeStruct((1, MB * ROWS, D), LOW),
            jax.ShapeDtypeStruct((1, MB * ROWS, D), LOW),
        ],
        in_specs=[in_smem(), in_smem(), whole(), whole()] + [anywhere()] * (len(operands) - 4),
        out_specs=[pl.BlockSpec(memory_space=pltpu.VMEM)] * 4,
        scratch_shapes=[
            pltpu.VMEM((MB * ROWS, D), LOW),
            pltpu.VMEM((MB, ROWS, 3 * D), LOW),
            pltpu.VMEM((MB, PAIRS, ROWS, 2 * ROWS), F32),
            pltpu.VMEM((MB * ROWS, D), LOW),
            pltpu.VMEM((MB * ROWS, D), LOW),
            pltpu.VMEM((MB * ROWS, D), LOW),
            pltpu.VMEM((MB * ROWS, 3 * D), LOW),
            pltpu.VMEM((D, 3 * D), LOW),
            pltpu.VMEM((D, D), LOW),
            pltpu.SemaphoreType.DMA((10,)),
        ],
        compiler_params=pltpu.CompilerParams(vmem_limit_bytes=VMEM_LIMIT),
        cost_estimate=pl.CostEstimate(
            flops=2 * 256 * D * 5000, bytes_accessed=12_000_000, transcendentals=1000
        ),
        name="late_stage",
    )(*operands)


def chip_sum_kernel(keep_a, got_a, keep_b, got_b, total):
    total[:EARLY] = (keep_a[...] + got_a[...].astype(F32)).astype(LOW)
    total[EARLY:] = (keep_b[...] + got_b[...].astype(F32)).astype(LOW)


def chip_sum(keep_a, got_a, keep_b, got_b):
    return pl.pallas_call(
        chip_sum_kernel,
        out_shape=jax.ShapeDtypeStruct((BLOCKS, HALF, D), LOW),
        in_specs=[pl.BlockSpec(memory_space=pltpu.VMEM)] * 4,
        out_specs=pl.BlockSpec(memory_space=pltpu.VMEM),
        compiler_params=pltpu.CompilerParams(vmem_limit_bytes=VMEM_LIMIT),
        name="chip_sum",
    )(keep_a, got_a, keep_b, got_b)


def unpack_kernel(core_ref, own, other, g_qkv, g_out, g_cross, g_up, g_down, slots, sems):
    core = core_ref[0]
    places = (
        [(g_cross.at[0, :, pl.ds(p * D, D)]) for p in range(2)]
        + [(g_up.at[0, :, pl.ds(p * D, D)]) for p in range(4)]
        + [(g_down.at[0, pl.ds(p * D, D), :]) for p in range(4)]
        + [g_out.at[0]]
        + [(g_qkv.at[0, :, pl.ds(p * D, D)]) for p in range(3)]
    )
    depth = slots.shape[0]
    here = pl.ds(pl.multiple_of(core * HALF, HALF), HALF)
    there = pl.ds(pl.multiple_of((1 - core) * HALF, HALF), HALF)
    copies = []
    for block, place in enumerate(places):
        slot = block % depth
        if block >= depth:
            copies[block - depth].wait()
        slots[slot, here, :] = own[block].astype(F32)
        slots[slot, there, :] = other[block].astype(F32)
        copies.append(fetch(slots.at[slot], place, sems.at[slot]))
    for copy in copies[-depth:]:
        copy.wait()


def unpack(core, own, other):
    shapes = ((1, D, 3 * D), (1, D, D), (1, D, 2 * D), (1, D, FF), (1, FF, D))
    return pl.pallas_call(
        unpack_kernel,
        out_shape=[jax.ShapeDtypeStruct(s, F32) for s in shapes],
        in_specs=[in_smem(), whole(), whole()],
        out_specs=[anywhere()] * 5,
        scratch_shapes=[pltpu.VMEM((4, D, D), F32), pltpu.SemaphoreType.DMA((4,))],
        compiler_params=pltpu.CompilerParams(vmem_limit_bytes=VMEM_LIMIT),
        name="unpack",
    )(core, own, other)


def ring_groups(count):
    chips = count // 2
    across = 2 if chips % 2 == 0 else 1
    along = chips // across
    order = [z * across for z in range(along)]
    if across == 2:
        order += [z * across + 1 for z in reversed(range(along))]
    return [[2 * chip + core for chip in order] for core in range(2)]


def swap_cores(value, count):
    return lax.ppermute(value, "dp", [(i, i ^ 1) for i in range(count)])


def on_device(inputs, lengths, w_qkv, w_attn_out, w_cross, w_up, w_down, cotangent):
    count = lax.axis_size("dp")
    section = lax.axis_index("section").astype(jnp.int32).reshape(1)
    core = (lax.axis_index("dp") % 2).astype(jnp.int32).reshape(1)
    weights = (w_qkv, w_attn_out, w_cross, w_up, w_down)
    names_one = ("proj", "mix", "mid_low", "wide", "act", "memory", "link", "probs")
    names_two = (
        "decoded",
        "link_grad",
        "cross_low",
        "cross_mix",
        "act",
        "grad_hidden",
        "cross_grad_low",
        "query_grad",
        "cross_grad",
    )
    ones, twos = [], []
    for micro in range(MB):
        one = dict(
            zip(names_one, forward_stage(micro, section, lengths, inputs, weights))
        )
        one["arrived"] = lax.ppermute(one["link"], "section", [(0, 1)])
        ones.append(one)
    for micro in range(MB):
        one = ones[micro]
        two = dict(
            zip(
                names_two,
                middle_stage(
                    micro,
                    section,
                    lengths,
                    one["wide"],
                    one["link"],
                    one["arrived"],
                    cotangent,
                    w_cross,
                    w_up,
                    w_down,
                ),
            )
        )
        one["lg"] = lax.ppermute(two["link_grad"], "section", [(1, 0)])
        twos.append(two)
    keep_a, send_a, residual = early_stage(
        section, core, cotangent, ones, twos, (w_cross, w_up, w_down)
    )
    got_a = swap_cores(send_a, count)
    keep_b, send_b, outputs, input_grad = late_stage(
        section, core, inputs, residual, ones, twos, w_qkv, w_attn_out
    )
    got_b = swap_cores(send_b, count)
    total = chip_sum(keep_a, got_a, keep_b, got_b).reshape(BLOCKS * HALF, D)
    groups = ring_groups(count)
    piece = lax.psum_scatter(
        total, "dp", scatter_dimension=0, tiled=True, axis_index_groups=groups
    )
    own = lax.all_gather(piece, "dp", axis=0, tiled=True, axis_index_groups=groups)
    other = swap_cores(own, count)
    grads = unpack(
        core, own.reshape(BLOCKS, HALF, D), other.reshape(BLOCKS, HALF, D)
    )
    return (outputs, input_grad, *grads)


def solution(mesh):
    return jax.shard_map(
        on_device,
        mesh=mesh,
        in_specs=(
            P("section", "dp", None),
            P("dp", None, None),
            P("section", None, None),
            P("section", None, None),
            P("section", None, None),
            P("section", None, None),
            P("section", None, None),
            P("section", "dp", None),
        ),
        out_specs=(
            P("section", "dp", None),
            P("section", "dp", None),
            P("section", None, None),
            P("section", None, None),
            P("section", None, None),
            P("section", None, None),
            P("section", None, None),
        ),
        check_vma=False,
    )
```

time: 506 us -> 215 us (0.42)
  waiting for transfers between devices: 299 us -> 117 us
  matrix products: 59.3 us -> 0 us
  local copies, waits for them, and re-layouts: 78.9 us -> 32 us
  Pallas kernels: 0 us -> 42.4 us
  other arithmetic: 40.1 us -> 0 us
    psum x1 -> x0, waiting for transfers between devices: 265 us -> none  [on_device(): lax.psum((running[0], running[1], running[2], running[3], running[4]), 'dp')]
    dot_general x44 -> x0, matrix products: 59.3 us -> none  [the longest x10 23.5 us: weight_dot(): lax.dot_general(values_in, grad_in, (((0,), (0,)), ((), ())), preferred_e...]
    all_gather x0 -> x1, waiting for transfers between devices: none -> 44.5 us  [on_device(): lax.all_gather(piece, 'dp', axis=0, tiled=True, axis_index_groups=groups)]
    reduce_scatter x0 -> x1, waiting for transfers between devices: none -> 44 us  [on_device(): lax.psum_scatter(total, 'dp', scatter_dimension=0, tiled=True, axis_index...]
    pallas_call x0 -> x8, Pallas kernels: none -> 42.4 us  [the longest x1 10.5 us: early_stage(): pl.pallas_call(early_kernel, out_shape=[jax.ShapeDtypeStruct((EARLY, HALF...]
    cond x96 -> x0, local copies, waits for them, and re-layouts: 35.8 us -> none  [the longest x8 29 us: on_device(): lax.cond(is_first, encode_back, silenced(encode_back), (tokens_now, upstr...]
    broadcast_in_dim x7 -> x0, other arithmetic: 30.5 us -> none  [the longest x1 7.79 us: on_device(): running[3][None]]
    another operation x23 -> x0, local copies, waits for them, and re-layouts: 25.2 us -> none
  transfers between devices with their start and end apart: 5 -> 9, of which waited for: 4 -> 7; matrix products, arithmetic and copies ran while one was open for 16% -> 0% of each run, Pallas kernels for 0% -> 7%
where the time goes in v1:
time: 215 us; the launch traced here: 214 us
  waiting for transfers between devices  117 us (54%)
  Pallas kernels  42.4 us (20%)
  local copies, waits for them, and re-layouts  32 us (15%)
  between operations  14.4 us (7%)
  starting transfers between devices  8.1 us (4%)
    all_gather x1, waiting for transfers between devices, on_device(): lax.all_gather(piece, 'dp', axis=0, tiled=True, axis_index_groups=groups)  44.5 us
    reduce_scatter x1, waiting for transfers between devices, on_device(): lax.psum_scatter(total, 'dp', scatter_dimension=0, tiled=True, axis_index...  44 us
    unnamed x106, local copies, waits for them, and re-layouts  32 us
    ppermute x2, waiting for transfers between devices, on_device(): one['lg'] = lax.ppermute(two['link_grad'], 'section', [(1, 0)])  18.3 us
    pallas_call x1, Pallas kernels, early_stage(): pl.pallas_call(early_kernel, out_shape=[jax.ShapeDtypeStruct((EARLY, HALF...  10.5 us
    pallas_call x2, Pallas kernels, forward_stage(): pl.pallas_call(functools.partial(forward_kernel, micro), out_shape=[jax.S...  10.1 us
    ppermute x3, waiting for transfers between devices, swap_cores(): return lax.ppermute(value, 'dp', [(i, i ^ 1) for i in range(count)])  8.91 us
    pallas_call x1, Pallas kernels, unpack(): pl.pallas_call(unpack_kernel, out_shape=[jax.ShapeDtypeStruct(s, F32) for...  7.33 us
  transfers between devices with their start and end apart: 9, of which 7 were waited for; matrix products, arithmetic and copies ran while one was open for 0% of the time, Pallas kernels for 7%

profile of v1, /device:TPU:0, one launch (start us, length us, event | category | flops | bytes accessed | tf_op | source)
XLA Modules:
  0.0 214.0 jit_solution(4863546226607568619)
XLA Ops:
  7.2 0.0 reduce-scatter.2.cloned.1.call-start
  7.2 0.0 copy-start
  7.2 1.2 copy-done
  8.4 1.0 copy-done.2
  9.5 0.9 copy-done.7
  10.4 0.7 copy-done.50
  11.1 5.1 %forward_stage.2 = (bf16[128,1536]{1,0:T(8,128)(2,1)S(1)}, bf16[128,512]{1,0:T(8,128)(2,1)S(1)}, bf16[128,512]{1,0:T(8,128)(2,1)S(1)}, f32[128,2048]{1,0:T(8,128...) custom-call(s32[1]{0:T(128)} %bitcast.section_ref, ...), custom_call_target="tpu_custom_call" | custom-call | flops 939524096 | bytes 10000000 | tf_op jit(solution)/shard_map/forward_stage/pallas_call | solution.py:251
  16.2 0.7 copy-done.16
  16.9 0.6 copy-done.42
  17.6 3.5 %collective-permute-start = (bf16[128,1024]{1,0:T(8,128)(2,1)S(1)}, bf16[128,1024]{1,0:T(8,128)(2,1)S(1)}, u32[]{:S(2)}, u32[]{:S(2)}) collective-permute-start(bf16[128,1024]{1,0:T(8,128)(2,1)S(1)} %get-tuple-element.56.query_ref), channel_id=1, source_target_pairs={{0,16},{1,17},{2,18},{3,19},{4,20},{5,21},{6,22},{7,23},{8,24},{9,... | collective-permute-start | bytes 786440 | tf_op jit(solution)/shard_map/ppermute | solution.py:774
  21.2 5.1 %forward_stage.3 = (bf16[128,1536]{1,0:T(8,128)(2,1)S(1)}, bf16[128,512]{1,0:T(8,128)(2,1)S(1)}, bf16[128,512]{1,0:T(8,128)(2,1)S(1)}, f32[128,2048]{1,0:T(8,128...) custom-call(s32[1]{0:T(128)} %bitcast.section_ref, ...), custom_call_target="tpu_custom_call" | custom-call | flops 939524096 | bytes 10000000 | tf_op jit(solution)/shard_map/forward_stage/pallas_call | solution.py:251
  26.2 0.7 copy-done.18
  27.0 0.7 copy-done.24
  27.6 0.6 copy-done.44
  28.3 1.3 collective-permute-start.2
  29.6 0.0 collective-permute-done.link_ref
  29.6 1.3 middle_stage.2
  31.0 0.0 copy-start.11
  31.0 0.8 copy-done.11
  31.8 0.7 copy-done.20
  32.5 1.3 collective-permute-start.1
  33.8 1.3 collective-permute-done.2.link_ref
  35.1 1.5 middle_stage.3
  36.7 0.0 copy-start.13
  36.7 0.8 copy-done.13
  37.5 0.8 copy-done.15
  38.3 0.7 copy-done.22
  39.0 0.6 copy-done.34
  39.6 0.7 copy-done.36
  40.3 0.6 copy-done.38
  40.9 0.7 copy-done.40
  41.6 0.6 copy-done.48
  42.2 1.3 collective-permute-start.3
  43.5 2.4 %collective-permute-done.1.lg0 = bf16[128,1024]{1,0:T(8,128)(2,1)} collective-permute-done((bf16[128,1024]{1,0:T(8,128)(2,1)}, bf16[128,1024]{1,0:T(8,128)(2,1)}, u32[]{:S(2)}, u32[]{:S(2)}) %collective-permute-start.1) | collective-permute-done | bytes 262176 | tf_op jit(solution)/shard_map/ppermute | solution.py:795
  45.9 15.9 %collective-permute-done.3.lg1 = bf16[128,1024]{1,0:T(8,128)(2,1)} collective-permute-done((bf16[128,1024]{1,0:T(8,128)(2,1)}, bf16[128,1024]{1,0:T(8,128)(2,1)}, u32[]{:S(2)}, u32[]{:S(2)}) %collective-permute-start.3) | collective-permute-done | bytes 262176 | tf_op jit(solution)/shard_map/ppermute | solution.py:795
  61.9 1.0 copy-done.12
  62.9 1.0 copy-done.14
  63.9 0.9 copy-done.21
  64.9 0.9 copy-done.23
  65.8 0.9 copy-done.25
  66.7 0.9 copy-done.27
  67.6 0.9 copy-done.29
  68.6 0.9 copy-done.31
  69.5 0.9 copy-done.33
  70.4 0.9 copy-done.35
  71.3 0.9 copy-done.37
  72.2 0.9 copy-done.39
  73.1 0.9 copy-done.41
  74.0 10.5 %early_stage.1 = (f32[10,256,512]{2,1,0:T(8,128)}, bf16[10,256,512]{2,1,0:T(8,128)(2,1)}, f32[256,512]{1,0:T(8,128)S(1)}) custom-call(s32[1]{0:T(128)} %bitcast.section_ref, s32[1]{0:T(128)} %bitcast.1.core_ref, bf16[1,256,512]{2,1,0:T(8,128)(2,1)S(1)} %copy-done.9, bf16[128,512]{1,0:T(8,128)(2,1)S(1)} %get-tuple-element.53.memory0, ...), custom_call_target="tpu_custom_call" | custom-call | flops 2621440000 | bytes 20000000 | tf_op jit(solution)/shard_map/early_stage/pallas_call | solution.py:530
  84.5 0.1 collective-permute-start.4
  84.7 6.7 %late_stage.1 = (f32[4,256,512]{2,1,0:T(8,128)}, bf16[4,256,512]{2,1,0:T(8,128)(2,1)S(1)}, bf16[1,256,512]{2,1,0:T(8,128)(2,1)}, bf16[1,256,512]{2,1,0:T(8,128)(2,1)}) custom-call(s32[1]{0:T(128)} %bitcast.section_ref, s32[1]{0:T(128)} %bitcast.1.core_ref, bf16[1,256,512]{2,1,0:T(8,128)(2,1)S(1)} %copy-done.8, ...), custom_call_target="tpu_custom_call" | custom-call | flops 1310720000 | bytes 12000000 | tf_op jit(solution)/shard_map/late_stage/pallas_call | solution.py:655
  91.4 0.5 collective-permute-start.5
  91.9 2.3 %collective-permute-done.5.got_b = bf16[4,256,512]{2,1,0:T(8,128)(2,1)S(1)} collective-permute-done((bf16[4,256,512]{2,1,0:T(8,128)(2,1)S(1)}, bf16[4,256,512]{2,1,0:T(8,128)(2,1)S(1)}, u32[]{:S(2)}, u32[]{:S(2)}) %collective-permute-start.5) | collective-permute-done | bytes 1048608 | tf_op jit(solution)/shard_map/ppermute | solution.py:749
  94.2 1.6 copy-done.10
  95.8 4.9 %chip_sum.1 = bf16[14,256,512]{2,1,0:T(8,128)(2,1)} custom-call(f32[10,256,512]{2,1,0:T(8,128)} %get-tuple-element.90.keep_a, bf16[10,256,512]{2,1,0:T(8,128)(2,1)S(1)} %collective-permute-done.4.got_a, f32[4,256,512]{2,1,0:T(8,128)S(1)} %copy-done.10, bf16[4,256,512]{2,1,0:T(8,128)(2,1)S(1)} %collective-permute-done.5.got_b), custom_call_target="tpu_custom_call" | custom-call | tf_op jit(solution)/shard_map/chip_sum/pallas_call | solution.py:691
  100.7 0.0 reduce-scatter.2.cloned.1.call-update
  100.7 0.0 all-gather.2.cloned.1.call-start
  100.8 44.0 %reduce-scatter.2.cloned.1.call-done = bf16[448,512]{1,0:T(8,128)(2,1)} async-done(((bf16[3584,512]{1,0:T(8,128)(2,1)}), bf16[448,512]{1,0:T(8,128)(2,1)}) %reduce-scatter.2.cloned.1.call-update) | async-done | bytes 458768 | tf_op jit(solution)/shard_map/reduce_scatter | solution.py:807
  144.8 0.0 all-gather.2.cloned.1.call-update
  144.8 44.5 %all-gather.2.cloned.1.call-done = bf16[3584,512]{1,0:T(8,128)(2,1)} async-done(((bf16[448,512]{1,0:T(8,128)(2,1)}), bf16[3584,512]{1,0:T(8,128)(2,1)}) %all-gather.2.cloned.1.call-update) | async-done | bytes 3670032 | tf_op jit(solution)/shard_map/all_gather | solution.py:810
  189.3 6.6 %collective-permute-done.6 = bf16[3584,512]{1,0:T(8,128)(2,1)S(1)} collective-permute-done((bf16[3584,512]{1,0:T(8,128)(2,1)}, bf16[3584,512]{1,0:T(8,128)(2,1)S(1)}, u32[]{:S(2)}, u32[]{:S(2)}) %collective-permute-start.6) | collective-permute-done | bytes 3670048 | tf_op jit(solution)/shard_map/ppermute | solution.py:749
  195.9 1.8 copy-done.52
  197.8 2.0 copy-done.6
  199.8 7.3 %unpack.1 = (f32[1,512,1536]{2,1,0:T(8,128)}, f32[1,512,512]{2,1,0:T(8,128)}, f32[1,512,1024]{2,1,0:T(8,128)}, f32[1,512,2048]{2,1,0:T(8,128)}, f32[1,2048,512]{2,1,0:T(8,128)}) custom-call(s32[1]{0:T(128)} %bitcast.1.core_ref, bf16[14,256,512]{2,1,0:T(8,128)(2,1)S(1)} %bitcast.5, bf16[14,256,512]{2,1,0:T(8,128)(2,1)} %bitcast.7), custom_call_target="tpu_custom_call" | custom-call | tf_op jit(solution)/shard_map/unpack/pallas_call | solution.py:727
  (70 shorter events, 0.1 us)
Async XLA Ops:
  7.2 137.6 %reduce-scatter.2.cloned.1.call-start = ((), (), s32[]{:S(2)}) async-start(), calls=%async_computation.1 | async-start | bytes 4128768 | tf_op jit(solution)/shard_map/reduce_scatter | solution.py:807
  7.2 1.2 copy-start
  8.4 1.0 copy-start.2
  9.5 0.9 copy-start.7
  10.4 0.7 copy-start.50
  11.1 10.0 %copy-start.8 = (bf16[1,256,512]{2,1,0:T(8,128)(2,1)S(1)}, bf16[1,256,512]{2,1,0:T(8,128)(2,1)}, u32[]{:S(2)}) copy-start(bf16[1,256,512]{2,1,0:T(8,128)(2,1)} %tokens_ref.5) | copy-start | bytes 786436
  11.1 10.0 %copy-start.51 = (s32[2,2,16]{2,1,0:T(2,128)S(1)}, s32[2,2,16]{2,1,0:T(2,128)}, u32[]{:S(2)}) copy-start(s32[2,2,16]{2,1,0:T(2,128)} %lengths_ref.7) | copy-start | bytes 772
  16.2 0.7 copy-start.16
  16.9 0.6 copy-start.42
  17.6 12.0 %copy-start.4 = (f32[128,2048]{1,0:T(8,128)}, f32[128,2048]{1,0:T(8,128)S(1)}, u32[]{:S(2)}) copy-start(f32[128,2048]{1,0:T(8,128)S(1)} %get-tuple-element.55.mid_ref.wide0) | copy-start | bytes 3145732
  17.6 12.0 %copy-start.1 = (bf16[1,512,1024]{2,1,0:T(8,128)(2,1)S(1)}, bf16[1,512,1024]{2,1,0:T(8,128)(2,1)}, u32[]{:S(2)}) copy-start(bf16[1,512,1024]{2,1,0:T(8,128)(2,1)} %w_cross.9) | copy-start | bytes 3145732
  17.6 12.0 %copy-start.9 = (bf16[1,256,512]{2,1,0:T(8,128)(2,1)S(1)}, bf16[1,256,512]{2,1,0:T(8,128)(2,1)}, u32[]{:S(2)}) copy-start(bf16[1,256,512]{2,1,0:T(8,128)(2,1)} %cotangent_ref.5) | copy-start | bytes 786436
  17.6 12.0 %collective-permute-start = (bf16[128,1024]{1,0:T(8,128)(2,1)S(1)}, bf16[128,1024]{1,0:T(8,128)(2,1)S(1)}, u32[]{:S(2)}, u32[]{:S(2)}) collective-permute-start(bf16[128,1024]{1,0:T(8,128)(2,1)S(1)} %get-tuple-element.56.query_ref), channel_id=1, source_target_pairs={{0,16},{1,17},{2,18},{3,19},{4,20},{5,21},{6,22},{7,23},{8,24},{9,... | collective-permute-start | bytes 786440 | tf_op jit(solution)/shard_map/ppermute | solution.py:774
  26.2 0.8 copy-start.18
  27.0 0.7 copy-start.24
  27.6 0.6 copy-start.44
  28.3 6.8 %copy-start.5 = (f32[128,2048]{1,0:T(8,128)}, f32[128,2048]{1,0:T(8,128)S(1)}, u32[]{:S(2)}) copy-start(f32[128,2048]{1,0:T(8,128)S(1)} %get-tuple-element.58.mid_ref.wide1) | copy-start | bytes 3145732
  28.3 6.8 %collective-permute-start.2 = (bf16[128,1024]{1,0:T(8,128)(2,1)S(1)}, bf16[128,1024]{1,0:T(8,128)(2,1)S(1)}, u32[]{:S(2)}, u32[]{:S(2)}) collective-permute-start(bf16[128,1024]{1,0:T(8,128)(2,1)S(1)} %get-tuple-element.59.query_ref), channel_id=1, source_target_pairs={{0,16},{1,17},{2,18},{3,19},{4,20},{5,21},{6,22},{7,23},{8,24},{9,... | collective-permute-start | bytes 786440 | tf_op jit(solution)/shard_map/ppermute | solution.py:774
  31.0 0.8 copy-start.11
  31.8 0.7 copy-start.20
  32.5 4.2 %copy-start.26 = (bf16[128,512]{1,0:T(8,128)(2,1)}, bf16[128,512]{1,0:T(8,128)(2,1)S(1)}, u32[]{:S(2)}) copy-start(bf16[128,512]{1,0:T(8,128)(2,1)S(1)} %get-tuple-element.65.cl0) | copy-start | bytes 393220
  32.5 4.2 %copy-start.28 = (bf16[128,512]{1,0:T(8,128)(2,1)}, bf16[128,512]{1,0:T(8,128)(2,1)S(1)}, u32[]{:S(2)}) copy-start(bf16[128,512]{1,0:T(8,128)(2,1)S(1)} %get-tuple-element.67.cm0) | copy-start | bytes 393220
  32.5 4.2 %copy-start.30 = (bf16[128,512]{1,0:T(8,128)(2,1)}, bf16[128,512]{1,0:T(8,128)(2,1)S(1)}, u32[]{:S(2)}) copy-start(bf16[128,512]{1,0:T(8,128)(2,1)S(1)} %get-tuple-element.73.cgl0) | copy-start | bytes 393220
  32.5 4.2 %copy-start.32 = (bf16[128,512]{1,0:T(8,128)(2,1)}, bf16[128,512]{1,0:T(8,128)(2,1)S(1)}, u32[]{:S(2)}) copy-start(bf16[128,512]{1,0:T(8,128)(2,1)S(1)} %get-tuple-element.75.qg0) | copy-start | bytes 393220
  32.5 4.2 %copy-start.46 = (bf16[128,512]{1,0:T(8,128)(2,1)}, bf16[128,512]{1,0:T(8,128)(2,1)S(1)}, u32[]{:S(2)}) copy-start(bf16[128,512]{1,0:T(8,128)(2,1)S(1)} %get-tuple-element.86.decoded0) | copy-start | bytes 393220
  32.5 13.4 %collective-permute-start.1 = (bf16[128,1024]{1,0:T(8,128)(2,1)}, bf16[128,1024]{1,0:T(8,128)(2,1)}, u32[]{:S(2)}, u32[]{:S(2)}) collective-permute-start(bf16[128,1024]{1,0:T(8,128)(2,1)} %get-tuple-element.57), channel_id=1, source_target_pairs={{16,0},{17,1},{18,2},{19,3},{20,4},{21,5},{22,6},{23,7},{24,8},{25... | collective-permute-start | bytes 786440 | tf_op jit(solution)/shard_map/ppermute | solution.py:795
  36.7 0.8 copy-start.13
  37.5 0.8 copy-start.15
  38.3 0.7 copy-start.22
  39.0 0.6 copy-start.34
  39.6 0.7 copy-start.36
  40.3 0.6 copy-start.38
  40.9 0.7 copy-start.40
  41.6 0.6 copy-start.48
  42.2 19.6 %collective-permute-start.3 = (bf16[128,1024]{1,0:T(8,128)(2,1)}, bf16[128,1024]{1,0:T(8,128)(2,1)}, u32[]{:S(2)}, u32[]{:S(2)}) collective-permute-start(bf16[128,1024]{1,0:T(8,128)(2,1)} %get-tuple-element.60), channel_id=1, source_target_pairs={{16,0},{17,1},{18,2},{19,3},{20,4},{21,5},{22,6},{23,7},{24,8},{25... | collective-permute-start | bytes 786440 | tf_op jit(solution)/shard_map/ppermute | solution.py:795
  61.8 1.0 copy-start.12
  62.9 1.0 copy-start.14
  63.9 0.9 copy-start.21
  64.9 0.9 copy-start.23
  65.8 0.9 copy-start.25
  66.7 0.9 copy-start.27
  67.6 0.9 copy-start.29
  68.5 0.9 copy-start.31
  69.5 0.9 copy-start.33
  70.4 0.9 copy-start.35
  71.3 0.9 copy-start.37
  72.2 0.9 copy-start.39
  73.1 0.9 copy-start.41
  74.0 10.6 %copy-start.3 = (bf16[1,512,512]{2,1,0:T(8,128)(2,1)S(1)}, bf16[1,512,512]{2,1,0:T(8,128)(2,1)}, u32[]{:S(2)}) copy-start(bf16[1,512,512]{2,1,0:T(8,128)(2,1)} %w_out.5) | copy-start | bytes 1572868
  74.0 10.6 %copy-start.17 = (bf16[128,1536]{1,0:T(8,128)(2,1)S(1)}, bf16[128,1536]{1,0:T(8,128)(2,1)}, u32[]{:S(2)}) copy-start(bf16[128,1536]{1,0:T(8,128)(2,1)} %copy-done.16) | copy-start | bytes 1179652
  74.0 10.6 %copy-start.19 = (bf16[128,1536]{1,0:T(8,128)(2,1)S(1)}, bf16[128,1536]{1,0:T(8,128)(2,1)}, u32[]{:S(2)}) copy-start(bf16[128,1536]{1,0:T(8,128)(2,1)} %copy-done.18) | copy-start | bytes 1179652
  74.0 10.6 %copy-start.43 = (bf16[128,512]{1,0:T(8,128)(2,1)S(1)}, bf16[128,512]{1,0:T(8,128)(2,1)}, u32[]{:S(2)}) copy-start(bf16[128,512]{1,0:T(8,128)(2,1)} %copy-done.42) | copy-start | bytes 393220
  74.0 10.6 %copy-start.45 = (bf16[128,512]{1,0:T(8,128)(2,1)S(1)}, bf16[128,512]{1,0:T(8,128)(2,1)}, u32[]{:S(2)}) copy-start(bf16[128,512]{1,0:T(8,128)(2,1)} %copy-done.44) | copy-start | bytes 393220
  74.0 10.6 %copy-start.47 = (bf16[128,512]{1,0:T(8,128)(2,1)S(1)}, bf16[128,512]{1,0:T(8,128)(2,1)}, u32[]{:S(2)}) copy-start(bf16[128,512]{1,0:T(8,128)(2,1)} %copy-done.46) | copy-start | bytes 393220
  74.0 10.6 %copy-start.49 = (bf16[128,512]{1,0:T(8,128)(2,1)S(1)}, bf16[128,512]{1,0:T(8,128)(2,1)}, u32[]{:S(2)}) copy-start(bf16[128,512]{1,0:T(8,128)(2,1)} %copy-done.48) | copy-start | bytes 393220
  84.5 9.7 %collective-permute-start.4 = (bf16[10,256,512]{2,1,0:T(8,128)(2,1)}, bf16[10,256,512]{2,1,0:T(8,128)(2,1)S(1)}, u32[]{:S(2)}, u32[]{:S(2)}) collective-permute-start(bf16[10,256,512]{2,1,0:T(8,128)(2,1)} %get-tuple-element.91), channel_id=1, source_target_pairs={{0,1},{1,0},{2,3},{3,2},{4,5},{5,4},{6,7},{7,6},{8,9},{9,8},{10,11... | collective-permute-start | bytes 7864328 | tf_op jit(solution)/shard_map/ppermute | solution.py:749
  91.4 2.8 %collective-permute-start.5 = (bf16[4,256,512]{2,1,0:T(8,128)(2,1)S(1)}, bf16[4,256,512]{2,1,0:T(8,128)(2,1)S(1)}, u32[]{:S(2)}, u32[]{:S(2)}) collective-permute-start(bf16[4,256,512]{2,1,0:T(8,128)(2,1)S(1)} %get-tuple-element.93), channel_id=1, source_target_pairs={{0,1},{1,0},{2,3},{3,2},{4,5},{5,4},{6,7},{7,6},{8,9},{9,8},{10,11... | collective-permute-start | bytes 3145736 | tf_op jit(solution)/shard_map/ppermute | solution.py:749
  94.2 1.6 copy-start.10
  100.7 88.6 %all-gather.2.cloned.1.call-start = ((), (), s32[]{:S(2)}) async-start(), calls=%async_computation.2 | async-start | bytes 4128768 | tf_op jit(solution)/shard_map/all_gather | solution.py:810
  189.3 6.6 %collective-permute-start.6 = (bf16[3584,512]{1,0:T(8,128)(2,1)}, bf16[3584,512]{1,0:T(8,128)(2,1)S(1)}, u32[]{:S(2)}, u32[]{:S(2)}) collective-permute-start(bf16[3584,512]{1,0:T(8,128)(2,1)} %all-gather.2.cloned.1.call-done), channel_id=1, source_target_pairs={{0,1},{1,0},{2,3},{3,2},{4,5},{5,4},{6,7},{7,6},{8,9},{9,8},{10,11... | collective-permute-start | bytes 11010056 | tf_op jit(solution)/shard_map/ppermute | solution.py:749
  195.9 1.8 copy-start.52
  197.8 2.0 copy-start.6
Sparse Core Ops, SparseCore 0:
  100.9 43.8 reduce-scatter.1
  146.3 42.9 all-gather.1

commit v2 on v0

v2 whole, which is shorter than its diff:
```python
import functools

import jax
import jax.numpy as jnp
from jax import lax
from jax.experimental import pallas as pl
from jax.experimental.pallas import tpu as pltpu
from jax.sharding import PartitionSpec as P

D = 512
HEADS = 8
HEAD_DIM = 64
FF = 2048
ROWS = 128
SLOTS = 16
MB = 2
PAIRS = HEADS // 2
LANES = 2 * HEAD_DIM
HALF = D // 2
SCALE = HEAD_DIM ** (-0.5)
GELU_IN = 0.7978845608028654
GELU_CUBE = 0.044715
LOW = jnp.bfloat16
F32 = jnp.float32
SPLIT = True

CROSS_AT, UP_AT, DOWN_AT, OUT_AT, QKV_AT = 0, 2, 6, 10, 11
BLOCKS = 14
EARLY = 10
LATE = BLOCKS - EARLY


def mm(left, right):
    return jnp.dot(left, right, preferred_element_type=F32)


def mm_nt(left, right):
    return lax.dot_general(left, right, (((1,), (1,)), ((), ())), preferred_element_type=F32)


def mm_tn(left, right):
    return lax.dot_general(left, right, (((0,), (0,)), ((), ())), preferred_element_type=F32)


def gelu(hidden):
    inner = GELU_IN * (hidden + GELU_CUBE * (hidden * hidden * hidden))
    return hidden * (0.5 * (1.0 + jnp.tanh(inner)))


def gelu_slope(hidden):
    square = hidden * hidden
    inner = GELU_IN * (hidden + GELU_CUBE * (square * hidden))
    bent = jnp.tanh(inner)
    inner_slope = GELU_IN * (1.0 + (3.0 * GELU_CUBE) * square)
    return 0.5 * (1.0 + bent) + 0.5 * hidden * (1.0 - bent * bent) * inner_slope


def segments(lengths_ref, micro, which, dim):
    position = lax.broadcasted_iota(jnp.int32, (ROWS, ROWS), dim)
    end = jnp.int32(0)
    seg = jnp.zeros((ROWS, ROWS), jnp.int32)
    for slot in range(SLOTS):
        end = end + lengths_ref[micro, which, slot]
        seg = seg + (position >= end).astype(jnp.int32)
    return seg


def low_lanes():
    return lax.broadcasted_iota(jnp.int32, (ROWS, LANES), 1) < HEAD_DIM


def two_heads(pair, lanes):
    nothing = jnp.zeros_like(pair)
    return jnp.concatenate(
        [jnp.where(lanes, pair, nothing), jnp.where(lanes, nothing, pair)], axis=0
    )


def softmax(scores):
    highest = jnp.max(scores, axis=1, keepdims=True)
    raised = jnp.exp(scores - highest)
    return raised * (1.0 / jnp.sum(raised, axis=1, keepdims=True))


def attend(read_q, read_k, read_v, mask, write_probs, write_mix):
    lanes = low_lanes()
    for pair in range(PAIRS):
        query = (read_q(pair).astype(F32) * SCALE).astype(LOW)
        scores = mm_nt(query, two_heads(read_k(pair), lanes))
        probs = jnp.concatenate(
            [
                softmax(jnp.where(mask, scores[:, :ROWS], -1e30)),
                softmax(jnp.where(mask, scores[:, ROWS:], -1e30)),
            ],
            axis=1,
        )
        write_probs(pair, probs)
        write_mix(pair, mm(probs.astype(LOW), two_heads(read_v(pair), lanes)).astype(LOW))


def attend_back(read_q, read_k, read_v, read_probs, read_grad, write):
    lanes = low_lanes()
    for pair in range(PAIRS):
        query = (read_q(pair).astype(F32) * SCALE).astype(LOW)
        probs = read_probs(pair)
        grad = read_grad(pair)
        grad_probs = mm_nt(grad, two_heads(read_v(pair), lanes))
        product = probs * grad_probs
        slopes = []
        for head in range(2):
            cut = slice(head * ROWS, (head + 1) * ROWS)
            total = jnp.sum(product[:, cut], axis=1, keepdims=True)
            slopes.append((probs[:, cut] * (grad_probs[:, cut] - total)).astype(LOW))
        probs_low = probs.astype(LOW)
        grad_q = mm(jnp.concatenate(slopes, axis=1), two_heads(read_k(pair), lanes)) * SCALE
        grad_k = mm_tn(jnp.concatenate(slopes, axis=0), two_heads(query, lanes))
        grad_v = mm_tn(
            jnp.concatenate([probs_low[:, :ROWS], probs_low[:, ROWS:]], axis=0),
            two_heads(grad, lanes),
        )
        write(pair, grad_q.astype(LOW), grad_k.astype(LOW), grad_v.astype(LOW))


def columns(ref, rows, start):
    def read(pair):
        return ref[rows, start + pair * LANES : start + (pair + 1) * LANES]

    return read


def fetch(source, target, sem):
    copy = pltpu.make_async_copy(source, target, sem)
    copy.start()
    return copy


STATE = {
    "proj": ((MB * ROWS, 3 * D), LOW),
    "mix": ((MB * ROWS, D), LOW),
    "probs": ((MB, PAIRS, ROWS, 2 * ROWS), F32),
    "wide": ((MB * ROWS, FF), F32),
    "act": ((MB * ROWS, FF), LOW),
    "narrow": ((MB * ROWS, D), LOW),
    "result": ((MB * ROWS, D), LOW),
    "mid_low": ((MB * ROWS, D), LOW),
    "query": ((MB * ROWS, D), LOW),
    "across": ((MB * ROWS, ROWS), F32),
}
BACK = {
    "cross_mix": ((MB * ROWS, D), LOW),
    "grad_hidden": ((MB * ROWS, FF), LOW),
    "grad_low": ((MB * ROWS, D), LOW),
    "query_grad": ((MB * ROWS, D), LOW),
    "grad": ((MB * ROWS, D), F32),
}
WEIGHTS = {
    "w_qkv": ((D, 3 * D), LOW),
    "w_out": ((D, D), LOW),
    "w_cross": ((D, 2 * D), LOW),
    "w_up": ((D, FF), LOW),
    "w_down": ((FF, D), LOW),
}
HELD = {"tokens": ((MB * ROWS, D), LOW), "cotangent": ((MB * ROWS, D), LOW)}


def shaped(table):
    return [pltpu.VMEM(shape, kind) for shape, kind in table.values()]


def same_shape(arrays):
    return [pltpu.VMEM(value.shape, value.dtype) for value in arrays]


def held(arrays):
    return [pltpu.with_memory_space_constraint(value, pltpu.VMEM) for value in arrays]


def left(arrays):
    return [pltpu.with_memory_space_constraint(value, pltpu.HBM) for value in arrays]


def in_vmem():
    return pl.BlockSpec(memory_space=pltpu.VMEM)


def in_smem():
    return pl.BlockSpec(memory_space=pltpu.SMEM)


def in_hbm():
    return pl.BlockSpec(memory_space=pltpu.HBM)


def call(kernel, name, place, reads, keeps, makes, scratch=(), vmem_mib=16, cost=(0, 0)):
    kept = list(keeps)
    out_shape = same_shape(keeps.values()) + shaped(makes)
    read_count, kept_count, made_count = len(reads), len(kept), len(makes)

    def body(place_ref, *refs):
        refs = list(refs)
        named = dict(zip(reads, refs[:read_count]))
        refs = refs[read_count + kept_count :]
        named.update(zip(kept, refs[:kept_count]))
        named.update(zip(makes, refs[kept_count : kept_count + made_count]))
        kernel(place_ref, named, *refs[kept_count + made_count :])

    results = pl.pallas_call(
        body,
        out_shape=out_shape,
        in_specs=[in_smem()] + [in_vmem()] * (read_count + kept_count),
        out_specs=[in_vmem()] * len(out_shape),
        scratch_shapes=list(scratch),
        input_output_aliases={1 + read_count + i: i for i in range(kept_count)},
        compiler_params=pltpu.CompilerParams(vmem_limit_bytes=vmem_mib * 1024 * 1024),
        cost_estimate=pl.CostEstimate(flops=cost[0], bytes_accessed=cost[1], transcendentals=0),
        name=name,
    )(place, *held(reads.values()), *held(keeps.values()))
    return dict(zip(list(kept) + list(makes), results))


def forward_step(micro, first, lengths_ref, ref, link, ready):
    rows = slice(micro * ROWS, (micro + 1) * ROWS)
    ready("lengths")
    seg_q_tgt = segments(lengths_ref, micro, 1, 0)
    seg_k_src = segments(lengths_ref, micro, 0, 1)
    ref["across"][rows, :] = (seg_q_tgt == seg_k_src).astype(F32)
    later = lax.broadcasted_iota(jnp.int32, (ROWS, ROWS), 0) >= lax.broadcasted_iota(
        jnp.int32, (ROWS, ROWS), 1
    )
    source_mask = (segments(lengths_ref, micro, 0, 0) == seg_k_src).astype(jnp.int32)
    target_mask = ((seg_q_tgt == segments(lengths_ref, micro, 1, 1)) & later).astype(jnp.int32)
    mask = jnp.where(first, source_mask, target_mask) != 0
    ready("tokens")
    tokens = ref["tokens"][rows, :]
    proj, mix, probs = ref["proj"], ref["mix"], ref["probs"]
    ready("w_qkv")
    for part in range(3):
        cut = slice(part * D, (part + 1) * D)
        proj[rows, cut] = mm(tokens, ref["w_qkv"][:, cut]).astype(LOW)

    def write_probs(pair, value):
        probs[micro, pair] = value

    def write_mix(pair, value):
        mix[rows, pair * LANES : (pair + 1) * LANES] = value

    attend(
        columns(proj, rows, 0),
        columns(proj, rows, D),
        columns(proj, rows, 2 * D),
        mask,
        write_probs,
        write_mix,
    )
    ready("w_out")
    mid = tokens.astype(F32) + mm(mix[rows, :], ref["w_out"][...])

    @pl.when(first)
    def _():
        narrow, act, result = ref["narrow"], ref["act"], ref["result"]
        narrow[rows, :] = mid.astype(LOW)
        ready("w_up")
        ready("w_down")
        total = mid
        for part in range(4):
            cut = slice(part * D, (part + 1) * D)
            hidden = mm(narrow[rows, :], ref["w_up"][:, cut])
            ref["wide"][rows, cut] = hidden
            act[rows, cut] = gelu(hidden).astype(LOW)
            total = total + mm(act[rows, cut], ref["w_down"][cut, :])
        result[rows, :] = total.astype(LOW)
        ready("w_cross")
        for part in range(2):
            cut = slice(part * D, (part + 1) * D)
            link[:, cut] = mm(result[rows, :], ref["w_cross"][:, cut]).astype(LOW)

    @pl.when(jnp.logical_not(first))
    def _():
        ref["mid_low"][rows, :] = mid.astype(LOW)
        ref["wide"][rows, :D] = mid
        ready("w_up")
        ready("w_down")
        ready("w_cross")
        ref["query"][rows, :] = mm(ref["mid_low"][rows, :], ref["w_cross"][:, :D]).astype(LOW)


FETCHED = ("lengths", "tokens", "w_qkv", "w_out", "w_up", "w_down", "w_cross", "cotangent")


def first_kernel(place_ref, *refs):
    inputs = refs[: len(FETCHED)]
    outs = list(WEIGHTS) + list(HELD) + list(STATE)
    ref = dict(zip(outs, refs[len(FETCHED) :]))
    link, lengths_ref, sems = refs[len(FETCHED) + len(outs) :]
    copies = {}
    for at, (name, source) in enumerate(zip(FETCHED, inputs)):
        if name == "lengths":
            copies[name] = fetch(source, lengths_ref, sems.at[at])
        else:
            copies[name] = fetch(source.at[0], ref[name], sems.at[at])
    forward_step(0, place_ref[0] == 0, lengths_ref, ref, link, lambda name: copies[name].wait())
    copies["cotangent"].wait()


def first_stage(place, lengths, tokens, cotangent, weights):
    given = {"lengths": lengths, "tokens": tokens, "cotangent": cotangent, **weights}
    makes = {**WEIGHTS, **HELD, **STATE, "link": ((ROWS, 2 * D), LOW)}
    results = pl.pallas_call(
        first_kernel,
        out_shape=shaped(makes),
        in_specs=[in_smem()] + [in_hbm()] * len(FETCHED),
        out_specs=[in_vmem()] * len(makes),
        scratch_shapes=[
            pltpu.SMEM((MB, 2, SLOTS), jnp.int32),
            pltpu.SemaphoreType.DMA((len(FETCHED),)),
        ],
        compiler_params=pltpu.CompilerParams(vmem_limit_bytes=16 * 1024 * 1024),
        cost_estimate=pl.CostEstimate(
            flops=2 * ROWS * D * 7168, bytes_accessed=10_000_000, transcendentals=0
        ),
        name="first_stage",
    )(place, *left([given[name] for name in FETCHED]))
    return dict(zip(makes, results))


def second_stage(place, lengths, state):
    reads = {name: state[name] for name in list(WEIGHTS) + ["tokens"]}
    keeps = {name: state[name] for name in STATE}

    def body(place_ref, lengths_hbm, *refs):
        refs = list(refs)
        ref = dict(zip(reads, refs[: len(reads)]))
        refs = refs[len(reads) + len(keeps) :]
        ref.update(zip(keeps, refs[: len(keeps)]))
        link, lengths_ref, sems = refs[len(keeps) :]
        copy = fetch(lengths_hbm, lengths_ref, sems.at[0])
        forward_step(
            1,
            place_ref[0] == 0,
            lengths_ref,
            ref,
            link,
            lambda name: copy.wait() if name == "lengths" else None,
        )

    results = pl.pallas_call(
        body,
        out_shape=same_shape(keeps.values()) + [pltpu.VMEM((ROWS, 2 * D), LOW)],
        in_specs=[in_smem(), in_hbm()] + [in_vmem()] * (len(reads) + len(keeps)),
        out_specs=[in_vmem()] * (len(keeps) + 1),
        scratch_shapes=[
            pltpu.SMEM((MB, 2, SLOTS), jnp.int32),
            pltpu.SemaphoreType.DMA((1,)),
        ],
        input_output_aliases={2 + len(reads) + i: i for i in range(len(keeps))},
        compiler_params=pltpu.CompilerParams(vmem_limit_bytes=16 * 1024 * 1024),
        cost_estimate=pl.CostEstimate(
            flops=2 * ROWS * D * 7168, bytes_accessed=10_000_000, transcendentals=0
        ),
        name="second_stage",
    )(place, *left([lengths]), *held(reads.values()), *held(keeps.values()))
    return dict(zip(list(keeps) + ["link"], results))


def middle_step(micros, ref, link_grad, links, hidden_v, probs_v, mixed_v):
    rows = slice(micros[0] * ROWS, (micros[-1] + 1) * ROWS)
    readers = []
    for at, micro in enumerate(micros):
        mine = slice(micro * ROWS, (micro + 1) * ROWS)
        mask = ref["across"][mine, :] != 0.0
        whole = slice(0, ROWS)
        reads = (
            columns(ref["query"], mine, 0),
            columns(links[at], whole, 0),
            columns(links[at], whole, D),
        )

        def write_probs(pair, value, at=at):
            probs_v[at, pair] = value

        def write_mix(pair, value, mine=mine):
            ref["cross_mix"][mine, pair * LANES : (pair + 1) * LANES] = value

        attend(*reads, mask, write_probs, write_mix)
        readers.append((mine, reads))
    w_back = ref["w_cross"][:, D:]
    after = ref["wide"][rows, :D] + mm(ref["cross_mix"][rows, :], w_back)
    narrow, act = ref["narrow"], ref["act"]
    narrow[rows, :] = after.astype(LOW)
    total = after
    for part in range(4):
        cut = slice(part * D, (part + 1) * D)
        hidden = mm(narrow[rows, :], ref["w_up"][:, cut])
        hidden_v[:, cut] = hidden
        act[rows, cut] = gelu(hidden).astype(LOW)
        total = total + mm(act[rows, cut], ref["w_down"][cut, :])
    ref["result"][rows, :] = total.astype(LOW)
    cotangent = ref["cotangent"][rows, :]
    grad = cotangent.astype(F32)
    for part in range(4):
        cut = slice(part * D, (part + 1) * D)
        grad_act = mm_nt(cotangent, ref["w_down"][cut, :])
        grad_hidden = (gelu_slope(hidden_v[:, cut]) * grad_act).astype(LOW)
        ref["grad_hidden"][rows, cut] = grad_hidden
        grad = grad + mm_nt(grad_hidden, ref["w_up"][:, cut])
    ref["grad"][rows, :] = grad
    ref["grad_low"][rows, :] = grad.astype(LOW)
    mixed_v[...] = mm_nt(ref["grad_low"][rows, :], w_back).astype(LOW)
    for at, (mine, reads) in enumerate(readers):

        def write(pair, grad_q, grad_k, grad_v, mine=mine, at=at):
            ref["query_grad"][mine, pair * LANES : (pair + 1) * LANES] = grad_q
            link_grad[at, :, pair * LANES : (pair + 1) * LANES] = grad_k
            link_grad[at, :, D + pair * LANES : D + (pair + 1) * LANES] = grad_v

        attend_back(
            *reads,
            lambda pair, at=at: probs_v[at, pair],
            columns(mixed_v, slice(at * ROWS, (at + 1) * ROWS), 0),
            write,
        )


def middle_stage(micros, place, state, back, links):
    count = len(micros)
    names = ("query", "across", "wide", "cotangent", "w_cross", "w_up", "w_down")
    reads = {name: state[name] for name in names}
    reads.update({f"link{i}": link for i, link in enumerate(links)})
    keeps = {name: state[name] for name in ("narrow", "act", "result")}
    makes = {"link_grad": ((count, ROWS, 2 * D), LOW)}
    if back is None:
        makes.update(BACK)
    else:
        keeps.update(back)

    def kernel(place_ref, ref, *scratch):
        @pl.when(place_ref[0] != 0)
        def _():
            arrived = [ref[f"link{i}"] for i in range(count)]
            middle_step(micros, ref, ref["link_grad"], arrived, *scratch)

    return call(
        kernel,
        "middle_stage",
        place,
        reads,
        keeps,
        makes,
        scratch=(
            pltpu.VMEM((count * ROWS, FF), F32),
            pltpu.VMEM((count, PAIRS, ROWS, 2 * ROWS), F32),
            pltpu.VMEM((count * ROWS, D), LOW),
        ),
        cost=(2 * count * ROWS * D * 10000, 8_000_000),
    )


def put_block(core, keep, send, at, left_ref, left_at, right):
    own = pl.ds(pl.multiple_of(left_at + core * HALF, HALF), HALF)
    other = pl.ds(pl.multiple_of(left_at + (1 - core) * HALF, HALF), HALF)
    send[at] = mm_tn(left_ref[:, other], right).astype(LOW)
    keep[at] = mm_tn(left_ref[:, own], right)


def back_step(micro, first, ref):
    rows = slice(micro * ROWS, (micro + 1) * ROWS)

    @pl.when(first)
    def _():
        cotangent = ref["cotangent"][rows, :].astype(F32)
        grad = cotangent + mm_nt(ref["link_grad"][...], ref["w_cross"][...])
        grad_low = grad.astype(LOW)
        ref["grad_low"][rows, :] = grad_low
        for part in range(4):
            cut = slice(part * D, (part + 1) * D)
            grad_act = mm_nt(grad_low, ref["w_down"][cut, :])
            grad_hidden = (gelu_slope(ref["wide"][rows, cut]) * grad_act).astype(LOW)
            ref["grad_hidden"][rows, cut] = grad_hidden
            grad = grad + mm_nt(grad_hidden, ref["w_up"][:, cut])
        ref["grad"][rows, :] = grad

    @pl.when(jnp.logical_not(first))
    def _():
        through = mm_nt(ref["query_grad"][rows, :], ref["w_cross"][:, :D])
        ref["grad"][rows, :] = ref["grad"][rows, :] + through


def back_stage(micro, place, state, back, link_grad):
    names = ("cotangent", "w_cross", "w_up", "w_down", "wide")
    reads = {name: state[name] for name in names}
    reads["query_grad"] = back["query_grad"]
    reads["link_grad"] = link_grad
    keeps = {name: back[name] for name in ("grad_hidden", "grad_low", "grad")}

    def kernel(place_ref, ref):
        back_step(micro, place_ref[0] == 0, ref)

    return call(
        kernel,
        "back_stage",
        place,
        reads,
        keeps,
        {},
        cost=(2 * ROWS * D * 5000, 5_000_000),
    )


def early_kernel(place_ref, ref, right_v):
    core = place_ref[1]
    keep, send = ref["keep"], ref["send"]

    @pl.when(place_ref[0] == 0)
    def _():
        for micro in range(MB):
            right_v[micro * ROWS : (micro + 1) * ROWS, :] = ref[f"link_grad{micro}"][...]
        for part in range(2):
            cut = slice(part * D, (part + 1) * D)
            put_block(core, keep, send, CROSS_AT + part, ref["result"], 0, right_v[:, cut])
        right_v[:, :D] = ref["grad_low"][...]

    @pl.when(place_ref[0] != 0)
    def _():
        put_block(core, keep, send, CROSS_AT, ref["mid_low"], 0, ref["query_grad"][...])
        put_block(core, keep, send, CROSS_AT + 1, ref["cross_mix"], 0, ref["grad_low"][...])
        right_v[:, :D] = ref["cotangent"][...]

    for part in range(4):
        cut = slice(part * D, (part + 1) * D)
        put_block(core, keep, send, UP_AT + part, ref["narrow"], 0, ref["grad_hidden"][:, cut])
        put_block(core, keep, send, DOWN_AT + part, ref["act"], part * D, right_v[:, :D])


def early_stage(place, state, back, link_grads):
    reads = {name: state[name] for name in ("cotangent", "narrow", "act", "result", "mid_low")}
    names = ("cross_mix", "grad_hidden", "grad_low", "query_grad")
    reads.update({name: back[name] for name in names})
    reads.update({f"link_grad{i}": value for i, value in enumerate(link_grads)})
    makes = {"keep": ((EARLY, HALF, D), F32), "send": ((EARLY, HALF, D), LOW)}
    return call(
        early_kernel,
        "early_stage",
        place,
        reads,
        {},
        makes,
        scratch=(pltpu.VMEM((MB * ROWS, 2 * D), LOW),),
        cost=(2 * 256 * D * 5000, 20_000_000),
    )


def late_kernel(place_ref, ref, g_v, mixed_v, grad_proj):
    core = place_ref[1]
    keep, send = ref["keep"], ref["send"]
    g_v[...] = ref["grad"][...].astype(LOW)
    mixed_v[...] = mm_nt(g_v[...], ref["w_out"][...]).astype(LOW)
    for micro in range(MB):
        rows = slice(micro * ROWS, (micro + 1) * ROWS)

        def write(pair, grad_q, grad_k, grad_v, rows=rows):
            for part, value in enumerate((grad_q, grad_k, grad_v)):
                at = part * D + pair * LANES
                grad_proj[rows, at : at + LANES] = value

        attend_back(
            columns(ref["proj"], rows, 0),
            columns(ref["proj"], rows, D),
            columns(ref["proj"], rows, 2 * D),
            lambda pair, micro=micro: ref["probs"][micro, pair],
            columns(mixed_v, rows, 0),
            write,
        )
    put_block(core, keep, send, 0, ref["mix"], 0, g_v[...])
    for part in range(3):
        cut = slice(part * D, (part + 1) * D)
        put_block(core, keep, send, 1 + part, ref["tokens"], 0, grad_proj[:, cut])
    grad_in = ref["grad"][...] + mm_nt(grad_proj[...], ref["w_qkv"][...])
    ref["input_grad"][0] = grad_in.astype(LOW)
    ref["outputs"][0] = ref["result"][...]


def late_stage(place, state, grad):
    names = ("tokens", "mix", "proj", "probs", "result", "w_qkv", "w_out")
    reads = {name: state[name] for name in names}
    reads["grad"] = grad
    makes = {
        "keep": ((LATE, HALF, D), F32),
        "send": ((LATE, HALF, D), LOW),
        "outputs": ((1, MB * ROWS, D), LOW),
        "input_grad": ((1, MB * ROWS, D), LOW),
    }
    return call(
        late_kernel,
        "late_stage",
        place,
        reads,
        {},
        makes,
        scratch=(
            pltpu.VMEM((MB * ROWS, D), LOW),
            pltpu.VMEM((MB * ROWS, D), LOW),
            pltpu.VMEM((MB * ROWS, 3 * D), LOW),
        ),
        cost=(2 * 256 * D * 5000, 12_000_000),
    )


def chip_sum_kernel(keep_a, got_a, keep_b, got_b, total):
    total[:EARLY] = (keep_a[...] + got_a[...].astype(F32)).astype(LOW)
    total[EARLY:] = (keep_b[...] + got_b[...].astype(F32)).astype(LOW)


def chip_sum(keep_a, got_a, keep_b, got_b):
    return pl.pallas_call(
        chip_sum_kernel,
        out_shape=jax.ShapeDtypeStruct((BLOCKS, HALF, D), LOW),
        in_specs=[in_vmem()] * 4,
        out_specs=in_vmem(),
        compiler_params=pltpu.CompilerParams(vmem_limit_bytes=16 * 1024 * 1024),
        name="chip_sum",
    )(*held([keep_a, got_a, keep_b, got_b]))


GRADS = (((1, D, 3 * D), F32), ((1, D, D), F32), ((1, D, 2 * D), F32), ((1, D, FF), F32), ((1, FF, D), F32))


def unpack_half(half, packed, grads, slots, sems):
    g_qkv, g_out, g_cross, g_up, g_down = grads
    rows = pl.ds(pl.multiple_of(half * HALF, HALF), HALF)
    places = (
        [g_cross.at[0, rows, pl.ds(p * D, D)] for p in range(2)]
        + [g_up.at[0, rows, pl.ds(p * D, D)] for p in range(4)]
        + [
            g_down.at[0, pl.ds(pl.multiple_of(p * D + half * HALF, HALF), HALF), :]
            for p in range(4)
        ]
        + [g_out.at[0, rows, :]]
        + [g_qkv.at[0, rows, pl.ds(p * D, D)] for p in range(3)]
    )
    copies = []
    for block, place in enumerate(places):
        slots[block] = packed[block * HALF : (block + 1) * HALF, :].astype(F32)
        copies.append(fetch(slots.at[block], place, sems.at[block]))
    for copy in copies:
        copy.wait()


def unpack(place, own, other):
    out_shape = [jax.ShapeDtypeStruct(shape, kind) for shape, kind in GRADS]
    scratch = [pltpu.VMEM((BLOCKS, HALF, D), F32), pltpu.SemaphoreType.DMA((BLOCKS,))]

    def own_kernel(place_ref, packed, *refs):
        unpack_half(place_ref[1], packed, refs[:5], *refs[5:])

    def other_kernel(place_ref, packed, *refs):
        unpack_half(1 - place_ref[1], packed, refs[5:10], *refs[10:])

    grads = pl.pallas_call(
        own_kernel,
        out_shape=out_shape,
        in_specs=[in_smem(), in_vmem()],
        out_specs=[in_hbm()] * 5,
        scratch_shapes=scratch,
        name="unpack_own",
    )(place, own)
    return pl.pallas_call(
        other_kernel,
        out_shape=out_shape,
        in_specs=[in_smem(), in_vmem()] + [in_hbm()] * 5,
        out_specs=[in_hbm()] * 5,
        scratch_shapes=scratch,
        input_output_aliases={2 + i: i for i in range(5)},
        name="unpack_other",
    )(place, other, *grads)


def ring_groups(count):
    chips = count // 2
    across = 2 if chips % 2 == 0 else 1
    along = chips // across
    order = [z * across for z in range(along)]
    if across == 2:
        order += [z * across + 1 for z in reversed(range(along))]
    return [[2 * chip + core for chip in order] for core in range(2)]


def swap_cores(value, count):
    return lax.ppermute(value, "dp", [(i, i ^ 1) for i in range(count)])


def on_device(inputs, lengths, w_qkv, w_attn_out, w_cross, w_up, w_down, cotangent):
    count = lax.axis_size("dp")
    place = jnp.stack([lax.axis_index("section"), lax.axis_index("dp") % 2]).astype(jnp.int32)
    weights = dict(zip(WEIGHTS, (w_qkv, w_attn_out, w_cross, w_up, w_down)))

    def to_decoder(link):
        return lax.ppermute(link, "section", [(0, 1)])

    def to_encoder(link_grad):
        return lax.ppermute(link_grad, "section", [(1, 0)])

    state = first_stage(place, lengths, inputs, cotangent, weights)
    link0 = to_decoder(state.pop("link"))
    state.update(second_stage(place, lengths, state))
    link1 = to_decoder(state.pop("link"))
    if SPLIT:
        back = middle_stage((0,), place, state, None, [link0])
        grad0 = to_encoder(back.pop("link_grad"))
        state.update({name: back.pop(name) for name in ("narrow", "act", "result")})
        back = middle_stage((1,), place, state, back, [link1])
        grad1 = to_encoder(back.pop("link_grad"))
        state.update({name: back.pop(name) for name in ("narrow", "act", "result")})
        link_grads = [grad0[0], grad1[0]]
    else:
        back = middle_stage((0, 1), place, state, None, [link0, link1])
        grads = to_encoder(back.pop("link_grad"))
        state.update({name: back.pop(name) for name in ("narrow", "act", "result")})
        link_grads = [grads[0], grads[1]]
    for micro in range(MB):
        back.update(back_stage(micro, place, state, back, link_grads[micro]))
    early = early_stage(place, state, back, link_grads)
    got_a = swap_cores(early["send"], count)
    late = late_stage(place, state, back["grad"])
    got_b = swap_cores(late["send"], count)
    total = chip_sum(early["keep"], got_a, late["keep"], got_b).reshape(BLOCKS * HALF, D)
    groups = ring_groups(count)
    piece = lax.psum_scatter(
        total, "dp", scatter_dimension=0, tiled=True, axis_index_groups=groups
    )
    own = lax.all_gather(piece, "dp", axis=0, tiled=True, axis_index_groups=groups)
    grads = unpack(place, own, swap_cores(own, count))
    return (late["outputs"], late["input_grad"], *grads)


def solution(mesh):
    return jax.shard_map(
        on_device,
        mesh=mesh,
        in_specs=(
            P("section", "dp", None),
            P("dp", None, None),
            P("section", None, None),
            P("section", None, None),
            P("section", None, None),
            P("section", None, None),
            P("section", None, None),
            P("section", "dp", None),
        ),
        out_specs=(
            P("section", "dp", None),
            P("section", "dp", None),
            P("section", None, None),
            P("section", None, None),
            P("section", None, None),
            P("section", None, None),
            P("section", None, None),
        ),
        check_vma=False,
    )
```

time: 506 us -> 167 us (0.33); the launches traced: 500 us -> 167 us
  waiting for transfers between devices: 299 us -> 107 us
  local copies, waits for them, and re-layouts: 78.9 us -> 3.24 us
  matrix products: 59.3 us -> 0 us
  other arithmetic: 40.1 us -> 0.08 us
  Pallas kernels: 0 us -> 34.4 us
    psum x1 -> x0, waiting for transfers between devices: 265 us -> none  [on_device(): lax.psum((running[0], running[1], running[2], running[3], running[4]), 'dp')]
    dot_general x44 -> x0, matrix products: 59.3 us -> none  [the longest x10 23.5 us: weight_dot(): lax.dot_general(values_in, grad_in, (((0,), (0,)), ((), ())), preferred_e...]
    all_gather x0 -> x1, waiting for transfers between devices: none -> 44.5 us  [on_device(): lax.all_gather(piece, 'dp', axis=0, tiled=True, axis_index_groups=groups)]
    reduce_scatter x0 -> x1, waiting for transfers between devices: none -> 44 us  [on_device(): lax.psum_scatter(total, 'dp', scatter_dimension=0, tiled=True, axis_index...]
    cond x96 -> x0, local copies, waits for them, and re-layouts: 35.8 us -> none  [the longest x8 29 us: on_device(): lax.cond(is_first, encode_back, silenced(encode_back), (tokens_now, upstr...]
    pallas_call x0 -> x11, Pallas kernels: none -> 34.4 us  [the longest x6 13.9 us: call(): pl.pallas_call(body, out_shape=out_shape, in_specs=[in_smem()] + [in_vmem...]
    broadcast_in_dim x7 -> x0, other arithmetic: 30.5 us -> none  [the longest x1 7.79 us: on_device(): running[3][None]]
    another operation x23 -> x0, local copies, waits for them, and re-layouts: 25.2 us -> none
  transfers between devices with their start and end apart: 5 -> 9, of which waited for: 4 -> 7; matrix products, arithmetic and copies ran while one was open for 16% -> 1% of each run, Pallas kernels for 0% -> 11%
where the time goes in v2:
time: 167 us
  waiting for transfers between devices  107 us (64%)
  Pallas kernels  34.4 us (21%)
  between operations  14.2 us (9%)
  starting transfers between devices  8.2 us (5%)
  local copies, waits for them, and re-layouts  3.24 us (2%)
    all_gather x1, waiting for transfers between devices, on_device(): lax.all_gather(piece, 'dp', axis=0, tiled=True, axis_index_groups=groups)  44.5 us
    reduce_scatter x1, waiting for transfers between devices, on_device(): lax.psum_scatter(total, 'dp', scatter_dimension=0, tiled=True, axis_index...  44 us
    pallas_call x6, Pallas kernels, call(): pl.pallas_call(body, out_shape=out_shape, in_specs=[in_smem()] + [in_vmem...  13.9 us
    ppermute x2, waiting for transfers between devices, to_encoder(): return lax.ppermute(link_grad, 'section', [(1, 0)])  12.3 us
    pallas_call x1, Pallas kernels, first_stage(): pl.pallas_call(first_kernel, out_shape=shaped(makes), in_specs=[in_smem()...  5.29 us
    pallas_call x1, Pallas kernels, unpack(): pl.pallas_call(other_kernel, out_shape=out_shape, in_specs=[in_smem(), in...  5.16 us
    pallas_call x1, Pallas kernels, unpack(): pl.pallas_call(own_kernel, out_shape=out_shape, in_specs=[in_smem(), in_v...  5.16 us
    ppermute x2, starting transfers between devices, to_decoder(): return lax.ppermute(link, 'section', [(0, 1)])  4.91 us
  transfers between devices with their start and end apart: 9, of which 7 were waited for; matrix products, arithmetic and copies ran while one was open for 1% of the time, Pallas kernels for 11%

profile of v2, /device:TPU:0, one launch (start us, length us, event | category | flops | bytes accessed | tf_op | source)
XLA Modules:
  0.0 167.2 jit_solution(9883415626359236058)
XLA Ops:
  7.2 0.0 reduce-scatter.2.cloned.1.call-start
  7.2 0.1 pad_add_fusion.place_ref
  7.3 0.0 copy-start.1
  7.3 5.3 %first_stage.1 = (bf16[512,1536]{1,0:T(8,128)(2,1)S(1)}, bf16[512,512]{1,0:T(8,128)(2,1)S(1)}, bf16[512,1024]{1,0:T(8,128)(2,1)S(1)}, bf16[512,2048]{1,0:T(8,128...) custom-call(s32[2]{0:T(128)S(1)} %pad_add_fusion.place_ref, ...), custom_call_target="tpu_custom_call" | custom-call | flops 939524096 | bytes 10000000 | tf_op jit(solution)/shard_map/first_stage/pallas_call | solution.py:308
  12.6 3.6 %collective-permute-start.1 = (bf16[128,1024]{1,0:T(8,128)(2,1)S(1)}, bf16[128,1024]{1,0:T(8,128)(2,1)S(1)}, u32[]{:S(2)}, u32[]{:S(2)}) collective-permute-start(bf16[128,1024]{1,0:T(8,128)(2,1)S(1)} %get-tuple-element.100), channel_id=1, source_target_pairs={{0,16},{1,17},{2,18},{3,19},{4,20},{5,21},{6,22},{7,23},{8,24},{9,... | collective-permute-start | bytes 786440 | tf_op jit(solution)/shard_map/ppermute | solution.py:697
  16.2 4.3 %second_stage.1 = (bf16[256,1536]{1,0:T(8,128)(2,1)S(1)}, bf16[256,512]{1,0:T(8,128)(2,1)S(1)}, f32[2,4,128,256]{3,2,1,0:T(8,128)S(1)}, f32[256,2048]{1,0:T(8,12...) custom-call(s32[2]{0:T(128)S(1)} %pad_add_fusion.place_ref, ...), custom_call_target="tpu_custom_call", output_to_operand_aliasing={{0}: (8, {}), {1}: (9, {}), {2}: (10, {}), {3}: (11, {}), {... | custom-call | flops 939524096 | bytes 10000000 | tf_op jit(solution)/shard_map/second_stage/pallas_call | solution.py:346
  20.5 1.3 collective-permute-start
  21.8 0.0 collective-permute-done.1.refs_7_
  21.8 0.6 middle_stage.2
  22.4 1.3 collective-permute-start.3
  23.7 3.7 %collective-permute-done.refs_7_ = bf16[128,1024]{1,0:T(8,128)(2,1)S(1)} collective-permute-done((bf16[128,1024]{1,0:T(8,128)(2,1)S(1)}, bf16[128,1024]{1,0:T(8,128)(2,1)S(1)}, u32[]{:S(2)}, u32[]{:S(2)}) %collective-permute-start) | collective-permute-done | bytes 262176 | tf_op jit(solution)/shard_map/ppermute | solution.py:697
  27.4 0.7 middle_stage.3
  28.1 1.3 collective-permute-start.2
  29.4 7.6 %collective-permute-done.3 = bf16[1,128,1024]{2,1,0:T(8,128)(2,1)S(1)} collective-permute-done((bf16[1,128,1024]{2,1,0:T(8,128)(2,1)S(1)}, bf16[1,128,1024]{2,1,0:T(8,128)(2,1)S(1)}, u32[]{:S(2)}, u32[]{:S(2)}) %collective-permute-start.3) | collective-permute-done | bytes 262176 | tf_op jit(solution)/shard_map/ppermute | solution.py:700
  37.0 2.8 %back_stage.2 = (bf16[256,2048]{1,0:T(8,128)(2,1)S(1)}, bf16[256,512]{1,0:T(8,128)(2,1)S(1)}, f32[256,512]{1,0:T(8,128)S(1)}) custom-call(s32[2]{0:T(128)S(1)} %pad_add_fusion.place_ref, bf16[256,512]{1,0:T(8,128)(2,1)S(1)} %get-tuple-element.98.refs_3_.refs_0_, ...), custom_call_target="tpu_custom_call", output_to_operand_aliasing={{0}: (8, {}), {1}: (9, {}), {2}: (10, {})} | custom-call | flops 655360000 | bytes 5000000 | tf_op jit(solution)/shard_map/back_stage/pallas_call | solution.py:207
  39.8 4.7 %collective-permute-done.2 = bf16[1,128,1024]{2,1,0:T(8,128)(2,1)S(1)} collective-permute-done((bf16[1,128,1024]{2,1,0:T(8,128)(2,1)S(1)}, bf16[1,128,1024]{2,1,0:T(8,128)(2,1)S(1)}, u32[]{:S(2)}, u32[]{:S(2)}) %collective-permute-start.2) | collective-permute-done | bytes 262176 | tf_op jit(solution)/shard_map/ppermute | solution.py:700
  44.6 2.8 %back_stage.3 = (bf16[256,2048]{1,0:T(8,128)(2,1)S(1)}, bf16[256,512]{1,0:T(8,128)(2,1)S(1)}, f32[256,512]{1,0:T(8,128)S(1)}) custom-call(s32[2]{0:T(128)S(1)} %pad_add_fusion.place_ref, bf16[256,512]{1,0:T(8,128)(2,1)S(1)} %get-tuple-element.98.refs_3_.refs_0_, ...), custom_call_target="tpu_custom_call", output_to_operand_aliasing={{0}: (8, {}), {1}: (9, {}), {2}: (10, {})} | custom-call | flops 655360000 | bytes 5000000 | tf_op jit(solution)/shard_map/back_stage/pallas_call | solution.py:207
  47.4 2.6 %early_stage.1 = (f32[10,256,512]{2,1,0:T(8,128)S(1)}, bf16[10,256,512]{2,1,0:T(8,128)(2,1)S(1)}) custom-call(s32[2]{0:T(128)S(1)} %pad_add_fusion.place_ref, bf16[256,512]{1,0:T(8,128)(2,1)S(1)} %get-tuple-element.98.refs_3_.refs_0_, bf16[256,512]{1,0:T(8,128)(2,1)S(1)} %get-tuple-element.125.refs_1_, bf16[256,2048]{1,0:T(8,128)(2,1)S(1)} %get-tuple-element.126.refs_2_, ...), custom_call_target="tpu_custom_call" | custom-call | flops 1310720000 | bytes 20000000 | tf_op jit(solution)/shard_map/early_stage/pallas_call | solution.py:207
  50.0 0.1 collective-permute-start.4
  50.0 0.0 copy-done.1
  50.0 4.4 %late_stage.1 = (f32[4,256,512]{2,1,0:T(8,128)S(1)}, bf16[4,256,512]{2,1,0:T(8,128)(2,1)S(1)}, bf16[1,256,512]{2,1,0:T(8,128)(2,1)S(1)}, bf16[1,256,512]{2,1,0:T(8,128)(2,1)S(1)}) custom-call(s32[2]{0:T(128)S(1)} %pad_add_fusion.place_ref, bf16[256,512]{1,0:T(8,128)(2,1)S(1)} %get-tuple-element.76.refs_5_.refs_0_, ...), custom_call_target="tpu_custom_call" | custom-call | flops 1310720000 | bytes 12000000 | tf_op jit(solution)/shard_map/late_stage/pallas_call | solution.py:207
  54.4 0.6 collective-permute-start.5
  55.0 2.3 %collective-permute-done.5.got_b = bf16[4,256,512]{2,1,0:T(8,128)(2,1)S(1)} collective-permute-done((bf16[4,256,512]{2,1,0:T(8,128)(2,1)S(1)}, bf16[4,256,512]{2,1,0:T(8,128)(2,1)S(1)}, u32[]{:S(2)}, u32[]{:S(2)}) %collective-permute-start.5) | collective-permute-done | bytes 1048608 | tf_op jit(solution)/shard_map/ppermute | solution.py:688
  57.3 0.0 collective-permute-done.4.got_a
  57.3 0.7 chip_sum.1
  57.9 0.0 copy-start
  58.0 1.8 %copy-done = bf16[14,256,512]{2,1,0:T(8,128)(2,1)} copy-done((bf16[14,256,512]{2,1,0:T(8,128)(2,1)}, bf16[14,256,512]{2,1,0:T(8,128)(2,1)S(1)}, u32[]{:S(2)}) %copy-start) | copy-done | bytes 3670040
  59.8 0.0 reduce-scatter.2.cloned.1.call-update
  59.8 0.0 all-gather.2.cloned.1.call-start
  59.9 44.0 %reduce-scatter.2.cloned.1.call-done = bf16[448,512]{1,0:T(8,128)(2,1)} async-done(((bf16[3584,512]{1,0:T(8,128)(2,1)}), bf16[448,512]{1,0:T(8,128)(2,1)}) %reduce-scatter.2.cloned.1.call-update) | async-done | bytes 458768 | tf_op jit(solution)/shard_map/reduce_scatter | solution.py:727
  103.8 0.0 all-gather.2.cloned.1.call-update
  103.8 44.5 %all-gather.2.cloned.1.call-done.packed = bf16[3584,512]{1,0:T(8,128)(2,1)} async-done(((bf16[448,512]{1,0:T(8,128)(2,1)}), bf16[3584,512]{1,0:T(8,128)(2,1)}) %all-gather.2.cloned.1.call-update) | async-done | bytes 3670032 | tf_op jit(solution)/shard_map/all_gather | solution.py:730
  148.4 0.0 collective-permute-start.6
  148.4 0.7 copy.79
  149.1 0.7 copy.80
  149.8 5.2 %unpack_own.1 = (f32[1,512,1536]{2,1,0:T(8,128)}, f32[1,512,512]{2,1,0:T(8,128)}, f32[1,512,1024]{2,1,0:T(8,128)}, f32[1,512,2048]{2,1,0:T(8,128)}, f32[1,2048,512]{2,1,0:T(8,128)}) custom-call(s32[2]{0:T(128)} %copy-done.1, bf16[3584,512]{1,0:T(8,128)(2,1)} %all-gather.2.cloned.1.call-done.packed), custom_call_target="tpu_custom_call" | custom-call | tf_op jit(solution)/shard_map/unpack_own/pallas_call | solution.py:658
  155.0 0.2 collective-permute-done.6.packed
  155.1 5.2 %unpack_other.1 = (f32[1,512,1536]{2,1,0:T(8,128)}, f32[1,512,512]{2,1,0:T(8,128)}, f32[1,512,1024]{2,1,0:T(8,128)}, f32[1,512,2048]{2,1,0:T(8,128)}, f32[1,2048,512]{2,1,0:T(8,128)}) custom-call(s32[2]{0:T(128)} %copy-done.1, ...), custom_call_target="tpu_custom_call", output_to_operand_aliasing={{0}: (2, {}), {1}: (3, {}), {2}: (4, {}), {3}: (5, {}), {4}... | custom-call | tf_op jit(solution)/shard_map/unpack_other/pallas_call | solution.py:666
Async XLA Ops:
  7.2 96.7 %reduce-scatter.2.cloned.1.call-start = ((), (), s32[]{:S(2)}) async-start(), calls=%async_computation.1 | async-start | bytes 4128768 | tf_op jit(solution)/shard_map/reduce_scatter | solution.py:727
  7.3 42.7 %copy-start.1 = (s32[2]{0:T(128)}, s32[2]{0:T(128)S(1)}, u32[]{:S(2)}) copy-start(s32[2]{0:T(128)S(1)} %pad_add_fusion.place_ref) | copy-start | bytes 28
  12.6 9.2 %collective-permute-start.1 = (bf16[128,1024]{1,0:T(8,128)(2,1)S(1)}, bf16[128,1024]{1,0:T(8,128)(2,1)S(1)}, u32[]{:S(2)}, u32[]{:S(2)}) collective-permute-start(bf16[128,1024]{1,0:T(8,128)(2,1)S(1)} %get-tuple-element.100), channel_id=1, source_target_pairs={{0,16},{1,17},{2,18},{3,19},{4,20},{5,21},{6,22},{7,23},{8,24},{9,... | collective-permute-start | bytes 786440 | tf_op jit(solution)/shard_map/ppermute | solution.py:697
  20.5 6.9 %collective-permute-start = (bf16[128,1024]{1,0:T(8,128)(2,1)S(1)}, bf16[128,1024]{1,0:T(8,128)(2,1)S(1)}, u32[]{:S(2)}, u32[]{:S(2)}) collective-permute-start(bf16[128,1024]{1,0:T(8,128)(2,1)S(1)} %get-tuple-element.99), channel_id=1, source_target_pairs={{0,16},{1,17},{2,18},{3,19},{4,20},{5,21},{6,22},{7,23},{8,24},{9,... | collective-permute-start | bytes 786440 | tf_op jit(solution)/shard_map/ppermute | solution.py:697
  22.4 14.6 %collective-permute-start.3 = (bf16[1,128,1024]{2,1,0:T(8,128)(2,1)S(1)}, bf16[1,128,1024]{2,1,0:T(8,128)(2,1)S(1)}, u32[]{:S(2)}, u32[]{:S(2)}) collective-permute-start(bf16[1,128,1024]{2,1,0:T(8,128)(2,1)S(1)} %get-tuple-element.115), channel_id=1, source_target_pairs={{16,0},{17,1},{18,2},{19,3},{20,4},{21,5},{22,6},{23,7},{24,8},{25... | collective-permute-start | bytes 786440 | tf_op jit(solution)/shard_map/ppermute | solution.py:700
  28.1 16.5 %collective-permute-start.2 = (bf16[1,128,1024]{2,1,0:T(8,128)(2,1)S(1)}, bf16[1,128,1024]{2,1,0:T(8,128)(2,1)S(1)}, u32[]{:S(2)}, u32[]{:S(2)}) collective-permute-start(bf16[1,128,1024]{2,1,0:T(8,128)(2,1)S(1)} %get-tuple-element.114), channel_id=1, source_target_pairs={{16,0},{17,1},{18,2},{19,3},{20,4},{21,5},{22,6},{23,7},{24,8},{25... | collective-permute-start | bytes 786440 | tf_op jit(solution)/shard_map/ppermute | solution.py:700
  50.0 7.3 %collective-permute-start.4 = (bf16[10,256,512]{2,1,0:T(8,128)(2,1)S(1)}, bf16[10,256,512]{2,1,0:T(8,128)(2,1)S(1)}, u32[]{:S(2)}, u32[]{:S(2)}) collective-permute-start(bf16[10,256,512]{2,1,0:T(8,128)(2,1)S(1)} %get-tuple-element.132), channel_id=1, source_target_pairs={{0,1},{1,0},{2,3},{3,2},{4,5},{5,4},{6,7},{7,6},{8,9},{9,8},{10,11... | collective-permute-start | bytes 7864328 | tf_op jit(solution)/shard_map/ppermute | solution.py:688
  54.4 2.8 %collective-permute-start.5 = (bf16[4,256,512]{2,1,0:T(8,128)(2,1)S(1)}, bf16[4,256,512]{2,1,0:T(8,128)(2,1)S(1)}, u32[]{:S(2)}, u32[]{:S(2)}) collective-permute-start(bf16[4,256,512]{2,1,0:T(8,128)(2,1)S(1)} %get-tuple-element.134), channel_id=1, source_target_pairs={{0,1},{1,0},{2,3},{3,2},{4,5},{5,4},{6,7},{7,6},{8,9},{9,8},{10,11... | collective-permute-start | bytes 3145736 | tf_op jit(solution)/shard_map/ppermute | solution.py:688
  57.9 1.8 %copy-start = (bf16[14,256,512]{2,1,0:T(8,128)(2,1)}, bf16[14,256,512]{2,1,0:T(8,128)(2,1)S(1)}, u32[]{:S(2)}) copy-start(bf16[14,256,512]{2,1,0:T(8,128)(2,1)S(1)} %chip_sum.1) | copy-start | bytes 11010052
  59.8 88.6 %all-gather.2.cloned.1.call-start = ((), (), s32[]{:S(2)}) async-start(), calls=%async_computation.2 | async-start | bytes 4128768 | tf_op jit(solution)/shard_map/all_gather | solution.py:730
  148.4 6.8 %collective-permute-start.6 = (bf16[3584,512]{1,0:T(8,128)(2,1)}, bf16[3584,512]{1,0:T(8,128)(2,1)}, u32[]{:S(2)}, u32[]{:S(2)}) collective-permute-start(bf16[3584,512]{1,0:T(8,128)(2,1)} %all-gather.2.cloned.1.call-done.packed), channel_id=1, source_target_pairs={{0,1},{1,0},{2,3},{3,2},{4,5},{5,4},{6,7},{7,6},{8,9},{9,8},{10,11... | collective-permute-start | bytes 11010056 | tf_op jit(solution)/shard_map/ppermute | solution.py:688
Sparse Core Ops, SparseCore 0:
  59.9 43.8 reduce-scatter.1
  105.4 42.9 all-gather.1

commit v3 on v0

v3 whole, which is shorter than its diff:
```python
from types import SimpleNamespace

import jax
import jax.numpy as jnp
from jax import lax
from jax.experimental import pallas as pl
from jax.experimental.pallas import tpu as pltpu
from jax.sharding import PartitionSpec as P

D = 512
HEADS = 8
HEAD_DIM = 64
FF = 2048
ROWS = 128
SLOTS = 16
MB = 2
BOTH = MB * ROWS
PAIRS = HEADS // 2
LANES = 2 * HEAD_DIM
HALF = D // 2
SCALE = HEAD_DIM ** (-0.5)
GELU_IN = 0.7978845608028654
GELU_CUBE = 0.044715
LOW = jnp.bfloat16
F32 = jnp.float32
MIB = 1024 * 1024
DP = "dp"
SECTION = "section"
PLACE = 4


def mm(left, right):
    return jnp.dot(left, right, preferred_element_type=F32)


def mm_nt(left, right):
    return lax.dot_general(left, right, (((1,), (1,)), ((), ())), preferred_element_type=F32)


def mm_tn(left, right):
    return lax.dot_general(left, right, (((0,), (0,)), ((), ())), preferred_element_type=F32)


def gelu(hidden):
    inner = GELU_IN * (hidden + GELU_CUBE * (hidden * hidden * hidden))
    return hidden * (0.5 * (1.0 + jnp.tanh(inner)))


def gelu_slope(hidden):
    square = hidden * hidden
    inner = GELU_IN * (hidden + GELU_CUBE * (square * hidden))
    bent = jnp.tanh(inner)
    inner_slope = GELU_IN * (1.0 + (3.0 * GELU_CUBE) * square)
    return 0.5 * (1.0 + bent) + 0.5 * hidden * (1.0 - bent * bent) * inner_slope


def segments(lengths_ref, micro, which, dim):
    position = lax.broadcasted_iota(jnp.int32, (ROWS, ROWS), dim)
    end = jnp.int32(0)
    seg = jnp.zeros((ROWS, ROWS), jnp.int32)
    for slot in range(SLOTS):
        end = end + lengths_ref[micro, which, slot]
        seg = seg + (position >= end).astype(jnp.int32)
    return seg


def low_lanes():
    return lax.broadcasted_iota(jnp.int32, (ROWS, LANES), 1) < HEAD_DIM


def two_heads(pair, lanes):
    nothing = jnp.zeros_like(pair)
    return jnp.concatenate(
        [jnp.where(lanes, pair, nothing), jnp.where(lanes, nothing, pair)], axis=0
    )


def softmax(scores):
    highest = jnp.max(scores, axis=0, keepdims=True)
    raised = jnp.exp(scores - highest)
    return raised * (1.0 / jnp.sum(raised, axis=0, keepdims=True))


def two_halves(value):
    return value[:ROWS, :], value[ROWS:, :]


def attend(read_q, read_k, read_v, mask, write_probs, write_mix):
    lanes = low_lanes()
    for pair in range(PAIRS):
        query = (read_q(pair).astype(F32) * SCALE).astype(LOW)
        scores = mm_nt(two_heads(read_k(pair), lanes), query)
        heads = [softmax(jnp.where(mask, part, -1e30)) for part in two_halves(scores)]
        probs = jnp.concatenate(heads, axis=0)
        write_probs(pair, probs)
        write_mix(pair, mm_tn(probs.astype(LOW), two_heads(read_v(pair), lanes)).astype(LOW))


def attend_back(read_q, read_k, read_v, read_probs, read_grad, write):
    lanes = low_lanes()
    for pair in range(PAIRS):
        query = (read_q(pair).astype(F32) * SCALE).astype(LOW)
        probs = read_probs(pair)
        grad = read_grad(pair)
        grad_probs = mm_nt(two_heads(read_v(pair), lanes), grad)
        slopes = []
        for head, change in zip(two_halves(probs), two_halves(grad_probs)):
            total = jnp.sum(head * change, axis=0, keepdims=True)
            slopes.append((head * (change - total)).astype(LOW))
        slopes = jnp.concatenate(slopes, axis=0)
        grad_q = mm_tn(slopes, two_heads(read_k(pair), lanes)) * SCALE
        grad_k = jnp.where(lanes, *two_halves(mm(slopes, query)))
        grad_v = jnp.where(lanes, *two_halves(mm(probs.astype(LOW), grad)))
        write(pair, grad_q.astype(LOW), grad_k.astype(LOW), grad_v.astype(LOW))


def columns(ref, rows, start):
    def read(pair):
        return ref[rows, start + pair * LANES : start + (pair + 1) * LANES]

    return read


def fetch(source, target, sem):
    copy = pltpu.make_async_copy(source, target, sem)
    copy.start()
    return copy


WEIGHTS = dict(
    w_qkv=((D, 3 * D), LOW),
    w_out=((D, D), LOW),
    w_cross=((D, 2 * D), LOW),
    w_up=((D, FF), LOW),
    w_down=((FF, D), LOW),
)
HELD = dict(tokens=((BOTH, D), LOW), cotangent=((BOTH, D), LOW))
STATE = dict(
    proj=((BOTH, 3 * D), LOW),
    mix=((BOTH, D), LOW),
    probs=((MB, PAIRS, 2 * ROWS, ROWS), F32),
    wide=((BOTH, FF), F32),
    mid=((BOTH, D), F32),
    act=((BOTH, FF), LOW),
    narrow=((BOTH, D), LOW),
    result=((BOTH, D), LOW),
    left_a=((BOTH, D), LOW),
    query=((BOTH, D), LOW),
    across=((BOTH, ROWS), F32),
)
BACK = dict(
    hidden=((BOTH, FF), F32),
    across_mid=((BOTH, D), F32),
    left_b=((BOTH, D), LOW),
    right=((BOTH, 2 * D), LOW),
    grad_hidden=((BOTH, FF), LOW),
    gate=((BOTH, D), LOW),
    grad=((BOTH, D), F32),
    grad_low=((BOTH, D), LOW),
)


def shaped(table):
    return [pltpu.VMEM(shape, kind) for shape, kind in table.values()]


def same_shape(arrays):
    return [pltpu.VMEM(value.shape, value.dtype) for value in arrays]


def held(arrays):
    return [pltpu.with_memory_space_constraint(value, pltpu.VMEM) for value in arrays]


def in_place(place):
    return pltpu.with_memory_space_constraint(place, pltpu.SMEM)


def left(arrays):
    return [pltpu.with_memory_space_constraint(value, pltpu.HBM) for value in arrays]


def in_vmem():
    return pl.BlockSpec(memory_space=pltpu.VMEM)


def in_smem():
    return pl.BlockSpec(memory_space=pltpu.SMEM)


def in_hbm():
    return pl.BlockSpec(memory_space=pltpu.HBM)


TOKEN = ((8, LANES), F32)


def mflop(count):
    return count * 1_000_000, 0


def call(
    kernel, name, place, token, reads, keeps, makes, stores=None, scratch=(), cost=(0, 0), patches=None
):
    stores, patches = stores or {}, patches or {}
    out_shape = same_shape(keeps.values()) + shaped(makes) + shaped(dict(token=TOKEN))
    out_shape += [pltpu.HBM(shape, kind) for shape, kind in stores.values()]
    out_shape += [pltpu.HBM(value.shape, value.dtype) for value in patches.values()]
    reads_n, keeps_n, makes_n = len(reads), len(keeps), len(makes)
    stores_n, patches_n = len(stores), len(patches)
    aliases = {2 + reads_n + i: i for i in range(keeps_n)}
    for i in range(patches_n):
        aliases[2 + reads_n + keeps_n + i] = keeps_n + makes_n + 1 + stores_n + i

    def body(place_ref, token_in, *refs):
        del token_in
        refs = list(refs)
        named = dict(zip(reads, refs[:reads_n]))
        refs = refs[reads_n + keeps_n + patches_n :]
        named.update(zip(keeps, refs[:keeps_n]))
        named.update(zip(makes, refs[keeps_n : keeps_n + makes_n]))
        refs = refs[keeps_n + makes_n :]
        refs[0][...] = jnp.zeros(*TOKEN)
        named.update(zip(stores, refs[1 : 1 + stores_n]))
        refs = refs[1 + stores_n :]
        named.update(zip(patches, refs[:patches_n]))
        kernel(place_ref, SimpleNamespace(**named), *refs[patches_n:])

    results = pl.pallas_call(
        body,
        out_shape=out_shape,
        in_specs=[in_smem()] + [in_vmem()] * (1 + reads_n + keeps_n) + [in_hbm()] * patches_n,
        out_specs=[in_vmem()] * (keeps_n + makes_n + 1) + [in_hbm()] * (stores_n + patches_n),
        scratch_shapes=list(scratch),
        input_output_aliases=aliases,
        compiler_params=pltpu.CompilerParams(vmem_limit_bytes=16 * MIB),
        cost_estimate=pl.CostEstimate(flops=cost[0], bytes_accessed=cost[1], transcendentals=0),
        name=name,
    )(
        in_place(place),
        *held([token]),
        *held(reads.values()),
        *held(keeps.values()),
        *left(patches.values()),
    )
    names = list(keeps) + list(makes)
    token = results[len(names)]
    made = dict(zip(names, results))
    made.update(zip(list(stores) + list(patches), results[len(names) + 1 :]))
    return token, made


def forward_step(micro, first, lengths_ref, ref, link, gets):
    rows = slice(micro * ROWS, (micro + 1) * ROWS)
    gets.lengths.wait()
    seg_q_tgt = segments(lengths_ref, micro, 1, 1)
    seg_k_src = segments(lengths_ref, micro, 0, 0)
    ref.across[rows, :] = (seg_k_src == seg_q_tgt).astype(F32)
    earlier = lax.broadcasted_iota(jnp.int32, (ROWS, ROWS), 0) <= lax.broadcasted_iota(
        jnp.int32, (ROWS, ROWS), 1
    )
    source_mask = (seg_k_src == segments(lengths_ref, micro, 0, 1)).astype(jnp.int32)
    target_mask = ((segments(lengths_ref, micro, 1, 0) == seg_q_tgt) & earlier).astype(jnp.int32)
    mask = jnp.where(first, source_mask, target_mask) != 0
    gets.tokens.wait()
    tokens = ref.tokens[rows, :]
    for part in range(3):
        cut = slice(part * D, (part + 1) * D)
        gets.w_qkv[part].wait()
        ref.proj[rows, cut] = mm(tokens, ref.w_qkv[:, cut]).astype(LOW)

    def write_probs(pair, value):
        ref.probs[micro, pair] = value

    def write_mix(pair, value):
        ref.mix[rows, pair * LANES : (pair + 1) * LANES] = value

    attend(
        columns(ref.proj, rows, 0),
        columns(ref.proj, rows, D),
        columns(ref.proj, rows, 2 * D),
        mask,
        write_probs,
        write_mix,
    )
    gets.w_out.wait()
    mid = tokens.astype(F32) + mm(ref.mix[rows, :], ref.w_out[...])

    @pl.when(first)
    def _():
        ref.narrow[rows, :] = mid.astype(LOW)
        gets.w_up.wait()
        gets.w_down.wait()
        total = mid
        for part in range(4):
            cut = slice(part * D, (part + 1) * D)
            hidden = mm(ref.narrow[rows, :], ref.w_up[:, cut])
            ref.wide[rows, cut] = hidden
            ref.act[rows, cut] = gelu(hidden).astype(LOW)
            total = total + mm(ref.act[rows, cut], ref.w_down[cut, :])
        ref.result[rows, :] = total.astype(LOW)
        gets.w_cross.wait()
        for part in range(2):
            cut = slice(part * D, (part + 1) * D)
            link[:, cut] = mm(ref.result[rows, :], ref.w_cross[:, cut]).astype(LOW)
        ref.left_a[rows, :] = ref.result[rows, :]

    @pl.when(jnp.logical_not(first))
    def _():
        ref.left_a[rows, :] = mid.astype(LOW)
        ref.mid[rows, :] = mid


def decoder_ahead(ref, gets):
    gets.w_cross.wait()
    ref.query[...] = mm(ref.left_a[...], ref.w_cross[:, :D]).astype(LOW)
    gets.cotangent.wait()
    gets.w_down.wait()
    for part in range(4):
        cut = slice(part * D, (part + 1) * D)
        ref.wide[:, cut] = mm_nt(ref.cotangent[...], ref.w_down[cut, :])
    gets.w_up.wait()


class Fetch:
    def __init__(self, source, target, sem):
        self.copy = pltpu.make_async_copy(source, target, sem)

    def start(self):
        self.copy.start()

    def wait(self):
        self.copy.wait()


class Arrived:
    def wait(self):
        pass


def first_stage(lengths, tokens, w_qkv, w_out, w_cross, w_up, w_down):
    given = (lengths, tokens, w_qkv, w_out, w_up, w_down, w_cross)
    makes = {**WEIGHTS, **HELD, **STATE, **dict(link=((ROWS, 2 * D), LOW), token=TOKEN)}

    def body(lengths_in, tokens_in, qkv_in, out_in, up_in, down_in, cross_in, *refs):
        place_ref, lengths_ref, sems = refs[len(makes) :]
        ref = SimpleNamespace(**dict(zip(makes, refs)))
        index = lax.axis_index(DP).astype(jnp.int32)
        section = lax.axis_index(SECTION).astype(jnp.int32)
        place_ref[0] = section
        for bit in range(PLACE - 1):
            place_ref[1 + bit] = (index >> bit) % 2
        first = section == 0
        gets = SimpleNamespace(
            lengths=Fetch(lengths_in, lengths_ref, sems.at[0]),
            tokens=Fetch(tokens_in.at[0], ref.tokens, sems.at[1]),
            w_qkv=[
                Fetch(
                    qkv_in.at[0, :, pl.ds(part * D, D)],
                    ref.w_qkv.at[:, pl.ds(part * D, D)],
                    sems.at[2 + part],
                )
                for part in range(3)
            ],
            w_out=Fetch(out_in.at[0], ref.w_out, sems.at[5]),
            w_up=Fetch(up_in.at[0], ref.w_up, sems.at[6]),
            w_down=Fetch(down_in.at[0], ref.w_down, sems.at[7]),
            w_cross=Fetch(cross_in.at[0], ref.w_cross, sems.at[8]),
        )
        for get in [gets.lengths, gets.tokens, *gets.w_qkv, gets.w_out]:
            get.start()

        @pl.when(first)
        def _():
            gets.w_up.start()
            gets.w_down.start()
            gets.w_cross.start()

        ref.token[...] = jnp.zeros(*TOKEN)
        forward_step(0, first, lengths_ref, ref, ref.link, gets)

    results = pl.pallas_call(
        body,
        out_shape=shaped(makes) + [pltpu.SMEM((PLACE,), jnp.int32)],
        in_specs=[in_hbm()] * len(given),
        out_specs=[in_vmem()] * len(makes) + [in_smem()],
        scratch_shapes=[pltpu.SMEM((MB, 2, SLOTS), jnp.int32), pltpu.SemaphoreType.DMA((9,))],
        compiler_params=pltpu.CompilerParams(vmem_limit_bytes=16 * MIB),
        cost_estimate=pl.CostEstimate(
            flops=2 * ROWS * D * 7168, bytes_accessed=10_000_000, transcendentals=0
        ),
        name="first_stage",
    )(*left(given))
    made = SimpleNamespace(**dict(zip(makes, results)))
    link, token = made.link, made.token
    del made.link, made.token
    return results[-1], token, link, made


def second_stage(place, state, lengths, cotangent, w_cross, w_up, w_down):
    given = (lengths, cotangent, w_cross, w_up, w_down)
    kept = {**WEIGHTS, **HELD, **STATE}
    keeps = [getattr(state, name) for name in kept]

    def body(place_ref, lengths_in, cotangent_in, cross_in, up_in, down_in, *refs):
        refs = refs[len(keeps) :]
        ref = SimpleNamespace(**dict(zip(kept, refs)))
        link, lengths_ref, sems = refs[len(keeps) :]
        first = place_ref[0] == 0
        here = Arrived()
        get_lengths = Fetch(lengths_in, lengths_ref, sems.at[0])
        get_cotangent = Fetch(cotangent_in.at[0], ref.cotangent, sems.at[1])
        late = SimpleNamespace(
            cotangent=get_cotangent,
            w_cross=Fetch(cross_in.at[0], ref.w_cross, sems.at[2]),
            w_down=Fetch(down_in.at[0], ref.w_down, sems.at[3]),
            w_up=Fetch(up_in.at[0], ref.w_up, sems.at[4]),
        )
        get_lengths.start()
        get_cotangent.start()

        @pl.when(jnp.logical_not(first))
        def _():
            late.w_cross.start()
            late.w_down.start()
            late.w_up.start()

        gets = SimpleNamespace(
            lengths=get_lengths,
            tokens=here,
            w_qkv=[here] * 3,
            w_out=here,
            w_up=here,
            w_down=here,
            w_cross=here,
        )
        forward_step(1, first, lengths_ref, ref, link, gets)

        @pl.when(first)
        def _():
            get_cotangent.wait()

        @pl.when(jnp.logical_not(first))
        def _():
            decoder_ahead(ref, late)

    results = pl.pallas_call(
        body,
        out_shape=same_shape(keeps) + [pltpu.VMEM((ROWS, 2 * D), LOW)],
        in_specs=[in_smem()] + [in_hbm()] * len(given) + [in_vmem()] * len(keeps),
        out_specs=[in_vmem()] * (len(keeps) + 1),
        scratch_shapes=[pltpu.SMEM((MB, 2, SLOTS), jnp.int32), pltpu.SemaphoreType.DMA((5,))],
        input_output_aliases={1 + len(given) + i: i for i in range(len(keeps))},
        compiler_params=pltpu.CompilerParams(vmem_limit_bytes=16 * MIB),
        cost_estimate=pl.CostEstimate(
            flops=2 * ROWS * D * 7168, bytes_accessed=10_000_000, transcendentals=0
        ),
        name="second_stage",
    )(in_place(place), *left(given), *held(keeps))
    vars(state).update(zip(kept, results))
    return results[-1]


def middle_step(micro, ref, probs_v, mixed_v):
    rows = slice(micro * ROWS, (micro + 1) * ROWS)
    whole = slice(0, ROWS)
    reads = (
        columns(ref.query, rows, 0),
        columns(ref.link, whole, 0),
        columns(ref.link, whole, D),
    )

    def write_probs(pair, value):
        probs_v[pair] = value

    def write_mix(pair, value):
        ref.left_b[rows, pair * LANES : (pair + 1) * LANES] = value

    attend(*reads, ref.across[rows, :] != 0.0, write_probs, write_mix)
    after = ref.mid[rows, :] + mm(ref.left_b[rows, :], ref.w_cross[:, D:])
    ref.across_mid[rows, :] = after
    ref.narrow[rows, :] = after.astype(LOW)
    grad = ref.cotangent[rows, :].astype(F32)
    for part in range(4):
        cut = slice(part * D, (part + 1) * D)
        hidden = mm(ref.narrow[rows, :], ref.w_up[:, cut])
        ref.hidden[rows, cut] = hidden
        grad_hidden = (gelu_slope(hidden) * ref.wide[rows, cut]).astype(LOW)
        ref.grad_hidden[rows, cut] = grad_hidden
        grad = grad + mm_nt(grad_hidden, ref.w_up[:, cut])
    ref.grad[rows, :] = grad
    ref.right[rows, D:] = grad.astype(LOW)
    mixed_v[...] = mm_nt(ref.right[rows, D:], ref.w_cross[:, D:]).astype(LOW)

    def write(pair, grad_q, grad_k, grad_v):
        cut = slice(pair * LANES, (pair + 1) * LANES)
        ref.right[rows, cut] = grad_q
        ref.link_grad[:, cut] = grad_k
        ref.link_grad[:, D + pair * LANES : D + (pair + 1) * LANES] = grad_v

    attend_back(*reads, lambda pair: probs_v[pair], columns(mixed_v, whole, 0), write)


def middle_stage(micro, place, token, state, link):
    reads = dict(
        query=state.query,
        across=state.across,
        mid=state.mid,
        cotangent=state.cotangent,
        w_cross=state.w_cross,
        w_up=state.w_up,
        link=link,
    )
    keeps = dict(narrow=state.narrow, wide=state.wide)
    makes = dict(link_grad=((ROWS, 2 * D), LOW))
    if micro == 0:
        makes.update(BACK)
    else:
        keeps.update((name, getattr(state, name)) for name in BACK)

    def kernel(place_ref, ref, *scratch):
        @pl.when(place_ref[0] != 0)
        def _():
            middle_step(micro, ref, *scratch)

        @pl.when(place_ref[0] == 0)
        def _():
            rows = slice(micro * ROWS, (micro + 1) * ROWS)
            for part in range(4):
                cut = slice(part * D, (part + 1) * D)
                ref.wide[rows, cut] = gelu_slope(ref.wide[rows, cut])

    token, made = call(
        kernel,
        "middle_stage",
        place,
        token,
        reads,
        keeps,
        makes,
        scratch=(pltpu.VMEM((PAIRS, 2 * ROWS, ROWS), F32), pltpu.VMEM((ROWS, D), LOW)),
        cost=(2 * ROWS * D * 10000, 8_000_000),
    )
    vars(state).update(made)
    return token


def gate_step(micro, first, ref):
    rows = slice(micro * ROWS, (micro + 1) * ROWS)

    @pl.when(first)
    def _():
        cotangent = ref.cotangent[rows, :].astype(F32)
        grad = cotangent + mm_nt(ref.link_grad[...], ref.w_cross[...])
        ref.grad[rows, :] = grad
        ref.gate[rows, :] = grad.astype(LOW)
        ref.right[rows, :] = ref.link_grad[...]
        ref.left_b[rows, :] = ref.left_a[rows, :]

    @pl.when(jnp.logical_not(first))
    def _():
        ref.gate[rows, :] = ref.cotangent[rows, :]
        for part in range(4):
            cut = slice(part * D, (part + 1) * D)
            ref.act[rows, cut] = gelu(ref.hidden[rows, cut]).astype(LOW)


def back_step(micro, first, ref):
    rows = slice(micro * ROWS, (micro + 1) * ROWS)

    @pl.when(first)
    def _():
        grad = ref.grad[rows, :]
        for part in range(4):
            cut = slice(part * D, (part + 1) * D)
            grad_act = mm_nt(ref.gate[rows, :], ref.w_down[cut, :])
            grad_hidden = (ref.wide[rows, cut] * grad_act).astype(LOW)
            ref.grad_hidden[rows, cut] = grad_hidden
            grad = grad + mm_nt(grad_hidden, ref.w_up[:, cut])
        ref.grad[rows, :] = grad
        ref.grad_low[rows, :] = grad.astype(LOW)

    @pl.when(jnp.logical_not(first))
    def _():
        grad = ref.grad[rows, :] + mm_nt(ref.right[rows, :D], ref.w_cross[:, :D])
        ref.grad[rows, :] = grad
        ref.grad_low[rows, :] = grad.astype(LOW)


def back_stage(micro, place, token, state, link_grad, parts, send=(), cost=5000):
    reads = dict(
        cotangent=state.cotangent,
        w_cross=state.w_cross,
        w_up=state.w_up,
        w_down=state.w_down,
        wide=state.wide,
        left_a=state.left_a,
        link_grad=link_grad,
        narrow=state.narrow,
        mix=state.mix,
    )
    keeps = {name: getattr(state, name) for name in BACK}
    keeps.update(act=state.act)
    makes = {}
    for at, chunk in enumerate(send):
        makes["send%d" % at] = ((chunk.rows, D), LOW)

    def kernel(place_ref, ref):
        for part in parts:
            part(micro, place_ref[0] == 0, ref)
        for at, chunk in enumerate(send):
            put_send(place_ref, ref, chunk, getattr(ref, "send%d" % at))

    token, made = call(kernel, "back_stage", place, token, reads, keeps, makes, cost=mflop(cost))
    sends = [made.pop(name) for name in makes]
    vars(state).update(made)
    return token, sends


def late_kernel(place_ref, ref, mixed_v):
    mixed_v[...] = mm_nt(ref.grad_low[...], ref.w_out[...]).astype(LOW)
    for micro in range(MB):
        rows = slice(micro * ROWS, (micro + 1) * ROWS)

        def write(pair, grad_q, grad_k, grad_v, rows=rows):
            for part, value in enumerate((grad_q, grad_k, grad_v)):
                at = part * D + pair * LANES
                ref.grad_proj[rows, at : at + LANES] = value

        attend_back(
            columns(ref.proj, rows, 0),
            columns(ref.proj, rows, D),
            columns(ref.proj, rows, 2 * D),
            lambda pair, micro=micro: ref.probs[micro, pair],
            columns(mixed_v, rows, 0),
            write,
        )
    put_send(place_ref, ref, QKV, ref.send)


def late_stage(place, token, state, cost):
    reads = dict(
        grad_low=state.grad_low,
        w_out=state.w_out,
        proj=state.proj,
        probs=state.probs,
        tokens=state.tokens,
        mix=state.mix,
    )
    makes = dict(grad_proj=((BOTH, 3 * D), LOW), send=((QKV.rows, D), LOW))
    scratch = (pltpu.VMEM((BOTH, D), LOW),)
    token, made = call(
        late_kernel, "late_stage", place, token, reads, {}, makes, None, scratch, mflop(cost)
    )
    state.grad_proj = made["grad_proj"]
    return token, made["send"]


def final_kernel(place_ref, ref, result_v, grad_v, sems):
    @pl.when(place_ref[0] == 0)
    def _():
        result_v[...] = ref.result[...]

    @pl.when(place_ref[0] != 0)
    def _():
        total = ref.across_mid[...]
        for part in range(4):
            cut = slice(part * D, (part + 1) * D)
            total = total + mm(ref.act[:, cut], ref.w_down[cut, :])
        result_v[...] = total.astype(LOW)

    first = fetch(result_v, ref.outputs.at[0], sems.at[0])
    grad_v[...] = (ref.grad[...] + mm_nt(ref.grad_proj[...], ref.w_qkv[...])).astype(LOW)
    second = fetch(grad_v, ref.input_grad.at[0], sems.at[1])
    first.wait()
    second.wait()


def final_stage(place, token, state, cost):
    reads = dict(
        grad=state.grad,
        grad_proj=state.grad_proj,
        w_qkv=state.w_qkv,
        result=state.result,
        across_mid=state.across_mid,
        act=state.act,
        w_down=state.w_down,
    )
    half = ((1, BOTH, D), LOW)
    stores = dict(outputs=half, input_grad=half)
    scratch = [pltpu.VMEM((BOTH, D), LOW)] * 2 + [pltpu.SemaphoreType.DMA((2,))]
    return call(
        final_kernel, "final_stage", place, token, reads, {}, {}, stores, scratch, mflop(cost)
    )


PIECE = HALF // 2
PIECES = 7

Y_FIRST = (1, 2, 3)
Z_FIRST = (2, 1, 3)


def cut_of(part):
    return slice(part * D, (part + 1) * D)


class Gradient:
    def __init__(self, sides, store, down=False):
        self.sides = sides
        self.store = store
        self.down = down

    def rows(self, part, half, first, count):
        start = (part * D if self.down else 0) + first * PIECE
        return pl.ds(pl.multiple_of(start + half * HALF, PIECE), count * PIECE)

    def product(self, ref, part, half, first, count):
        left_ref, right_ref, column = self.sides(ref, part)
        return mm_tn(left_ref[:, self.rows(part, half, first, count)], right_ref[:, cut_of(column)])

    def target(self, array, part, half, first, count):
        column = 0 if self.down else part * D
        return array.at[0, self.rows(part, half, first, count), pl.ds(column, D)]


G_DOWN = Gradient(lambda ref, part: (ref.act, ref.gate, 0), dict(g_down=((1, FF, D), F32)), down=True)
G_UP = Gradient(lambda ref, part: (ref.narrow, ref.grad_hidden, part), dict(g_up=((1, D, FF), F32)))
G_CROSS = Gradient(
    lambda ref, part: ((ref.left_a, ref.left_b)[part], ref.right, part),
    dict(g_cross=((1, D, 2 * D), F32)),
)
G_OUT = Gradient(lambda ref, part: (ref.mix, ref.grad_low, 0), dict(g_out=((1, D, D), F32)))
G_QKV = Gradient(
    lambda ref, part: (ref.tokens, ref.grad_proj, part), dict(g_qkv=((1, D, 3 * D), F32))
)


class Chunk:
    def __init__(self, levels, operands, runs):
        self.levels = levels
        self.operands = operands
        self.runs = runs
        self.rows = PIECES * PIECE
        self.stores = {}
        for run in runs:
            self.stores.update(run[0].store)

    def each(self):
        at = 0
        for gradient, part, first, count in self.runs:
            yield slice(at, at + count * PIECE), gradient, (part, first, count)
            at += count * PIECE


def product_of(gradient, ref, run, half):
    part, first, count = run
    return gradient.product(ref, part, half, first, count)


CROSS = Chunk(
    (Y_FIRST, Z_FIRST),
    lambda state: dict(
        left_a=state.left_a,
        left_b=state.left_b,
        right=state.right,
        mix=state.mix,
        grad_low=state.grad_low,
        act=state.act,
        gate=state.gate,
        narrow=state.narrow,
        grad_hidden=state.grad_hidden,
    ),
    [(G_CROSS, 0, 0, 2), (G_CROSS, 1, 0, 2), (G_OUT, 0, 0, 1), (G_DOWN, 3, 1, 1), (G_UP, 3, 1, 1)],
)
DOWN = Chunk(
    (Y_FIRST, Z_FIRST),
    lambda state: dict(act=state.act, gate=state.gate),
    [(G_DOWN, 0, 0, 2), (G_DOWN, 1, 0, 2), (G_DOWN, 2, 0, 2), (G_DOWN, 3, 0, 1)],
)
UP = Chunk(
    (Z_FIRST, Y_FIRST),
    lambda state: dict(narrow=state.narrow, grad_hidden=state.grad_hidden),
    [(G_UP, 0, 0, 2), (G_UP, 1, 0, 2), (G_UP, 2, 0, 2), (G_UP, 3, 0, 1)],
)
QKV = Chunk(
    (Z_FIRST, Y_FIRST),
    lambda state: dict(
        tokens=state.tokens, grad_proj=state.grad_proj, mix=state.mix, grad_low=state.grad_low
    ),
    [(G_QKV, 0, 0, 2), (G_QKV, 1, 0, 2), (G_QKV, 2, 0, 2), (G_OUT, 0, 1, 1)],
)


def put_send(place_ref, ref, chunk, send):
    for here, gradient, run in chunk.each():
        send[here, :] = product_of(gradient, ref, run, 1 - place_ref[1]).astype(LOW)


class Summing:
    def __init__(self, chunk, state, place, count):
        self.chunk = chunk
        self.state = state
        self.place = place
        self.count = count
        self.depth = count.bit_length() - 2
        self.step = 0

    def swap(self, value, level):
        def partner(i):
            bit = self.chunk.levels[i % 2][level - 1] if 0 < level < 4 else level
            return i ^ (1 << bit)

        return lax.ppermute(value, "dp", [(i, partner(i)) for i in range(self.count)])

    def call(self, kernel, token, reads, makes, stores=None, scratch=(), patches=None):
        name = "sum_%d" % self.step
        rest = (stores, scratch, mflop(self.cost), patches)
        return call(kernel, name, self.place, token, reads, {}, makes, *rest)

    def halves(self, place_ref, level, rows):
        first, second = (place_ref[1 + levels[level - 1]] for levels in self.chunk.levels)
        bit = jnp.where(place_ref[1] == 0, first, second)
        half = rows // 2
        own = pl.ds(pl.multiple_of(bit * half, half), half)
        return own, pl.ds(pl.multiple_of((1 - bit) * half, half), half)

    def launch(self, send):
        self.got = self.swap(send, 0)

    def start(self, token, cost):
        def kernel(place_ref, ref):
            put_send(place_ref, ref, self.chunk, ref.send)

        makes = dict(send=((self.chunk.rows, D), LOW))
        reads = self.chunk.operands(self.state)
        token, made = call(kernel, "product", self.place, token, reads, {}, makes, cost=mflop(cost))
        self.launch(made["send"])
        return token

    def advance(self, token, grads, cost):
        self.cost = cost
        rows = self.chunk.rows
        if self.step == 0:
            token = self.split_first(token, rows)
        elif self.step == 1:
            token = self.split(token, rows // 2)
        elif self.step == 2:
            token = self.round_off(token, rows // 4)
        elif self.step == 3:
            for level in range(4, self.depth + 1):
                token = self.pair_sum(token, rows // 4, level)
            token = self.pair_sum(token, rows // 4, 2)
        elif self.step == 4:
            token = self.merge(token, rows // 4, 1)
        elif self.step == 5:
            token = self.merge(token, rows // 2, 0)
        else:
            token = self.unpack(token, grads, False, cost)
        self.step += 1
        return token

    def split_first(self, token, rows):
        chunk = self.chunk

        def kernel(place_ref, ref, total):
            for here, gradient, run in chunk.each():
                own = product_of(gradient, ref, run, place_ref[1])
                total[here, :] = own + ref.got[here, :].astype(F32)
            own, other = self.halves(place_ref, 1, rows)
            ref.send[...] = total[other, :].astype(LOW)
            ref.keep[...] = total[own, :]

        reads = dict(got=self.got, **chunk.operands(self.state))
        makes = dict(send=((rows // 2, D), LOW), keep=((rows // 2, D), F32))
        scratch = (pltpu.VMEM((rows, D), F32),)
        token, made = self.call(kernel, token, reads, makes, scratch=scratch)
        self.keep = made["keep"]
        self.got = self.swap(made["send"], 1)
        return token

    def split(self, token, rows):
        def kernel(place_ref, ref):
            own, other = self.halves(place_ref, 2, rows)
            ref.send[...] = (ref.keep[other, :] + ref.got[other, :].astype(F32)).astype(LOW)
            ref.kept[...] = ref.keep[own, :] + ref.got[own, :].astype(F32)

        reads = dict(keep=self.keep, got=self.got)
        makes = dict(send=((rows // 2, D), LOW), kept=((rows // 2, D), F32))
        token, made = self.call(kernel, token, reads, makes)
        self.keep = made["kept"]
        self.got = self.swap(made["send"], 2)
        return token

    def round_off(self, token, rows):
        def kernel(place_ref, ref):
            ref.piece[...] = (ref.keep[...] + ref.got[...].astype(F32)).astype(LOW)

        makes = dict(piece=((rows, D), LOW))
        token, made = self.call(kernel, token, dict(keep=self.keep, got=self.got), makes)
        self.piece = made["piece"]
        self.got = self.swap(self.piece, 3)
        return token

    def pair_sum(self, token, rows, level):
        def kernel(place_ref, ref):
            both = ref.held[...].astype(F32) + ref.got[...].astype(F32)
            ref.piece[...] = both.astype(LOW)

        makes = dict(piece=((rows, D), LOW))
        token, made = self.call(kernel, token, dict(held=self.piece, got=self.got), makes)
        self.piece = made["piece"]
        self.got = self.swap(self.piece, level)
        return token

    def merge(self, token, rows, level):
        def kernel(place_ref, ref):
            own, other = self.halves(place_ref, level + 1, 2 * rows)
            ref.piece[own, :] = ref.held[...]
            ref.piece[other, :] = ref.got[...]

        makes = dict(piece=((2 * rows, D), LOW))
        token, made = self.call(kernel, token, dict(held=self.piece, got=self.got), makes)
        self.piece = made["piece"]
        self.got = self.swap(self.piece, level)
        return token

    def unpack(self, token, grads, own, cost):
        chunk = self.chunk
        patches = {name: grads[name] for name in chunk.stores if name in grads}
        stores = {name: kind for name, kind in chunk.stores.items() if name not in grads}

        def kernel(place_ref, ref, wide, sems):
            half = place_ref[1] if own else 1 - place_ref[1]
            copies = []
            for index, (here, gradient, (part, first, count)) in enumerate(chunk.each()):
                wide[here, :] = ref.source[here, :].astype(F32)
                array = getattr(ref, list(gradient.store)[0])
                target = gradient.target(array, part, half, first, count)
                rows = pl.ds(here.start, here.stop - here.start)
                copies.append(fetch(wide.at[rows], target, sems.at[index]))
            for copy in copies:
                copy.wait()

        scratch = (pltpu.VMEM((chunk.rows, D), F32), pltpu.SemaphoreType.DMA((len(chunk.runs),)))
        reads = dict(source=self.piece if own else self.got)
        name = "unpack_%d" % own
        token, made = call(
            kernel, name, self.place, token, reads, {}, {}, stores, scratch, mflop(cost), patches
        )
        grads.update(made)
        return token


CHUNKS = (DOWN, CROSS, UP, QKV)
GATE, BACK_ATTN, BACK_FFN, FINAL, MORE, OWN = 10, 11, 12, 13, 14, 20
ORDER = (GATE, BACK_FFN, 0, MORE, 1, BACK_ATTN) + (0, 2, 1, 3) * 2 + (0, FINAL, 2, 1, 3) + (0, 2, 1, 3)
ORDER += (0, 2, OWN, 1, 3, OWN + 1, 0, 2, 1, OWN + 2, 3, 2, OWN + 3, 3)
COSTS = (1000, 1000, 8000, 4000, 8000, 8000, 8000, 4000, 1000, 1000, 1000, 1000, 1000, 1000, 1000, 1000, 1000, 1000, 1000, 1000, 1000, 1000, 1000, 1000, 8000, 8000, 1000, 1000, 8000, 1000, 1000, 1000, 1000, 50, 3000, 1000, 1000)


def on_device(inputs, lengths, w_qkv, w_attn_out, w_cross, w_up, w_down, cotangent):
    count = lax.axis_size("dp")
    place, token, link, state = first_stage(
        lengths, inputs, w_qkv, w_attn_out, w_cross, w_up, w_down
    )
    links = [lax.ppermute(link, "section", [(0, 1)])]
    link = second_stage(place, state, lengths, cotangent, w_cross, w_up, w_down)
    links.append(lax.ppermute(link, "section", [(0, 1)]))
    grads = []
    for micro in range(MB):
        token = middle_stage(micro, place, token, state, links[micro])
        grads.append(lax.ppermute(state.link_grad, "section", [(1, 0)]))
    token, _ = back_stage(0, place, token, state, grads[0], (gate_step, back_step))
    chunks = [Summing(chunk, state, place, count) for chunk in CHUNKS]
    made = {}
    for task, cost in zip(ORDER, COSTS):
        if task == GATE:
            token, sends = back_stage(1, place, token, state, grads[1], (gate_step,), [DOWN], cost)
            chunks[0].launch(*sends)
        elif task == BACK_FFN:
            token, sends = back_stage(1, place, token, state, grads[1], (back_step,), [CROSS], cost)
            chunks[1].launch(*sends)
        elif task == MORE:
            token = chunks[2].start(token, cost)
        elif task == BACK_ATTN:
            token, send = late_stage(place, token, state, cost)
            chunks[3].launch(send)
        elif task == FINAL:
            token, ends = final_stage(place, token, state, cost)
            made.update(ends)
        elif task >= OWN:
            token = chunks[task - OWN].unpack(token, made, True, cost)
        else:
            token = chunks[task].advance(token, made, cost)
    done = SimpleNamespace(**made)
    return (
        done.outputs,
        done.input_grad,
        done.g_qkv,
        done.g_out,
        done.g_cross,
        done.g_up,
        done.g_down,
    )


def solution(mesh):
    return jax.shard_map(
        on_device,
        mesh=mesh,
        in_specs=(
            P("section", "dp", None),
            P("dp", None, None),
            P("section", None, None),
            P("section", None, None),
            P("section", None, None),
            P("section", None, None),
            P("section", None, None),
            P("section", "dp", None),
        ),
        out_specs=(
            P("section", "dp", None),
            P("section", "dp", None),
            P("section", None, None),
            P("section", None, None),
            P("section", None, None),
            P("section", None, None),
            P("section", None, None),
        ),
        check_vma=False,
    )
```

time: 506 us -> 133 us (0.26); the launches traced: 500 us -> 133 us
  waiting for transfers between devices: 299 us -> 53.4 us
  local copies, waits for them, and re-layouts: 78.9 us -> 0 us
  matrix products: 59.3 us -> 0 us
  other arithmetic: 40.1 us -> 0 us
  starting transfers between devices: 5.91 us -> 44.9 us
  Pallas kernels: 0 us -> 33.7 us
  between operations: 14.7 us -> 1.21 us
    psum x1 -> x0, waiting for transfers between devices: 265 us -> none  [on_device(): lax.psum((running[0], running[1], running[2], running[3], running[4]), 'dp')]
    dot_general x44 -> x0, matrix products: 59.3 us -> none  [the longest x10 23.5 us: weight_dot(): lax.dot_general(values_in, grad_in, (((0,), (0,)), ((), ())), preferred_e...]
    ppermute x4 -> x32, starting transfers between devices: 5.87 us -> 44.9 us  [the longest x28 38.4 us: swap(): lax.ppermute(value, 'dp', [(i, partner(i)) for i in range(self.count)])]
    cond x96 -> x0, local copies, waits for them, and re-layouts: 35.8 us -> none  [the longest x8 29 us: on_device(): lax.cond(is_first, encode_back, silenced(encode_back), (tokens_now, upstr...]
    pallas_call x0 -> x42, Pallas kernels: none -> 33.7 us  [the longest x40 25.1 us: call(): pl.pallas_call(body, out_shape=out_shape, in_specs=[in_smem()] + [in_vmem...]
    broadcast_in_dim x7 -> x0, other arithmetic: 30.5 us -> none  [the longest x1 7.79 us: on_device(): running[3][None]]
    another operation x23 -> x0, local copies, waits for them, and re-layouts: 25.2 us -> none
    ppermute x4 -> x32, waiting for transfers between devices: 34.4 us -> 53.4 us  [the longest x28 39.7 us: swap(): lax.ppermute(value, 'dp', [(i, partner(i)) for i in range(self.count)])]
  transfers between devices with their start and end apart: 5 -> 32, of which waited for: 4 -> 13; matrix products, arithmetic and copies ran while one was open for 16% -> 0% of each run, Pallas kernels for 0% -> 20%
where the time goes in v3:
time: 133 us
  waiting for transfers between devices  53.4 us (40%)
  starting transfers between devices  44.9 us (34%)
  Pallas kernels  33.7 us (25%)
    ppermute x28, waiting for transfers between devices, swap(): lax.ppermute(value, 'dp', [(i, partner(i)) for i in range(self.count)])  39.7 us
    ppermute x28, starting transfers between devices, swap(): lax.ppermute(value, 'dp', [(i, partner(i)) for i in range(self.count)])  38.4 us
    pallas_call x40, Pallas kernels, call(): pl.pallas_call(body, out_shape=out_shape, in_specs=[in_smem()] + [in_vmem...  25.1 us
    ppermute x2, waiting for transfers between devices, on_device(): grads.append(lax.ppermute(state.link_grad, 'section', [(1, 0)]))  9.44 us
    pallas_call x1, Pallas kernels, first_stage(): pl.pallas_call(body, out_shape=shaped(makes) + [pltpu.SMEM((PLACE,), jnp....  4.81 us
    pallas_call x1, Pallas kernels, second_stage(): pl.pallas_call(body, out_shape=same_shape(keeps) + [pltpu.VMEM((ROWS, 2 *...  3.73 us
    ppermute x1, waiting for transfers between devices, on_device(): links.append(lax.ppermute(link, 'section', [(0, 1)]))  3.24 us
  transfers between devices with their start and end apart: 32, of which 13 were waited for; matrix products, arithmetic and copies ran while one was open for 0% of the time, Pallas kernels for 20%

profile of v3, /device:TPU:0, one launch (start us, length us, event | category | flops | bytes accessed | tf_op | source)
XLA Modules:
  0.0 133.1 jit_solution(8709944822052827080)
XLA Ops:
  0.6 4.8 %first_stage.1 = (bf16[512,1536]{1,0:T(8,128)(2,1)S(1)}, bf16[512,512]{1,0:T(8,128)(2,1)S(1)}, bf16[512,1024]{1,0:T(8,128)(2,1)S(1)}, bf16[512,2048]{1,0:T(8,128...) custom-call(s32[2,2,16]{2,1,0:T(2,128)} %lengths_in.3, ...), custom_call_target="tpu_custom_call" | custom-call | flops 939524096 | bytes 10000000 | tf_op jit(solution)/shard_map/first_stage/pallas_call | solution.py:382
  5.5 2.7 %collective-permute-start = (bf16[128,1024]{1,0:T(8,128)(2,1)S(1)}, bf16[128,1024]{1,0:T(8,128)(2,1)S(1)}, u32[]{:S(2)}, u32[]{:S(2)}) collective-permute-start(bf16[128,1024]{1,0:T(8,128)(2,1)S(1)} %get-tuple-element.215), channel_id=1, source_target_pairs={{0,16},{1,17},{2,18},{3,19},{4,20},{5,21},{6,22},{7,23},{8,24},{9,... | collective-permute-start | bytes 786440 | tf_op jit(solution)/shard_map/ppermute | solution.py:967
  8.1 3.7 %second_stage.1 = (bf16[512,1536]{1,0:T(8,128)(2,1)S(1)}, bf16[512,512]{1,0:T(8,128)(2,1)S(1)}, bf16[512,1024]{1,0:T(8,128)(2,1)S(1)}, bf16[512,2048]{1,0:T(8,12...) custom-call(s32[4]{0:T(128)S(4)} %get-tuple-element.189.place_ref, ...), custom_call_target="tpu_custom_call", output_to_operand_aliasing={{0}: (6, {}), {1}: (7, {}), {2}: (8, {}), {3}: (9, {}), {4}... | custom-call | flops 939524096 | bytes 10000000 | tf_op jit(solution)/shard_map/second_stage/pallas_call | solution.py:447
  11.9 1.3 collective-permute-start.1
  13.2 1.0 collective-permute-done.refs_6_
  14.1 0.6 middle_stage.2
  14.7 1.3 collective-permute-start.2
  16.0 3.2 %collective-permute-done.1.refs_6_ = bf16[128,1024]{1,0:T(8,128)(2,1)S(1)} collective-permute-done((bf16[128,1024]{1,0:T(8,128)(2,1)S(1)}, bf16[128,1024]{1,0:T(8,128)(2,1)S(1)}, u32[]{:S(2)}, u32[]{:S(2)}) %collective-permute-start.1) | collective-permute-done | bytes 262176 | tf_op jit(solution)/shard_map/ppermute | solution.py:969
  19.3 0.6 middle_stage.3
  19.8 1.3 collective-permute-start.3
  21.1 5.4 %collective-permute-done.2.refs_6_ = bf16[128,1024]{1,0:T(8,128)(2,1)S(1)} collective-permute-done((bf16[128,1024]{1,0:T(8,128)(2,1)S(1)}, bf16[128,1024]{1,0:T(8,128)(2,1)S(1)}, u32[]{:S(2)}, u32[]{:S(2)}) %collective-permute-start.2) | collective-permute-done | bytes 262176 | tf_op jit(solution)/shard_map/ppermute | solution.py:973
  26.6 2.1 %back_stage.3 = (f32[256,2048]{1,0:T(8,128)S(1)}, f32[256,512]{1,0:T(8,128)S(1)}, bf16[256,512]{1,0:T(8,128)(2,1)S(1)}, bf16[256,1024]{1,0:T(8,128)(2,1)S(1)}, b...) custom-call(s32[4]{0:T(128)S(4)} %get-tuple-element.189.place_ref, ...), custom_call_target="tpu_custom_call", output_to_operand_aliasing={{0}: (11, {}), {1}: (12, {}), {2}: (13, {}), {3}: (14, {}),... | custom-call | flops 5000000000 | tf_op jit(solution)/shard_map/back_stage/pallas_call | solution.py:229
  28.7 4.0 %collective-permute-done.3.refs_6_ = bf16[128,1024]{1,0:T(8,128)(2,1)S(1)} collective-permute-done((bf16[128,1024]{1,0:T(8,128)(2,1)S(1)}, bf16[128,1024]{1,0:T(8,128)(2,1)S(1)}, u32[]{:S(2)}, u32[]{:S(2)}) %collective-permute-start.3) | collective-permute-done | bytes 262176 | tf_op jit(solution)/shard_map/ppermute | solution.py:973
  32.7 0.9 back_stage.4
  33.8 2.1 %back_stage.5 = (f32[256,2048]{1,0:T(8,128)S(1)}, f32[256,512]{1,0:T(8,128)S(1)}, bf16[256,512]{1,0:T(8,128)(2,1)S(1)}, bf16[256,1024]{1,0:T(8,128)(2,1)S(1)}, b...) custom-call(s32[4]{0:T(128)S(4)} %get-tuple-element.189.place_ref, ...), custom_call_target="tpu_custom_call", output_to_operand_aliasing={{0}: (11, {}), {1}: (12, {}), {2}: (13, {}), {3}: (14, {}),... | custom-call | flops 1000000000 | tf_op jit(solution)/shard_map/back_stage/pallas_call | solution.py:229
  35.9 0.5 collective-permute-start.5
  36.4 0.5 sum_0.4
  37.0 2.1 %collective-permute-start.6 = (bf16[448,512]{1,0:T(8,128)(2,1)S(1)}, bf16[448,512]{1,0:T(8,128)(2,1)S(1)}, u32[]{:S(2)}, u32[]{:S(2)}) collective-permute-start(bf16[448,512]{1,0:T(8,128)(2,1)S(1)} %get-tuple-element.285), channel_id=1, source_target_pairs={{0,2},{1,5},{2,0},{3,7},{4,6},{5,1},{6,4},{7,3},{8,10},{9,13},{10,... | collective-permute-start | bytes 1376264 | tf_op jit(solution)/shard_map/ppermute | solution.py:814
  39.0 0.4 product.1
  39.5 0.6 sum_0.5
  40.1 1.1 collective-permute-start.8
  41.1 0.1 collective-permute-start.7
  41.3 2.4 %late_stage.1 = (bf16[256,1536]{1,0:T(8,128)(2,1)S(1)}, bf16[896,512]{1,0:T(8,128)(2,1)S(1)}, f32[8,128]{1,0:T(8,128)S(1)}) custom-call(s32[4]{0:T(128)S(4)} %get-tuple-element.189.place_ref, f32[8,128]{1,0:T(8,128)S(1)} %get-tuple-element.278.token_in, bf16[256,512]{1,0:T(8,128)(2,1)S(1)} %get-tuple-element.277.refs_5_.refs_0_.refs_4_, ...), custom_call_target="tpu_custom_call" | custom-call | flops 8000000000 | tf_op jit(solution)/shard_map/late_stage/pallas_call | solution.py:229
  43.7 0.4 collective-permute-start.9
  44.1 1.4 %collective-permute-done.6.refs_1_ = bf16[448,512]{1,0:T(8,128)(2,1)S(1)} collective-permute-done((bf16[448,512]{1,0:T(8,128)(2,1)S(1)}, bf16[448,512]{1,0:T(8,128)(2,1)S(1)}, u32[]{:S(2)}, u32[]{:S(2)}) %collective-permute-start.6) | collective-permute-done | bytes 458784 | tf_op jit(solution)/shard_map/ppermute | solution.py:814
  45.5 0.1 sum_1.4
  45.6 0.6 sum_0.6
  46.2 2.1 %collective-permute-start.11 = (bf16[448,512]{1,0:T(8,128)(2,1)S(1)}, bf16[448,512]{1,0:T(8,128)(2,1)S(1)}, u32[]{:S(2)}, u32[]{:S(2)}) collective-permute-start(bf16[448,512]{1,0:T(8,128)(2,1)S(1)} %get-tuple-element.299), channel_id=1, source_target_pairs={{0,4},{1,3},{2,6},{3,1},{4,0},{5,7},{6,2},{7,5},{8,12},{9,11},{10,... | collective-permute-start | bytes 1376264 | tf_op jit(solution)/shard_map/ppermute | solution.py:814
  48.4 4.0 %collective-permute-done.8.refs_1_ = bf16[448,512]{1,0:T(8,128)(2,1)S(1)} collective-permute-done((bf16[448,512]{1,0:T(8,128)(2,1)S(1)}, bf16[448,512]{1,0:T(8,128)(2,1)S(1)}, u32[]{:S(2)}, u32[]{:S(2)}) %collective-permute-start.8) | collective-permute-done | bytes 458784 | tf_op jit(solution)/shard_map/ppermute | solution.py:814
  52.5 0.5 sum_0.7
  53.1 2.4 %collective-permute-start.13 = (bf16[448,512]{1,0:T(8,128)(2,1)S(1)}, bf16[448,512]{1,0:T(8,128)(2,1)S(1)}, u32[]{:S(2)}, u32[]{:S(2)}) collective-permute-start(bf16[448,512]{1,0:T(8,128)(2,1)S(1)} %get-tuple-element.305), channel_id=1, source_target_pairs={{0,4},{1,3},{2,6},{3,1},{4,0},{5,7},{6,2},{7,5},{8,12},{9,11},{10,... | collective-permute-start | bytes 1376264 | tf_op jit(solution)/shard_map/ppermute | solution.py:814
  55.6 1.7 %collective-permute-done.10.refs_1_ = bf16[224,512]{1,0:T(8,128)(2,1)S(1)} collective-permute-done((bf16[224,512]{1,0:T(8,128)(2,1)S(1)}, bf16[224,512]{1,0:T(8,128)(2,1)S(1)}, u32[]{:S(2)}, u32[]{:S(2)}) %collective-permute-start.10) | collective-permute-done | bytes 229408 | tf_op jit(solution)/shard_map/ppermute | solution.py:814
  57.3 3.1 %collective-permute-start.14 = (bf16[224,512]{1,0:T(8,128)(2,1)S(1)}, bf16[224,512]{1,0:T(8,128)(2,1)S(1)}, u32[]{:S(2)}, u32[]{:S(2)}) collective-permute-start(bf16[224,512]{1,0:T(8,128)(2,1)S(1)} %get-tuple-element.307.refs_0_), channel_id=1, source_target_pairs={{0,8},{1,9},{2,10},{3,11},{4,12},{5,13},{6,14},{7,15},{8,0},{9,1},... | collective-permute-start | bytes 688136 | tf_op jit(solution)/shard_map/ppermute | solution.py:814
  60.4 0.1 sum_1.6
  60.5 9.3 %collective-permute-done.12.refs_1_ = bf16[224,512]{1,0:T(8,128)(2,1)S(1)} collective-permute-done((bf16[224,512]{1,0:T(8,128)(2,1)S(1)}, bf16[224,512]{1,0:T(8,128)(2,1)S(1)}, u32[]{:S(2)}, u32[]{:S(2)}) %collective-permute-start.12) | collective-permute-done | bytes 229408 | tf_op jit(solution)/shard_map/ppermute | solution.py:814
  69.9 0.3 collective-permute-start.16
  70.2 1.7 %collective-permute-start.15 = (bf16[224,512]{1,0:T(8,128)(2,1)S(1)}, bf16[224,512]{1,0:T(8,128)(2,1)S(1)}, u32[]{:S(2)}, u32[]{:S(2)}) collective-permute-start(bf16[224,512]{1,0:T(8,128)(2,1)S(1)} %get-tuple-element.317), channel_id=1, source_target_pairs={{0,2},{1,5},{2,0},{3,7},{4,6},{5,1},{6,4},{7,3},{8,10},{9,13},{10,... | collective-permute-start | bytes 688136 | tf_op jit(solution)/shard_map/ppermute | solution.py:814
  72.1 5.2 %collective-permute-start.18 = (bf16[224,512]{1,0:T(8,128)(2,1)S(1)}, bf16[224,512]{1,0:T(8,128)(2,1)S(1)}, u32[]{:S(2)}, u32[]{:S(2)}) collective-permute-start(bf16[224,512]{1,0:T(8,128)(2,1)S(1)} %get-tuple-element.324.refs_0_), channel_id=1, source_target_pairs={{0,4},{1,3},{2,6},{3,1},{4,0},{5,7},{6,2},{7,5},{8,12},{9,11},{10,... | collective-permute-start | bytes 688136 | tf_op jit(solution)/shard_map/ppermute | solution.py:814
  77.3 1.4 %collective-permute-start.17 = (bf16[224,512]{1,0:T(8,128)(2,1)S(1)}, bf16[224,512]{1,0:T(8,128)(2,1)S(1)}, u32[]{:S(2)}, u32[]{:S(2)}) collective-permute-start(bf16[224,512]{1,0:T(8,128)(2,1)S(1)} %get-tuple-element.322), channel_id=1, source_target_pairs={{0,2},{1,5},{2,0},{3,7},{4,6},{5,1},{6,4},{7,3},{8,10},{9,13},{10,... | collective-permute-start | bytes 688136 | tf_op jit(solution)/shard_map/ppermute | solution.py:814
  78.7 1.6 %final_stage.1 = (f32[8,128]{1,0:T(8,128)S(1)}, bf16[1,256,512]{2,1,0:T(8,128)(2,1)}, bf16[1,256,512]{2,1,0:T(8,128)(2,1)}) custom-call(s32[4]{0:T(128)S(4)} %get-tuple-element.189.place_ref, f32[8,128]{1,0:T(8,128)S(1)} %get-tuple-element.308.token_in, f32[256,512]{1,0:T(8,128)S(1)} %get-tuple-element.309.refs_0_, ...), custom_call_target="tpu_custom_call" | custom-call | flops 1000000000 | tf_op jit(solution)/shard_map/final_stage/pallas_call | solution.py:229
  80.3 3.9 %collective-permute-start.19 = (bf16[224,512]{1,0:T(8,128)(2,1)S(1)}, bf16[224,512]{1,0:T(8,128)(2,1)S(1)}, u32[]{:S(2)}, u32[]{:S(2)}) collective-permute-start(bf16[224,512]{1,0:T(8,128)(2,1)S(1)} %get-tuple-element.326.refs_0_), channel_id=1, source_target_pairs={{0,8},{1,9},{2,10},{3,11},{4,12},{5,13},{6,14},{7,15},{8,0},{9,1},... | collective-permute-start | bytes 688136 | tf_op jit(solution)/shard_map/ppermute | solution.py:814
  84.3 5.2 %collective-permute-done.18.refs_1_ = bf16[224,512]{1,0:T(8,128)(2,1)S(1)} collective-permute-done((bf16[224,512]{1,0:T(8,128)(2,1)S(1)}, bf16[224,512]{1,0:T(8,128)(2,1)S(1)}, u32[]{:S(2)}, u32[]{:S(2)}) %collective-permute-start.18) | collective-permute-done | bytes 229408 | tf_op jit(solution)/shard_map/ppermute | solution.py:814
  89.5 1.2 collective-permute-start.22
  90.8 2.8 %collective-permute-start.21 = (bf16[224,512]{1,0:T(8,128)(2,1)S(1)}, bf16[224,512]{1,0:T(8,128)(2,1)S(1)}, u32[]{:S(2)}, u32[]{:S(2)}) collective-permute-start(bf16[224,512]{1,0:T(8,128)(2,1)S(1)} %get-tuple-element.330.refs_0_), channel_id=1, source_target_pairs={{0,8},{1,9},{2,10},{3,11},{4,12},{5,13},{6,14},{7,15},{8,0},{9,1},... | collective-permute-start | bytes 688136 | tf_op jit(solution)/shard_map/ppermute | solution.py:814
  93.6 0.4 collective-permute-done.19.refs_1_
  94.1 0.7 collective-permute-start.23
  94.7 9.1 %collective-permute-done.20.refs_1_ = bf16[224,512]{1,0:T(8,128)(2,1)S(1)} collective-permute-done((bf16[224,512]{1,0:T(8,128)(2,1)S(1)}, bf16[224,512]{1,0:T(8,128)(2,1)S(1)}, u32[]{:S(2)}, u32[]{:S(2)}) %collective-permute-start.20) | collective-permute-done | bytes 229408 | tf_op jit(solution)/shard_map/ppermute | solution.py:814
  104.0 1.3 collective-permute-start.25
  105.3 0.8 collective-permute-start.24
  106.2 1.2 collective-permute-start.27
  107.4 1.8 %collective-permute-start.26 = (bf16[896,512]{1,0:T(8,128)(2,1)S(1)}, bf16[896,512]{1,0:T(8,128)(2,1)S(1)}, u32[]{:S(2)}, u32[]{:S(2)}) collective-permute-start(bf16[896,512]{1,0:T(8,128)(2,1)S(1)} %get-tuple-element.336.refs_0_), channel_id=1, source_target_pairs={{0,1},{1,0},{2,3},{3,2},{4,5},{5,4},{6,7},{7,6},{8,9},{9,8},{10,11... | collective-permute-start | bytes 2752520 | tf_op jit(solution)/shard_map/ppermute | solution.py:814
  109.2 1.3 unpack_1.4
  110.5 7.9 %collective-permute-done.24.refs_1_ = bf16[448,512]{1,0:T(8,128)(2,1)S(1)} collective-permute-done((bf16[448,512]{1,0:T(8,128)(2,1)S(1)}, bf16[448,512]{1,0:T(8,128)(2,1)S(1)}, u32[]{:S(2)}, u32[]{:S(2)}) %collective-permute-start.24) | collective-permute-done | bytes 458784 | tf_op jit(solution)/shard_map/ppermute | solution.py:814
  118.6 2.7 %collective-permute-start.29 = (bf16[448,512]{1,0:T(8,128)(2,1)S(1)}, bf16[448,512]{1,0:T(8,128)(2,1)S(1)}, u32[]{:S(2)}, u32[]{:S(2)}) collective-permute-start(bf16[448,512]{1,0:T(8,128)(2,1)S(1)} %get-tuple-element.357.refs_0_), channel_id=1, source_target_pairs={{0,4},{1,3},{2,6},{3,1},{4,0},{5,7},{6,2},{7,5},{8,12},{9,11},{10,... | collective-permute-start | bytes 1376264 | tf_op jit(solution)/shard_map/ppermute | solution.py:814
  121.3 1.3 unpack_1.5
  122.6 1.3 unpack_0.4
  124.0 0.5 collective-permute-start.30
  124.5 1.3 unpack_0.5
  125.8 1.3 unpack_1.6
  127.1 0.6 collective-permute-done.29.refs_1_
  127.8 0.7 collective-permute-start.31
  128.5 1.3 unpack_0.6
  129.8 1.3 unpack_1.7
  131.1 1.9 %unpack_0.7 = (f32[8,128]{1,0:T(8,128)}, f32[1,512,1536]{2,1,0:T(8,128)}, f32[1,512,512]{2,1,0:T(8,128)}) custom-call(s32[4]{0:T(128)S(4)} %get-tuple-element.189.place_ref, f32[8,128]{1,0:T(8,128)S(1)} %get-tuple-element.363.token_in, bf16[896,512]{1,0:T(8,128)(2,1)S(1)} %collective-permute-done.31.refs_0_, ...), custom_call_target="tpu_custom_call", output_to_operand_aliasing={{1}: (3, {}), {2}: (4, {})} | custom-call | flops 1000000000 | tf_op jit(solution)/shard_map/unpack_0/pallas_call | solution.py:229
  (42 shorter events, 1.3 us)
Async XLA Ops:
  5.5 8.7 %collective-permute-start = (bf16[128,1024]{1,0:T(8,128)(2,1)S(1)}, bf16[128,1024]{1,0:T(8,128)(2,1)S(1)}, u32[]{:S(2)}, u32[]{:S(2)}) collective-permute-start(bf16[128,1024]{1,0:T(8,128)(2,1)S(1)} %get-tuple-element.215), channel_id=1, source_target_pairs={{0,16},{1,17},{2,18},{3,19},{4,20},{5,21},{6,22},{7,23},{8,24},{9,... | collective-permute-start | bytes 786440 | tf_op jit(solution)/shard_map/ppermute | solution.py:967
  11.9 7.4 %collective-permute-start.1 = (bf16[128,1024]{1,0:T(8,128)(2,1)S(1)}, bf16[128,1024]{1,0:T(8,128)(2,1)S(1)}, u32[]{:S(2)}, u32[]{:S(2)}) collective-permute-start(bf16[128,1024]{1,0:T(8,128)(2,1)S(1)} %get-tuple-element.219), channel_id=1, source_target_pairs={{0,16},{1,17},{2,18},{3,19},{4,20},{5,21},{6,22},{7,23},{8,24},{9,... | collective-permute-start | bytes 786440 | tf_op jit(solution)/shard_map/ppermute | solution.py:969
  14.7 11.9 %collective-permute-start.2 = (bf16[128,1024]{1,0:T(8,128)(2,1)S(1)}, bf16[128,1024]{1,0:T(8,128)(2,1)S(1)}, u32[]{:S(2)}, u32[]{:S(2)}) collective-permute-start(bf16[128,1024]{1,0:T(8,128)(2,1)S(1)} %get-tuple-element.234), channel_id=1, source_target_pairs={{16,0},{17,1},{18,2},{19,3},{20,4},{21,5},{22,6},{23,7},{24,8},{25... | collective-permute-start | bytes 786440 | tf_op jit(solution)/shard_map/ppermute | solution.py:973
  19.8 12.9 %collective-permute-start.3 = (bf16[128,1024]{1,0:T(8,128)(2,1)S(1)}, bf16[128,1024]{1,0:T(8,128)(2,1)S(1)}, u32[]{:S(2)}, u32[]{:S(2)}) collective-permute-start(bf16[128,1024]{1,0:T(8,128)(2,1)S(1)} %get-tuple-element.247), channel_id=1, source_target_pairs={{16,0},{17,1},{18,2},{19,3},{20,4},{21,5},{22,6},{23,7},{24,8},{25... | collective-permute-start | bytes 786440 | tf_op jit(solution)/shard_map/ppermute | solution.py:973
  33.7 2.7 %collective-permute-start.4 = (bf16[896,512]{1,0:T(8,128)(2,1)S(1)}, bf16[896,512]{1,0:T(8,128)(2,1)S(1)}, u32[]{:S(2)}, u32[]{:S(2)}) collective-permute-start(bf16[896,512]{1,0:T(8,128)(2,1)S(1)} %get-tuple-element.268), channel_id=1, source_target_pairs={{0,1},{1,0},{2,3},{3,2},{4,5},{5,4},{6,7},{7,6},{8,9},{9,8},{10,11... | collective-permute-start | bytes 2752520 | tf_op jit(solution)/shard_map/ppermute | solution.py:814
  35.9 3.6 %collective-permute-start.5 = (bf16[896,512]{1,0:T(8,128)(2,1)S(1)}, bf16[896,512]{1,0:T(8,128)(2,1)S(1)}, u32[]{:S(2)}, u32[]{:S(2)}) collective-permute-start(bf16[896,512]{1,0:T(8,128)(2,1)S(1)} %get-tuple-element.274), channel_id=1, source_target_pairs={{0,1},{1,0},{2,3},{3,2},{4,5},{5,4},{6,7},{7,6},{8,9},{9,8},{10,11... | collective-permute-start | bytes 2752520 | tf_op jit(solution)/shard_map/ppermute | solution.py:814
  37.0 8.5 %collective-permute-start.6 = (bf16[448,512]{1,0:T(8,128)(2,1)S(1)}, bf16[448,512]{1,0:T(8,128)(2,1)S(1)}, u32[]{:S(2)}, u32[]{:S(2)}) collective-permute-start(bf16[448,512]{1,0:T(8,128)(2,1)S(1)} %get-tuple-element.285), channel_id=1, source_target_pairs={{0,2},{1,5},{2,0},{3,7},{4,6},{5,1},{6,4},{7,3},{8,10},{9,13},{10,... | collective-permute-start | bytes 1376264 | tf_op jit(solution)/shard_map/ppermute | solution.py:814
  40.1 12.4 %collective-permute-start.8 = (bf16[448,512]{1,0:T(8,128)(2,1)S(1)}, bf16[448,512]{1,0:T(8,128)(2,1)S(1)}, u32[]{:S(2)}, u32[]{:S(2)}) collective-permute-start(bf16[448,512]{1,0:T(8,128)(2,1)S(1)} %get-tuple-element.290), channel_id=1, source_target_pairs={{0,2},{1,5},{2,0},{3,7},{4,6},{5,1},{6,4},{7,3},{8,10},{9,13},{10,... | collective-permute-start | bytes 1376264 | tf_op jit(solution)/shard_map/ppermute | solution.py:814
  41.1 4.5 %collective-permute-start.7 = (bf16[896,512]{1,0:T(8,128)(2,1)S(1)}, bf16[896,512]{1,0:T(8,128)(2,1)S(1)}, u32[]{:S(2)}, u32[]{:S(2)}) collective-permute-start(bf16[896,512]{1,0:T(8,128)(2,1)S(1)} %get-tuple-element.287), channel_id=1, source_target_pairs={{0,1},{1,0},{2,3},{3,2},{4,5},{5,4},{6,7},{7,6},{8,9},{9,8},{10,11... | collective-permute-start | bytes 2752520 | tf_op jit(solution)/shard_map/ppermute | solution.py:814
  43.7 8.9 %collective-permute-start.9 = (bf16[896,512]{1,0:T(8,128)(2,1)S(1)}, bf16[896,512]{1,0:T(8,128)(2,1)S(1)}, u32[]{:S(2)}, u32[]{:S(2)}) collective-permute-start(bf16[896,512]{1,0:T(8,128)(2,1)S(1)} %get-tuple-element.292), channel_id=1, source_target_pairs={{0,1},{1,0},{2,3},{3,2},{4,5},{5,4},{6,7},{7,6},{8,9},{9,8},{10,11... | collective-permute-start | bytes 2752520 | tf_op jit(solution)/shard_map/ppermute | solution.py:814
  46.2 14.2 %collective-permute-start.11 = (bf16[448,512]{1,0:T(8,128)(2,1)S(1)}, bf16[448,512]{1,0:T(8,128)(2,1)S(1)}, u32[]{:S(2)}, u32[]{:S(2)}) collective-permute-start(bf16[448,512]{1,0:T(8,128)(2,1)S(1)} %get-tuple-element.299), channel_id=1, source_target_pairs={{0,4},{1,3},{2,6},{3,1},{4,0},{5,7},{6,2},{7,5},{8,12},{9,11},{10,... | collective-permute-start | bytes 1376264 | tf_op jit(solution)/shard_map/ppermute | solution.py:814
  48.3 8.9 %collective-permute-start.10 = (bf16[224,512]{1,0:T(8,128)(2,1)S(1)}, bf16[224,512]{1,0:T(8,128)(2,1)S(1)}, u32[]{:S(2)}, u32[]{:S(2)}) collective-permute-start(bf16[224,512]{1,0:T(8,128)(2,1)S(1)} %get-tuple-element.296), channel_id=1, source_target_pairs={{0,4},{1,3},{2,6},{3,1},{4,0},{5,7},{6,2},{7,5},{8,12},{9,11},{10,... | collective-permute-start | bytes 688136 | tf_op jit(solution)/shard_map/ppermute | solution.py:814
  53.1 18.8 %collective-permute-start.13 = (bf16[448,512]{1,0:T(8,128)(2,1)S(1)}, bf16[448,512]{1,0:T(8,128)(2,1)S(1)}, u32[]{:S(2)}, u32[]{:S(2)}) collective-permute-start(bf16[448,512]{1,0:T(8,128)(2,1)S(1)} %get-tuple-element.305), channel_id=1, source_target_pairs={{0,4},{1,3},{2,6},{3,1},{4,0},{5,7},{6,2},{7,5},{8,12},{9,11},{10,... | collective-permute-start | bytes 1376264 | tf_op jit(solution)/shard_map/ppermute | solution.py:814
  55.5 14.3 %collective-permute-start.12 = (bf16[224,512]{1,0:T(8,128)(2,1)S(1)}, bf16[224,512]{1,0:T(8,128)(2,1)S(1)}, u32[]{:S(2)}, u32[]{:S(2)}) collective-permute-start(bf16[224,512]{1,0:T(8,128)(2,1)S(1)} %get-tuple-element.302), channel_id=1, source_target_pairs={{0,4},{1,3},{2,6},{3,1},{4,0},{5,7},{6,2},{7,5},{8,12},{9,11},{10,... | collective-permute-start | bytes 688136 | tf_op jit(solution)/shard_map/ppermute | solution.py:814
  57.3 14.7 %collective-permute-start.14 = (bf16[224,512]{1,0:T(8,128)(2,1)S(1)}, bf16[224,512]{1,0:T(8,128)(2,1)S(1)}, u32[]{:S(2)}, u32[]{:S(2)}) collective-permute-start(bf16[224,512]{1,0:T(8,128)(2,1)S(1)} %get-tuple-element.307.refs_0_), channel_id=1, source_target_pairs={{0,8},{1,9},{2,10},{3,11},{4,12},{5,13},{6,14},{7,15},{8,0},{9,1},... | collective-permute-start | bytes 688136 | tf_op jit(solution)/shard_map/ppermute | solution.py:814
  69.9 14.3 %collective-permute-start.16 = (bf16[224,512]{1,0:T(8,128)(2,1)S(1)}, bf16[224,512]{1,0:T(8,128)(2,1)S(1)}, u32[]{:S(2)}, u32[]{:S(2)}) collective-permute-start(bf16[224,512]{1,0:T(8,128)(2,1)S(1)} %get-tuple-element.319.refs_0_), channel_id=1, source_target_pairs={{0,8},{1,9},{2,10},{3,11},{4,12},{5,13},{6,14},{7,15},{8,0},{9,1},... | collective-permute-start | bytes 688136 | tf_op jit(solution)/shard_map/ppermute | solution.py:814
  70.2 10.1 %collective-permute-start.15 = (bf16[224,512]{1,0:T(8,128)(2,1)S(1)}, bf16[224,512]{1,0:T(8,128)(2,1)S(1)}, u32[]{:S(2)}, u32[]{:S(2)}) collective-permute-start(bf16[224,512]{1,0:T(8,128)(2,1)S(1)} %get-tuple-element.317), channel_id=1, source_target_pairs={{0,2},{1,5},{2,0},{3,7},{4,6},{5,1},{6,4},{7,3},{8,10},{9,13},{10,... | collective-permute-start | bytes 688136 | tf_op jit(solution)/shard_map/ppermute | solution.py:814
  72.1 17.4 %collective-permute-start.18 = (bf16[224,512]{1,0:T(8,128)(2,1)S(1)}, bf16[224,512]{1,0:T(8,128)(2,1)S(1)}, u32[]{:S(2)}, u32[]{:S(2)}) collective-permute-start(bf16[224,512]{1,0:T(8,128)(2,1)S(1)} %get-tuple-element.324.refs_0_), channel_id=1, source_target_pairs={{0,4},{1,3},{2,6},{3,1},{4,0},{5,7},{6,2},{7,5},{8,12},{9,11},{10,... | collective-permute-start | bytes 688136 | tf_op jit(solution)/shard_map/ppermute | solution.py:814
  77.3 7.0 %collective-permute-start.17 = (bf16[224,512]{1,0:T(8,128)(2,1)S(1)}, bf16[224,512]{1,0:T(8,128)(2,1)S(1)}, u32[]{:S(2)}, u32[]{:S(2)}) collective-permute-start(bf16[224,512]{1,0:T(8,128)(2,1)S(1)} %get-tuple-element.322), channel_id=1, source_target_pairs={{0,2},{1,5},{2,0},{3,7},{4,6},{5,1},{6,4},{7,3},{8,10},{9,13},{10,... | collective-permute-start | bytes 688136 | tf_op jit(solution)/shard_map/ppermute | solution.py:814
  80.3 13.7 %collective-permute-start.19 = (bf16[224,512]{1,0:T(8,128)(2,1)S(1)}, bf16[224,512]{1,0:T(8,128)(2,1)S(1)}, u32[]{:S(2)}, u32[]{:S(2)}) collective-permute-start(bf16[224,512]{1,0:T(8,128)(2,1)S(1)} %get-tuple-element.326.refs_0_), channel_id=1, source_target_pairs={{0,8},{1,9},{2,10},{3,11},{4,12},{5,13},{6,14},{7,15},{8,0},{9,1},... | collective-permute-start | bytes 688136 | tf_op jit(solution)/shard_map/ppermute | solution.py:814
  89.5 16.6 %collective-permute-start.22 = (bf16[448,512]{1,0:T(8,128)(2,1)S(1)}, bf16[448,512]{1,0:T(8,128)(2,1)S(1)}, u32[]{:S(2)}, u32[]{:S(2)}) collective-permute-start(bf16[448,512]{1,0:T(8,128)(2,1)S(1)} %get-tuple-element.332.refs_0_), channel_id=1, source_target_pairs={{0,2},{1,5},{2,0},{3,7},{4,6},{5,1},{6,4},{7,3},{8,10},{9,13},{10,... | collective-permute-start | bytes 1376264 | tf_op jit(solution)/shard_map/ppermute | solution.py:814
  90.8 13.1 %collective-permute-start.20 = (bf16[224,512]{1,0:T(8,128)(2,1)S(1)}, bf16[224,512]{1,0:T(8,128)(2,1)S(1)}, u32[]{:S(2)}, u32[]{:S(2)}) collective-permute-start(bf16[224,512]{1,0:T(8,128)(2,1)S(1)} %get-tuple-element.328.refs_0_), channel_id=1, source_target_pairs={{0,4},{1,3},{2,6},{3,1},{4,0},{5,7},{6,2},{7,5},{8,12},{9,11},{10,... | collective-permute-start | bytes 688136 | tf_op jit(solution)/shard_map/ppermute | solution.py:814
  90.8 13.2 %collective-permute-start.21 = (bf16[224,512]{1,0:T(8,128)(2,1)S(1)}, bf16[224,512]{1,0:T(8,128)(2,1)S(1)}, u32[]{:S(2)}, u32[]{:S(2)}) collective-permute-start(bf16[224,512]{1,0:T(8,128)(2,1)S(1)} %get-tuple-element.330.refs_0_), channel_id=1, source_target_pairs={{0,8},{1,9},{2,10},{3,11},{4,12},{5,13},{6,14},{7,15},{8,0},{9,1},... | collective-permute-start | bytes 688136 | tf_op jit(solution)/shard_map/ppermute | solution.py:814
  94.1 12.1 %collective-permute-start.23 = (bf16[224,512]{1,0:T(8,128)(2,1)S(1)}, bf16[224,512]{1,0:T(8,128)(2,1)S(1)}, u32[]{:S(2)}, u32[]{:S(2)}) collective-permute-start(bf16[224,512]{1,0:T(8,128)(2,1)S(1)} %get-tuple-element.334.refs_0_), channel_id=1, source_target_pairs={{0,2},{1,5},{2,0},{3,7},{4,6},{5,1},{6,4},{7,3},{8,10},{9,13},{10,... | collective-permute-start | bytes 688136 | tf_op jit(solution)/shard_map/ppermute | solution.py:814
  104.0 14.5 %collective-permute-start.25 = (bf16[224,512]{1,0:T(8,128)(2,1)S(1)}, bf16[224,512]{1,0:T(8,128)(2,1)S(1)}, u32[]{:S(2)}, u32[]{:S(2)}) collective-permute-start(bf16[224,512]{1,0:T(8,128)(2,1)S(1)} %get-tuple-element.340.refs_0_), channel_id=1, source_target_pairs={{0,2},{1,5},{2,0},{3,7},{4,6},{5,1},{6,4},{7,3},{8,10},{9,13},{10,... | collective-permute-start | bytes 688136 | tf_op jit(solution)/shard_map/ppermute | solution.py:814
  105.3 13.2 %collective-permute-start.24 = (bf16[448,512]{1,0:T(8,128)(2,1)S(1)}, bf16[448,512]{1,0:T(8,128)(2,1)S(1)}, u32[]{:S(2)}, u32[]{:S(2)}) collective-permute-start(bf16[448,512]{1,0:T(8,128)(2,1)S(1)} %get-tuple-element.338.refs_0_), channel_id=1, source_target_pairs={{0,2},{1,5},{2,0},{3,7},{4,6},{5,1},{6,4},{7,3},{8,10},{9,13},{10,... | collective-permute-start | bytes 1376264 | tf_op jit(solution)/shard_map/ppermute | solution.py:814
  106.2 17.7 %collective-permute-start.27 = (bf16[448,512]{1,0:T(8,128)(2,1)S(1)}, bf16[448,512]{1,0:T(8,128)(2,1)S(1)}, u32[]{:S(2)}, u32[]{:S(2)}) collective-permute-start(bf16[448,512]{1,0:T(8,128)(2,1)S(1)} %get-tuple-element.347.refs_0_), channel_id=1, source_target_pairs={{0,4},{1,3},{2,6},{3,1},{4,0},{5,7},{6,2},{7,5},{8,12},{9,11},{10,... | collective-permute-start | bytes 1376264 | tf_op jit(solution)/shard_map/ppermute | solution.py:814
  107.4 15.2 %collective-permute-start.26 = (bf16[896,512]{1,0:T(8,128)(2,1)S(1)}, bf16[896,512]{1,0:T(8,128)(2,1)S(1)}, u32[]{:S(2)}, u32[]{:S(2)}) collective-permute-start(bf16[896,512]{1,0:T(8,128)(2,1)S(1)} %get-tuple-element.336.refs_0_), channel_id=1, source_target_pairs={{0,1},{1,0},{2,3},{3,2},{4,5},{5,4},{6,7},{7,6},{8,9},{9,8},{10,11... | collective-permute-start | bytes 2752520 | tf_op jit(solution)/shard_map/ppermute | solution.py:814
  118.6 9.1 %collective-permute-start.29 = (bf16[448,512]{1,0:T(8,128)(2,1)S(1)}, bf16[448,512]{1,0:T(8,128)(2,1)S(1)}, u32[]{:S(2)}, u32[]{:S(2)}) collective-permute-start(bf16[448,512]{1,0:T(8,128)(2,1)S(1)} %get-tuple-element.357.refs_0_), channel_id=1, source_target_pairs={{0,4},{1,3},{2,6},{3,1},{4,0},{5,7},{6,2},{7,5},{8,12},{9,11},{10,... | collective-permute-start | bytes 1376264 | tf_op jit(solution)/shard_map/ppermute | solution.py:814
  121.2 3.3 %collective-permute-start.28 = (bf16[896,512]{1,0:T(8,128)(2,1)S(1)}, bf16[896,512]{1,0:T(8,128)(2,1)S(1)}, u32[]{:S(2)}, u32[]{:S(2)}) collective-permute-start(bf16[896,512]{1,0:T(8,128)(2,1)S(1)} %get-tuple-element.342.refs_0_), channel_id=1, source_target_pairs={{0,1},{1,0},{2,3},{3,2},{4,5},{5,4},{6,7},{7,6},{8,9},{9,8},{10,11... | collective-permute-start | bytes 2752520 | tf_op jit(solution)/shard_map/ppermute | solution.py:814
  124.0 4.5 %collective-permute-start.30 = (bf16[896,512]{1,0:T(8,128)(2,1)S(1)}, bf16[896,512]{1,0:T(8,128)(2,1)S(1)}, u32[]{:S(2)}, u32[]{:S(2)}) collective-permute-start(bf16[896,512]{1,0:T(8,128)(2,1)S(1)} %get-tuple-element.354.refs_0_), channel_id=1, source_target_pairs={{0,1},{1,0},{2,3},{3,2},{4,5},{5,4},{6,7},{7,6},{8,9},{9,8},{10,11... | collective-permute-start | bytes 2752520 | tf_op jit(solution)/shard_map/ppermute | solution.py:814
  127.8 3.3 %collective-permute-start.31 = (bf16[896,512]{1,0:T(8,128)(2,1)S(1)}, bf16[896,512]{1,0:T(8,128)(2,1)S(1)}, u32[]{:S(2)}, u32[]{:S(2)}) collective-permute-start(bf16[896,512]{1,0:T(8,128)(2,1)S(1)} %get-tuple-element.361.refs_0_), channel_id=1, source_target_pairs={{0,1},{1,0},{2,3},{3,2},{4,5},{5,4},{6,7},{7,6},{8,9},{9,8},{10,11... | collective-permute-start | bytes 2752520 | tf_op jit(solution)/shard_map/ppermute | solution.py:814

commit v4 on v3

--- a/solution.py
+++ b/solution.py
@@ -29,6 +29,11 @@
 PLACE = 4
 
 
+def in_two(value):
+    rounded = value.astype(LOW)
+    return rounded, (value - rounded.astype(F32)).astype(LOW)
+
+
 def mm(left, right):
     return jnp.dot(left, right, preferred_element_type=F32)
 
@@ -96,13 +101,19 @@
         write_mix(pair, mm_tn(probs.astype(LOW), two_heads(read_v(pair), lanes)).astype(LOW))
 
 
-def attend_back(read_q, read_k, read_v, read_probs, read_grad, write):
+def attend_back_values(read_probs, read_grad, write):
+    lanes = low_lanes()
+    for pair in range(PAIRS):
+        grad_v = mm(read_probs(pair).astype(LOW), read_grad(pair))
+        write(pair, jnp.where(lanes, *two_halves(grad_v)))
+
+
+def attend_back_keys(read_q, read_k, read_v, read_probs, read_grad, write):
     lanes = low_lanes()
     for pair in range(PAIRS):
         query = (read_q(pair).astype(F32) * SCALE).astype(LOW)
         probs = read_probs(pair)
-        grad = read_grad(pair)
-        grad_probs = mm_nt(two_heads(read_v(pair), lanes), grad)
+        grad_probs = mm_nt(two_heads(read_v(pair), lanes), read_grad(pair))
         slopes = []
         for head, change in zip(two_halves(probs), two_halves(grad_probs)):
             total = jnp.sum(head * change, axis=0, keepdims=True)
@@ -110,8 +121,7 @@
         slopes = jnp.concatenate(slopes, axis=0)
         grad_q = mm_tn(slopes, two_heads(read_k(pair), lanes)) * SCALE
         grad_k = jnp.where(lanes, *two_halves(mm(slopes, query)))
-        grad_v = jnp.where(lanes, *two_halves(mm(probs.astype(LOW), grad)))
-        write(pair, grad_q.astype(LOW), grad_k.astype(LOW), grad_v.astype(LOW))
+        write(pair, grad_q, grad_k)
 
 
 def columns(ref, rows, start):
@@ -250,23 +260,26 @@
     return token, made
 
 
-def forward_step(micro, first, lengths_ref, ref, link, gets):
+def forward_step(micro, encoder, lengths_ref, ref, link, gets):
     rows = slice(micro * ROWS, (micro + 1) * ROWS)
-    gets.lengths.wait()
-    seg_q_tgt = segments(lengths_ref, micro, 1, 1)
-    seg_k_src = segments(lengths_ref, micro, 0, 0)
-    ref.across[rows, :] = (seg_k_src == seg_q_tgt).astype(F32)
-    earlier = lax.broadcasted_iota(jnp.int32, (ROWS, ROWS), 0) <= lax.broadcasted_iota(
-        jnp.int32, (ROWS, ROWS), 1
-    )
-    source_mask = (seg_k_src == segments(lengths_ref, micro, 0, 1)).astype(jnp.int32)
-    target_mask = ((segments(lengths_ref, micro, 1, 0) == seg_q_tgt) & earlier).astype(jnp.int32)
-    mask = jnp.where(first, source_mask, target_mask) != 0
     gets.tokens.wait()
     tokens = ref.tokens[rows, :]
+    gets.w_qkv[0].wait()
+    gets.lengths.wait()
+    if encoder:
+        mask = segments(lengths_ref, micro, 0, 0) == segments(lengths_ref, micro, 0, 1)
+    else:
+        seg_tgt = segments(lengths_ref, micro, 1, 1)
+        source = segments(lengths_ref, micro, 0, 0)
+        ref.across[rows, :] = (source == seg_tgt).astype(F32)
+        earlier = lax.broadcasted_iota(jnp.int32, (ROWS, ROWS), 0) <= lax.broadcasted_iota(
+            jnp.int32, (ROWS, ROWS), 1
+        )
+        mask = (segments(lengths_ref, micro, 1, 0) == seg_tgt) & earlier
     for part in range(3):
         cut = slice(part * D, (part + 1) * D)
-        gets.w_qkv[part].wait()
+        if part:
+            gets.w_qkv[part].wait()
         ref.proj[rows, cut] = mm(tokens, ref.w_qkv[:, cut]).astype(LOW)
 
     def write_probs(pair, value):
@@ -286,29 +299,23 @@
     gets.w_out.wait()
     mid = tokens.astype(F32) + mm(ref.mix[rows, :], ref.w_out[...])
 
-    @pl.when(first)
-    def _():
-        ref.narrow[rows, :] = mid.astype(LOW)
-        gets.w_up.wait()
-        gets.w_down.wait()
-        total = mid
-        for part in range(4):
-            cut = slice(part * D, (part + 1) * D)
-            hidden = mm(ref.narrow[rows, :], ref.w_up[:, cut])
-            ref.wide[rows, cut] = hidden
-            ref.act[rows, cut] = gelu(hidden).astype(LOW)
-            total = total + mm(ref.act[rows, cut], ref.w_down[cut, :])
-        ref.result[rows, :] = total.astype(LOW)
-        gets.w_cross.wait()
-        for part in range(2):
-            cut = slice(part * D, (part + 1) * D)
-            link[:, cut] = mm(ref.result[rows, :], ref.w_cross[:, cut]).astype(LOW)
-        ref.left_a[rows, :] = ref.result[rows, :]
-
-    @pl.when(jnp.logical_not(first))
-    def _():
+    if not encoder:
         ref.left_a[rows, :] = mid.astype(LOW)
         ref.mid[rows, :] = mid
+        return
+    ref.narrow[rows, :] = mid.astype(LOW)
+    gets.w_up.wait()
+    gets.w_down.wait()
+    for part in range(4):
+        cut = slice(part * D, (part + 1) * D)
+        hidden = mm(ref.narrow[rows, :], ref.w_up[:, cut])
+        ref.wide[rows, cut] = hidden
+        ref.act[rows, cut] = gelu(hidden).astype(LOW)
+    total = mid + mm(ref.act[rows, :], ref.w_down[...])
+    ref.result[rows, :] = total.astype(LOW)
+    gets.w_cross.wait()
+    link[...] = mm(ref.result[rows, :], ref.w_cross[...]).astype(LOW)
+    ref.left_a[rows, :] = ref.result[rows, :]
 
 
 def decoder_ahead(ref, gets):
@@ -338,53 +345,59 @@
         pass
 
 
-def first_stage(lengths, tokens, w_qkv, w_out, w_cross, w_up, w_down):
-    given = (lengths, tokens, w_qkv, w_out, w_up, w_down, w_cross)
+def fetches(ref, sems, lengths_ref, sources):
+    lengths_in, tokens_in, qkv_in, out_in, up_in, down_in, cross_in, cotangent_in = sources
+    parts = [pl.ds(part * D, D) for part in range(3)]
+    return SimpleNamespace(
+        lengths=Fetch(lengths_in, lengths_ref, sems.at[0]),
+        tokens=Fetch(tokens_in.at[0], ref.tokens, sems.at[1]),
+        w_qkv=[
+            Fetch(qkv_in.at[0, :, part], ref.w_qkv.at[:, part], sems.at[2 + at])
+            for at, part in enumerate(parts)
+        ],
+        w_out=Fetch(out_in.at[0], ref.w_out, sems.at[5]),
+        w_up=Fetch(up_in.at[0], ref.w_up, sems.at[6]),
+        w_down=Fetch(down_in.at[0], ref.w_down, sems.at[7]),
+        w_cross=Fetch(cross_in.at[0], ref.w_cross, sems.at[8]),
+        cotangent=Fetch(cotangent_in.at[0], ref.cotangent, sems.at[9]),
+    )
+
+
+def start_all(gets):
+    order = [gets.lengths, gets.tokens, *gets.w_qkv, gets.w_out, gets.w_up, gets.w_down, gets.w_cross]
+    for get in order:
+        get.start()
+
+
+FETCHED = 8
+FETCH_SCRATCH = [pltpu.SMEM((MB, 2, SLOTS), jnp.int32), pltpu.SemaphoreType.DMA((FETCHED + 2,))]
+
+
+def first_stage(given):
     makes = {**WEIGHTS, **HELD, **STATE, **dict(link=((ROWS, 2 * D), LOW), token=TOKEN)}
 
-    def body(lengths_in, tokens_in, qkv_in, out_in, up_in, down_in, cross_in, *refs):
-        place_ref, lengths_ref, sems = refs[len(makes) :]
-        ref = SimpleNamespace(**dict(zip(makes, refs)))
+    def body(*refs):
+        place_ref, lengths_ref, sems = refs[FETCHED + len(makes) :]
+        ref = SimpleNamespace(**dict(zip(makes, refs[FETCHED:])))
         index = lax.axis_index(DP).astype(jnp.int32)
         section = lax.axis_index(SECTION).astype(jnp.int32)
         place_ref[0] = section
         for bit in range(PLACE - 1):
             place_ref[1 + bit] = (index >> bit) % 2
-        first = section == 0
-        gets = SimpleNamespace(
-            lengths=Fetch(lengths_in, lengths_ref, sems.at[0]),
-            tokens=Fetch(tokens_in.at[0], ref.tokens, sems.at[1]),
-            w_qkv=[
-                Fetch(
-                    qkv_in.at[0, :, pl.ds(part * D, D)],
-                    ref.w_qkv.at[:, pl.ds(part * D, D)],
-                    sems.at[2 + part],
-                )
-                for part in range(3)
-            ],
-            w_out=Fetch(out_in.at[0], ref.w_out, sems.at[5]),
-            w_up=Fetch(up_in.at[0], ref.w_up, sems.at[6]),
-            w_down=Fetch(down_in.at[0], ref.w_down, sems.at[7]),
-            w_cross=Fetch(cross_in.at[0], ref.w_cross, sems.at[8]),
-        )
-        for get in [gets.lengths, gets.tokens, *gets.w_qkv, gets.w_out]:
-            get.start()
-
-        @pl.when(first)
+        ref.token[...] = jnp.zeros(*TOKEN)
+
+        @pl.when(section == 0)
         def _():
-            gets.w_up.start()
-            gets.w_down.start()
-            gets.w_cross.start()
-
-        ref.token[...] = jnp.zeros(*TOKEN)
-        forward_step(0, first, lengths_ref, ref, ref.link, gets)
+            gets = fetches(ref, sems, lengths_ref, refs[:FETCHED])
+            start_all(gets)
+            forward_step(0, True, lengths_ref, ref, ref.link, gets)
 
     results = pl.pallas_call(
         body,
         out_shape=shaped(makes) + [pltpu.SMEM((PLACE,), jnp.int32)],
-        in_specs=[in_hbm()] * len(given),
+        in_specs=[in_hbm()] * FETCHED,
         out_specs=[in_vmem()] * len(makes) + [in_smem()],
-        scratch_shapes=[pltpu.SMEM((MB, 2, SLOTS), jnp.int32), pltpu.SemaphoreType.DMA((9,))],
+        scratch_shapes=FETCH_SCRATCH,
         compiler_params=pltpu.CompilerParams(vmem_limit_bytes=16 * MIB),
         cost_estimate=pl.CostEstimate(
             flops=2 * ROWS * D * 7168, bytes_accessed=10_000_000, transcendentals=0
@@ -397,60 +410,50 @@
     return results[-1], token, link, made
 
 
-def second_stage(place, state, lengths, cotangent, w_cross, w_up, w_down):
-    given = (lengths, cotangent, w_cross, w_up, w_down)
+def second_stage(place, state, given):
     kept = {**WEIGHTS, **HELD, **STATE}
     keeps = [getattr(state, name) for name in kept]
 
-    def body(place_ref, lengths_in, cotangent_in, cross_in, up_in, down_in, *refs):
-        refs = refs[len(keeps) :]
+    def body(place_ref, *refs):
+        sources = refs[:FETCHED]
+        refs = refs[FETCHED + len(keeps) :]
         ref = SimpleNamespace(**dict(zip(kept, refs)))
         link, lengths_ref, sems = refs[len(keeps) :]
-        first = place_ref[0] == 0
+        gets = fetches(ref, sems, lengths_ref, sources)
         here = Arrived()
-        get_lengths = Fetch(lengths_in, lengths_ref, sems.at[0])
-        get_cotangent = Fetch(cotangent_in.at[0], ref.cotangent, sems.at[1])
-        late = SimpleNamespace(
-            cotangent=get_cotangent,
-            w_cross=Fetch(cross_in.at[0], ref.w_cross, sems.at[2]),
-            w_down=Fetch(down_in.at[0], ref.w_down, sems.at[3]),
-            w_up=Fetch(up_in.at[0], ref.w_up, sems.at[4]),
-        )
-        get_lengths.start()
-        get_cotangent.start()
-
-        @pl.when(jnp.logical_not(first))
+
+        @pl.when(place_ref[0] == 0)
         def _():
-            late.w_cross.start()
-            late.w_down.start()
-            late.w_up.start()
-
-        gets = SimpleNamespace(
-            lengths=get_lengths,
-            tokens=here,
-            w_qkv=[here] * 3,
-            w_out=here,
-            w_up=here,
-            w_down=here,
-            w_cross=here,
-        )
-        forward_step(1, first, lengths_ref, ref, link, gets)
-
-        @pl.when(first)
+            gets.lengths.start()
+            gets.cotangent.start()
+            arrived = SimpleNamespace(
+                lengths=gets.lengths,
+                tokens=here,
+                w_qkv=[here] * 3,
+                w_out=here,
+                w_up=here,
+                w_down=here,
+                w_cross=here,
+            )
+            forward_step(1, True, lengths_ref, ref, link, arrived)
+            gets.cotangent.wait()
+
+        @pl.when(place_ref[0] != 0)
         def _():
-            get_cotangent.wait()
-
-        @pl.when(jnp.logical_not(first))
-        def _():
-            decoder_ahead(ref, late)
+            start_all(gets)
+            gets.cotangent.start()
+            forward_step(0, False, lengths_ref, ref, link, gets)
+            arrived = SimpleNamespace(lengths=here, tokens=here, w_qkv=[here] * 3, w_out=here)
+            forward_step(1, False, lengths_ref, ref, link, arrived)
+            decoder_ahead(ref, gets)
 
     results = pl.pallas_call(
         body,
         out_shape=same_shape(keeps) + [pltpu.VMEM((ROWS, 2 * D), LOW)],
-        in_specs=[in_smem()] + [in_hbm()] * len(given) + [in_vmem()] * len(keeps),
+        in_specs=[in_smem()] + [in_hbm()] * FETCHED + [in_vmem()] * len(keeps),
         out_specs=[in_vmem()] * (len(keeps) + 1),
-        scratch_shapes=[pltpu.SMEM((MB, 2, SLOTS), jnp.int32), pltpu.SemaphoreType.DMA((5,))],
-        input_output_aliases={1 + len(given) + i: i for i in range(len(keeps))},
+        scratch_shapes=FETCH_SCRATCH,
+        input_output_aliases={1 + FETCHED + i: i for i in range(len(keeps))},
         compiler_params=pltpu.CompilerParams(vmem_limit_bytes=16 * MIB),
         cost_estimate=pl.CostEstimate(
             flops=2 * ROWS * D * 7168, bytes_accessed=10_000_000, transcendentals=0
@@ -461,22 +464,24 @@
     return results[-1]
 
 
-def middle_step(micro, ref, probs_v, mixed_v):
+def middle_step(micro, ref):
     rows = slice(micro * ROWS, (micro + 1) * ROWS)
     whole = slice(0, ROWS)
-    reads = (
+
+    def write_probs(pair, value):
+        ref.link_probs[pair] = value
+
+    def write_mix(pair, value):
+        ref.left_b[rows, pair * LANES : (pair + 1) * LANES] = value
+
+    attend(
         columns(ref.query, rows, 0),
         columns(ref.link, whole, 0),
         columns(ref.link, whole, D),
-    )
-
-    def write_probs(pair, value):
-        probs_v[pair] = value
-
-    def write_mix(pair, value):
-        ref.left_b[rows, pair * LANES : (pair + 1) * LANES] = value
-
-    attend(*reads, ref.across[rows, :] != 0.0, write_probs, write_mix)
+        ref.across[rows, :] != 0.0,
+        write_probs,
+        write_mix,
+    )
     after = ref.mid[rows, :] + mm(ref.left_b[rows, :], ref.w_cross[:, D:])
     ref.across_mid[rows, :] = after
     ref.narrow[rows, :] = after.astype(LOW)
@@ -490,15 +495,39 @@
         grad = grad + mm_nt(grad_hidden, ref.w_up[:, cut])
     ref.grad[rows, :] = grad
     ref.right[rows, D:] = grad.astype(LOW)
-    mixed_v[...] = mm_nt(ref.right[rows, D:], ref.w_cross[:, D:]).astype(LOW)
-
-    def write(pair, grad_q, grad_k, grad_v):
+    ref.mixed[...] = mm_nt(ref.right[rows, D:], ref.w_cross[:, D:]).astype(LOW)
+
+    def write(pair, grad_v):
+        ref.values_grad[:, pair * LANES : (pair + 1) * LANES] = grad_v.astype(LOW)
+
+    attend_back_values(lambda pair: ref.link_probs[pair], columns(ref.mixed, whole, 0), write)
+
+
+def middle_keys(micro, ref):
+    rows = slice(micro * ROWS, (micro + 1) * ROWS)
+    whole = slice(0, ROWS)
+
+    def write(pair, grad_q, grad_k):
         cut = slice(pair * LANES, (pair + 1) * LANES)
-        ref.right[rows, cut] = grad_q
-        ref.link_grad[:, cut] = grad_k
-        ref.link_grad[:, D + pair * LANES : D + (pair + 1) * LANES] = grad_v
-
-    attend_back(*reads, lambda pair: probs_v[pair], columns(mixed_v, whole, 0), write)
+        ref.right[rows, cut] = grad_q.astype(LOW)
+        ref.keys_grad[:, cut] = grad_k.astype(LOW)
+
+    attend_back_keys(
+        columns(ref.query, rows, 0),
+        columns(ref.link, whole, 0),
+        columns(ref.link, whole, D),
+        lambda pair: ref.link_probs[pair],
+        columns(ref.mixed, whole, 0),
+        write,
+    )
+
+
+def two_sides(link_grad):
+    return link_grad.at[pl.ds(0, ROWS)], link_grad.at[pl.ds(ROWS, ROWS)]
+
+
+LINK_STATE = dict(link_probs=((PAIRS, 2 * ROWS, ROWS), F32), mixed=((ROWS, D), LOW))
+SIDE = ((ROWS, D), LOW)
 
 
 def middle_stage(micro, place, token, state, link):
@@ -512,16 +541,24 @@
         link=link,
     )
     keeps = dict(narrow=state.narrow, wide=state.wide)
-    makes = dict(link_grad=((ROWS, 2 * D), LOW))
+    makes, scratch = {}, ()
     if micro == 0:
-        makes.update(BACK)
+        makes.update(link_grad=((2 * ROWS, D), LOW), **BACK)
+        scratch = shaped(LINK_STATE)
     else:
+        makes.update(values_grad=SIDE, **LINK_STATE)
         keeps.update((name, getattr(state, name)) for name in BACK)
 
-    def kernel(place_ref, ref, *scratch):
+    def kernel(place_ref, ref, *own):
+        vars(ref).update(zip(LINK_STATE, own))
+
         @pl.when(place_ref[0] != 0)
         def _():
-            middle_step(micro, ref, *scratch)
+            if micro == 0:
+                ref.keys_grad, ref.values_grad = two_sides(ref.link_grad)
+            middle_step(micro, ref)
+            if micro == 0:
+                middle_keys(micro, ref)
 
         @pl.when(place_ref[0] == 0)
         def _():
@@ -530,31 +567,48 @@
                 cut = slice(part * D, (part + 1) * D)
                 ref.wide[rows, cut] = gelu_slope(ref.wide[rows, cut])
 
+    cost = (2 * ROWS * D * 10000, 8_000_000)
     token, made = call(
-        kernel,
-        "middle_stage",
-        place,
-        token,
-        reads,
-        keeps,
-        makes,
-        scratch=(pltpu.VMEM((PAIRS, 2 * ROWS, ROWS), F32), pltpu.VMEM((ROWS, D), LOW)),
-        cost=(2 * ROWS * D * 10000, 8_000_000),
+        kernel, "middle_stage", place, token, reads, keeps, makes, scratch=scratch, cost=cost
     )
     vars(state).update(made)
     return token
 
 
-def gate_step(micro, first, ref):
+def middle_keys_stage(micro, place, token, state, link):
+    reads = dict(query=state.query, link=link, link_probs=state.link_probs, mixed=state.mixed)
+
+    def kernel(place_ref, ref):
+        @pl.when(place_ref[0] != 0)
+        def _():
+            middle_keys(micro, ref)
+
+    cost = mflop(200)
+    keeps, makes = dict(right=state.right), dict(keys_grad=SIDE)
+    token, made = call(kernel, "middle_keys", place, token, reads, keeps, makes, cost=cost)
+    vars(state).update(made)
+    return token
+
+
+def values_step(micro, first, ref):
     rows = slice(micro * ROWS, (micro + 1) * ROWS)
 
     @pl.when(first)
     def _():
         cotangent = ref.cotangent[rows, :].astype(F32)
-        grad = cotangent + mm_nt(ref.link_grad[...], ref.w_cross[...])
+        ref.grad[rows, :] = cotangent + mm_nt(ref.values_grad[...], ref.w_cross[:, D:])
+        ref.right[rows, D:] = ref.values_grad[...]
+
+
+def gate_step(micro, first, ref):
+    rows = slice(micro * ROWS, (micro + 1) * ROWS)
+
+    @pl.when(first)
+    def _():
+        grad = ref.grad[rows, :] + mm_nt(ref.keys_grad[...], ref.w_cross[:, :D])
         ref.grad[rows, :] = grad
         ref.gate[rows, :] = grad.astype(LOW)
-        ref.right[rows, :] = ref.link_grad[...]
+        ref.right[rows, :D] = ref.keys_grad[...]
         ref.left_b[rows, :] = ref.left_a[rows, :]
 
     @pl.when(jnp.logical_not(first))
@@ -595,7 +649,7 @@
         w_down=state.w_down,
         wide=state.wide,
         left_a=state.left_a,
-        link_grad=link_grad,
+        **link_grad,
         narrow=state.narrow,
         mix=state.mix,
     )
@@ -606,6 +660,8 @@
         makes["send%d" % at] = ((chunk.rows, D), LOW)
 
     def kernel(place_ref, ref):
+        if micro == 0:
+            ref.keys_grad, ref.values_grad = two_sides(ref.link_grad)
         for part in parts:
             part(micro, place_ref[0] == 0, ref)
         for at, chunk in enumerate(send):
@@ -622,20 +678,32 @@
     for micro in range(MB):
         rows = slice(micro * ROWS, (micro + 1) * ROWS)
 
-        def write(pair, grad_q, grad_k, grad_v, rows=rows):
-            for part, value in enumerate((grad_q, grad_k, grad_v)):
-                at = part * D + pair * LANES
-                ref.grad_proj[rows, at : at + LANES] = value
-
-        attend_back(
+        def write(pair, *grads, rows=rows, first=0):
+            for part, value in enumerate(grads):
+                at = (first + part) * D + pair * LANES
+                rounded, rest = in_two(value)
+                ref.grad_proj[rows, at : at + LANES] = rounded
+                ref.grad_rest[rows, at : at + LANES] = rest
+
+        def read_probs(pair, micro=micro):
+            return ref.probs[micro, pair]
+
+        attend_back_keys(
             columns(ref.proj, rows, 0),
             columns(ref.proj, rows, D),
             columns(ref.proj, rows, 2 * D),
-            lambda pair, micro=micro: ref.probs[micro, pair],
+            read_probs,
             columns(mixed_v, rows, 0),
             write,
         )
-    put_send(place_ref, ref, QKV, ref.send)
+        attend_back_values(
+            read_probs,
+            columns(mixed_v, rows, 0),
+            lambda pair, value, write=write: write(pair, value, first=2),
+        )
+    for here, gradient, run in QKV.each():
+        value = product_of(gradient, ref, run, 1 - place_ref[1])
+        ref.send[here, :], ref.more[here, :] = in_two(value)
 
 
 def late_stage(place, token, state, cost):
@@ -647,13 +715,15 @@
         tokens=state.tokens,
         mix=state.mix,
     )
-    makes = dict(grad_proj=((BOTH, 3 * D), LOW), send=((QKV.rows, D), LOW))
+    wide, side = ((BOTH, 3 * D), LOW), ((QKV.rows, D), LOW)
+    makes = dict(grad_proj=wide, grad_rest=wide, send=side, more=side)
     scratch = (pltpu.VMEM((BOTH, D), LOW),)
     token, made = call(
         late_kernel, "late_stage", place, token, reads, {}, makes, None, scratch, mflop(cost)
     )
-    state.grad_proj = made["grad_proj"]
-    return token, made["send"]
+    sends = made.pop("send"), made.pop("more")
+    vars(state).update(made)
+    return token, sends
 
 
 def final_kernel(place_ref, ref, result_v, grad_v, sems):
@@ -716,8 +786,12 @@
         return pl.ds(pl.multiple_of(start + half * HALF, PIECE), count * PIECE)
 
     def product(self, ref, part, half, first, count):
-        left_ref, right_ref, column = self.sides(ref, part)
-        return mm_tn(left_ref[:, self.rows(part, half, first, count)], right_ref[:, cut_of(column)])
+        left_ref, right_ref, column, *rest = self.sides(ref, part)
+        value = left_ref[:, self.rows(part, half, first, count)]
+        total = mm_tn(value, right_ref[:, cut_of(column)])
+        for rest_ref in rest:
+            total = total + mm_tn(value, rest_ref[:, cut_of(column)])
+        return total
 
     def target(self, array, part, half, first, count):
         column = 0 if self.down else part * D
@@ -732,13 +806,15 @@
 )
 G_OUT = Gradient(lambda ref, part: (ref.mix, ref.grad_low, 0), dict(g_out=((1, D, D), F32)))
 G_QKV = Gradient(
-    lambda ref, part: (ref.tokens, ref.grad_proj, part), dict(g_qkv=((1, D, 3 * D), F32))
+    lambda ref, part: (ref.tokens, ref.grad_proj, part, ref.grad_rest),
+    dict(g_qkv=((1, D, 3 * D), F32)),
 )
 
 
 class Chunk:
-    def __init__(self, levels, operands, runs):
+    def __init__(self, levels, operands, runs, fine=False):
         self.levels = levels
+        self.fine = fine
         self.operands = operands
         self.runs = runs
         self.rows = PIECES * PIECE
@@ -779,16 +855,21 @@
     [(G_DOWN, 0, 0, 2), (G_DOWN, 1, 0, 2), (G_DOWN, 2, 0, 2), (G_DOWN, 3, 0, 1)],
 )
 UP = Chunk(
-    (Z_FIRST, Y_FIRST),
+    (Y_FIRST, Z_FIRST),
     lambda state: dict(narrow=state.narrow, grad_hidden=state.grad_hidden),
     [(G_UP, 0, 0, 2), (G_UP, 1, 0, 2), (G_UP, 2, 0, 2), (G_UP, 3, 0, 1)],
 )
 QKV = Chunk(
     (Z_FIRST, Y_FIRST),
     lambda state: dict(
-        tokens=state.tokens, grad_proj=state.grad_proj, mix=state.mix, grad_low=state.grad_low
+        tokens=state.tokens,
+        grad_proj=state.grad_proj,
+        grad_rest=state.grad_rest,
+        mix=state.mix,
+        grad_low=state.grad_low,
     ),
     [(G_QKV, 0, 0, 2), (G_QKV, 1, 0, 2), (G_QKV, 2, 0, 2), (G_OUT, 0, 1, 1)],
+    fine=True,
 )
 
 
@@ -825,8 +906,9 @@
         own = pl.ds(pl.multiple_of(bit * half, half), half)
         return own, pl.ds(pl.multiple_of((1 - bit) * half, half), half)
 
-    def launch(self, send):
+    def launch(self, send, *more):
         self.got = self.swap(send, 0)
+        self.more = dict(more=self.swap(*more, 0)) if more else {}
 
     def start(self, token, cost):
         def kernel(place_ref, ref):
@@ -849,8 +931,8 @@
             token = self.round_off(token, rows // 4)
         elif self.step == 3:
             for level in range(4, self.depth + 1):
-                token = self.pair_sum(token, rows // 4, level)
-            token = self.pair_sum(token, rows // 4, 2)
+                token = self.pair_sum(token, rows // 4, level, False)
+            token = self.pair_sum(token, rows // 4, 2, True)
         elif self.step == 4:
             token = self.merge(token, rows // 4, 1)
         elif self.step == 5:
@@ -867,11 +949,13 @@
             for here, gradient, run in chunk.each():
                 own = product_of(gradient, ref, run, place_ref[1])
                 total[here, :] = own + ref.got[here, :].astype(F32)
+                if chunk.fine:
+                    total[here, :] = total[here, :] + ref.more[here, :].astype(F32)
             own, other = self.halves(place_ref, 1, rows)
             ref.send[...] = total[other, :].astype(LOW)
             ref.keep[...] = total[own, :]
 
-        reads = dict(got=self.got, **chunk.operands(self.state))
+        reads = dict(got=self.got, **self.more, **chunk.operands(self.state))
         makes = dict(send=((rows // 2, D), LOW), keep=((rows // 2, D), F32))
         scratch = (pltpu.VMEM((rows, D), F32),)
         token, made = self.call(kernel, token, reads, makes, scratch=scratch)
@@ -893,24 +977,47 @@
         return token
 
     def round_off(self, token, rows):
+        fine = False
+
         def kernel(place_ref, ref):
-            ref.piece[...] = (ref.keep[...] + ref.got[...].astype(F32)).astype(LOW)
-
-        makes = dict(piece=((rows, D), LOW))
+            total = ref.keep[...] + ref.got[...].astype(F32)
+            if fine:
+                ref.piece[...], ref.rest[...] = in_two(total)
+            else:
+                ref.piece[...] = total.astype(LOW)
+
+        side = ((rows, D), LOW)
+        makes = dict(piece=side, rest=side) if fine else dict(piece=side)
         token, made = self.call(kernel, token, dict(keep=self.keep, got=self.got), makes)
-        self.piece = made["piece"]
-        self.got = self.swap(self.piece, 3)
+        self.spread(made, 3)
         return token
 
-    def pair_sum(self, token, rows, level):
-        def kernel(place_ref, ref):
-            both = ref.held[...].astype(F32) + ref.got[...].astype(F32)
-            ref.piece[...] = both.astype(LOW)
-
-        makes = dict(piece=((rows, D), LOW))
-        token, made = self.call(kernel, token, dict(held=self.piece, got=self.got), makes)
+    def spread(self, made, level):
         self.piece = made["piece"]
         self.got = self.swap(self.piece, level)
+        self.more = {}
+        if "rest" in made:
+            self.more = dict(rest=made["rest"], more=self.swap(made["rest"], level))
+
+    def pair_sum(self, token, rows, level, last):
+        fine = False
+
+        def kernel(place_ref, ref):
+            own, other = ref.held[...].astype(F32), ref.got[...].astype(F32)
+            if fine:
+                own, other = own + ref.rest[...].astype(F32), other + ref.more[...].astype(F32)
+            if fine and not last:
+                ref.piece[...], ref.rest_out[...] = in_two(own + other)
+            else:
+                ref.piece[...] = (own + other).astype(LOW)
+
+        side = ((rows, D), LOW)
+        makes = dict(piece=side, rest_out=side) if fine and not last else dict(piece=side)
+        reads = dict(held=self.piece, got=self.got, **self.more)
+        token, made = self.call(kernel, token, reads, makes)
+        if "rest_out" in made:
+            made["rest"] = made.pop("rest_out")
+        self.spread(made, level)
         return token
 
     def merge(self, token, rows, level):
@@ -954,24 +1061,29 @@
 
 CHUNKS = (DOWN, CROSS, UP, QKV)
 GATE, BACK_ATTN, BACK_FFN, FINAL, MORE, OWN = 10, 11, 12, 13, 14, 20
-ORDER = (GATE, BACK_FFN, 0, MORE, 1, BACK_ATTN) + (0, 2, 1, 3) * 2 + (0, FINAL, 2, 1, 3) + (0, 2, 1, 3)
-ORDER += (0, 2, OWN, 1, 3, OWN + 1, 0, 2, 1, OWN + 2, 3, 2, OWN + 3, 3)
-COSTS = (1000, 1000, 8000, 4000, 8000, 8000, 8000, 4000, 1000, 1000, 1000, 1000, 1000, 1000, 1000, 1000, 1000, 1000, 1000, 1000, 1000, 1000, 1000, 1000, 8000, 8000, 1000, 1000, 8000, 1000, 1000, 1000, 1000, 50, 3000, 1000, 1000)
+ORDER = (10, 12, 0, 14, 1, 11, 0, 2, 1, 3, 0, 2, 1, 3, 0, 13, 2, 1, 3, 0, 2, 1, 3, 0, 2, 20, 1, 21, 3, 0, 2, 1, 22, 3, 2, 23, 3)
+COSTS = (1000, 1000, 8000, 4000, 8000, 8000, 8000, 4000, 1000, 1000, 1000, 1000, 1000, 1000, 1000, 1000, 1000, 1000, 1000, 1000, 1000, 1000, 1000, 1000, 8000, 8000, 1000, 8000, 1000, 1000, 1000, 1000, 1000, 50, 3000, 1000, 1000)
 
 
 def on_device(inputs, lengths, w_qkv, w_attn_out, w_cross, w_up, w_down, cotangent):
     count = lax.axis_size("dp")
-    place, token, link, state = first_stage(
-        lengths, inputs, w_qkv, w_attn_out, w_cross, w_up, w_down
-    )
+    given = (lengths, inputs, w_qkv, w_attn_out, w_up, w_down, w_cross, cotangent)
+    place, token, link, state = first_stage(given)
     links = [lax.ppermute(link, "section", [(0, 1)])]
-    link = second_stage(place, state, lengths, cotangent, w_cross, w_up, w_down)
+    link = second_stage(place, state, given)
     links.append(lax.ppermute(link, "section", [(0, 1)]))
-    grads = []
-    for micro in range(MB):
-        token = middle_stage(micro, place, token, state, links[micro])
-        grads.append(lax.ppermute(state.link_grad, "section", [(1, 0)]))
-    token, _ = back_stage(0, place, token, state, grads[0], (gate_step, back_step))
+
+    def to_encoder(side):
+        return lax.ppermute(side, "section", [(1, 0)])
+
+    token = middle_stage(0, place, token, state, links[0])
+    grads = [dict(link_grad=to_encoder(state.link_grad))]
+    token = middle_stage(1, place, token, state, links[1])
+    values = to_encoder(state.values_grad)
+    token = middle_keys_stage(1, place, token, state, links[1])
+    grads.append(dict(keys_grad=to_encoder(state.keys_grad)))
+    token, _ = back_stage(0, place, token, state, grads[0], (values_step, gate_step, back_step), cost=900)
+    token, _ = back_stage(1, place, token, state, dict(values_grad=values), (values_step,), cost=300)
     chunks = [Summing(chunk, state, place, count) for chunk in CHUNKS]
     made = {}
     for task, cost in zip(ORDER, COSTS):
@@ -984,8 +1096,8 @@
         elif task == MORE:
             token = chunks[2].start(token, cost)
         elif task == BACK_ATTN:
-            token, send = late_stage(place, token, state, cost)
-            chunks[3].launch(send)
+            token, sends = late_stage(place, token, state, cost)
+            chunks[3].launch(*sends)
         elif task == FINAL:
             token, ends = final_stage(place, token, state, cost)
             made.update(ends)

time: 133 us -> 129 us (0.970)
  starting transfers between devices: 44.9 us -> 36.5 us
  waiting for transfers between devices: 53.4 us -> 57 us
    ppermute x28 -> x29, starting transfers between devices: 38.4 us -> 28.8 us  [swap(): lax.ppermute(value, 'dp', [(i, partner(i)) for i in range(self.count)])]
    ppermute x28 -> x29, waiting for transfers between devices: 39.7 us -> 44 us  [swap(): lax.ppermute(value, 'dp', [(i, partner(i)) for i in range(self.count)])]
    ppermute x1, starting transfers between devices: 2.65 us -> 1.31 us  [on_device(): links = [lax.ppermute(link, 'section', [(0, 1)])]]
    pallas_call x40 -> x42, Pallas kernels: 25.1 us -> 26.4 us  [call(): pl.pallas_call(body, out_shape=out_shape, in_specs=[in_smem()] + [in_vmem...]
    ppermute x2 -> x3, starting transfers between devices: 2.58 us -> 3.88 us  [to_encoder(): return lax.ppermute(side, 'section', [(1, 0)])]
    ppermute x2 -> x3, waiting for transfers between devices: 9.44 us -> 8.33 us  [to_encoder(): return lax.ppermute(side, 'section', [(1, 0)])]
  transfers between devices with their start and end apart: 32 -> 34, of which waited for: 13 -> 16; matrix products, arithmetic and copies ran while one was open for 0% -> 0% of each run, Pallas kernels for 20% -> 21%
where the time goes in v4:
time: 129 us; the launch traced here: 128 us
  waiting for transfers between devices  57 us (44%)
  starting transfers between devices  36.5 us (28%)
  Pallas kernels  33.8 us (26%)
    ppermute x29, waiting for transfers between devices, swap(): lax.ppermute(value, 'dp', [(i, partner(i)) for i in range(self.count)])  44 us
    ppermute x29, starting transfers between devices, swap(): lax.ppermute(value, 'dp', [(i, partner(i)) for i in range(self.count)])  28.8 us
    pallas_call x42, Pallas kernels, call(): pl.pallas_call(body, out_shape=out_shape, in_specs=[in_smem()] + [in_vmem...  26.4 us
    ppermute x3, waiting for transfers between devices, to_encoder(): return lax.ppermute(side, 'section', [(1, 0)])  8.33 us
    pallas_call x1, Pallas kernels, first_stage(): pl.pallas_call(body, out_shape=shaped(makes) + [pltpu.SMEM((PLACE,), jnp....  4.37 us
    ppermute x3, starting transfers between devices, to_encoder(): return lax.ppermute(side, 'section', [(1, 0)])  3.88 us
    ppermute x1, waiting for transfers between devices, on_device(): links.append(lax.ppermute(link, 'section', [(0, 1)]))  3.5 us
    pallas_call x1, Pallas kernels, second_stage(): pl.pallas_call(body, out_shape=same_shape(keeps) + [pltpu.VMEM((ROWS, 2 *...  3.01 us
  transfers between devices with their start and end apart: 34, of which 16 were waited for; matrix products, arithmetic and copies ran while one was open for 0% of the time, Pallas kernels for 21%

profile of v4, /device:TPU:0, one launch (start us, length us, event | category | flops | bytes accessed | tf_op | source)
XLA Modules:
  0.0 128.5 jit_solution(17573225721956854397)
XLA Ops:
  0.6 4.4 %first_stage.1 = (bf16[512,1536]{1,0:T(8,128)(2,1)S(1)}, bf16[512,512]{1,0:T(8,128)(2,1)S(1)}, bf16[512,1024]{1,0:T(8,128)(2,1)S(1)}, bf16[512,2048]{1,0:T(8,128...) custom-call(s32[2,2,16]{2,1,0:T(2,128)} %refs_0_.3, ...), custom_call_target="tpu_custom_call" | custom-call | flops 939524096 | bytes 10000000 | tf_op jit(solution)/shard_map/first_stage/pallas_call | solution.py:395
  5.0 1.3 %collective-permute-start = (bf16[128,1024]{1,0:T(8,128)(2,1)S(1)}, bf16[128,1024]{1,0:T(8,128)(2,1)S(1)}, u32[]{:S(2)}, u32[]{:S(2)}) collective-permute-start(bf16[128,1024]{1,0:T(8,128)(2,1)S(1)} %get-tuple-element.232), channel_id=1, source_target_pairs={{0,16},{1,17},{2,18},{3,19},{4,20},{5,21},{6,22},{7,23},{8,24},{9,... | collective-permute-start | bytes 786440 | tf_op jit(solution)/shard_map/ppermute | solution.py:1072
  6.3 3.0 %second_stage.1 = (bf16[512,1536]{1,0:T(8,128)(2,1)S(1)}, bf16[512,512]{1,0:T(8,128)(2,1)S(1)}, bf16[512,1024]{1,0:T(8,128)(2,1)S(1)}, bf16[512,2048]{1,0:T(8,12...) custom-call(s32[4]{0:T(128)S(4)} %get-tuple-element.206.place_ref, ...), custom_call_target="tpu_custom_call", output_to_operand_aliasing={{0}: (9, {}), {1}: (10, {}), {2}: (11, {}), {3}: (12, {}), ... | custom-call | flops 939524096 | bytes 10000000 | tf_op jit(solution)/shard_map/second_stage/pallas_call | solution.py:450
  9.3 2.5 %collective-permute-start.1 = (bf16[128,1024]{1,0:T(8,128)(2,1)S(1)}, bf16[128,1024]{1,0:T(8,128)(2,1)S(1)}, u32[]{:S(2)}, u32[]{:S(2)}) collective-permute-start(bf16[128,1024]{1,0:T(8,128)(2,1)S(1)} %get-tuple-element.236), channel_id=1, source_target_pairs={{0,16},{1,17},{2,18},{3,19},{4,20},{5,21},{6,22},{7,23},{8,24},{9,... | collective-permute-start | bytes 786440 | tf_op jit(solution)/shard_map/ppermute | solution.py:1074
  11.8 1.2 collective-permute-done.refs_6_
  13.0 0.6 middle_stage.2
  13.6 1.3 %collective-permute-start.2 = (bf16[256,512]{1,0:T(8,128)(2,1)S(1)}, bf16[256,512]{1,0:T(8,128)(2,1)S(1)}, u32[]{:S(2)}, u32[]{:S(2)}) collective-permute-start(bf16[256,512]{1,0:T(8,128)(2,1)S(1)} %get-tuple-element.255), channel_id=1, source_target_pairs={{16,0},{17,1},{18,2},{19,3},{20,4},{21,5},{22,6},{23,7},{24,8},{25... | collective-permute-start | bytes 786440 | tf_op jit(solution)/shard_map/ppermute | solution.py:1077
  14.9 3.5 %collective-permute-done.1.refs_6_.refs_1_ = bf16[128,1024]{1,0:T(8,128)(2,1)S(1)} collective-permute-done((bf16[128,1024]{1,0:T(8,128)(2,1)S(1)}, bf16[128,1024]{1,0:T(8,128)(2,1)S(1)}, u32[]{:S(2)}, u32[]{:S(2)}) %collective-permute-start.1) | collective-permute-done | bytes 262176 | tf_op jit(solution)/shard_map/ppermute | solution.py:1074
  18.4 0.6 middle_stage.3
  19.0 1.3 %collective-permute-start.3 = (bf16[128,512]{1,0:T(8,128)(2,1)S(1)}, bf16[128,512]{1,0:T(8,128)(2,1)S(1)}, u32[]{:S(2)}, u32[]{:S(2)}) collective-permute-start(bf16[128,512]{1,0:T(8,128)(2,1)S(1)} %get-tuple-element.268), channel_id=1, source_target_pairs={{16,0},{17,1},{18,2},{19,3},{20,4},{21,5},{22,6},{23,7},{24,8},{25... | collective-permute-start | bytes 393224 | tf_op jit(solution)/shard_map/ppermute | solution.py:1077
  20.3 1.3 %collective-permute-start.4 = (bf16[128,512]{1,0:T(8,128)(2,1)S(1)}, bf16[128,512]{1,0:T(8,128)(2,1)S(1)}, u32[]{:S(2)}, u32[]{:S(2)}) collective-permute-start(bf16[128,512]{1,0:T(8,128)(2,1)S(1)} %get-tuple-element.279), channel_id=1, source_target_pairs={{16,0},{17,1},{18,2},{19,3},{20,4},{21,5},{22,6},{23,7},{24,8},{25... | collective-permute-start | bytes 393224 | tf_op jit(solution)/shard_map/ppermute | solution.py:1077
  21.6 5.9 %collective-permute-done.2.refs_6_ = bf16[256,512]{1,0:T(8,128)(2,1)S(1)} collective-permute-done((bf16[256,512]{1,0:T(8,128)(2,1)S(1)}, bf16[256,512]{1,0:T(8,128)(2,1)S(1)}, u32[]{:S(2)}, u32[]{:S(2)}) %collective-permute-start.2) | collective-permute-done | bytes 262176 | tf_op jit(solution)/shard_map/ppermute | solution.py:1077
  27.5 2.3 %back_stage.4 = (f32[256,2048]{1,0:T(8,128)S(1)}, f32[256,512]{1,0:T(8,128)S(1)}, bf16[256,512]{1,0:T(8,128)(2,1)S(1)}, bf16[256,1024]{1,0:T(8,128)(2,1)S(1)}, b...) custom-call(s32[4]{0:T(128)S(4)} %get-tuple-element.206.place_ref, ...), custom_call_target="tpu_custom_call", output_to_operand_aliasing={{0}: (11, {}), {1}: (12, {}), {2}: (13, {}), {3}: (14, {}),... | custom-call | flops 900000000 | tf_op jit(solution)/shard_map/back_stage/pallas_call | solution.py:239
  29.8 0.5 collective-permute-done.3.refs_6_
  30.3 0.3 back_stage.5
  30.6 1.9 %collective-permute-done.4.refs_6_ = bf16[128,512]{1,0:T(8,128)(2,1)S(1)} collective-permute-done((bf16[128,512]{1,0:T(8,128)(2,1)S(1)}, bf16[128,512]{1,0:T(8,128)(2,1)S(1)}, u32[]{:S(2)}, u32[]{:S(2)}) %collective-permute-start.4) | collective-permute-done | bytes 131104 | tf_op jit(solution)/shard_map/ppermute | solution.py:1077
  32.5 0.8 back_stage.6
  33.3 2.1 %back_stage.7 = (f32[256,2048]{1,0:T(8,128)S(1)}, f32[256,512]{1,0:T(8,128)S(1)}, bf16[256,512]{1,0:T(8,128)(2,1)S(1)}, bf16[256,1024]{1,0:T(8,128)(2,1)S(1)}, b...) custom-call(s32[4]{0:T(128)S(4)} %get-tuple-element.206.place_ref, ...), custom_call_target="tpu_custom_call", output_to_operand_aliasing={{0}: (11, {}), {1}: (12, {}), {2}: (13, {}), {3}: (14, {}),... | custom-call | flops 1000000000 | tf_op jit(solution)/shard_map/back_stage/pallas_call | solution.py:239
  35.4 0.5 collective-permute-start.6
  36.0 0.6 sum_0.4
  36.5 1.8 %collective-permute-start.7 = (bf16[448,512]{1,0:T(8,128)(2,1)S(1)}, bf16[448,512]{1,0:T(8,128)(2,1)S(1)}, u32[]{:S(2)}, u32[]{:S(2)}) collective-permute-start(bf16[448,512]{1,0:T(8,128)(2,1)S(1)} %get-tuple-element.317), channel_id=1, source_target_pairs={{0,2},{1,5},{2,0},{3,7},{4,6},{5,1},{6,4},{7,3},{8,10},{9,13},{10,... | collective-permute-start | bytes 1376264 | tf_op jit(solution)/shard_map/ppermute | solution.py:895
  38.3 0.5 product.1
  38.8 0.6 sum_0.5
  39.4 1.1 collective-permute-start.9
  40.4 0.1 collective-permute-start.8
  40.6 3.2 %late_stage.1 = (bf16[256,1536]{1,0:T(8,128)(2,1)S(1)}, bf16[256,1536]{1,0:T(8,128)(2,1)S(1)}, bf16[896,512]{1,0:T(8,128)(2,1)S(1)}, bf16[896,512]{1,0:T(8,128)(2,1)S(1)}, f32[8,128]{1,0:T(8,128)S(1)}) custom-call(s32[4]{0:T(128)S(4)} %get-tuple-element.206.place_ref, f32[8,128]{1,0:T(8,128)S(1)} %get-tuple-element.310.token_in, ...), custom_call_target="tpu_custom_call" | custom-call | flops 8000000000 | tf_op jit(solution)/shard_map/late_stage/pallas_call | solution.py:239
  43.8 0.4 collective-permute-start.10
  44.2 0.1 collective-permute-start.11
  44.3 0.7 collective-permute-done.7.refs_1_
  45.2 1.9 %collective-permute-start.12 = (bf16[224,512]{1,0:T(8,128)(2,1)S(1)}, bf16[224,512]{1,0:T(8,128)(2,1)S(1)}, u32[]{:S(2)}, u32[]{:S(2)}) collective-permute-start(bf16[224,512]{1,0:T(8,128)(2,1)S(1)} %get-tuple-element.330), channel_id=1, source_target_pairs={{0,4},{1,3},{2,6},{3,1},{4,0},{5,7},{6,2},{7,5},{8,12},{9,11},{10,... | collective-permute-start | bytes 688136 | tf_op jit(solution)/shard_map/ppermute | solution.py:895
  47.1 0.5 sum_0.6
  47.6 1.6 %collective-permute-start.13 = (bf16[448,512]{1,0:T(8,128)(2,1)S(1)}, bf16[448,512]{1,0:T(8,128)(2,1)S(1)}, u32[]{:S(2)}, u32[]{:S(2)}) collective-permute-start(bf16[448,512]{1,0:T(8,128)(2,1)S(1)} %get-tuple-element.333), channel_id=1, source_target_pairs={{0,2},{1,5},{2,0},{3,7},{4,6},{5,1},{6,4},{7,3},{8,10},{9,13},{10,... | collective-permute-start | bytes 1376264 | tf_op jit(solution)/shard_map/ppermute | solution.py:895
  49.2 3.3 %collective-permute-done.9.refs_1_ = bf16[448,512]{1,0:T(8,128)(2,1)S(1)} collective-permute-done((bf16[448,512]{1,0:T(8,128)(2,1)S(1)}, bf16[448,512]{1,0:T(8,128)(2,1)S(1)}, u32[]{:S(2)}, u32[]{:S(2)}) %collective-permute-start.9) | collective-permute-done | bytes 458784 | tf_op jit(solution)/shard_map/ppermute | solution.py:895
  52.6 0.8 sum_0.7
  53.3 1.9 %collective-permute-start.15 = (bf16[448,512]{1,0:T(8,128)(2,1)S(1)}, bf16[448,512]{1,0:T(8,128)(2,1)S(1)}, u32[]{:S(2)}, u32[]{:S(2)}) collective-permute-start(bf16[448,512]{1,0:T(8,128)(2,1)S(1)} %get-tuple-element.339), channel_id=1, source_target_pairs={{0,4},{1,3},{2,6},{3,1},{4,0},{5,7},{6,2},{7,5},{8,12},{9,11},{10,... | collective-permute-start | bytes 1376264 | tf_op jit(solution)/shard_map/ppermute | solution.py:895
  55.2 0.2 collective-permute-start.14
  55.5 2.9 %collective-permute-start.16 = (bf16[224,512]{1,0:T(8,128)(2,1)S(1)}, bf16[224,512]{1,0:T(8,128)(2,1)S(1)}, u32[]{:S(2)}, u32[]{:S(2)}) collective-permute-start(bf16[224,512]{1,0:T(8,128)(2,1)S(1)} %get-tuple-element.341.refs_0_), channel_id=1, source_target_pairs={{0,8},{1,9},{2,10},{3,11},{4,12},{5,13},{6,14},{7,15},{8,0},{9,1},... | collective-permute-start | bytes 688136 | tf_op jit(solution)/shard_map/ppermute | solution.py:895
  58.4 3.3 %collective-permute-done.13.refs_1_ = bf16[448,512]{1,0:T(8,128)(2,1)S(1)} collective-permute-done((bf16[448,512]{1,0:T(8,128)(2,1)S(1)}, bf16[448,512]{1,0:T(8,128)(2,1)S(1)}, u32[]{:S(2)}, u32[]{:S(2)}) %collective-permute-start.13) | collective-permute-done | bytes 458784 | tf_op jit(solution)/shard_map/ppermute | solution.py:895
  61.8 7.0 %collective-permute-done.14.refs_1_ = bf16[224,512]{1,0:T(8,128)(2,1)S(1)} collective-permute-done((bf16[224,512]{1,0:T(8,128)(2,1)S(1)}, bf16[224,512]{1,0:T(8,128)(2,1)S(1)}, u32[]{:S(2)}, u32[]{:S(2)}) %collective-permute-start.14) | collective-permute-done | bytes 229408 | tf_op jit(solution)/shard_map/ppermute | solution.py:895
  68.8 2.2 %collective-permute-start.18 = (bf16[224,512]{1,0:T(8,128)(2,1)S(1)}, bf16[224,512]{1,0:T(8,128)(2,1)S(1)}, u32[]{:S(2)}, u32[]{:S(2)}) collective-permute-start(bf16[224,512]{1,0:T(8,128)(2,1)S(1)} %get-tuple-element.353.refs_0_), channel_id=1, source_target_pairs={{0,8},{1,9},{2,10},{3,11},{4,12},{5,13},{6,14},{7,15},{8,0},{9,1},... | collective-permute-start | bytes 688136 | tf_op jit(solution)/shard_map/ppermute | solution.py:895
  71.1 2.5 %collective-permute-start.17 = (bf16[224,512]{1,0:T(8,128)(2,1)S(1)}, bf16[224,512]{1,0:T(8,128)(2,1)S(1)}, u32[]{:S(2)}, u32[]{:S(2)}) collective-permute-start(bf16[224,512]{1,0:T(8,128)(2,1)S(1)} %get-tuple-element.351), channel_id=1, source_target_pairs={{0,4},{1,3},{2,6},{3,1},{4,0},{5,7},{6,2},{7,5},{8,12},{9,11},{10,... | collective-permute-start | bytes 688136 | tf_op jit(solution)/shard_map/ppermute | solution.py:895
  73.8 1.4 %collective-permute-start.19 = (bf16[224,512]{1,0:T(8,128)(2,1)S(1)}, bf16[224,512]{1,0:T(8,128)(2,1)S(1)}, u32[]{:S(2)}, u32[]{:S(2)}) collective-permute-start(bf16[224,512]{1,0:T(8,128)(2,1)S(1)} %get-tuple-element.356), channel_id=1, source_target_pairs={{0,2},{1,5},{2,0},{3,7},{4,6},{5,1},{6,4},{7,3},{8,10},{9,13},{10,... | collective-permute-start | bytes 688136 | tf_op jit(solution)/shard_map/ppermute | solution.py:895
  75.1 1.6 %final_stage.1 = (f32[8,128]{1,0:T(8,128)S(1)}, bf16[1,256,512]{2,1,0:T(8,128)(2,1)}, bf16[1,256,512]{2,1,0:T(8,128)(2,1)}) custom-call(s32[4]{0:T(128)S(4)} %get-tuple-element.206.place_ref, f32[8,128]{1,0:T(8,128)S(1)} %get-tuple-element.342.token_in, f32[256,512]{1,0:T(8,128)S(1)} %get-tuple-element.343.refs_0_, ...), custom_call_target="tpu_custom_call" | custom-call | flops 1000000000 | tf_op jit(solution)/shard_map/final_stage/pallas_call | solution.py:239
  76.7 4.1 %collective-permute-done.17.refs_1_ = bf16[224,512]{1,0:T(8,128)(2,1)S(1)} collective-permute-done((bf16[224,512]{1,0:T(8,128)(2,1)S(1)}, bf16[224,512]{1,0:T(8,128)(2,1)S(1)}, u32[]{:S(2)}, u32[]{:S(2)}) %collective-permute-start.17) | collective-permute-done | bytes 229408 | tf_op jit(solution)/shard_map/ppermute | solution.py:895
  80.8 3.2 %collective-permute-start.21 = (bf16[224,512]{1,0:T(8,128)(2,1)S(1)}, bf16[224,512]{1,0:T(8,128)(2,1)S(1)}, u32[]{:S(2)}, u32[]{:S(2)}) collective-permute-start(bf16[224,512]{1,0:T(8,128)(2,1)S(1)} %get-tuple-element.360.refs_0_), channel_id=1, source_target_pairs={{0,8},{1,9},{2,10},{3,11},{4,12},{5,13},{6,14},{7,15},{8,0},{9,1},... | collective-permute-start | bytes 688136 | tf_op jit(solution)/shard_map/ppermute | solution.py:895
  84.2 5.5 %collective-permute-done.20.refs_1_ = bf16[224,512]{1,0:T(8,128)(2,1)S(1)} collective-permute-done((bf16[224,512]{1,0:T(8,128)(2,1)S(1)}, bf16[224,512]{1,0:T(8,128)(2,1)S(1)}, u32[]{:S(2)}, u32[]{:S(2)}) %collective-permute-start.20) | collective-permute-done | bytes 229408 | tf_op jit(solution)/shard_map/ppermute | solution.py:895
  89.7 1.8 %collective-permute-start.24 = (bf16[448,512]{1,0:T(8,128)(2,1)S(1)}, bf16[448,512]{1,0:T(8,128)(2,1)S(1)}, u32[]{:S(2)}, u32[]{:S(2)}) collective-permute-start(bf16[448,512]{1,0:T(8,128)(2,1)S(1)} %get-tuple-element.366.refs_0_), channel_id=1, source_target_pairs={{0,2},{1,5},{2,0},{3,7},{4,6},{5,1},{6,4},{7,3},{8,10},{9,13},{10,... | collective-permute-start | bytes 1376264 | tf_op jit(solution)/shard_map/ppermute | solution.py:895
  91.5 2.2 %collective-permute-start.23 = (bf16[224,512]{1,0:T(8,128)(2,1)S(1)}, bf16[224,512]{1,0:T(8,128)(2,1)S(1)}, u32[]{:S(2)}, u32[]{:S(2)}) collective-permute-start(bf16[224,512]{1,0:T(8,128)(2,1)S(1)} %get-tuple-element.364.refs_0_), channel_id=1, source_target_pairs={{0,8},{1,9},{2,10},{3,11},{4,12},{5,13},{6,14},{7,15},{8,0},{9,1},... | collective-permute-start | bytes 688136 | tf_op jit(solution)/shard_map/ppermute | solution.py:895
  93.8 8.7 %collective-permute-done.22.refs_1_ = bf16[224,512]{1,0:T(8,128)(2,1)S(1)} collective-permute-done((bf16[224,512]{1,0:T(8,128)(2,1)S(1)}, bf16[224,512]{1,0:T(8,128)(2,1)S(1)}, u32[]{:S(2)}, u32[]{:S(2)}) %collective-permute-start.22) | collective-permute-done | bytes 229408 | tf_op jit(solution)/shard_map/ppermute | solution.py:895
  102.6 0.4 collective-permute-start.27
  102.9 1.7 %collective-permute-start.26 = (bf16[448,512]{1,0:T(8,128)(2,1)S(1)}, bf16[448,512]{1,0:T(8,128)(2,1)S(1)}, u32[]{:S(2)}, u32[]{:S(2)}) collective-permute-start(bf16[448,512]{1,0:T(8,128)(2,1)S(1)} %get-tuple-element.372.refs_0_), channel_id=1, source_target_pairs={{0,2},{1,5},{2,0},{3,7},{4,6},{5,1},{6,4},{7,3},{8,10},{9,13},{10,... | collective-permute-start | bytes 1376264 | tf_op jit(solution)/shard_map/ppermute | solution.py:895
  104.8 2.6 %collective-permute-done.25.refs_1_ = bf16[224,512]{1,0:T(8,128)(2,1)S(1)} collective-permute-done((bf16[224,512]{1,0:T(8,128)(2,1)S(1)}, bf16[224,512]{1,0:T(8,128)(2,1)S(1)}, u32[]{:S(2)}, u32[]{:S(2)}) %collective-permute-start.25) | collective-permute-done | bytes 229408 | tf_op jit(solution)/shard_map/ppermute | solution.py:895
  107.4 0.4 collective-permute-start.29
  107.8 1.3 %unpack_1.4 = (f32[8,128]{1,0:T(8,128)S(1)}, f32[1,2048,512]{2,1,0:T(8,128)}) custom-call(s32[4]{0:T(128)S(4)} %get-tuple-element.206.place_ref, f32[8,128]{1,0:T(8,128)S(1)} %get-tuple-element.369.token_in, bf16[896,512]{1,0:T(8,128)(2,1)S(1)} %get-tuple-element.370.refs_0_), custom_call_target="tpu_custom_call" | custom-call | flops 8000000000 | tf_op jit(solution)/shard_map/unpack_1/pallas_call | solution.py:239
  109.1 4.5 %collective-permute-done.26.refs_1_ = bf16[448,512]{1,0:T(8,128)(2,1)S(1)} collective-permute-done((bf16[448,512]{1,0:T(8,128)(2,1)S(1)}, bf16[448,512]{1,0:T(8,128)(2,1)S(1)}, u32[]{:S(2)}, u32[]{:S(2)}) %collective-permute-start.26) | collective-permute-done | bytes 458784 | tf_op jit(solution)/shard_map/ppermute | solution.py:895
  113.7 1.3 %unpack_1.5 = (f32[8,128]{1,0:T(8,128)S(1)}, f32[1,512,1024]{2,1,0:T(8,128)}, f32[1,512,512]{2,1,0:T(8,128)}, f32[1,512,2048]{2,1,0:T(8,128)}, f32[1,2048,512]{2,1,0:T(8,128)}) custom-call(s32[4]{0:T(128)S(4)} %get-tuple-element.206.place_ref, f32[8,128]{1,0:T(8,128)S(1)} %get-tuple-element.373.token_in, ...), custom_call_target="tpu_custom_call", output_to_operand_aliasing={{4}: (3, {})} | custom-call | flops 8000000000 | tf_op jit(solution)/shard_map/unpack_1/pallas_call | solution.py:239
  115.2 1.3 %unpack_0.4 = (f32[8,128]{1,0:T(8,128)S(1)}, f32[1,2048,512]{2,1,0:T(8,128)}) custom-call(s32[4]{0:T(128)S(4)} %get-tuple-element.206.place_ref, f32[8,128]{1,0:T(8,128)S(1)} %get-tuple-element.378.token_in, bf16[896,512]{1,0:T(8,128)(2,1)S(1)} %collective-permute-done.28.refs_0_, ...), custom_call_target="tpu_custom_call", output_to_operand_aliasing={{1}: (3, {})} | custom-call | flops 1000000000 | tf_op jit(solution)/shard_map/unpack_0/pallas_call | solution.py:239
  116.5 2.2 %collective-permute-done.29.refs_1_ = bf16[448,512]{1,0:T(8,128)(2,1)S(1)} collective-permute-done((bf16[448,512]{1,0:T(8,128)(2,1)S(1)}, bf16[448,512]{1,0:T(8,128)(2,1)S(1)}, u32[]{:S(2)}, u32[]{:S(2)}) %collective-permute-start.29) | collective-permute-done | bytes 458784 | tf_op jit(solution)/shard_map/ppermute | solution.py:895
  118.8 1.3 %unpack_0.5 = (f32[8,128]{1,0:T(8,128)S(1)}, f32[1,512,1024]{2,1,0:T(8,128)}, f32[1,512,512]{2,1,0:T(8,128)}, f32[1,2048,512]{2,1,0:T(8,128)}, f32[1,512,2048]{2,1,0:T(8,128)}) custom-call(s32[4]{0:T(128)S(4)} %get-tuple-element.206.place_ref, ...), custom_call_target="tpu_custom_call", output_to_operand_aliasing={{1}: (3, {}), {2}: (4, {}), {3}: (5, {}), {4}: (6, {})} | custom-call | flops 1000000000 | tf_op jit(solution)/shard_map/unpack_0/pallas_call | solution.py:239
  120.1 1.3 %unpack_1.6 = (f32[8,128]{1,0:T(8,128)S(1)}, f32[1,512,2048]{2,1,0:T(8,128)}) custom-call(s32[4]{0:T(128)S(4)} %get-tuple-element.206.place_ref, f32[8,128]{1,0:T(8,128)S(1)} %get-tuple-element.387.token_in, bf16[896,512]{1,0:T(8,128)(2,1)S(1)} %get-tuple-element.388.refs_0_, f32[1,512,2048]{2,1,0:T(8,128)} %get-tuple-element.389.refs_1_), custom_call_target="tpu_custom_call", output_to_operand_aliasing={{1}: (3, {})} | custom-call | flops 1000000000 | tf_op jit(solution)/shard_map/unpack_1/pallas_call | solution.py:239
  121.5 2.2 %collective-permute-done.31.refs_1_ = bf16[448,512]{1,0:T(8,128)(2,1)S(1)} collective-permute-done((bf16[448,512]{1,0:T(8,128)(2,1)S(1)}, bf16[448,512]{1,0:T(8,128)(2,1)S(1)}, u32[]{:S(2)}, u32[]{:S(2)}) %collective-permute-start.31) | collective-permute-done | bytes 458784 | tf_op jit(solution)/shard_map/ppermute | solution.py:895
  123.8 1.3 %unpack_0.6 = (f32[8,128]{1,0:T(8,128)S(1)}, f32[1,512,2048]{2,1,0:T(8,128)}) custom-call(s32[4]{0:T(128)S(4)} %get-tuple-element.206.place_ref, f32[8,128]{1,0:T(8,128)S(1)} %get-tuple-element.392.token_in, bf16[896,512]{1,0:T(8,128)(2,1)S(1)} %collective-permute-done.32.refs_0_, ...), custom_call_target="tpu_custom_call", output_to_operand_aliasing={{1}: (3, {})} | custom-call | flops 3000000000 | tf_op jit(solution)/shard_map/unpack_0/pallas_call | solution.py:239
  125.1 1.3 %unpack_1.7 = (f32[8,128]{1,0:T(8,128)S(1)}, f32[1,512,1536]{2,1,0:T(8,128)}, f32[1,512,512]{2,1,0:T(8,128)}) custom-call(s32[4]{0:T(128)S(4)} %get-tuple-element.206.place_ref, f32[8,128]{1,0:T(8,128)S(1)} %get-tuple-element.394.token_in, bf16[896,512]{1,0:T(8,128)(2,1)S(1)} %get-tuple-element.395.refs_0_, ...), custom_call_target="tpu_custom_call", output_to_operand_aliasing={{2}: (3, {})} | custom-call | flops 1000000000 | tf_op jit(solution)/shard_map/unpack_1/pallas_call | solution.py:239
  126.4 1.9 %unpack_0.7 = (f32[8,128]{1,0:T(8,128)}, f32[1,512,1536]{2,1,0:T(8,128)}, f32[1,512,512]{2,1,0:T(8,128)}) custom-call(s32[4]{0:T(128)S(4)} %get-tuple-element.206.place_ref, f32[8,128]{1,0:T(8,128)S(1)} %get-tuple-element.397.token_in, bf16[896,512]{1,0:T(8,128)(2,1)S(1)} %collective-permute-done.33.refs_0_, ...), custom_call_target="tpu_custom_call", output_to_operand_aliasing={{1}: (3, {}), {2}: (4, {})} | custom-call | flops 1000000000 | tf_op jit(solution)/shard_map/unpack_0/pallas_call | solution.py:239
  (48 shorter events, 1.8 us)
Async XLA Ops:
  5.0 8.0 %collective-permute-start = (bf16[128,1024]{1,0:T(8,128)(2,1)S(1)}, bf16[128,1024]{1,0:T(8,128)(2,1)S(1)}, u32[]{:S(2)}, u32[]{:S(2)}) collective-permute-start(bf16[128,1024]{1,0:T(8,128)(2,1)S(1)} %get-tuple-element.232), channel_id=1, source_target_pairs={{0,16},{1,17},{2,18},{3,19},{4,20},{5,21},{6,22},{7,23},{8,24},{9,... | collective-permute-start | bytes 786440 | tf_op jit(solution)/shard_map/ppermute | solution.py:1072
  9.3 9.0 %collective-permute-start.1 = (bf16[128,1024]{1,0:T(8,128)(2,1)S(1)}, bf16[128,1024]{1,0:T(8,128)(2,1)S(1)}, u32[]{:S(2)}, u32[]{:S(2)}) collective-permute-start(bf16[128,1024]{1,0:T(8,128)(2,1)S(1)} %get-tuple-element.236), channel_id=1, source_target_pairs={{0,16},{1,17},{2,18},{3,19},{4,20},{5,21},{6,22},{7,23},{8,24},{9,... | collective-permute-start | bytes 786440 | tf_op jit(solution)/shard_map/ppermute | solution.py:1074
  13.6 13.9 %collective-permute-start.2 = (bf16[256,512]{1,0:T(8,128)(2,1)S(1)}, bf16[256,512]{1,0:T(8,128)(2,1)S(1)}, u32[]{:S(2)}, u32[]{:S(2)}) collective-permute-start(bf16[256,512]{1,0:T(8,128)(2,1)S(1)} %get-tuple-element.255), channel_id=1, source_target_pairs={{16,0},{17,1},{18,2},{19,3},{20,4},{21,5},{22,6},{23,7},{24,8},{25... | collective-permute-start | bytes 786440 | tf_op jit(solution)/shard_map/ppermute | solution.py:1077
  19.0 11.4 %collective-permute-start.3 = (bf16[128,512]{1,0:T(8,128)(2,1)S(1)}, bf16[128,512]{1,0:T(8,128)(2,1)S(1)}, u32[]{:S(2)}, u32[]{:S(2)}) collective-permute-start(bf16[128,512]{1,0:T(8,128)(2,1)S(1)} %get-tuple-element.268), channel_id=1, source_target_pairs={{16,0},{17,1},{18,2},{19,3},{20,4},{21,5},{22,6},{23,7},{24,8},{25... | collective-permute-start | bytes 393224 | tf_op jit(solution)/shard_map/ppermute | solution.py:1077
  20.3 12.2 %collective-permute-start.4 = (bf16[128,512]{1,0:T(8,128)(2,1)S(1)}, bf16[128,512]{1,0:T(8,128)(2,1)S(1)}, u32[]{:S(2)}, u32[]{:S(2)}) collective-permute-start(bf16[128,512]{1,0:T(8,128)(2,1)S(1)} %get-tuple-element.279), channel_id=1, source_target_pairs={{16,0},{17,1},{18,2},{19,3},{20,4},{21,5},{22,6},{23,7},{24,8},{25... | collective-permute-start | bytes 393224 | tf_op jit(solution)/shard_map/ppermute | solution.py:1077
  33.3 2.7 %collective-permute-start.5 = (bf16[896,512]{1,0:T(8,128)(2,1)S(1)}, bf16[896,512]{1,0:T(8,128)(2,1)S(1)}, u32[]{:S(2)}, u32[]{:S(2)}) collective-permute-start(bf16[896,512]{1,0:T(8,128)(2,1)S(1)} %get-tuple-element.300), channel_id=1, source_target_pairs={{0,1},{1,0},{2,3},{3,2},{4,5},{5,4},{6,7},{7,6},{8,9},{9,8},{10,11... | collective-permute-start | bytes 2752520 | tf_op jit(solution)/shard_map/ppermute | solution.py:895
  35.4 3.4 %collective-permute-start.6 = (bf16[896,512]{1,0:T(8,128)(2,1)S(1)}, bf16[896,512]{1,0:T(8,128)(2,1)S(1)}, u32[]{:S(2)}, u32[]{:S(2)}) collective-permute-start(bf16[896,512]{1,0:T(8,128)(2,1)S(1)} %get-tuple-element.306), channel_id=1, source_target_pairs={{0,1},{1,0},{2,3},{3,2},{4,5},{5,4},{6,7},{7,6},{8,9},{9,8},{10,11... | collective-permute-start | bytes 2752520 | tf_op jit(solution)/shard_map/ppermute | solution.py:895
  36.5 8.5 %collective-permute-start.7 = (bf16[448,512]{1,0:T(8,128)(2,1)S(1)}, bf16[448,512]{1,0:T(8,128)(2,1)S(1)}, u32[]{:S(2)}, u32[]{:S(2)}) collective-permute-start(bf16[448,512]{1,0:T(8,128)(2,1)S(1)} %get-tuple-element.317), channel_id=1, source_target_pairs={{0,2},{1,5},{2,0},{3,7},{4,6},{5,1},{6,4},{7,3},{8,10},{9,13},{10,... | collective-permute-start | bytes 1376264 | tf_op jit(solution)/shard_map/ppermute | solution.py:895
  39.4 13.1 %collective-permute-start.9 = (bf16[448,512]{1,0:T(8,128)(2,1)S(1)}, bf16[448,512]{1,0:T(8,128)(2,1)S(1)}, u32[]{:S(2)}, u32[]{:S(2)}) collective-permute-start(bf16[448,512]{1,0:T(8,128)(2,1)S(1)} %get-tuple-element.322), channel_id=1, source_target_pairs={{0,2},{1,5},{2,0},{3,7},{4,6},{5,1},{6,4},{7,3},{8,10},{9,13},{10,... | collective-permute-start | bytes 1376264 | tf_op jit(solution)/shard_map/ppermute | solution.py:895
  40.4 6.6 %collective-permute-start.8 = (bf16[896,512]{1,0:T(8,128)(2,1)S(1)}, bf16[896,512]{1,0:T(8,128)(2,1)S(1)}, u32[]{:S(2)}, u32[]{:S(2)}) collective-permute-start(bf16[896,512]{1,0:T(8,128)(2,1)S(1)} %get-tuple-element.319), channel_id=1, source_target_pairs={{0,1},{1,0},{2,3},{3,2},{4,5},{5,4},{6,7},{7,6},{8,9},{9,8},{10,11... | collective-permute-start | bytes 2752520 | tf_op jit(solution)/shard_map/ppermute | solution.py:895
  43.8 8.8 %collective-permute-start.10 = (bf16[896,512]{1,0:T(8,128)(2,1)S(1)}, bf16[896,512]{1,0:T(8,128)(2,1)S(1)}, u32[]{:S(2)}, u32[]{:S(2)}) collective-permute-start(bf16[896,512]{1,0:T(8,128)(2,1)S(1)} %get-tuple-element.324), channel_id=1, source_target_pairs={{0,1},{1,0},{2,3},{3,2},{4,5},{5,4},{6,7},{7,6},{8,9},{9,8},{10,11... | collective-permute-start | bytes 2752520 | tf_op jit(solution)/shard_map/ppermute | solution.py:895
  44.2 8.4 %collective-permute-start.11 = (bf16[896,512]{1,0:T(8,128)(2,1)S(1)}, bf16[896,512]{1,0:T(8,128)(2,1)S(1)}, u32[]{:S(2)}, u32[]{:S(2)}) collective-permute-start(bf16[896,512]{1,0:T(8,128)(2,1)S(1)} %get-tuple-element.325), channel_id=1, source_target_pairs={{0,1},{1,0},{2,3},{3,2},{4,5},{5,4},{6,7},{7,6},{8,9},{9,8},{10,11... | collective-permute-start | bytes 2752520 | tf_op jit(solution)/shard_map/ppermute | solution.py:895
  45.2 10.2 %collective-permute-start.12 = (bf16[224,512]{1,0:T(8,128)(2,1)S(1)}, bf16[224,512]{1,0:T(8,128)(2,1)S(1)}, u32[]{:S(2)}, u32[]{:S(2)}) collective-permute-start(bf16[224,512]{1,0:T(8,128)(2,1)S(1)} %get-tuple-element.330), channel_id=1, source_target_pairs={{0,4},{1,3},{2,6},{3,1},{4,0},{5,7},{6,2},{7,5},{8,12},{9,11},{10,... | collective-permute-start | bytes 688136 | tf_op jit(solution)/shard_map/ppermute | solution.py:895
  47.6 14.1 %collective-permute-start.13 = (bf16[448,512]{1,0:T(8,128)(2,1)S(1)}, bf16[448,512]{1,0:T(8,128)(2,1)S(1)}, u32[]{:S(2)}, u32[]{:S(2)}) collective-permute-start(bf16[448,512]{1,0:T(8,128)(2,1)S(1)} %get-tuple-element.333), channel_id=1, source_target_pairs={{0,2},{1,5},{2,0},{3,7},{4,6},{5,1},{6,4},{7,3},{8,10},{9,13},{10,... | collective-permute-start | bytes 1376264 | tf_op jit(solution)/shard_map/ppermute | solution.py:895
  53.3 20.2 %collective-permute-start.15 = (bf16[448,512]{1,0:T(8,128)(2,1)S(1)}, bf16[448,512]{1,0:T(8,128)(2,1)S(1)}, u32[]{:S(2)}, u32[]{:S(2)}) collective-permute-start(bf16[448,512]{1,0:T(8,128)(2,1)S(1)} %get-tuple-element.339), channel_id=1, source_target_pairs={{0,4},{1,3},{2,6},{3,1},{4,0},{5,7},{6,2},{7,5},{8,12},{9,11},{10,... | collective-permute-start | bytes 1376264 | tf_op jit(solution)/shard_map/ppermute | solution.py:895
  55.2 13.6 %collective-permute-start.14 = (bf16[224,512]{1,0:T(8,128)(2,1)S(1)}, bf16[224,512]{1,0:T(8,128)(2,1)S(1)}, u32[]{:S(2)}, u32[]{:S(2)}) collective-permute-start(bf16[224,512]{1,0:T(8,128)(2,1)S(1)} %get-tuple-element.336), channel_id=1, source_target_pairs={{0,4},{1,3},{2,6},{3,1},{4,0},{5,7},{6,2},{7,5},{8,12},{9,11},{10,... | collective-permute-start | bytes 688136 | tf_op jit(solution)/shard_map/ppermute | solution.py:895
  55.5 18.1 %collective-permute-start.16 = (bf16[224,512]{1,0:T(8,128)(2,1)S(1)}, bf16[224,512]{1,0:T(8,128)(2,1)S(1)}, u32[]{:S(2)}, u32[]{:S(2)}) collective-permute-start(bf16[224,512]{1,0:T(8,128)(2,1)S(1)} %get-tuple-element.341.refs_0_), channel_id=1, source_target_pairs={{0,8},{1,9},{2,10},{3,11},{4,12},{5,13},{6,14},{7,15},{8,0},{9,1},... | collective-permute-start | bytes 688136 | tf_op jit(solution)/shard_map/ppermute | solution.py:895
  68.8 15.2 %collective-permute-start.18 = (bf16[224,512]{1,0:T(8,128)(2,1)S(1)}, bf16[224,512]{1,0:T(8,128)(2,1)S(1)}, u32[]{:S(2)}, u32[]{:S(2)}) collective-permute-start(bf16[224,512]{1,0:T(8,128)(2,1)S(1)} %get-tuple-element.353.refs_0_), channel_id=1, source_target_pairs={{0,8},{1,9},{2,10},{3,11},{4,12},{5,13},{6,14},{7,15},{8,0},{9,1},... | collective-permute-start | bytes 688136 | tf_op jit(solution)/shard_map/ppermute | solution.py:895
  71.1 9.7 %collective-permute-start.17 = (bf16[224,512]{1,0:T(8,128)(2,1)S(1)}, bf16[224,512]{1,0:T(8,128)(2,1)S(1)}, u32[]{:S(2)}, u32[]{:S(2)}) collective-permute-start(bf16[224,512]{1,0:T(8,128)(2,1)S(1)} %get-tuple-element.351), channel_id=1, source_target_pairs={{0,4},{1,3},{2,6},{3,1},{4,0},{5,7},{6,2},{7,5},{8,12},{9,11},{10,... | collective-permute-start | bytes 688136 | tf_op jit(solution)/shard_map/ppermute | solution.py:895
  73.7 16.0 %collective-permute-start.20 = (bf16[224,512]{1,0:T(8,128)(2,1)S(1)}, bf16[224,512]{1,0:T(8,128)(2,1)S(1)}, u32[]{:S(2)}, u32[]{:S(2)}) collective-permute-start(bf16[224,512]{1,0:T(8,128)(2,1)S(1)} %get-tuple-element.358.refs_0_), channel_id=1, source_target_pairs={{0,4},{1,3},{2,6},{3,1},{4,0},{5,7},{6,2},{7,5},{8,12},{9,11},{10,... | collective-permute-start | bytes 688136 | tf_op jit(solution)/shard_map/ppermute | solution.py:895
  73.8 10.3 %collective-permute-start.19 = (bf16[224,512]{1,0:T(8,128)(2,1)S(1)}, bf16[224,512]{1,0:T(8,128)(2,1)S(1)}, u32[]{:S(2)}, u32[]{:S(2)}) collective-permute-start(bf16[224,512]{1,0:T(8,128)(2,1)S(1)} %get-tuple-element.356), channel_id=1, source_target_pairs={{0,2},{1,5},{2,0},{3,7},{4,6},{5,1},{6,4},{7,3},{8,10},{9,13},{10,... | collective-permute-start | bytes 688136 | tf_op jit(solution)/shard_map/ppermute | solution.py:895
  80.8 12.8 %collective-permute-start.21 = (bf16[224,512]{1,0:T(8,128)(2,1)S(1)}, bf16[224,512]{1,0:T(8,128)(2,1)S(1)}, u32[]{:S(2)}, u32[]{:S(2)}) collective-permute-start(bf16[224,512]{1,0:T(8,128)(2,1)S(1)} %get-tuple-element.360.refs_0_), channel_id=1, source_target_pairs={{0,8},{1,9},{2,10},{3,11},{4,12},{5,13},{6,14},{7,15},{8,0},{9,1},... | collective-permute-start | bytes 688136 | tf_op jit(solution)/shard_map/ppermute | solution.py:895
  89.7 15.0 %collective-permute-start.24 = (bf16[448,512]{1,0:T(8,128)(2,1)S(1)}, bf16[448,512]{1,0:T(8,128)(2,1)S(1)}, u32[]{:S(2)}, u32[]{:S(2)}) collective-permute-start(bf16[448,512]{1,0:T(8,128)(2,1)S(1)} %get-tuple-element.366.refs_0_), channel_id=1, source_target_pairs={{0,2},{1,5},{2,0},{3,7},{4,6},{5,1},{6,4},{7,3},{8,10},{9,13},{10,... | collective-permute-start | bytes 1376264 | tf_op jit(solution)/shard_map/ppermute | solution.py:895
  91.5 11.0 %collective-permute-start.22 = (bf16[224,512]{1,0:T(8,128)(2,1)S(1)}, bf16[224,512]{1,0:T(8,128)(2,1)S(1)}, u32[]{:S(2)}, u32[]{:S(2)}) collective-permute-start(bf16[224,512]{1,0:T(8,128)(2,1)S(1)} %get-tuple-element.362.refs_0_), channel_id=1, source_target_pairs={{0,4},{1,3},{2,6},{3,1},{4,0},{5,7},{6,2},{7,5},{8,12},{9,11},{10,... | collective-permute-start | bytes 688136 | tf_op jit(solution)/shard_map/ppermute | solution.py:895
  91.5 11.0 %collective-permute-start.23 = (bf16[224,512]{1,0:T(8,128)(2,1)S(1)}, bf16[224,512]{1,0:T(8,128)(2,1)S(1)}, u32[]{:S(2)}, u32[]{:S(2)}) collective-permute-start(bf16[224,512]{1,0:T(8,128)(2,1)S(1)} %get-tuple-element.364.refs_0_), channel_id=1, source_target_pairs={{0,8},{1,9},{2,10},{3,11},{4,12},{5,13},{6,14},{7,15},{8,0},{9,1},... | collective-permute-start | bytes 688136 | tf_op jit(solution)/shard_map/ppermute | solution.py:895
  93.7 13.7 %collective-permute-start.25 = (bf16[224,512]{1,0:T(8,128)(2,1)S(1)}, bf16[224,512]{1,0:T(8,128)(2,1)S(1)}, u32[]{:S(2)}, u32[]{:S(2)}) collective-permute-start(bf16[224,512]{1,0:T(8,128)(2,1)S(1)} %get-tuple-element.368.refs_0_), channel_id=1, source_target_pairs={{0,4},{1,3},{2,6},{3,1},{4,0},{5,7},{6,2},{7,5},{8,12},{9,11},{10,... | collective-permute-start | bytes 688136 | tf_op jit(solution)/shard_map/ppermute | solution.py:895
  102.6 12.5 %collective-permute-start.27 = (bf16[224,512]{1,0:T(8,128)(2,1)S(1)}, bf16[224,512]{1,0:T(8,128)(2,1)S(1)}, u32[]{:S(2)}, u32[]{:S(2)}) collective-permute-start(bf16[224,512]{1,0:T(8,128)(2,1)S(1)} %get-tuple-element.377.refs_0_), channel_id=1, source_target_pairs={{0,2},{1,5},{2,0},{3,7},{4,6},{5,1},{6,4},{7,3},{8,10},{9,13},{10,... | collective-permute-start | bytes 688136 | tf_op jit(solution)/shard_map/ppermute | solution.py:895
  102.9 10.6 %collective-permute-start.26 = (bf16[448,512]{1,0:T(8,128)(2,1)S(1)}, bf16[448,512]{1,0:T(8,128)(2,1)S(1)}, u32[]{:S(2)}, u32[]{:S(2)}) collective-permute-start(bf16[448,512]{1,0:T(8,128)(2,1)S(1)} %get-tuple-element.372.refs_0_), channel_id=1, source_target_pairs={{0,2},{1,5},{2,0},{3,7},{4,6},{5,1},{6,4},{7,3},{8,10},{9,13},{10,... | collective-permute-start | bytes 1376264 | tf_op jit(solution)/shard_map/ppermute | solution.py:895
  107.4 11.3 %collective-permute-start.29 = (bf16[448,512]{1,0:T(8,128)(2,1)S(1)}, bf16[448,512]{1,0:T(8,128)(2,1)S(1)}, u32[]{:S(2)}, u32[]{:S(2)}) collective-permute-start(bf16[448,512]{1,0:T(8,128)(2,1)S(1)} %get-tuple-element.381.refs_0_), channel_id=1, source_target_pairs={{0,2},{1,5},{2,0},{3,7},{4,6},{5,1},{6,4},{7,3},{8,10},{9,13},{10,... | collective-permute-start | bytes 1376264 | tf_op jit(solution)/shard_map/ppermute | solution.py:895
  107.8 7.4 %collective-permute-start.28 = (bf16[896,512]{1,0:T(8,128)(2,1)S(1)}, bf16[896,512]{1,0:T(8,128)(2,1)S(1)}, u32[]{:S(2)}, u32[]{:S(2)}) collective-permute-start(bf16[896,512]{1,0:T(8,128)(2,1)S(1)} %get-tuple-element.370.refs_0_), channel_id=1, source_target_pairs={{0,1},{1,0},{2,3},{3,2},{4,5},{5,4},{6,7},{7,6},{8,9},{9,8},{10,11... | collective-permute-start | bytes 2752520 | tf_op jit(solution)/shard_map/ppermute | solution.py:895
  113.7 5.2 %collective-permute-start.30 = (bf16[896,512]{1,0:T(8,128)(2,1)S(1)}, bf16[896,512]{1,0:T(8,128)(2,1)S(1)}, u32[]{:S(2)}, u32[]{:S(2)}) collective-permute-start(bf16[896,512]{1,0:T(8,128)(2,1)S(1)} %get-tuple-element.374.refs_0_), channel_id=1, source_target_pairs={{0,1},{1,0},{2,3},{3,2},{4,5},{5,4},{6,7},{7,6},{8,9},{9,8},{10,11... | collective-permute-start | bytes 2752520 | tf_op jit(solution)/shard_map/ppermute | solution.py:895
  115.1 8.5 %collective-permute-start.31 = (bf16[448,512]{1,0:T(8,128)(2,1)S(1)}, bf16[448,512]{1,0:T(8,128)(2,1)S(1)}, u32[]{:S(2)}, u32[]{:S(2)}) collective-permute-start(bf16[448,512]{1,0:T(8,128)(2,1)S(1)} %get-tuple-element.391.refs_0_), channel_id=1, source_target_pairs={{0,4},{1,3},{2,6},{3,1},{4,0},{5,7},{6,2},{7,5},{8,12},{9,11},{10,... | collective-permute-start | bytes 1376264 | tf_op jit(solution)/shard_map/ppermute | solution.py:895
  118.7 5.1 %collective-permute-start.32 = (bf16[896,512]{1,0:T(8,128)(2,1)S(1)}, bf16[896,512]{1,0:T(8,128)(2,1)S(1)}, u32[]{:S(2)}, u32[]{:S(2)}) collective-permute-start(bf16[896,512]{1,0:T(8,128)(2,1)S(1)} %get-tuple-element.388.refs_0_), channel_id=1, source_target_pairs={{0,1},{1,0},{2,3},{3,2},{4,5},{5,4},{6,7},{7,6},{8,9},{9,8},{10,11... | collective-permute-start | bytes 2752520 | tf_op jit(solution)/shard_map/ppermute | solution.py:895
  123.7 2.7 %collective-permute-start.33 = (bf16[896,512]{1,0:T(8,128)(2,1)S(1)}, bf16[896,512]{1,0:T(8,128)(2,1)S(1)}, u32[]{:S(2)}, u32[]{:S(2)}) collective-permute-start(bf16[896,512]{1,0:T(8,128)(2,1)S(1)} %get-tuple-element.395.refs_0_), channel_id=1, source_target_pairs={{0,1},{1,0},{2,3},{3,2},{4,5},{5,4},{6,7},{7,6},{8,9},{9,8},{10,11... | collective-permute-start | bytes 2752520 | tf_op jit(solution)/shard_map/ppermute | solution.py:895

commit v5 on v4

--- a/solution.py
+++ b/solution.py
@@ -952,43 +952,70 @@
                 if chunk.fine:
                     total[here, :] = total[here, :] + ref.more[here, :].astype(F32)
             own, other = self.halves(place_ref, 1, rows)
-            ref.send[...] = total[other, :].astype(LOW)
+            if chunk.fine:
+                ref.send[...], ref.more_out[...] = in_two(total[other, :])
+            else:
+                ref.send[...] = total[other, :].astype(LOW)
             ref.keep[...] = total[own, :]
 
         reads = dict(got=self.got, **self.more, **chunk.operands(self.state))
-        makes = dict(send=((rows // 2, D), LOW), keep=((rows // 2, D), F32))
+        side = ((rows // 2, D), LOW)
+        makes = dict(send=side, keep=((rows // 2, D), F32))
+        if chunk.fine:
+            makes.update(more_out=side)
         scratch = (pltpu.VMEM((rows, D), F32),)
         token, made = self.call(kernel, token, reads, makes, scratch=scratch)
         self.keep = made["keep"]
-        self.got = self.swap(made["send"], 1)
+        self.send_on(made, 1)
         return token
 
+    def send_on(self, made, level):
+        self.got = self.swap(made["send"], level)
+        self.more = {}
+        if self.chunk.fine:
+            self.more = dict(more=self.swap(made["more_out"], level))
+
     def split(self, token, rows):
+        fine = self.chunk.fine
+
         def kernel(place_ref, ref):
             own, other = self.halves(place_ref, 2, rows)
-            ref.send[...] = (ref.keep[other, :] + ref.got[other, :].astype(F32)).astype(LOW)
-            ref.kept[...] = ref.keep[own, :] + ref.got[own, :].astype(F32)
-
-        reads = dict(keep=self.keep, got=self.got)
-        makes = dict(send=((rows // 2, D), LOW), kept=((rows // 2, D), F32))
+
+            def total(part):
+                value = ref.keep[part, :] + ref.got[part, :].astype(F32)
+                return value + ref.more[part, :].astype(F32) if fine else value
+
+            if fine:
+                ref.send[...], ref.more_out[...] = in_two(total(other))
+            else:
+                ref.send[...] = total(other).astype(LOW)
+            ref.kept[...] = total(own)
+
+        side = ((rows // 2, D), LOW)
+        makes = dict(send=side, kept=((rows // 2, D), F32))
+        if fine:
+            makes.update(more_out=side)
+        reads = dict(keep=self.keep, got=self.got, **self.more)
         token, made = self.call(kernel, token, reads, makes)
         self.keep = made["kept"]
-        self.got = self.swap(made["send"], 2)
+        self.send_on(made, 2)
         return token
 
     def round_off(self, token, rows):
-        fine = False
+        fine = self.chunk.fine
 
         def kernel(place_ref, ref):
             total = ref.keep[...] + ref.got[...].astype(F32)
             if fine:
+                total = total + ref.more[...].astype(F32)
                 ref.piece[...], ref.rest[...] = in_two(total)
             else:
                 ref.piece[...] = total.astype(LOW)
 
         side = ((rows, D), LOW)
         makes = dict(piece=side, rest=side) if fine else dict(piece=side)
-        token, made = self.call(kernel, token, dict(keep=self.keep, got=self.got), makes)
+        reads = dict(keep=self.keep, got=self.got, **self.more)
+        token, made = self.call(kernel, token, reads, makes)
         self.spread(made, 3)
         return token
 
@@ -1000,7 +1027,7 @@
             self.more = dict(rest=made["rest"], more=self.swap(made["rest"], level))
 
     def pair_sum(self, token, rows, level, last):
-        fine = False
+        fine = self.chunk.fine
 
         def kernel(place_ref, ref):
             own, other = ref.held[...].astype(F32), ref.got[...].astype(F32)

time: 129 us -> 146 us (1.13)
  waiting for transfers between devices: 57 us -> 73.6 us
    ppermute x29 -> x32, waiting for transfers between devices: 44 us -> 60.6 us  [swap(): lax.ppermute(value, 'dp', [(i, partner(i)) for i in range(self.count)])]
    ppermute x29 -> x32, starting transfers between devices: 28.8 us -> 29.2 us  [swap(): lax.ppermute(value, 'dp', [(i, partner(i)) for i in range(self.count)])]
  transfers between devices with their start and end apart: 34 -> 37, of which waited for: 16 -> 18; matrix products, arithmetic and copies ran while one was open for 0% -> 0% of each run, Pallas kernels for 21% -> 19%
where the time goes in v5:
time: 146 us
  waiting for transfers between devices  73.6 us (50%)
  starting transfers between devices  36.9 us (25%)
  Pallas kernels  34 us (23%)
    ppermute x32, waiting for transfers between devices, swap(): lax.ppermute(value, 'dp', [(i, partner(i)) for i in range(self.count)])  60.6 us
    ppermute x32, starting transfers between devices, swap(): lax.ppermute(value, 'dp', [(i, partner(i)) for i in range(self.count)])  29.2 us
    pallas_call x42, Pallas kernels, call(): pl.pallas_call(body, out_shape=out_shape, in_specs=[in_smem()] + [in_vmem...  26.6 us
    ppermute x3, waiting for transfers between devices, to_encoder(): return lax.ppermute(side, 'section', [(1, 0)])  8.33 us
    pallas_call x1, Pallas kernels, first_stage(): pl.pallas_call(body, out_shape=shaped(makes) + [pltpu.SMEM((PLACE,), jnp....  4.37 us
    ppermute x3, starting transfers between devices, to_encoder(): return lax.ppermute(side, 'section', [(1, 0)])  3.88 us
    ppermute x1, waiting for transfers between devices, on_device(): links.append(lax.ppermute(link, 'section', [(0, 1)]))  3.5 us
    pallas_call x1, Pallas kernels, second_stage(): pl.pallas_call(body, out_shape=same_shape(keeps) + [pltpu.VMEM((ROWS, 2 *...  3.01 us
  transfers between devices with their start and end apart: 37, of which 18 were waited for; matrix products, arithmetic and copies ran while one was open for 0% of the time, Pallas kernels for 19%

profile of v5, /device:TPU:0, one launch (start us, length us, event | category | flops | bytes accessed | tf_op | source)
XLA Modules:
  0.0 145.7 jit_solution(1464452933595945097)
XLA Ops:
  0.6 4.4 %first_stage.1 = (bf16[512,1536]{1,0:T(8,128)(2,1)S(1)}, bf16[512,512]{1,0:T(8,128)(2,1)S(1)}, bf16[512,1024]{1,0:T(8,128)(2,1)S(1)}, bf16[512,2048]{1,0:T(8,128...) custom-call(s32[2,2,16]{2,1,0:T(2,128)} %refs_0_.3, ...), custom_call_target="tpu_custom_call" | custom-call | flops 939524096 | bytes 10000000 | tf_op jit(solution)/shard_map/first_stage/pallas_call | solution.py:395
  5.0 1.3 collective-permute-start
  6.3 3.0 %second_stage.1 = (bf16[512,1536]{1,0:T(8,128)(2,1)S(1)}, bf16[512,512]{1,0:T(8,128)(2,1)S(1)}, bf16[512,1024]{1,0:T(8,128)(2,1)S(1)}, bf16[512,2048]{1,0:T(8,12...) custom-call(s32[4]{0:T(128)S(4)} %get-tuple-element.209.place_ref, ...), custom_call_target="tpu_custom_call", output_to_operand_aliasing={{0}: (9, {}), {1}: (10, {}), {2}: (11, {}), {3}: (12, {}), ... | custom-call | flops 939524096 | bytes 10000000 | tf_op jit(solution)/shard_map/second_stage/pallas_call | solution.py:450
  9.3 2.5 %collective-permute-start.1 = (bf16[128,1024]{1,0:T(8,128)(2,1)S(1)}, bf16[128,1024]{1,0:T(8,128)(2,1)S(1)}, u32[]{:S(2)}, u32[]{:S(2)}) collective-permute-start(bf16[128,1024]{1,0:T(8,128)(2,1)S(1)} %get-tuple-element.239), channel_id=1, source_target_pairs={{0,16},{1,17},{2,18},{3,19},{4,20},{5,21},{6,22},{7,23},{8,24},{9,... | collective-permute-start | bytes 786440 | tf_op jit(solution)/shard_map/ppermute | solution.py:1101
  11.8 1.2 collective-permute-done.refs_6_
  13.0 0.6 middle_stage.2
  13.6 1.3 collective-permute-start.2
  14.9 3.5 %collective-permute-done.1.refs_6_.refs_1_ = bf16[128,1024]{1,0:T(8,128)(2,1)S(1)} collective-permute-done((bf16[128,1024]{1,0:T(8,128)(2,1)S(1)}, bf16[128,1024]{1,0:T(8,128)(2,1)S(1)}, u32[]{:S(2)}, u32[]{:S(2)}) %collective-permute-start.1) | collective-permute-done | bytes 262176 | tf_op jit(solution)/shard_map/ppermute | solution.py:1101
  18.4 0.6 middle_stage.3
  19.0 1.3 collective-permute-start.3
  20.3 1.3 collective-permute-start.4
  21.6 5.9 %collective-permute-done.2.refs_6_ = bf16[256,512]{1,0:T(8,128)(2,1)S(1)} collective-permute-done((bf16[256,512]{1,0:T(8,128)(2,1)S(1)}, bf16[256,512]{1,0:T(8,128)(2,1)S(1)}, u32[]{:S(2)}, u32[]{:S(2)}) %collective-permute-start.2) | collective-permute-done | bytes 262176 | tf_op jit(solution)/shard_map/ppermute | solution.py:1104
  27.5 2.3 %back_stage.4 = (f32[256,2048]{1,0:T(8,128)S(1)}, f32[256,512]{1,0:T(8,128)S(1)}, bf16[256,512]{1,0:T(8,128)(2,1)S(1)}, bf16[256,1024]{1,0:T(8,128)(2,1)S(1)}, b...) custom-call(s32[4]{0:T(128)S(4)} %get-tuple-element.209.place_ref, ...), custom_call_target="tpu_custom_call", output_to_operand_aliasing={{0}: (11, {}), {1}: (12, {}), {2}: (13, {}), {3}: (14, {}),... | custom-call | flops 900000000 | tf_op jit(solution)/shard_map/back_stage/pallas_call | solution.py:239
  29.8 0.5 collective-permute-done.3.refs_6_
  30.6 1.9 %collective-permute-done.4.refs_6_ = bf16[128,512]{1,0:T(8,128)(2,1)S(1)} collective-permute-done((bf16[128,512]{1,0:T(8,128)(2,1)S(1)}, bf16[128,512]{1,0:T(8,128)(2,1)S(1)}, u32[]{:S(2)}, u32[]{:S(2)}) %collective-permute-start.4) | collective-permute-done | bytes 131104 | tf_op jit(solution)/shard_map/ppermute | solution.py:1104
  32.5 0.8 back_stage.6
  33.3 2.1 %back_stage.7 = (f32[256,2048]{1,0:T(8,128)S(1)}, f32[256,512]{1,0:T(8,128)S(1)}, bf16[256,512]{1,0:T(8,128)(2,1)S(1)}, bf16[256,1024]{1,0:T(8,128)(2,1)S(1)}, b...) custom-call(s32[4]{0:T(128)S(4)} %get-tuple-element.209.place_ref, ...), custom_call_target="tpu_custom_call", output_to_operand_aliasing={{0}: (11, {}), {1}: (12, {}), {2}: (13, {}), {3}: (14, {}),... | custom-call | flops 1000000000 | tf_op jit(solution)/shard_map/back_stage/pallas_call | solution.py:239
  35.4 0.5 collective-permute-start.6
  36.0 0.6 sum_0.4
  36.5 1.8 %collective-permute-start.7 = (bf16[448,512]{1,0:T(8,128)(2,1)S(1)}, bf16[448,512]{1,0:T(8,128)(2,1)S(1)}, u32[]{:S(2)}, u32[]{:S(2)}) collective-permute-start(bf16[448,512]{1,0:T(8,128)(2,1)S(1)} %get-tuple-element.320), channel_id=1, source_target_pairs={{0,2},{1,5},{2,0},{3,7},{4,6},{5,1},{6,4},{7,3},{8,10},{9,13},{10,... | collective-permute-start | bytes 1376264 | tf_op jit(solution)/shard_map/ppermute | solution.py:895
  38.3 0.5 product.1
  38.8 0.6 sum_0.5
  39.4 1.1 collective-permute-start.9
  40.6 3.2 %late_stage.1 = (bf16[256,1536]{1,0:T(8,128)(2,1)S(1)}, bf16[256,1536]{1,0:T(8,128)(2,1)S(1)}, bf16[896,512]{1,0:T(8,128)(2,1)S(1)}, bf16[896,512]{1,0:T(8,128)(2,1)S(1)}, f32[8,128]{1,0:T(8,128)S(1)}) custom-call(s32[4]{0:T(128)S(4)} %get-tuple-element.209.place_ref, f32[8,128]{1,0:T(8,128)S(1)} %get-tuple-element.313.token_in, ...), custom_call_target="tpu_custom_call" | custom-call | flops 8000000000 | tf_op jit(solution)/shard_map/late_stage/pallas_call | solution.py:239
  43.8 0.4 collective-permute-start.10
  44.3 0.7 collective-permute-done.7.refs_1_
  45.2 1.9 %collective-permute-start.12 = (bf16[224,512]{1,0:T(8,128)(2,1)S(1)}, bf16[224,512]{1,0:T(8,128)(2,1)S(1)}, u32[]{:S(2)}, u32[]{:S(2)}) collective-permute-start(bf16[224,512]{1,0:T(8,128)(2,1)S(1)} %get-tuple-element.333), channel_id=1, source_target_pairs={{0,4},{1,3},{2,6},{3,1},{4,0},{5,7},{6,2},{7,5},{8,12},{9,11},{10,... | collective-permute-start | bytes 688136 | tf_op jit(solution)/shard_map/ppermute | solution.py:895
  47.1 0.5 sum_0.6
  47.6 1.6 %collective-permute-start.13 = (bf16[448,512]{1,0:T(8,128)(2,1)S(1)}, bf16[448,512]{1,0:T(8,128)(2,1)S(1)}, u32[]{:S(2)}, u32[]{:S(2)}) collective-permute-start(bf16[448,512]{1,0:T(8,128)(2,1)S(1)} %get-tuple-element.336), channel_id=1, source_target_pairs={{0,2},{1,5},{2,0},{3,7},{4,6},{5,1},{6,4},{7,3},{8,10},{9,13},{10,... | collective-permute-start | bytes 1376264 | tf_op jit(solution)/shard_map/ppermute | solution.py:895
  49.2 3.3 %collective-permute-done.9.refs_1_ = bf16[448,512]{1,0:T(8,128)(2,1)S(1)} collective-permute-done((bf16[448,512]{1,0:T(8,128)(2,1)S(1)}, bf16[448,512]{1,0:T(8,128)(2,1)S(1)}, u32[]{:S(2)}, u32[]{:S(2)}) %collective-permute-start.9) | collective-permute-done | bytes 458784 | tf_op jit(solution)/shard_map/ppermute | solution.py:895
  52.6 0.9 sum_0.7
  53.5 1.9 %collective-permute-start.15 = (bf16[448,512]{1,0:T(8,128)(2,1)S(1)}, bf16[448,512]{1,0:T(8,128)(2,1)S(1)}, u32[]{:S(2)}, u32[]{:S(2)}) collective-permute-start(bf16[448,512]{1,0:T(8,128)(2,1)S(1)} %get-tuple-element.342), channel_id=1, source_target_pairs={{0,4},{1,3},{2,6},{3,1},{4,0},{5,7},{6,2},{7,5},{8,12},{9,11},{10,... | collective-permute-start | bytes 1376264 | tf_op jit(solution)/shard_map/ppermute | solution.py:895
  55.6 1.8 %collective-permute-start.14 = (bf16[224,512]{1,0:T(8,128)(2,1)S(1)}, bf16[224,512]{1,0:T(8,128)(2,1)S(1)}, u32[]{:S(2)}, u32[]{:S(2)}) collective-permute-start(bf16[224,512]{1,0:T(8,128)(2,1)S(1)} %get-tuple-element.339), channel_id=1, source_target_pairs={{0,4},{1,3},{2,6},{3,1},{4,0},{5,7},{6,2},{7,5},{8,12},{9,11},{10,... | collective-permute-start | bytes 688136 | tf_op jit(solution)/shard_map/ppermute | solution.py:895
  57.5 2.7 %collective-permute-start.17 = (bf16[224,512]{1,0:T(8,128)(2,1)S(1)}, bf16[224,512]{1,0:T(8,128)(2,1)S(1)}, u32[]{:S(2)}, u32[]{:S(2)}) collective-permute-start(bf16[224,512]{1,0:T(8,128)(2,1)S(1)} %get-tuple-element.345.refs_0_), channel_id=1, source_target_pairs={{0,8},{1,9},{2,10},{3,11},{4,12},{5,13},{6,14},{7,15},{8,0},{9,1},... | collective-permute-start | bytes 688136 | tf_op jit(solution)/shard_map/ppermute | solution.py:895
  60.1 1.4 collective-permute-done.13.refs_1_
  61.6 12.7 %collective-permute-done.14.refs_1_ = bf16[224,512]{1,0:T(8,128)(2,1)S(1)} collective-permute-done((bf16[224,512]{1,0:T(8,128)(2,1)S(1)}, bf16[224,512]{1,0:T(8,128)(2,1)S(1)}, u32[]{:S(2)}, u32[]{:S(2)}) %collective-permute-start.14) | collective-permute-done | bytes 229408 | tf_op jit(solution)/shard_map/ppermute | solution.py:895
  74.3 2.1 %collective-permute-start.19 = (bf16[224,512]{1,0:T(8,128)(2,1)S(1)}, bf16[224,512]{1,0:T(8,128)(2,1)S(1)}, u32[]{:S(2)}, u32[]{:S(2)}) collective-permute-start(bf16[224,512]{1,0:T(8,128)(2,1)S(1)} %get-tuple-element.357.refs_0_), channel_id=1, source_target_pairs={{0,8},{1,9},{2,10},{3,11},{4,12},{5,13},{6,14},{7,15},{8,0},{9,1},... | collective-permute-start | bytes 688136 | tf_op jit(solution)/shard_map/ppermute | solution.py:895
  76.4 2.5 %collective-permute-start.18 = (bf16[224,512]{1,0:T(8,128)(2,1)S(1)}, bf16[224,512]{1,0:T(8,128)(2,1)S(1)}, u32[]{:S(2)}, u32[]{:S(2)}) collective-permute-start(bf16[224,512]{1,0:T(8,128)(2,1)S(1)} %get-tuple-element.355), channel_id=1, source_target_pairs={{0,4},{1,3},{2,6},{3,1},{4,0},{5,7},{6,2},{7,5},{8,12},{9,11},{10,... | collective-permute-start | bytes 688136 | tf_op jit(solution)/shard_map/ppermute | solution.py:895
  79.2 1.2 collective-permute-start.20
  80.4 0.9 collective-permute-start.21
  81.3 1.3 final_stage.1
  82.6 8.4 %collective-permute-done.18.refs_1_ = bf16[224,512]{1,0:T(8,128)(2,1)S(1)} collective-permute-done((bf16[224,512]{1,0:T(8,128)(2,1)S(1)}, bf16[224,512]{1,0:T(8,128)(2,1)S(1)}, u32[]{:S(2)}, u32[]{:S(2)}) %collective-permute-start.18) | collective-permute-done | bytes 229408 | tf_op jit(solution)/shard_map/ppermute | solution.py:895
  91.4 2.6 %collective-permute-done.22.refs_1_ = bf16[224,512]{1,0:T(8,128)(2,1)S(1)} collective-permute-done((bf16[224,512]{1,0:T(8,128)(2,1)S(1)}, bf16[224,512]{1,0:T(8,128)(2,1)S(1)}, u32[]{:S(2)}, u32[]{:S(2)}) %collective-permute-start.22) | collective-permute-done | bytes 229408 | tf_op jit(solution)/shard_map/ppermute | solution.py:895
  94.0 1.5 %collective-permute-start.27 = (bf16[448,512]{1,0:T(8,128)(2,1)S(1)}, bf16[448,512]{1,0:T(8,128)(2,1)S(1)}, u32[]{:S(2)}, u32[]{:S(2)}) collective-permute-start(bf16[448,512]{1,0:T(8,128)(2,1)S(1)} %get-tuple-element.372.refs_0_), channel_id=1, source_target_pairs={{0,2},{1,5},{2,0},{3,7},{4,6},{5,1},{6,4},{7,3},{8,10},{9,13},{10,... | collective-permute-start | bytes 1376264 | tf_op jit(solution)/shard_map/ppermute | solution.py:895
  95.6 2.0 %collective-permute-start.25 = (bf16[224,512]{1,0:T(8,128)(2,1)S(1)}, bf16[224,512]{1,0:T(8,128)(2,1)S(1)}, u32[]{:S(2)}, u32[]{:S(2)}) collective-permute-start(bf16[224,512]{1,0:T(8,128)(2,1)S(1)} %get-tuple-element.369.refs_0_), channel_id=1, source_target_pairs={{0,8},{1,9},{2,10},{3,11},{4,12},{5,13},{6,14},{7,15},{8,0},{9,1},... | collective-permute-start | bytes 688136 | tf_op jit(solution)/shard_map/ppermute | solution.py:895
  97.6 0.9 collective-permute-start.26
  98.5 3.2 %collective-permute-done.23.refs_1_ = bf16[224,512]{1,0:T(8,128)(2,1)S(1)} collective-permute-done((bf16[224,512]{1,0:T(8,128)(2,1)S(1)}, bf16[224,512]{1,0:T(8,128)(2,1)S(1)}, u32[]{:S(2)}, u32[]{:S(2)}) %collective-permute-start.23) | collective-permute-done | bytes 229408 | tf_op jit(solution)/shard_map/ppermute | solution.py:895
  101.9 7.1 %collective-permute-done.24.refs_1_ = bf16[224,512]{1,0:T(8,128)(2,1)S(1)} collective-permute-done((bf16[224,512]{1,0:T(8,128)(2,1)S(1)}, bf16[224,512]{1,0:T(8,128)(2,1)S(1)}, u32[]{:S(2)}, u32[]{:S(2)}) %collective-permute-start.24) | collective-permute-done | bytes 229408 | tf_op jit(solution)/shard_map/ppermute | solution.py:895
  109.1 7.4 %collective-permute-done.25.refs_1_ = bf16[224,512]{1,0:T(8,128)(2,1)S(1)} collective-permute-done((bf16[224,512]{1,0:T(8,128)(2,1)S(1)}, bf16[224,512]{1,0:T(8,128)(2,1)S(1)}, u32[]{:S(2)}, u32[]{:S(2)}) %collective-permute-start.25) | collective-permute-done | bytes 229408 | tf_op jit(solution)/shard_map/ppermute | solution.py:895
  116.4 3.3 %collective-permute-done.26.refs_3_ = bf16[224,512]{1,0:T(8,128)(2,1)S(1)} collective-permute-done((bf16[224,512]{1,0:T(8,128)(2,1)S(1)}, bf16[224,512]{1,0:T(8,128)(2,1)S(1)}, u32[]{:S(2)}, u32[]{:S(2)}) %collective-permute-start.26) | collective-permute-done | bytes 229408 | tf_op jit(solution)/shard_map/ppermute | solution.py:895
  119.8 1.4 collective-permute-start.30
  121.2 0.7 collective-permute-start.29
  122.1 1.4 collective-permute-start.32
  123.5 1.3 unpack_1.4
  124.8 6.1 %collective-permute-done.29.refs_1_ = bf16[448,512]{1,0:T(8,128)(2,1)S(1)} collective-permute-done((bf16[448,512]{1,0:T(8,128)(2,1)S(1)}, bf16[448,512]{1,0:T(8,128)(2,1)S(1)}, u32[]{:S(2)}, u32[]{:S(2)}) %collective-permute-start.29) | collective-permute-done | bytes 458784 | tf_op jit(solution)/shard_map/ppermute | solution.py:895
  131.0 1.3 unpack_1.5
  132.5 1.3 unpack_0.4
  133.8 2.2 %collective-permute-done.32.refs_1_ = bf16[448,512]{1,0:T(8,128)(2,1)S(1)} collective-permute-done((bf16[448,512]{1,0:T(8,128)(2,1)S(1)}, bf16[448,512]{1,0:T(8,128)(2,1)S(1)}, u32[]{:S(2)}, u32[]{:S(2)}) %collective-permute-start.32) | collective-permute-done | bytes 458784 | tf_op jit(solution)/shard_map/ppermute | solution.py:895
  136.1 1.3 unpack_0.5
  137.4 1.3 unpack_1.6
  138.7 2.2 %collective-permute-done.34.refs_1_ = bf16[448,512]{1,0:T(8,128)(2,1)S(1)} collective-permute-done((bf16[448,512]{1,0:T(8,128)(2,1)S(1)}, bf16[448,512]{1,0:T(8,128)(2,1)S(1)}, u32[]{:S(2)}, u32[]{:S(2)}) %collective-permute-start.34) | collective-permute-done | bytes 458784 | tf_op jit(solution)/shard_map/ppermute | solution.py:895
  141.1 1.3 unpack_0.6
  142.4 1.3 unpack_1.7
  143.7 1.9 %unpack_0.7 = (f32[8,128]{1,0:T(8,128)}, f32[1,512,1536]{2,1,0:T(8,128)}, f32[1,512,512]{2,1,0:T(8,128)}) custom-call(s32[4]{0:T(128)S(4)} %get-tuple-element.209.place_ref, f32[8,128]{1,0:T(8,128)S(1)} %get-tuple-element.403.token_in, bf16[896,512]{1,0:T(8,128)(2,1)S(1)} %collective-permute-done.36.refs_0_, ...), custom_call_target="tpu_custom_call", output_to_operand_aliasing={{1}: (3, {}), {2}: (4, {})} | custom-call | flops 1000000000 | tf_op jit(solution)/shard_map/unpack_0/pallas_call | solution.py:239
  (54 shorter events, 3.0 us)
Async XLA Ops:
  5.0 8.0 %collective-permute-start = (bf16[128,1024]{1,0:T(8,128)(2,1)S(1)}, bf16[128,1024]{1,0:T(8,128)(2,1)S(1)}, u32[]{:S(2)}, u32[]{:S(2)}) collective-permute-start(bf16[128,1024]{1,0:T(8,128)(2,1)S(1)} %get-tuple-element.235), channel_id=1, source_target_pairs={{0,16},{1,17},{2,18},{3,19},{4,20},{5,21},{6,22},{7,23},{8,24},{9,... | collective-permute-start | bytes 786440 | tf_op jit(solution)/shard_map/ppermute | solution.py:1099
  9.3 9.0 %collective-permute-start.1 = (bf16[128,1024]{1,0:T(8,128)(2,1)S(1)}, bf16[128,1024]{1,0:T(8,128)(2,1)S(1)}, u32[]{:S(2)}, u32[]{:S(2)}) collective-permute-start(bf16[128,1024]{1,0:T(8,128)(2,1)S(1)} %get-tuple-element.239), channel_id=1, source_target_pairs={{0,16},{1,17},{2,18},{3,19},{4,20},{5,21},{6,22},{7,23},{8,24},{9,... | collective-permute-start | bytes 786440 | tf_op jit(solution)/shard_map/ppermute | solution.py:1101
  13.6 13.9 %collective-permute-start.2 = (bf16[256,512]{1,0:T(8,128)(2,1)S(1)}, bf16[256,512]{1,0:T(8,128)(2,1)S(1)}, u32[]{:S(2)}, u32[]{:S(2)}) collective-permute-start(bf16[256,512]{1,0:T(8,128)(2,1)S(1)} %get-tuple-element.258), channel_id=1, source_target_pairs={{16,0},{17,1},{18,2},{19,3},{20,4},{21,5},{22,6},{23,7},{24,8},{25... | collective-permute-start | bytes 786440 | tf_op jit(solution)/shard_map/ppermute | solution.py:1104
  19.0 11.4 %collective-permute-start.3 = (bf16[128,512]{1,0:T(8,128)(2,1)S(1)}, bf16[128,512]{1,0:T(8,128)(2,1)S(1)}, u32[]{:S(2)}, u32[]{:S(2)}) collective-permute-start(bf16[128,512]{1,0:T(8,128)(2,1)S(1)} %get-tuple-element.271), channel_id=1, source_target_pairs={{16,0},{17,1},{18,2},{19,3},{20,4},{21,5},{22,6},{23,7},{24,8},{25... | collective-permute-start | bytes 393224 | tf_op jit(solution)/shard_map/ppermute | solution.py:1104
  20.3 12.2 %collective-permute-start.4 = (bf16[128,512]{1,0:T(8,128)(2,1)S(1)}, bf16[128,512]{1,0:T(8,128)(2,1)S(1)}, u32[]{:S(2)}, u32[]{:S(2)}) collective-permute-start(bf16[128,512]{1,0:T(8,128)(2,1)S(1)} %get-tuple-element.282), channel_id=1, source_target_pairs={{16,0},{17,1},{18,2},{19,3},{20,4},{21,5},{22,6},{23,7},{24,8},{25... | collective-permute-start | bytes 393224 | tf_op jit(solution)/shard_map/ppermute | solution.py:1104
  33.3 2.7 %collective-permute-start.5 = (bf16[896,512]{1,0:T(8,128)(2,1)S(1)}, bf16[896,512]{1,0:T(8,128)(2,1)S(1)}, u32[]{:S(2)}, u32[]{:S(2)}) collective-permute-start(bf16[896,512]{1,0:T(8,128)(2,1)S(1)} %get-tuple-element.303), channel_id=1, source_target_pairs={{0,1},{1,0},{2,3},{3,2},{4,5},{5,4},{6,7},{7,6},{8,9},{9,8},{10,11... | collective-permute-start | bytes 2752520 | tf_op jit(solution)/shard_map/ppermute | solution.py:895
  35.4 3.4 %collective-permute-start.6 = (bf16[896,512]{1,0:T(8,128)(2,1)S(1)}, bf16[896,512]{1,0:T(8,128)(2,1)S(1)}, u32[]{:S(2)}, u32[]{:S(2)}) collective-permute-start(bf16[896,512]{1,0:T(8,128)(2,1)S(1)} %get-tuple-element.309), channel_id=1, source_target_pairs={{0,1},{1,0},{2,3},{3,2},{4,5},{5,4},{6,7},{7,6},{8,9},{9,8},{10,11... | collective-permute-start | bytes 2752520 | tf_op jit(solution)/shard_map/ppermute | solution.py:895
  36.5 8.5 %collective-permute-start.7 = (bf16[448,512]{1,0:T(8,128)(2,1)S(1)}, bf16[448,512]{1,0:T(8,128)(2,1)S(1)}, u32[]{:S(2)}, u32[]{:S(2)}) collective-permute-start(bf16[448,512]{1,0:T(8,128)(2,1)S(1)} %get-tuple-element.320), channel_id=1, source_target_pairs={{0,2},{1,5},{2,0},{3,7},{4,6},{5,1},{6,4},{7,3},{8,10},{9,13},{10,... | collective-permute-start | bytes 1376264 | tf_op jit(solution)/shard_map/ppermute | solution.py:895
  39.4 13.1 %collective-permute-start.9 = (bf16[448,512]{1,0:T(8,128)(2,1)S(1)}, bf16[448,512]{1,0:T(8,128)(2,1)S(1)}, u32[]{:S(2)}, u32[]{:S(2)}) collective-permute-start(bf16[448,512]{1,0:T(8,128)(2,1)S(1)} %get-tuple-element.325), channel_id=1, source_target_pairs={{0,2},{1,5},{2,0},{3,7},{4,6},{5,1},{6,4},{7,3},{8,10},{9,13},{10,... | collective-permute-start | bytes 1376264 | tf_op jit(solution)/shard_map/ppermute | solution.py:895
  40.4 6.6 %collective-permute-start.8 = (bf16[896,512]{1,0:T(8,128)(2,1)S(1)}, bf16[896,512]{1,0:T(8,128)(2,1)S(1)}, u32[]{:S(2)}, u32[]{:S(2)}) collective-permute-start(bf16[896,512]{1,0:T(8,128)(2,1)S(1)} %get-tuple-element.322), channel_id=1, source_target_pairs={{0,1},{1,0},{2,3},{3,2},{4,5},{5,4},{6,7},{7,6},{8,9},{9,8},{10,11... | collective-permute-start | bytes 2752520 | tf_op jit(solution)/shard_map/ppermute | solution.py:895
  43.8 8.8 %collective-permute-start.10 = (bf16[896,512]{1,0:T(8,128)(2,1)S(1)}, bf16[896,512]{1,0:T(8,128)(2,1)S(1)}, u32[]{:S(2)}, u32[]{:S(2)}) collective-permute-start(bf16[896,512]{1,0:T(8,128)(2,1)S(1)} %get-tuple-element.327), channel_id=1, source_target_pairs={{0,1},{1,0},{2,3},{3,2},{4,5},{5,4},{6,7},{7,6},{8,9},{9,8},{10,11... | collective-permute-start | bytes 2752520 | tf_op jit(solution)/shard_map/ppermute | solution.py:895
  44.2 8.4 %collective-permute-start.11 = (bf16[896,512]{1,0:T(8,128)(2,1)S(1)}, bf16[896,512]{1,0:T(8,128)(2,1)S(1)}, u32[]{:S(2)}, u32[]{:S(2)}) collective-permute-start(bf16[896,512]{1,0:T(8,128)(2,1)S(1)} %get-tuple-element.328), channel_id=1, source_target_pairs={{0,1},{1,0},{2,3},{3,2},{4,5},{5,4},{6,7},{7,6},{8,9},{9,8},{10,11... | collective-permute-start | bytes 2752520 | tf_op jit(solution)/shard_map/ppermute | solution.py:895
  45.2 12.2 %collective-permute-start.12 = (bf16[224,512]{1,0:T(8,128)(2,1)S(1)}, bf16[224,512]{1,0:T(8,128)(2,1)S(1)}, u32[]{:S(2)}, u32[]{:S(2)}) collective-permute-start(bf16[224,512]{1,0:T(8,128)(2,1)S(1)} %get-tuple-element.333), channel_id=1, source_target_pairs={{0,4},{1,3},{2,6},{3,1},{4,0},{5,7},{6,2},{7,5},{8,12},{9,11},{10,... | collective-permute-start | bytes 688136 | tf_op jit(solution)/shard_map/ppermute | solution.py:895
  47.6 13.9 %collective-permute-start.13 = (bf16[448,512]{1,0:T(8,128)(2,1)S(1)}, bf16[448,512]{1,0:T(8,128)(2,1)S(1)}, u32[]{:S(2)}, u32[]{:S(2)}) collective-permute-start(bf16[448,512]{1,0:T(8,128)(2,1)S(1)} %get-tuple-element.336), channel_id=1, source_target_pairs={{0,2},{1,5},{2,0},{3,7},{4,6},{5,1},{6,4},{7,3},{8,10},{9,13},{10,... | collective-permute-start | bytes 1376264 | tf_op jit(solution)/shard_map/ppermute | solution.py:895
  53.5 25.3 %collective-permute-start.15 = (bf16[448,512]{1,0:T(8,128)(2,1)S(1)}, bf16[448,512]{1,0:T(8,128)(2,1)S(1)}, u32[]{:S(2)}, u32[]{:S(2)}) collective-permute-start(bf16[448,512]{1,0:T(8,128)(2,1)S(1)} %get-tuple-element.342), channel_id=1, source_target_pairs={{0,4},{1,3},{2,6},{3,1},{4,0},{5,7},{6,2},{7,5},{8,12},{9,11},{10,... | collective-permute-start | bytes 1376264 | tf_op jit(solution)/shard_map/ppermute | solution.py:895
  55.4 23.5 %collective-permute-start.16 = (bf16[448,512]{1,0:T(8,128)(2,1)S(1)}, bf16[448,512]{1,0:T(8,128)(2,1)S(1)}, u32[]{:S(2)}, u32[]{:S(2)}) collective-permute-start(bf16[448,512]{1,0:T(8,128)(2,1)S(1)} %get-tuple-element.343), channel_id=1, source_target_pairs={{0,4},{1,3},{2,6},{3,1},{4,0},{5,7},{6,2},{7,5},{8,12},{9,11},{10,... | collective-permute-start | bytes 1376264 | tf_op jit(solution)/shard_map/ppermute | solution.py:895
  55.6 18.6 %collective-permute-start.14 = (bf16[224,512]{1,0:T(8,128)(2,1)S(1)}, bf16[224,512]{1,0:T(8,128)(2,1)S(1)}, u32[]{:S(2)}, u32[]{:S(2)}) collective-permute-start(bf16[224,512]{1,0:T(8,128)(2,1)S(1)} %get-tuple-element.339), channel_id=1, source_target_pairs={{0,4},{1,3},{2,6},{3,1},{4,0},{5,7},{6,2},{7,5},{8,12},{9,11},{10,... | collective-permute-start | bytes 688136 | tf_op jit(solution)/shard_map/ppermute | solution.py:895
  57.5 21.6 %collective-permute-start.17 = (bf16[224,512]{1,0:T(8,128)(2,1)S(1)}, bf16[224,512]{1,0:T(8,128)(2,1)S(1)}, u32[]{:S(2)}, u32[]{:S(2)}) collective-permute-start(bf16[224,512]{1,0:T(8,128)(2,1)S(1)} %get-tuple-element.345.refs_0_), channel_id=1, source_target_pairs={{0,8},{1,9},{2,10},{3,11},{4,12},{5,13},{6,14},{7,15},{8,0},{9,1},... | collective-permute-start | bytes 688136 | tf_op jit(solution)/shard_map/ppermute | solution.py:895
  74.3 16.9 %collective-permute-start.19 = (bf16[224,512]{1,0:T(8,128)(2,1)S(1)}, bf16[224,512]{1,0:T(8,128)(2,1)S(1)}, u32[]{:S(2)}, u32[]{:S(2)}) collective-permute-start(bf16[224,512]{1,0:T(8,128)(2,1)S(1)} %get-tuple-element.357.refs_0_), channel_id=1, source_target_pairs={{0,8},{1,9},{2,10},{3,11},{4,12},{5,13},{6,14},{7,15},{8,0},{9,1},... | collective-permute-start | bytes 688136 | tf_op jit(solution)/shard_map/ppermute | solution.py:895
  76.4 14.6 %collective-permute-start.18 = (bf16[224,512]{1,0:T(8,128)(2,1)S(1)}, bf16[224,512]{1,0:T(8,128)(2,1)S(1)}, u32[]{:S(2)}, u32[]{:S(2)}) collective-permute-start(bf16[224,512]{1,0:T(8,128)(2,1)S(1)} %get-tuple-element.355), channel_id=1, source_target_pairs={{0,4},{1,3},{2,6},{3,1},{4,0},{5,7},{6,2},{7,5},{8,12},{9,11},{10,... | collective-permute-start | bytes 688136 | tf_op jit(solution)/shard_map/ppermute | solution.py:895
  79.1 14.9 %collective-permute-start.22 = (bf16[224,512]{1,0:T(8,128)(2,1)S(1)}, bf16[224,512]{1,0:T(8,128)(2,1)S(1)}, u32[]{:S(2)}, u32[]{:S(2)}) collective-permute-start(bf16[224,512]{1,0:T(8,128)(2,1)S(1)} %get-tuple-element.363.refs_0_), channel_id=1, source_target_pairs={{0,4},{1,3},{2,6},{3,1},{4,0},{5,7},{6,2},{7,5},{8,12},{9,11},{10,... | collective-permute-start | bytes 688136 | tf_op jit(solution)/shard_map/ppermute | solution.py:895
  79.2 12.0 %collective-permute-start.20 = (bf16[224,512]{1,0:T(8,128)(2,1)S(1)}, bf16[224,512]{1,0:T(8,128)(2,1)S(1)}, u32[]{:S(2)}, u32[]{:S(2)}) collective-permute-start(bf16[224,512]{1,0:T(8,128)(2,1)S(1)} %get-tuple-element.360), channel_id=1, source_target_pairs={{0,2},{1,5},{2,0},{3,7},{4,6},{5,1},{6,4},{7,3},{8,10},{9,13},{10,... | collective-permute-start | bytes 688136 | tf_op jit(solution)/shard_map/ppermute | solution.py:895
  80.4 10.9 %collective-permute-start.21 = (bf16[224,512]{1,0:T(8,128)(2,1)S(1)}, bf16[224,512]{1,0:T(8,128)(2,1)S(1)}, u32[]{:S(2)}, u32[]{:S(2)}) collective-permute-start(bf16[224,512]{1,0:T(8,128)(2,1)S(1)} %get-tuple-element.361), channel_id=1, source_target_pairs={{0,2},{1,5},{2,0},{3,7},{4,6},{5,1},{6,4},{7,3},{8,10},{9,13},{10,... | collective-permute-start | bytes 688136 | tf_op jit(solution)/shard_map/ppermute | solution.py:895
  91.1 10.6 %collective-permute-start.23 = (bf16[224,512]{1,0:T(8,128)(2,1)S(1)}, bf16[224,512]{1,0:T(8,128)(2,1)S(1)}, u32[]{:S(2)}, u32[]{:S(2)}) collective-permute-start(bf16[224,512]{1,0:T(8,128)(2,1)S(1)} %get-tuple-element.365.refs_0_), channel_id=1, source_target_pairs={{0,8},{1,9},{2,10},{3,11},{4,12},{5,13},{6,14},{7,15},{8,0},{9,1},... | collective-permute-start | bytes 688136 | tf_op jit(solution)/shard_map/ppermute | solution.py:895
  94.0 27.9 %collective-permute-start.27 = (bf16[448,512]{1,0:T(8,128)(2,1)S(1)}, bf16[448,512]{1,0:T(8,128)(2,1)S(1)}, u32[]{:S(2)}, u32[]{:S(2)}) collective-permute-start(bf16[448,512]{1,0:T(8,128)(2,1)S(1)} %get-tuple-element.372.refs_0_), channel_id=1, source_target_pairs={{0,2},{1,5},{2,0},{3,7},{4,6},{5,1},{6,4},{7,3},{8,10},{9,13},{10,... | collective-permute-start | bytes 1376264 | tf_op jit(solution)/shard_map/ppermute | solution.py:895
  95.6 13.4 %collective-permute-start.24 = (bf16[224,512]{1,0:T(8,128)(2,1)S(1)}, bf16[224,512]{1,0:T(8,128)(2,1)S(1)}, u32[]{:S(2)}, u32[]{:S(2)}) collective-permute-start(bf16[224,512]{1,0:T(8,128)(2,1)S(1)} %get-tuple-element.367.refs_0_), channel_id=1, source_target_pairs={{0,4},{1,3},{2,6},{3,1},{4,0},{5,7},{6,2},{7,5},{8,12},{9,11},{10,... | collective-permute-start | bytes 688136 | tf_op jit(solution)/shard_map/ppermute | solution.py:895
  95.6 20.8 %collective-permute-start.25 = (bf16[224,512]{1,0:T(8,128)(2,1)S(1)}, bf16[224,512]{1,0:T(8,128)(2,1)S(1)}, u32[]{:S(2)}, u32[]{:S(2)}) collective-permute-start(bf16[224,512]{1,0:T(8,128)(2,1)S(1)} %get-tuple-element.369.refs_0_), channel_id=1, source_target_pairs={{0,8},{1,9},{2,10},{3,11},{4,12},{5,13},{6,14},{7,15},{8,0},{9,1},... | collective-permute-start | bytes 688136 | tf_op jit(solution)/shard_map/ppermute | solution.py:895
  97.6 22.2 %collective-permute-start.26 = (bf16[224,512]{1,0:T(8,128)(2,1)S(1)}, bf16[224,512]{1,0:T(8,128)(2,1)S(1)}, u32[]{:S(2)}, u32[]{:S(2)}) collective-permute-start(bf16[224,512]{1,0:T(8,128)(2,1)S(1)} %get-tuple-element.370.refs_2_), channel_id=1, source_target_pairs={{0,8},{1,9},{2,10},{3,11},{4,12},{5,13},{6,14},{7,15},{8,0},{9,1},... | collective-permute-start | bytes 688136 | tf_op jit(solution)/shard_map/ppermute | solution.py:895
  101.8 20.2 %collective-permute-start.28 = (bf16[224,512]{1,0:T(8,128)(2,1)S(1)}, bf16[224,512]{1,0:T(8,128)(2,1)S(1)}, u32[]{:S(2)}, u32[]{:S(2)}) collective-permute-start(bf16[224,512]{1,0:T(8,128)(2,1)S(1)} %get-tuple-element.374.refs_0_), channel_id=1, source_target_pairs={{0,4},{1,3},{2,6},{3,1},{4,0},{5,7},{6,2},{7,5},{8,12},{9,11},{10,... | collective-permute-start | bytes 688136 | tf_op jit(solution)/shard_map/ppermute | solution.py:895
  119.8 12.5 %collective-permute-start.30 = (bf16[224,512]{1,0:T(8,128)(2,1)S(1)}, bf16[224,512]{1,0:T(8,128)(2,1)S(1)}, u32[]{:S(2)}, u32[]{:S(2)}) collective-permute-start(bf16[224,512]{1,0:T(8,128)(2,1)S(1)} %get-tuple-element.383.refs_0_), channel_id=1, source_target_pairs={{0,2},{1,5},{2,0},{3,7},{4,6},{5,1},{6,4},{7,3},{8,10},{9,13},{10,... | collective-permute-start | bytes 688136 | tf_op jit(solution)/shard_map/ppermute | solution.py:895
  121.2 9.6 %collective-permute-start.29 = (bf16[448,512]{1,0:T(8,128)(2,1)S(1)}, bf16[448,512]{1,0:T(8,128)(2,1)S(1)}, u32[]{:S(2)}, u32[]{:S(2)}) collective-permute-start(bf16[448,512]{1,0:T(8,128)(2,1)S(1)} %get-tuple-element.378.refs_0_), channel_id=1, source_target_pairs={{0,2},{1,5},{2,0},{3,7},{4,6},{5,1},{6,4},{7,3},{8,10},{9,13},{10,... | collective-permute-start | bytes 1376264 | tf_op jit(solution)/shard_map/ppermute | solution.py:895
  122.1 13.9 %collective-permute-start.32 = (bf16[448,512]{1,0:T(8,128)(2,1)S(1)}, bf16[448,512]{1,0:T(8,128)(2,1)S(1)}, u32[]{:S(2)}, u32[]{:S(2)}) collective-permute-start(bf16[448,512]{1,0:T(8,128)(2,1)S(1)} %get-tuple-element.387.refs_0_), channel_id=1, source_target_pairs={{0,2},{1,5},{2,0},{3,7},{4,6},{5,1},{6,4},{7,3},{8,10},{9,13},{10,... | collective-permute-start | bytes 1376264 | tf_op jit(solution)/shard_map/ppermute | solution.py:895
  123.5 9.0 %collective-permute-start.31 = (bf16[896,512]{1,0:T(8,128)(2,1)S(1)}, bf16[896,512]{1,0:T(8,128)(2,1)S(1)}, u32[]{:S(2)}, u32[]{:S(2)}) collective-permute-start(bf16[896,512]{1,0:T(8,128)(2,1)S(1)} %get-tuple-element.376.refs_0_), channel_id=1, source_target_pairs={{0,1},{1,0},{2,3},{3,2},{4,5},{5,4},{6,7},{7,6},{8,9},{9,8},{10,11... | collective-permute-start | bytes 2752520 | tf_op jit(solution)/shard_map/ppermute | solution.py:895
  130.9 5.2 %collective-permute-start.33 = (bf16[896,512]{1,0:T(8,128)(2,1)S(1)}, bf16[896,512]{1,0:T(8,128)(2,1)S(1)}, u32[]{:S(2)}, u32[]{:S(2)}) collective-permute-start(bf16[896,512]{1,0:T(8,128)(2,1)S(1)} %get-tuple-element.380.refs_0_), channel_id=1, source_target_pairs={{0,1},{1,0},{2,3},{3,2},{4,5},{5,4},{6,7},{7,6},{8,9},{9,8},{10,11... | collective-permute-start | bytes 2752520 | tf_op jit(solution)/shard_map/ppermute | solution.py:895
  132.4 8.5 %collective-permute-start.34 = (bf16[448,512]{1,0:T(8,128)(2,1)S(1)}, bf16[448,512]{1,0:T(8,128)(2,1)S(1)}, u32[]{:S(2)}, u32[]{:S(2)}) collective-permute-start(bf16[448,512]{1,0:T(8,128)(2,1)S(1)} %get-tuple-element.397.refs_0_), channel_id=1, source_target_pairs={{0,4},{1,3},{2,6},{3,1},{4,0},{5,7},{6,2},{7,5},{8,12},{9,11},{10,... | collective-permute-start | bytes 1376264 | tf_op jit(solution)/shard_map/ppermute | solution.py:895
  136.0 5.1 %collective-permute-start.35 = (bf16[896,512]{1,0:T(8,128)(2,1)S(1)}, bf16[896,512]{1,0:T(8,128)(2,1)S(1)}, u32[]{:S(2)}, u32[]{:S(2)}) collective-permute-start(bf16[896,512]{1,0:T(8,128)(2,1)S(1)} %get-tuple-element.394.refs_0_), channel_id=1, source_target_pairs={{0,1},{1,0},{2,3},{3,2},{4,5},{5,4},{6,7},{7,6},{8,9},{9,8},{10,11... | collective-permute-start | bytes 2752520 | tf_op jit(solution)/shard_map/ppermute | solution.py:895
  141.0 2.7 %collective-permute-start.36 = (bf16[896,512]{1,0:T(8,128)(2,1)S(1)}, bf16[896,512]{1,0:T(8,128)(2,1)S(1)}, u32[]{:S(2)}, u32[]{:S(2)}) collective-permute-start(bf16[896,512]{1,0:T(8,128)(2,1)S(1)} %get-tuple-element.401.refs_0_), channel_id=1, source_target_pairs={{0,1},{1,0},{2,3},{3,2},{4,5},{5,4},{6,7},{7,6},{8,9},{9,8},{10,11... | collective-permute-start | bytes 2752520 | tf_op jit(solution)/shard_map/ppermute | solution.py:895

commit v6 on v4

--- a/solution.py
+++ b/solution.py
@@ -1061,8 +1061,8 @@
 
 CHUNKS = (DOWN, CROSS, UP, QKV)
 GATE, BACK_ATTN, BACK_FFN, FINAL, MORE, OWN = 10, 11, 12, 13, 14, 20
-ORDER = (10, 12, 0, 14, 1, 11, 0, 2, 1, 3, 0, 2, 1, 3, 0, 13, 2, 1, 3, 0, 2, 1, 3, 0, 2, 20, 1, 21, 3, 0, 2, 1, 22, 3, 2, 23, 3)
-COSTS = (1000, 1000, 8000, 4000, 8000, 8000, 8000, 4000, 1000, 1000, 1000, 1000, 1000, 1000, 1000, 1000, 1000, 1000, 1000, 1000, 1000, 1000, 1000, 1000, 8000, 8000, 1000, 8000, 1000, 1000, 1000, 1000, 1000, 50, 3000, 1000, 1000)
+ORDER = (10, 12, 0, 14, 1, 11, 2, 0, 3, 1, 0, 2, 1, 3, 0, 13, 2, 1, 3, 0, 2, 1, 3, 0, 2, 20, 1, 21, 3, 0, 2, 1, 22, 3, 2, 23, 3)
+COSTS = (1000, 1000, 8000, 4000, 8000, 8000, 4000, 8000, 1000, 1000, 1000, 1000, 1000, 1000, 1000, 1000, 1000, 1000, 1000, 1000, 1000, 1000, 1000, 1000, 8000, 8000, 1000, 8000, 1000, 1000, 1000, 1000, 1000, 50, 3000, 1000, 1000)
 
 
 def on_device(inputs, lengths, w_qkv, w_attn_out, w_cross, w_up, w_down, cotangent):

time: 129 us -> 127 us (0.984)
  waiting for transfers between devices: 57 us -> 49.2 us
  starting transfers between devices: 36.5 us -> 42.8 us
    ppermute x29, waiting for transfers between devices: 44 us -> 36.2 us  [swap(): lax.ppermute(value, 'dp', [(i, partner(i)) for i in range(self.count)])]
    ppermute x29, starting transfers between devices: 28.8 us -> 35.1 us  [swap(): lax.ppermute(value, 'dp', [(i, partner(i)) for i in range(self.count)])]
where the time goes in v6:
time: 127 us
  waiting for transfers between devices  49.2 us (39%)
  starting transfers between devices  42.8 us (34%)
  Pallas kernels  33.7 us (27%)
    ppermute x29, waiting for transfers between devices, swap(): lax.ppermute(value, 'dp', [(i, partner(i)) for i in range(self.count)])  36.2 us
    ppermute x29, starting transfers between devices, swap(): lax.ppermute(value, 'dp', [(i, partner(i)) for i in range(self.count)])  35.1 us
    pallas_call x42, Pallas kernels, call(): pl.pallas_call(body, out_shape=out_shape, in_specs=[in_smem()] + [in_vmem...  26.4 us
    ppermute x3, waiting for transfers between devices, to_encoder(): return lax.ppermute(side, 'section', [(1, 0)])  8.33 us
    pallas_call x1, Pallas kernels, first_stage(): pl.pallas_call(body, out_shape=shaped(makes) + [pltpu.SMEM((PLACE,), jnp....  4.37 us
    ppermute x3, starting transfers between devices, to_encoder(): return lax.ppermute(side, 'section', [(1, 0)])  3.88 us
    ppermute x1, waiting for transfers between devices, on_device(): links.append(lax.ppermute(link, 'section', [(0, 1)]))  3.5 us
    pallas_call x1, Pallas kernels, second_stage(): pl.pallas_call(body, out_shape=same_shape(keeps) + [pltpu.VMEM((ROWS, 2 *...  3.01 us
  transfers between devices with their start and end apart: 34, of which 16 were waited for; matrix products, arithmetic and copies ran while one was open for 0% of the time, Pallas kernels for 21%

profile of v6, /device:TPU:0, one launch (start us, length us, event | category | flops | bytes accessed | tf_op | source)
XLA Modules:
  0.0 126.9 jit_solution(9000867223369058262)
XLA Ops:
  0.6 4.4 %first_stage.1 = (bf16[512,1536]{1,0:T(8,128)(2,1)S(1)}, bf16[512,512]{1,0:T(8,128)(2,1)S(1)}, bf16[512,1024]{1,0:T(8,128)(2,1)S(1)}, bf16[512,2048]{1,0:T(8,128...) custom-call(s32[2,2,16]{2,1,0:T(2,128)} %refs_0_.3, ...), custom_call_target="tpu_custom_call" | custom-call | flops 939524096 | bytes 10000000 | tf_op jit(solution)/shard_map/first_stage/pallas_call | solution.py:395
  5.0 1.3 %collective-permute-start = (bf16[128,1024]{1,0:T(8,128)(2,1)S(1)}, bf16[128,1024]{1,0:T(8,128)(2,1)S(1)}, u32[]{:S(2)}, u32[]{:S(2)}) collective-permute-start(bf16[128,1024]{1,0:T(8,128)(2,1)S(1)} %get-tuple-element.232), channel_id=1, source_target_pairs={{0,16},{1,17},{2,18},{3,19},{4,20},{5,21},{6,22},{7,23},{8,24},{9,... | collective-permute-start | bytes 786440 | tf_op jit(solution)/shard_map/ppermute | solution.py:1072
  6.3 3.0 %second_stage.1 = (bf16[512,1536]{1,0:T(8,128)(2,1)S(1)}, bf16[512,512]{1,0:T(8,128)(2,1)S(1)}, bf16[512,1024]{1,0:T(8,128)(2,1)S(1)}, bf16[512,2048]{1,0:T(8,12...) custom-call(s32[4]{0:T(128)S(4)} %get-tuple-element.206.place_ref, ...), custom_call_target="tpu_custom_call", output_to_operand_aliasing={{0}: (9, {}), {1}: (10, {}), {2}: (11, {}), {3}: (12, {}), ... | custom-call | flops 939524096 | bytes 10000000 | tf_op jit(solution)/shard_map/second_stage/pallas_call | solution.py:450
  9.3 2.5 %collective-permute-start.1 = (bf16[128,1024]{1,0:T(8,128)(2,1)S(1)}, bf16[128,1024]{1,0:T(8,128)(2,1)S(1)}, u32[]{:S(2)}, u32[]{:S(2)}) collective-permute-start(bf16[128,1024]{1,0:T(8,128)(2,1)S(1)} %get-tuple-element.236), channel_id=1, source_target_pairs={{0,16},{1,17},{2,18},{3,19},{4,20},{5,21},{6,22},{7,23},{8,24},{9,... | collective-permute-start | bytes 786440 | tf_op jit(solution)/shard_map/ppermute | solution.py:1074
  11.8 1.2 collective-permute-done.refs_6_
  13.0 0.6 middle_stage.2
  13.6 1.3 %collective-permute-start.2 = (bf16[256,512]{1,0:T(8,128)(2,1)S(1)}, bf16[256,512]{1,0:T(8,128)(2,1)S(1)}, u32[]{:S(2)}, u32[]{:S(2)}) collective-permute-start(bf16[256,512]{1,0:T(8,128)(2,1)S(1)} %get-tuple-element.255), channel_id=1, source_target_pairs={{16,0},{17,1},{18,2},{19,3},{20,4},{21,5},{22,6},{23,7},{24,8},{25... | collective-permute-start | bytes 786440 | tf_op jit(solution)/shard_map/ppermute | solution.py:1077
  14.9 3.5 %collective-permute-done.1.refs_6_.refs_1_ = bf16[128,1024]{1,0:T(8,128)(2,1)S(1)} collective-permute-done((bf16[128,1024]{1,0:T(8,128)(2,1)S(1)}, bf16[128,1024]{1,0:T(8,128)(2,1)S(1)}, u32[]{:S(2)}, u32[]{:S(2)}) %collective-permute-start.1) | collective-permute-done | bytes 262176 | tf_op jit(solution)/shard_map/ppermute | solution.py:1074
  18.4 0.6 middle_stage.3
  19.0 1.3 %collective-permute-start.3 = (bf16[128,512]{1,0:T(8,128)(2,1)S(1)}, bf16[128,512]{1,0:T(8,128)(2,1)S(1)}, u32[]{:S(2)}, u32[]{:S(2)}) collective-permute-start(bf16[128,512]{1,0:T(8,128)(2,1)S(1)} %get-tuple-element.268), channel_id=1, source_target_pairs={{16,0},{17,1},{18,2},{19,3},{20,4},{21,5},{22,6},{23,7},{24,8},{25... | collective-permute-start | bytes 393224 | tf_op jit(solution)/shard_map/ppermute | solution.py:1077
  20.3 1.3 %collective-permute-start.4 = (bf16[128,512]{1,0:T(8,128)(2,1)S(1)}, bf16[128,512]{1,0:T(8,128)(2,1)S(1)}, u32[]{:S(2)}, u32[]{:S(2)}) collective-permute-start(bf16[128,512]{1,0:T(8,128)(2,1)S(1)} %get-tuple-element.279), channel_id=1, source_target_pairs={{16,0},{17,1},{18,2},{19,3},{20,4},{21,5},{22,6},{23,7},{24,8},{25... | collective-permute-start | bytes 393224 | tf_op jit(solution)/shard_map/ppermute | solution.py:1077
  21.6 5.9 %collective-permute-done.2.refs_6_ = bf16[256,512]{1,0:T(8,128)(2,1)S(1)} collective-permute-done((bf16[256,512]{1,0:T(8,128)(2,1)S(1)}, bf16[256,512]{1,0:T(8,128)(2,1)S(1)}, u32[]{:S(2)}, u32[]{:S(2)}) %collective-permute-start.2) | collective-permute-done | bytes 262176 | tf_op jit(solution)/shard_map/ppermute | solution.py:1077
  27.5 2.3 %back_stage.4 = (f32[256,2048]{1,0:T(8,128)S(1)}, f32[256,512]{1,0:T(8,128)S(1)}, bf16[256,512]{1,0:T(8,128)(2,1)S(1)}, bf16[256,1024]{1,0:T(8,128)(2,1)S(1)}, b...) custom-call(s32[4]{0:T(128)S(4)} %get-tuple-element.206.place_ref, ...), custom_call_target="tpu_custom_call", output_to_operand_aliasing={{0}: (11, {}), {1}: (12, {}), {2}: (13, {}), {3}: (14, {}),... | custom-call | flops 900000000 | tf_op jit(solution)/shard_map/back_stage/pallas_call | solution.py:239
  29.8 0.5 collective-permute-done.3.refs_6_
  30.3 0.3 back_stage.5
  30.6 1.9 %collective-permute-done.4.refs_6_ = bf16[128,512]{1,0:T(8,128)(2,1)S(1)} collective-permute-done((bf16[128,512]{1,0:T(8,128)(2,1)S(1)}, bf16[128,512]{1,0:T(8,128)(2,1)S(1)}, u32[]{:S(2)}, u32[]{:S(2)}) %collective-permute-start.4) | collective-permute-done | bytes 131104 | tf_op jit(solution)/shard_map/ppermute | solution.py:1077
  32.5 0.8 back_stage.6
  33.3 2.1 %back_stage.7 = (f32[256,2048]{1,0:T(8,128)S(1)}, f32[256,512]{1,0:T(8,128)S(1)}, bf16[256,512]{1,0:T(8,128)(2,1)S(1)}, bf16[256,1024]{1,0:T(8,128)(2,1)S(1)}, b...) custom-call(s32[4]{0:T(128)S(4)} %get-tuple-element.206.place_ref, ...), custom_call_target="tpu_custom_call", output_to_operand_aliasing={{0}: (11, {}), {1}: (12, {}), {2}: (13, {}), {3}: (14, {}),... | custom-call | flops 1000000000 | tf_op jit(solution)/shard_map/back_stage/pallas_call | solution.py:239
  35.4 0.5 collective-permute-start.6
  36.0 0.6 sum_0.4
  36.5 1.8 %collective-permute-start.8 = (bf16[448,512]{1,0:T(8,128)(2,1)S(1)}, bf16[448,512]{1,0:T(8,128)(2,1)S(1)}, u32[]{:S(2)}, u32[]{:S(2)}) collective-permute-start(bf16[448,512]{1,0:T(8,128)(2,1)S(1)} %get-tuple-element.319), channel_id=1, source_target_pairs={{0,2},{1,5},{2,0},{3,7},{4,6},{5,1},{6,4},{7,3},{8,10},{9,13},{10,... | collective-permute-start | bytes 1376264 | tf_op jit(solution)/shard_map/ppermute | solution.py:895
  38.3 0.5 product.1
  38.9 0.6 sum_0.5
  39.5 1.4 %collective-permute-start.11 = (bf16[448,512]{1,0:T(8,128)(2,1)S(1)}, bf16[448,512]{1,0:T(8,128)(2,1)S(1)}, u32[]{:S(2)}, u32[]{:S(2)}) collective-permute-start(bf16[448,512]{1,0:T(8,128)(2,1)S(1)} %get-tuple-element.327), channel_id=1, source_target_pairs={{0,2},{1,5},{2,0},{3,7},{4,6},{5,1},{6,4},{7,3},{8,10},{9,13},{10,... | collective-permute-start | bytes 1376264 | tf_op jit(solution)/shard_map/ppermute | solution.py:895
  40.8 3.2 %late_stage.1 = (bf16[256,1536]{1,0:T(8,128)(2,1)S(1)}, bf16[256,1536]{1,0:T(8,128)(2,1)S(1)}, bf16[896,512]{1,0:T(8,128)(2,1)S(1)}, bf16[896,512]{1,0:T(8,128)(2,1)S(1)}, f32[8,128]{1,0:T(8,128)S(1)}) custom-call(s32[4]{0:T(128)S(4)} %get-tuple-element.206.place_ref, f32[8,128]{1,0:T(8,128)S(1)} %get-tuple-element.310.token_in, ...), custom_call_target="tpu_custom_call" | custom-call | flops 8000000000 | tf_op jit(solution)/shard_map/late_stage/pallas_call | solution.py:239
  44.0 0.6 collective-permute-start.9
  44.6 0.5 sum_0.6
  45.2 0.9 collective-permute-start.13
  46.2 1.5 %collective-permute-start.12 = (bf16[224,512]{1,0:T(8,128)(2,1)S(1)}, bf16[224,512]{1,0:T(8,128)(2,1)S(1)}, u32[]{:S(2)}, u32[]{:S(2)}) collective-permute-start(bf16[224,512]{1,0:T(8,128)(2,1)S(1)} %get-tuple-element.330), channel_id=1, source_target_pairs={{0,4},{1,3},{2,6},{3,1},{4,0},{5,7},{6,2},{7,5},{8,12},{9,11},{10,... | collective-permute-start | bytes 688136 | tf_op jit(solution)/shard_map/ppermute | solution.py:895
  47.7 0.3 collective-permute-done.10.refs_1_
  48.0 0.7 sum_0.7
  48.7 1.2 collective-permute-start.15
  49.9 1.1 collective-permute-done.11.refs_1_
  51.1 2.4 %collective-permute-start.14 = (bf16[224,512]{1,0:T(8,128)(2,1)S(1)}, bf16[224,512]{1,0:T(8,128)(2,1)S(1)}, u32[]{:S(2)}, u32[]{:S(2)}) collective-permute-start(bf16[224,512]{1,0:T(8,128)(2,1)S(1)} %get-tuple-element.336), channel_id=1, source_target_pairs={{0,4},{1,3},{2,6},{3,1},{4,0},{5,7},{6,2},{7,5},{8,12},{9,11},{10,... | collective-permute-start | bytes 688136 | tf_op jit(solution)/shard_map/ppermute | solution.py:895
  53.5 1.3 %collective-permute-done.12.refs_1_ = bf16[224,512]{1,0:T(8,128)(2,1)S(1)} collective-permute-done((bf16[224,512]{1,0:T(8,128)(2,1)S(1)}, bf16[224,512]{1,0:T(8,128)(2,1)S(1)}, u32[]{:S(2)}, u32[]{:S(2)}) %collective-permute-start.12) | collective-permute-done | bytes 229408 | tf_op jit(solution)/shard_map/ppermute | solution.py:895
  54.8 2.7 %collective-permute-start.16 = (bf16[224,512]{1,0:T(8,128)(2,1)S(1)}, bf16[224,512]{1,0:T(8,128)(2,1)S(1)}, u32[]{:S(2)}, u32[]{:S(2)}) collective-permute-start(bf16[224,512]{1,0:T(8,128)(2,1)S(1)} %get-tuple-element.341.refs_0_), channel_id=1, source_target_pairs={{0,8},{1,9},{2,10},{3,11},{4,12},{5,13},{6,14},{7,15},{8,0},{9,1},... | collective-permute-start | bytes 688136 | tf_op jit(solution)/shard_map/ppermute | solution.py:895
  57.5 3.3 %collective-permute-done.13.refs_1_ = bf16[448,512]{1,0:T(8,128)(2,1)S(1)} collective-permute-done((bf16[448,512]{1,0:T(8,128)(2,1)S(1)}, bf16[448,512]{1,0:T(8,128)(2,1)S(1)}, u32[]{:S(2)}, u32[]{:S(2)}) %collective-permute-start.13) | collective-permute-done | bytes 458784 | tf_op jit(solution)/shard_map/ppermute | solution.py:895
  60.9 2.4 %collective-permute-start.17 = (bf16[224,512]{1,0:T(8,128)(2,1)S(1)}, bf16[224,512]{1,0:T(8,128)(2,1)S(1)}, u32[]{:S(2)}, u32[]{:S(2)}) collective-permute-start(bf16[224,512]{1,0:T(8,128)(2,1)S(1)} %get-tuple-element.351), channel_id=1, source_target_pairs={{0,4},{1,3},{2,6},{3,1},{4,0},{5,7},{6,2},{7,5},{8,12},{9,11},{10,... | collective-permute-start | bytes 688136 | tf_op jit(solution)/shard_map/ppermute | solution.py:895
  63.3 5.5 %collective-permute-done.14.refs_1_ = bf16[224,512]{1,0:T(8,128)(2,1)S(1)} collective-permute-done((bf16[224,512]{1,0:T(8,128)(2,1)S(1)}, bf16[224,512]{1,0:T(8,128)(2,1)S(1)}, u32[]{:S(2)}, u32[]{:S(2)}) %collective-permute-start.14) | collective-permute-done | bytes 229408 | tf_op jit(solution)/shard_map/ppermute | solution.py:895
  68.8 1.9 %collective-permute-start.18 = (bf16[224,512]{1,0:T(8,128)(2,1)S(1)}, bf16[224,512]{1,0:T(8,128)(2,1)S(1)}, u32[]{:S(2)}, u32[]{:S(2)}) collective-permute-start(bf16[224,512]{1,0:T(8,128)(2,1)S(1)} %get-tuple-element.353.refs_0_), channel_id=1, source_target_pairs={{0,8},{1,9},{2,10},{3,11},{4,12},{5,13},{6,14},{7,15},{8,0},{9,1},... | collective-permute-start | bytes 688136 | tf_op jit(solution)/shard_map/ppermute | solution.py:895
  70.9 2.5 %collective-permute-start.20 = (bf16[224,512]{1,0:T(8,128)(2,1)S(1)}, bf16[224,512]{1,0:T(8,128)(2,1)S(1)}, u32[]{:S(2)}, u32[]{:S(2)}) collective-permute-start(bf16[224,512]{1,0:T(8,128)(2,1)S(1)} %get-tuple-element.358.refs_0_), channel_id=1, source_target_pairs={{0,4},{1,3},{2,6},{3,1},{4,0},{5,7},{6,2},{7,5},{8,12},{9,11},{10,... | collective-permute-start | bytes 688136 | tf_op jit(solution)/shard_map/ppermute | solution.py:895
  73.5 2.0 %collective-permute-start.19 = (bf16[224,512]{1,0:T(8,128)(2,1)S(1)}, bf16[224,512]{1,0:T(8,128)(2,1)S(1)}, u32[]{:S(2)}, u32[]{:S(2)}) collective-permute-start(bf16[224,512]{1,0:T(8,128)(2,1)S(1)} %get-tuple-element.356), channel_id=1, source_target_pairs={{0,2},{1,5},{2,0},{3,7},{4,6},{5,1},{6,4},{7,3},{8,10},{9,13},{10,... | collective-permute-start | bytes 688136 | tf_op jit(solution)/shard_map/ppermute | solution.py:895
  75.4 1.6 %final_stage.1 = (f32[8,128]{1,0:T(8,128)S(1)}, bf16[1,256,512]{2,1,0:T(8,128)(2,1)}, bf16[1,256,512]{2,1,0:T(8,128)(2,1)}) custom-call(s32[4]{0:T(128)S(4)} %get-tuple-element.206.place_ref, f32[8,128]{1,0:T(8,128)S(1)} %get-tuple-element.342.token_in, f32[256,512]{1,0:T(8,128)S(1)} %get-tuple-element.343.refs_0_, ...), custom_call_target="tpu_custom_call" | custom-call | flops 1000000000 | tf_op jit(solution)/shard_map/final_stage/pallas_call | solution.py:239
  77.1 1.8 %collective-permute-start.21 = (bf16[224,512]{1,0:T(8,128)(2,1)S(1)}, bf16[224,512]{1,0:T(8,128)(2,1)S(1)}, u32[]{:S(2)}, u32[]{:S(2)}) collective-permute-start(bf16[224,512]{1,0:T(8,128)(2,1)S(1)} %get-tuple-element.360.refs_0_), channel_id=1, source_target_pairs={{0,8},{1,9},{2,10},{3,11},{4,12},{5,13},{6,14},{7,15},{8,0},{9,1},... | collective-permute-start | bytes 688136 | tf_op jit(solution)/shard_map/ppermute | solution.py:895
  78.8 4.5 %collective-permute-done.18.refs_1_ = bf16[224,512]{1,0:T(8,128)(2,1)S(1)} collective-permute-done((bf16[224,512]{1,0:T(8,128)(2,1)S(1)}, bf16[224,512]{1,0:T(8,128)(2,1)S(1)}, u32[]{:S(2)}, u32[]{:S(2)}) %collective-permute-start.18) | collective-permute-done | bytes 229408 | tf_op jit(solution)/shard_map/ppermute | solution.py:895
  83.6 1.8 %collective-permute-start.24 = (bf16[448,512]{1,0:T(8,128)(2,1)S(1)}, bf16[448,512]{1,0:T(8,128)(2,1)S(1)}, u32[]{:S(2)}, u32[]{:S(2)}) collective-permute-start(bf16[448,512]{1,0:T(8,128)(2,1)S(1)} %get-tuple-element.366.refs_0_), channel_id=1, source_target_pairs={{0,2},{1,5},{2,0},{3,7},{4,6},{5,1},{6,4},{7,3},{8,10},{9,13},{10,... | collective-permute-start | bytes 1376264 | tf_op jit(solution)/shard_map/ppermute | solution.py:895
  85.3 1.6 %collective-permute-start.22 = (bf16[224,512]{1,0:T(8,128)(2,1)S(1)}, bf16[224,512]{1,0:T(8,128)(2,1)S(1)}, u32[]{:S(2)}, u32[]{:S(2)}) collective-permute-start(bf16[224,512]{1,0:T(8,128)(2,1)S(1)} %get-tuple-element.362.refs_0_), channel_id=1, source_target_pairs={{0,4},{1,3},{2,6},{3,1},{4,0},{5,7},{6,2},{7,5},{8,12},{9,11},{10,... | collective-permute-start | bytes 688136 | tf_op jit(solution)/shard_map/ppermute | solution.py:895
  86.9 5.0 %collective-permute-start.23 = (bf16[224,512]{1,0:T(8,128)(2,1)S(1)}, bf16[224,512]{1,0:T(8,128)(2,1)S(1)}, u32[]{:S(2)}, u32[]{:S(2)}) collective-permute-start(bf16[224,512]{1,0:T(8,128)(2,1)S(1)} %get-tuple-element.364.refs_0_), channel_id=1, source_target_pairs={{0,8},{1,9},{2,10},{3,11},{4,12},{5,13},{6,14},{7,15},{8,0},{9,1},... | collective-permute-start | bytes 688136 | tf_op jit(solution)/shard_map/ppermute | solution.py:895
  92.1 6.3 %collective-permute-done.22.refs_1_ = bf16[224,512]{1,0:T(8,128)(2,1)S(1)} collective-permute-done((bf16[224,512]{1,0:T(8,128)(2,1)S(1)}, bf16[224,512]{1,0:T(8,128)(2,1)S(1)}, u32[]{:S(2)}, u32[]{:S(2)}) %collective-permute-start.22) | collective-permute-done | bytes 229408 | tf_op jit(solution)/shard_map/ppermute | solution.py:895
  98.5 2.5 %collective-permute-done.23.refs_1_ = bf16[224,512]{1,0:T(8,128)(2,1)S(1)} collective-permute-done((bf16[224,512]{1,0:T(8,128)(2,1)S(1)}, bf16[224,512]{1,0:T(8,128)(2,1)S(1)}, u32[]{:S(2)}, u32[]{:S(2)}) %collective-permute-start.23) | collective-permute-done | bytes 229408 | tf_op jit(solution)/shard_map/ppermute | solution.py:895
  101.1 2.0 %collective-permute-start.26 = (bf16[448,512]{1,0:T(8,128)(2,1)S(1)}, bf16[448,512]{1,0:T(8,128)(2,1)S(1)}, u32[]{:S(2)}, u32[]{:S(2)}) collective-permute-start(bf16[448,512]{1,0:T(8,128)(2,1)S(1)} %get-tuple-element.372.refs_0_), channel_id=1, source_target_pairs={{0,2},{1,5},{2,0},{3,7},{4,6},{5,1},{6,4},{7,3},{8,10},{9,13},{10,... | collective-permute-start | bytes 1376264 | tf_op jit(solution)/shard_map/ppermute | solution.py:895
  103.2 0.1 collective-permute-start.29
  103.4 1.3 %unpack_1.4 = (f32[8,128]{1,0:T(8,128)S(1)}, f32[1,2048,512]{2,1,0:T(8,128)}) custom-call(s32[4]{0:T(128)S(4)} %get-tuple-element.206.place_ref, f32[8,128]{1,0:T(8,128)S(1)} %get-tuple-element.369.token_in, bf16[896,512]{1,0:T(8,128)(2,1)S(1)} %get-tuple-element.370.refs_0_), custom_call_target="tpu_custom_call" | custom-call | flops 8000000000 | tf_op jit(solution)/shard_map/unpack_1/pallas_call | solution.py:239
  104.7 7.3 %collective-permute-done.26.refs_1_ = bf16[448,512]{1,0:T(8,128)(2,1)S(1)} collective-permute-done((bf16[448,512]{1,0:T(8,128)(2,1)S(1)}, bf16[448,512]{1,0:T(8,128)(2,1)S(1)}, u32[]{:S(2)}, u32[]{:S(2)}) %collective-permute-start.26) | collective-permute-done | bytes 458784 | tf_op jit(solution)/shard_map/ppermute | solution.py:895
  112.2 1.3 %unpack_1.5 = (f32[8,128]{1,0:T(8,128)S(1)}, f32[1,512,1024]{2,1,0:T(8,128)}, f32[1,512,512]{2,1,0:T(8,128)}, f32[1,512,2048]{2,1,0:T(8,128)}, f32[1,2048,512]{2,1,0:T(8,128)}) custom-call(s32[4]{0:T(128)S(4)} %get-tuple-element.206.place_ref, f32[8,128]{1,0:T(8,128)S(1)} %get-tuple-element.373.token_in, ...), custom_call_target="tpu_custom_call", output_to_operand_aliasing={{4}: (3, {})} | custom-call | flops 8000000000 | tf_op jit(solution)/shard_map/unpack_1/pallas_call | solution.py:239
  113.5 0.4 collective-permute-start.31
  113.9 1.3 %unpack_0.4 = (f32[8,128]{1,0:T(8,128)S(1)}, f32[1,2048,512]{2,1,0:T(8,128)}) custom-call(s32[4]{0:T(128)S(4)} %get-tuple-element.206.place_ref, f32[8,128]{1,0:T(8,128)S(1)} %get-tuple-element.378.token_in, bf16[896,512]{1,0:T(8,128)(2,1)S(1)} %collective-permute-done.28.refs_0_, ...), custom_call_target="tpu_custom_call", output_to_operand_aliasing={{1}: (3, {})} | custom-call | flops 1000000000 | tf_op jit(solution)/shard_map/unpack_0/pallas_call | solution.py:239
  115.2 1.9 %collective-permute-done.29.refs_1_ = bf16[448,512]{1,0:T(8,128)(2,1)S(1)} collective-permute-done((bf16[448,512]{1,0:T(8,128)(2,1)S(1)}, bf16[448,512]{1,0:T(8,128)(2,1)S(1)}, u32[]{:S(2)}, u32[]{:S(2)}) %collective-permute-start.29) | collective-permute-done | bytes 458784 | tf_op jit(solution)/shard_map/ppermute | solution.py:895
  117.3 1.3 %unpack_0.5 = (f32[8,128]{1,0:T(8,128)S(1)}, f32[1,512,1024]{2,1,0:T(8,128)}, f32[1,512,512]{2,1,0:T(8,128)}, f32[1,2048,512]{2,1,0:T(8,128)}, f32[1,512,2048]{2,1,0:T(8,128)}) custom-call(s32[4]{0:T(128)S(4)} %get-tuple-element.206.place_ref, ...), custom_call_target="tpu_custom_call", output_to_operand_aliasing={{1}: (3, {}), {2}: (4, {}), {3}: (5, {}), {4}: (6, {})} | custom-call | flops 1000000000 | tf_op jit(solution)/shard_map/unpack_0/pallas_call | solution.py:239
  118.6 1.3 %unpack_1.6 = (f32[8,128]{1,0:T(8,128)S(1)}, f32[1,512,2048]{2,1,0:T(8,128)}) custom-call(s32[4]{0:T(128)S(4)} %get-tuple-element.206.place_ref, f32[8,128]{1,0:T(8,128)S(1)} %get-tuple-element.387.token_in, bf16[896,512]{1,0:T(8,128)(2,1)S(1)} %get-tuple-element.388.refs_0_, f32[1,512,2048]{2,1,0:T(8,128)} %get-tuple-element.389.refs_1_), custom_call_target="tpu_custom_call", output_to_operand_aliasing={{1}: (3, {})} | custom-call | flops 1000000000 | tf_op jit(solution)/shard_map/unpack_1/pallas_call | solution.py:239
  119.9 2.2 %collective-permute-done.31.refs_1_ = bf16[448,512]{1,0:T(8,128)(2,1)S(1)} collective-permute-done((bf16[448,512]{1,0:T(8,128)(2,1)S(1)}, bf16[448,512]{1,0:T(8,128)(2,1)S(1)}, u32[]{:S(2)}, u32[]{:S(2)}) %collective-permute-start.31) | collective-permute-done | bytes 458784 | tf_op jit(solution)/shard_map/ppermute | solution.py:895
  122.2 1.3 %unpack_0.6 = (f32[8,128]{1,0:T(8,128)S(1)}, f32[1,512,2048]{2,1,0:T(8,128)}) custom-call(s32[4]{0:T(128)S(4)} %get-tuple-element.206.place_ref, f32[8,128]{1,0:T(8,128)S(1)} %get-tuple-element.392.token_in, bf16[896,512]{1,0:T(8,128)(2,1)S(1)} %collective-permute-done.32.refs_0_, ...), custom_call_target="tpu_custom_call", output_to_operand_aliasing={{1}: (3, {})} | custom-call | flops 3000000000 | tf_op jit(solution)/shard_map/unpack_0/pallas_call | solution.py:239
  123.5 1.3 %unpack_1.7 = (f32[8,128]{1,0:T(8,128)S(1)}, f32[1,512,1536]{2,1,0:T(8,128)}, f32[1,512,512]{2,1,0:T(8,128)}) custom-call(s32[4]{0:T(128)S(4)} %get-tuple-element.206.place_ref, f32[8,128]{1,0:T(8,128)S(1)} %get-tuple-element.394.token_in, bf16[896,512]{1,0:T(8,128)(2,1)S(1)} %get-tuple-element.395.refs_0_, ...), custom_call_target="tpu_custom_call", output_to_operand_aliasing={{2}: (3, {})} | custom-call | flops 1000000000 | tf_op jit(solution)/shard_map/unpack_1/pallas_call | solution.py:239
  124.9 1.9 %unpack_0.7 = (f32[8,128]{1,0:T(8,128)}, f32[1,512,1536]{2,1,0:T(8,128)}, f32[1,512,512]{2,1,0:T(8,128)}) custom-call(s32[4]{0:T(128)S(4)} %get-tuple-element.206.place_ref, f32[8,128]{1,0:T(8,128)S(1)} %get-tuple-element.397.token_in, bf16[896,512]{1,0:T(8,128)(2,1)S(1)} %collective-permute-done.33.refs_0_, ...), custom_call_target="tpu_custom_call", output_to_operand_aliasing={{1}: (3, {}), {2}: (4, {})} | custom-call | flops 1000000000 | tf_op jit(solution)/shard_map/unpack_0/pallas_call | solution.py:239
  (48 shorter events, 1.9 us)
Async XLA Ops:
  5.0 8.0 %collective-permute-start = (bf16[128,1024]{1,0:T(8,128)(2,1)S(1)}, bf16[128,1024]{1,0:T(8,128)(2,1)S(1)}, u32[]{:S(2)}, u32[]{:S(2)}) collective-permute-start(bf16[128,1024]{1,0:T(8,128)(2,1)S(1)} %get-tuple-element.232), channel_id=1, source_target_pairs={{0,16},{1,17},{2,18},{3,19},{4,20},{5,21},{6,22},{7,23},{8,24},{9,... | collective-permute-start | bytes 786440 | tf_op jit(solution)/shard_map/ppermute | solution.py:1072
  9.3 9.0 %collective-permute-start.1 = (bf16[128,1024]{1,0:T(8,128)(2,1)S(1)}, bf16[128,1024]{1,0:T(8,128)(2,1)S(1)}, u32[]{:S(2)}, u32[]{:S(2)}) collective-permute-start(bf16[128,1024]{1,0:T(8,128)(2,1)S(1)} %get-tuple-element.236), channel_id=1, source_target_pairs={{0,16},{1,17},{2,18},{3,19},{4,20},{5,21},{6,22},{7,23},{8,24},{9,... | collective-permute-start | bytes 786440 | tf_op jit(solution)/shard_map/ppermute | solution.py:1074
  13.6 13.9 %collective-permute-start.2 = (bf16[256,512]{1,0:T(8,128)(2,1)S(1)}, bf16[256,512]{1,0:T(8,128)(2,1)S(1)}, u32[]{:S(2)}, u32[]{:S(2)}) collective-permute-start(bf16[256,512]{1,0:T(8,128)(2,1)S(1)} %get-tuple-element.255), channel_id=1, source_target_pairs={{16,0},{17,1},{18,2},{19,3},{20,4},{21,5},{22,6},{23,7},{24,8},{25... | collective-permute-start | bytes 786440 | tf_op jit(solution)/shard_map/ppermute | solution.py:1077
  19.0 11.4 %collective-permute-start.3 = (bf16[128,512]{1,0:T(8,128)(2,1)S(1)}, bf16[128,512]{1,0:T(8,128)(2,1)S(1)}, u32[]{:S(2)}, u32[]{:S(2)}) collective-permute-start(bf16[128,512]{1,0:T(8,128)(2,1)S(1)} %get-tuple-element.268), channel_id=1, source_target_pairs={{16,0},{17,1},{18,2},{19,3},{20,4},{21,5},{22,6},{23,7},{24,8},{25... | collective-permute-start | bytes 393224 | tf_op jit(solution)/shard_map/ppermute | solution.py:1077
  20.3 12.2 %collective-permute-start.4 = (bf16[128,512]{1,0:T(8,128)(2,1)S(1)}, bf16[128,512]{1,0:T(8,128)(2,1)S(1)}, u32[]{:S(2)}, u32[]{:S(2)}) collective-permute-start(bf16[128,512]{1,0:T(8,128)(2,1)S(1)} %get-tuple-element.279), channel_id=1, source_target_pairs={{16,0},{17,1},{18,2},{19,3},{20,4},{21,5},{22,6},{23,7},{24,8},{25... | collective-permute-start | bytes 393224 | tf_op jit(solution)/shard_map/ppermute | solution.py:1077
  33.3 2.7 %collective-permute-start.5 = (bf16[896,512]{1,0:T(8,128)(2,1)S(1)}, bf16[896,512]{1,0:T(8,128)(2,1)S(1)}, u32[]{:S(2)}, u32[]{:S(2)}) collective-permute-start(bf16[896,512]{1,0:T(8,128)(2,1)S(1)} %get-tuple-element.300), channel_id=1, source_target_pairs={{0,1},{1,0},{2,3},{3,2},{4,5},{5,4},{6,7},{7,6},{8,9},{9,8},{10,11... | collective-permute-start | bytes 2752520 | tf_op jit(solution)/shard_map/ppermute | solution.py:895
  35.4 3.5 %collective-permute-start.6 = (bf16[896,512]{1,0:T(8,128)(2,1)S(1)}, bf16[896,512]{1,0:T(8,128)(2,1)S(1)}, u32[]{:S(2)}, u32[]{:S(2)}) collective-permute-start(bf16[896,512]{1,0:T(8,128)(2,1)S(1)} %get-tuple-element.306), channel_id=1, source_target_pairs={{0,1},{1,0},{2,3},{3,2},{4,5},{5,4},{6,7},{7,6},{8,9},{9,8},{10,11... | collective-permute-start | bytes 2752520 | tf_op jit(solution)/shard_map/ppermute | solution.py:895
  36.5 9.5 %collective-permute-start.8 = (bf16[448,512]{1,0:T(8,128)(2,1)S(1)}, bf16[448,512]{1,0:T(8,128)(2,1)S(1)}, u32[]{:S(2)}, u32[]{:S(2)}) collective-permute-start(bf16[448,512]{1,0:T(8,128)(2,1)S(1)} %get-tuple-element.319), channel_id=1, source_target_pairs={{0,2},{1,5},{2,0},{3,7},{4,6},{5,1},{6,4},{7,3},{8,10},{9,13},{10,... | collective-permute-start | bytes 1376264 | tf_op jit(solution)/shard_map/ppermute | solution.py:895
  38.8 5.8 %collective-permute-start.7 = (bf16[896,512]{1,0:T(8,128)(2,1)S(1)}, bf16[896,512]{1,0:T(8,128)(2,1)S(1)}, u32[]{:S(2)}, u32[]{:S(2)}) collective-permute-start(bf16[896,512]{1,0:T(8,128)(2,1)S(1)} %get-tuple-element.316), channel_id=1, source_target_pairs={{0,1},{1,0},{2,3},{3,2},{4,5},{5,4},{6,7},{7,6},{8,9},{9,8},{10,11... | collective-permute-start | bytes 2752520 | tf_op jit(solution)/shard_map/ppermute | solution.py:895
  39.5 11.5 %collective-permute-start.11 = (bf16[448,512]{1,0:T(8,128)(2,1)S(1)}, bf16[448,512]{1,0:T(8,128)(2,1)S(1)}, u32[]{:S(2)}, u32[]{:S(2)}) collective-permute-start(bf16[448,512]{1,0:T(8,128)(2,1)S(1)} %get-tuple-element.327), channel_id=1, source_target_pairs={{0,2},{1,5},{2,0},{3,7},{4,6},{5,1},{6,4},{7,3},{8,10},{9,13},{10,... | collective-permute-start | bytes 1376264 | tf_op jit(solution)/shard_map/ppermute | solution.py:895
  44.0 3.7 %collective-permute-start.9 = (bf16[896,512]{1,0:T(8,128)(2,1)S(1)}, bf16[896,512]{1,0:T(8,128)(2,1)S(1)}, u32[]{:S(2)}, u32[]{:S(2)}) collective-permute-start(bf16[896,512]{1,0:T(8,128)(2,1)S(1)} %get-tuple-element.321), channel_id=1, source_target_pairs={{0,1},{1,0},{2,3},{3,2},{4,5},{5,4},{6,7},{7,6},{8,9},{9,8},{10,11... | collective-permute-start | bytes 2752520 | tf_op jit(solution)/shard_map/ppermute | solution.py:895
  44.5 3.4 %collective-permute-start.10 = (bf16[896,512]{1,0:T(8,128)(2,1)S(1)}, bf16[896,512]{1,0:T(8,128)(2,1)S(1)}, u32[]{:S(2)}, u32[]{:S(2)}) collective-permute-start(bf16[896,512]{1,0:T(8,128)(2,1)S(1)} %get-tuple-element.322), channel_id=1, source_target_pairs={{0,1},{1,0},{2,3},{3,2},{4,5},{5,4},{6,7},{7,6},{8,9},{9,8},{10,11... | collective-permute-start | bytes 2752520 | tf_op jit(solution)/shard_map/ppermute | solution.py:895
  45.2 15.6 %collective-permute-start.13 = (bf16[448,512]{1,0:T(8,128)(2,1)S(1)}, bf16[448,512]{1,0:T(8,128)(2,1)S(1)}, u32[]{:S(2)}, u32[]{:S(2)}) collective-permute-start(bf16[448,512]{1,0:T(8,128)(2,1)S(1)} %get-tuple-element.333), channel_id=1, source_target_pairs={{0,2},{1,5},{2,0},{3,7},{4,6},{5,1},{6,4},{7,3},{8,10},{9,13},{10,... | collective-permute-start | bytes 1376264 | tf_op jit(solution)/shard_map/ppermute | solution.py:895
  46.2 8.6 %collective-permute-start.12 = (bf16[224,512]{1,0:T(8,128)(2,1)S(1)}, bf16[224,512]{1,0:T(8,128)(2,1)S(1)}, u32[]{:S(2)}, u32[]{:S(2)}) collective-permute-start(bf16[224,512]{1,0:T(8,128)(2,1)S(1)} %get-tuple-element.330), channel_id=1, source_target_pairs={{0,4},{1,3},{2,6},{3,1},{4,0},{5,7},{6,2},{7,5},{8,12},{9,11},{10,... | collective-permute-start | bytes 688136 | tf_op jit(solution)/shard_map/ppermute | solution.py:895
  48.7 22.1 %collective-permute-start.15 = (bf16[448,512]{1,0:T(8,128)(2,1)S(1)}, bf16[448,512]{1,0:T(8,128)(2,1)S(1)}, u32[]{:S(2)}, u32[]{:S(2)}) collective-permute-start(bf16[448,512]{1,0:T(8,128)(2,1)S(1)} %get-tuple-element.339), channel_id=1, source_target_pairs={{0,4},{1,3},{2,6},{3,1},{4,0},{5,7},{6,2},{7,5},{8,12},{9,11},{10,... | collective-permute-start | bytes 1376264 | tf_op jit(solution)/shard_map/ppermute | solution.py:895
  51.1 17.7 %collective-permute-start.14 = (bf16[224,512]{1,0:T(8,128)(2,1)S(1)}, bf16[224,512]{1,0:T(8,128)(2,1)S(1)}, u32[]{:S(2)}, u32[]{:S(2)}) collective-permute-start(bf16[224,512]{1,0:T(8,128)(2,1)S(1)} %get-tuple-element.336), channel_id=1, source_target_pairs={{0,4},{1,3},{2,6},{3,1},{4,0},{5,7},{6,2},{7,5},{8,12},{9,11},{10,... | collective-permute-start | bytes 688136 | tf_op jit(solution)/shard_map/ppermute | solution.py:895
  54.8 16.0 %collective-permute-start.16 = (bf16[224,512]{1,0:T(8,128)(2,1)S(1)}, bf16[224,512]{1,0:T(8,128)(2,1)S(1)}, u32[]{:S(2)}, u32[]{:S(2)}) collective-permute-start(bf16[224,512]{1,0:T(8,128)(2,1)S(1)} %get-tuple-element.341.refs_0_), channel_id=1, source_target_pairs={{0,8},{1,9},{2,10},{3,11},{4,12},{5,13},{6,14},{7,15},{8,0},{9,1},... | collective-permute-start | bytes 688136 | tf_op jit(solution)/shard_map/ppermute | solution.py:895
  60.9 16.1 %collective-permute-start.17 = (bf16[224,512]{1,0:T(8,128)(2,1)S(1)}, bf16[224,512]{1,0:T(8,128)(2,1)S(1)}, u32[]{:S(2)}, u32[]{:S(2)}) collective-permute-start(bf16[224,512]{1,0:T(8,128)(2,1)S(1)} %get-tuple-element.351), channel_id=1, source_target_pairs={{0,4},{1,3},{2,6},{3,1},{4,0},{5,7},{6,2},{7,5},{8,12},{9,11},{10,... | collective-permute-start | bytes 688136 | tf_op jit(solution)/shard_map/ppermute | solution.py:895
  68.8 14.5 %collective-permute-start.18 = (bf16[224,512]{1,0:T(8,128)(2,1)S(1)}, bf16[224,512]{1,0:T(8,128)(2,1)S(1)}, u32[]{:S(2)}, u32[]{:S(2)}) collective-permute-start(bf16[224,512]{1,0:T(8,128)(2,1)S(1)} %get-tuple-element.353.refs_0_), channel_id=1, source_target_pairs={{0,8},{1,9},{2,10},{3,11},{4,12},{5,13},{6,14},{7,15},{8,0},{9,1},... | collective-permute-start | bytes 688136 | tf_op jit(solution)/shard_map/ppermute | solution.py:895
  70.9 12.6 %collective-permute-start.20 = (bf16[224,512]{1,0:T(8,128)(2,1)S(1)}, bf16[224,512]{1,0:T(8,128)(2,1)S(1)}, u32[]{:S(2)}, u32[]{:S(2)}) collective-permute-start(bf16[224,512]{1,0:T(8,128)(2,1)S(1)} %get-tuple-element.358.refs_0_), channel_id=1, source_target_pairs={{0,4},{1,3},{2,6},{3,1},{4,0},{5,7},{6,2},{7,5},{8,12},{9,11},{10,... | collective-permute-start | bytes 688136 | tf_op jit(solution)/shard_map/ppermute | solution.py:895
  73.5 10.0 %collective-permute-start.19 = (bf16[224,512]{1,0:T(8,128)(2,1)S(1)}, bf16[224,512]{1,0:T(8,128)(2,1)S(1)}, u32[]{:S(2)}, u32[]{:S(2)}) collective-permute-start(bf16[224,512]{1,0:T(8,128)(2,1)S(1)} %get-tuple-element.356), channel_id=1, source_target_pairs={{0,2},{1,5},{2,0},{3,7},{4,6},{5,1},{6,4},{7,3},{8,10},{9,13},{10,... | collective-permute-start | bytes 688136 | tf_op jit(solution)/shard_map/ppermute | solution.py:895
  77.1 14.9 %collective-permute-start.21 = (bf16[224,512]{1,0:T(8,128)(2,1)S(1)}, bf16[224,512]{1,0:T(8,128)(2,1)S(1)}, u32[]{:S(2)}, u32[]{:S(2)}) collective-permute-start(bf16[224,512]{1,0:T(8,128)(2,1)S(1)} %get-tuple-element.360.refs_0_), channel_id=1, source_target_pairs={{0,8},{1,9},{2,10},{3,11},{4,12},{5,13},{6,14},{7,15},{8,0},{9,1},... | collective-permute-start | bytes 688136 | tf_op jit(solution)/shard_map/ppermute | solution.py:895
  83.6 19.6 %collective-permute-start.24 = (bf16[448,512]{1,0:T(8,128)(2,1)S(1)}, bf16[448,512]{1,0:T(8,128)(2,1)S(1)}, u32[]{:S(2)}, u32[]{:S(2)}) collective-permute-start(bf16[448,512]{1,0:T(8,128)(2,1)S(1)} %get-tuple-element.366.refs_0_), channel_id=1, source_target_pairs={{0,2},{1,5},{2,0},{3,7},{4,6},{5,1},{6,4},{7,3},{8,10},{9,13},{10,... | collective-permute-start | bytes 1376264 | tf_op jit(solution)/shard_map/ppermute | solution.py:895
  85.3 13.1 %collective-permute-start.22 = (bf16[224,512]{1,0:T(8,128)(2,1)S(1)}, bf16[224,512]{1,0:T(8,128)(2,1)S(1)}, u32[]{:S(2)}, u32[]{:S(2)}) collective-permute-start(bf16[224,512]{1,0:T(8,128)(2,1)S(1)} %get-tuple-element.362.refs_0_), channel_id=1, source_target_pairs={{0,4},{1,3},{2,6},{3,1},{4,0},{5,7},{6,2},{7,5},{8,12},{9,11},{10,... | collective-permute-start | bytes 688136 | tf_op jit(solution)/shard_map/ppermute | solution.py:895
  86.9 14.0 %collective-permute-start.23 = (bf16[224,512]{1,0:T(8,128)(2,1)S(1)}, bf16[224,512]{1,0:T(8,128)(2,1)S(1)}, u32[]{:S(2)}, u32[]{:S(2)}) collective-permute-start(bf16[224,512]{1,0:T(8,128)(2,1)S(1)} %get-tuple-element.364.refs_0_), channel_id=1, source_target_pairs={{0,8},{1,9},{2,10},{3,11},{4,12},{5,13},{6,14},{7,15},{8,0},{9,1},... | collective-permute-start | bytes 688136 | tf_op jit(solution)/shard_map/ppermute | solution.py:895
  92.0 11.2 %collective-permute-start.25 = (bf16[224,512]{1,0:T(8,128)(2,1)S(1)}, bf16[224,512]{1,0:T(8,128)(2,1)S(1)}, u32[]{:S(2)}, u32[]{:S(2)}) collective-permute-start(bf16[224,512]{1,0:T(8,128)(2,1)S(1)} %get-tuple-element.368.refs_0_), channel_id=1, source_target_pairs={{0,4},{1,3},{2,6},{3,1},{4,0},{5,7},{6,2},{7,5},{8,12},{9,11},{10,... | collective-permute-start | bytes 688136 | tf_op jit(solution)/shard_map/ppermute | solution.py:895
  101.0 12.5 %collective-permute-start.27 = (bf16[224,512]{1,0:T(8,128)(2,1)S(1)}, bf16[224,512]{1,0:T(8,128)(2,1)S(1)}, u32[]{:S(2)}, u32[]{:S(2)}) collective-permute-start(bf16[224,512]{1,0:T(8,128)(2,1)S(1)} %get-tuple-element.377.refs_0_), channel_id=1, source_target_pairs={{0,2},{1,5},{2,0},{3,7},{4,6},{5,1},{6,4},{7,3},{8,10},{9,13},{10,... | collective-permute-start | bytes 688136 | tf_op jit(solution)/shard_map/ppermute | solution.py:895
  101.1 10.9 %collective-permute-start.26 = (bf16[448,512]{1,0:T(8,128)(2,1)S(1)}, bf16[448,512]{1,0:T(8,128)(2,1)S(1)}, u32[]{:S(2)}, u32[]{:S(2)}) collective-permute-start(bf16[448,512]{1,0:T(8,128)(2,1)S(1)} %get-tuple-element.372.refs_0_), channel_id=1, source_target_pairs={{0,2},{1,5},{2,0},{3,7},{4,6},{5,1},{6,4},{7,3},{8,10},{9,13},{10,... | collective-permute-start | bytes 1376264 | tf_op jit(solution)/shard_map/ppermute | solution.py:895
  103.2 13.9 %collective-permute-start.29 = (bf16[448,512]{1,0:T(8,128)(2,1)S(1)}, bf16[448,512]{1,0:T(8,128)(2,1)S(1)}, u32[]{:S(2)}, u32[]{:S(2)}) collective-permute-start(bf16[448,512]{1,0:T(8,128)(2,1)S(1)} %get-tuple-element.381.refs_0_), channel_id=1, source_target_pairs={{0,2},{1,5},{2,0},{3,7},{4,6},{5,1},{6,4},{7,3},{8,10},{9,13},{10,... | collective-permute-start | bytes 1376264 | tf_op jit(solution)/shard_map/ppermute | solution.py:895
  103.4 10.5 %collective-permute-start.28 = (bf16[896,512]{1,0:T(8,128)(2,1)S(1)}, bf16[896,512]{1,0:T(8,128)(2,1)S(1)}, u32[]{:S(2)}, u32[]{:S(2)}) collective-permute-start(bf16[896,512]{1,0:T(8,128)(2,1)S(1)} %get-tuple-element.370.refs_0_), channel_id=1, source_target_pairs={{0,1},{1,0},{2,3},{3,2},{4,5},{5,4},{6,7},{7,6},{8,9},{9,8},{10,11... | collective-permute-start | bytes 2752520 | tf_op jit(solution)/shard_map/ppermute | solution.py:895
  112.1 5.2 %collective-permute-start.30 = (bf16[896,512]{1,0:T(8,128)(2,1)S(1)}, bf16[896,512]{1,0:T(8,128)(2,1)S(1)}, u32[]{:S(2)}, u32[]{:S(2)}) collective-permute-start(bf16[896,512]{1,0:T(8,128)(2,1)S(1)} %get-tuple-element.374.refs_0_), channel_id=1, source_target_pairs={{0,1},{1,0},{2,3},{3,2},{4,5},{5,4},{6,7},{7,6},{8,9},{9,8},{10,11... | collective-permute-start | bytes 2752520 | tf_op jit(solution)/shard_map/ppermute | solution.py:895
  113.5 8.5 %collective-permute-start.31 = (bf16[448,512]{1,0:T(8,128)(2,1)S(1)}, bf16[448,512]{1,0:T(8,128)(2,1)S(1)}, u32[]{:S(2)}, u32[]{:S(2)}) collective-permute-start(bf16[448,512]{1,0:T(8,128)(2,1)S(1)} %get-tuple-element.391.refs_0_), channel_id=1, source_target_pairs={{0,4},{1,3},{2,6},{3,1},{4,0},{5,7},{6,2},{7,5},{8,12},{9,11},{10,... | collective-permute-start | bytes 1376264 | tf_op jit(solution)/shard_map/ppermute | solution.py:895
  117.2 5.1 %collective-permute-start.32 = (bf16[896,512]{1,0:T(8,128)(2,1)S(1)}, bf16[896,512]{1,0:T(8,128)(2,1)S(1)}, u32[]{:S(2)}, u32[]{:S(2)}) collective-permute-start(bf16[896,512]{1,0:T(8,128)(2,1)S(1)} %get-tuple-element.388.refs_0_), channel_id=1, source_target_pairs={{0,1},{1,0},{2,3},{3,2},{4,5},{5,4},{6,7},{7,6},{8,9},{9,8},{10,11... | collective-permute-start | bytes 2752520 | tf_op jit(solution)/shard_map/ppermute | solution.py:895
  122.2 2.7 %collective-permute-start.33 = (bf16[896,512]{1,0:T(8,128)(2,1)S(1)}, bf16[896,512]{1,0:T(8,128)(2,1)S(1)}, u32[]{:S(2)}, u32[]{:S(2)}) collective-permute-start(bf16[896,512]{1,0:T(8,128)(2,1)S(1)} %get-tuple-element.395.refs_0_), channel_id=1, source_target_pairs={{0,1},{1,0},{2,3},{3,2},{4,5},{5,4},{6,7},{7,6},{8,9},{9,8},{10,11... | collective-permute-start | bytes 2752520 | tf_op jit(solution)/shard_map/ppermute | solution.py:895

commit v7 on v6

--- a/solution.py
+++ b/solution.py
@@ -1061,7 +1061,7 @@
 
 CHUNKS = (DOWN, CROSS, UP, QKV)
 GATE, BACK_ATTN, BACK_FFN, FINAL, MORE, OWN = 10, 11, 12, 13, 14, 20
-ORDER = (10, 12, 0, 14, 1, 11, 2, 0, 3, 1, 0, 2, 1, 3, 0, 13, 2, 1, 3, 0, 2, 1, 3, 0, 2, 20, 1, 21, 3, 0, 2, 1, 22, 3, 2, 23, 3)
+ORDER = (10, 12, 0, 14, 1, 11, 2, 0, 3, 1, 0, 2, 13, 1, 3, 0, 2, 1, 3, 0, 2, 1, 3, 0, 2, 20, 1, 21, 3, 0, 2, 1, 22, 3, 2, 23, 3)
 COSTS = (1000, 1000, 8000, 4000, 8000, 8000, 4000, 8000, 1000, 1000, 1000, 1000, 1000, 1000, 1000, 1000, 1000, 1000, 1000, 1000, 1000, 1000, 1000, 1000, 8000, 8000, 1000, 8000, 1000, 1000, 1000, 1000, 1000, 50, 3000, 1000, 1000)
 
 

time: 127 us -> 125 us (0.984)
  waiting for transfers between devices: 49.2 us -> 46.9 us
    ppermute x29, waiting for transfers between devices: 36.2 us -> 33.9 us  [swap(): lax.ppermute(value, 'dp', [(i, partner(i)) for i in range(self.count)])]
where the time goes in v7:
time: 125 us
  waiting for transfers between devices  46.9 us (38%)
  starting transfers between devices  43.2 us (35%)
  Pallas kernels  33.8 us (27%)
    ppermute x29, starting transfers between devices, swap(): lax.ppermute(value, 'dp', [(i, partner(i)) for i in range(self.count)])  35.5 us
    ppermute x29, waiting for transfers between devices, swap(): lax.ppermute(value, 'dp', [(i, partner(i)) for i in range(self.count)])  33.9 us
    pallas_call x42, Pallas kernels, call(): pl.pallas_call(body, out_shape=out_shape, in_specs=[in_smem()] + [in_vmem...  26.4 us
    ppermute x3, waiting for transfers between devices, to_encoder(): return lax.ppermute(side, 'section', [(1, 0)])  8.33 us
    pallas_call x1, Pallas kernels, first_stage(): pl.pallas_call(body, out_shape=shaped(makes) + [pltpu.SMEM((PLACE,), jnp....  4.37 us
    ppermute x3, starting transfers between devices, to_encoder(): return lax.ppermute(side, 'section', [(1, 0)])  3.88 us
    ppermute x1, waiting for transfers between devices, on_device(): links.append(lax.ppermute(link, 'section', [(0, 1)]))  3.5 us
    pallas_call x1, Pallas kernels, second_stage(): pl.pallas_call(body, out_shape=same_shape(keeps) + [pltpu.VMEM((ROWS, 2 *...  3.01 us
  transfers between devices with their start and end apart: 34, of which 16 were waited for; matrix products, arithmetic and copies ran while one was open for 0% of the time, Pallas kernels for 21%

profile of v7, /device:TPU:0, one launch (start us, length us, event | category | flops | bytes accessed | tf_op | source)
XLA Modules:
  0.0 125.1 jit_solution(4847100069899885935)
XLA Ops:
  0.6 4.4 %first_stage.1 = (bf16[512,1536]{1,0:T(8,128)(2,1)S(1)}, bf16[512,512]{1,0:T(8,128)(2,1)S(1)}, bf16[512,1024]{1,0:T(8,128)(2,1)S(1)}, bf16[512,2048]{1,0:T(8,128...) custom-call(s32[2,2,16]{2,1,0:T(2,128)} %refs_0_.3, ...), custom_call_target="tpu_custom_call" | custom-call | flops 939524096 | bytes 10000000 | tf_op jit(solution)/shard_map/first_stage/pallas_call | solution.py:395
  5.0 1.3 %collective-permute-start = (bf16[128,1024]{1,0:T(8,128)(2,1)S(1)}, bf16[128,1024]{1,0:T(8,128)(2,1)S(1)}, u32[]{:S(2)}, u32[]{:S(2)}) collective-permute-start(bf16[128,1024]{1,0:T(8,128)(2,1)S(1)} %get-tuple-element.232), channel_id=1, source_target_pairs={{0,16},{1,17},{2,18},{3,19},{4,20},{5,21},{6,22},{7,23},{8,24},{9,... | collective-permute-start | bytes 786440 | tf_op jit(solution)/shard_map/ppermute | solution.py:1072
  6.3 3.0 %second_stage.1 = (bf16[512,1536]{1,0:T(8,128)(2,1)S(1)}, bf16[512,512]{1,0:T(8,128)(2,1)S(1)}, bf16[512,1024]{1,0:T(8,128)(2,1)S(1)}, bf16[512,2048]{1,0:T(8,12...) custom-call(s32[4]{0:T(128)S(4)} %get-tuple-element.206.place_ref, ...), custom_call_target="tpu_custom_call", output_to_operand_aliasing={{0}: (9, {}), {1}: (10, {}), {2}: (11, {}), {3}: (12, {}), ... | custom-call | flops 939524096 | bytes 10000000 | tf_op jit(solution)/shard_map/second_stage/pallas_call | solution.py:450
  9.3 2.5 %collective-permute-start.1 = (bf16[128,1024]{1,0:T(8,128)(2,1)S(1)}, bf16[128,1024]{1,0:T(8,128)(2,1)S(1)}, u32[]{:S(2)}, u32[]{:S(2)}) collective-permute-start(bf16[128,1024]{1,0:T(8,128)(2,1)S(1)} %get-tuple-element.236), channel_id=1, source_target_pairs={{0,16},{1,17},{2,18},{3,19},{4,20},{5,21},{6,22},{7,23},{8,24},{9,... | collective-permute-start | bytes 786440 | tf_op jit(solution)/shard_map/ppermute | solution.py:1074
  11.8 1.2 collective-permute-done.refs_6_
  13.0 0.6 middle_stage.2
  13.6 1.3 %collective-permute-start.2 = (bf16[256,512]{1,0:T(8,128)(2,1)S(1)}, bf16[256,512]{1,0:T(8,128)(2,1)S(1)}, u32[]{:S(2)}, u32[]{:S(2)}) collective-permute-start(bf16[256,512]{1,0:T(8,128)(2,1)S(1)} %get-tuple-element.255), channel_id=1, source_target_pairs={{16,0},{17,1},{18,2},{19,3},{20,4},{21,5},{22,6},{23,7},{24,8},{25... | collective-permute-start | bytes 786440 | tf_op jit(solution)/shard_map/ppermute | solution.py:1077
  14.9 3.5 %collective-permute-done.1.refs_6_.refs_1_ = bf16[128,1024]{1,0:T(8,128)(2,1)S(1)} collective-permute-done((bf16[128,1024]{1,0:T(8,128)(2,1)S(1)}, bf16[128,1024]{1,0:T(8,128)(2,1)S(1)}, u32[]{:S(2)}, u32[]{:S(2)}) %collective-permute-start.1) | collective-permute-done | bytes 262176 | tf_op jit(solution)/shard_map/ppermute | solution.py:1074
  18.4 0.6 middle_stage.3
  19.0 1.3 %collective-permute-start.3 = (bf16[128,512]{1,0:T(8,128)(2,1)S(1)}, bf16[128,512]{1,0:T(8,128)(2,1)S(1)}, u32[]{:S(2)}, u32[]{:S(2)}) collective-permute-start(bf16[128,512]{1,0:T(8,128)(2,1)S(1)} %get-tuple-element.268), channel_id=1, source_target_pairs={{16,0},{17,1},{18,2},{19,3},{20,4},{21,5},{22,6},{23,7},{24,8},{25... | collective-permute-start | bytes 393224 | tf_op jit(solution)/shard_map/ppermute | solution.py:1077
  20.3 1.3 %collective-permute-start.4 = (bf16[128,512]{1,0:T(8,128)(2,1)S(1)}, bf16[128,512]{1,0:T(8,128)(2,1)S(1)}, u32[]{:S(2)}, u32[]{:S(2)}) collective-permute-start(bf16[128,512]{1,0:T(8,128)(2,1)S(1)} %get-tuple-element.279), channel_id=1, source_target_pairs={{16,0},{17,1},{18,2},{19,3},{20,4},{21,5},{22,6},{23,7},{24,8},{25... | collective-permute-start | bytes 393224 | tf_op jit(solution)/shard_map/ppermute | solution.py:1077
  21.6 5.9 %collective-permute-done.2.refs_6_ = bf16[256,512]{1,0:T(8,128)(2,1)S(1)} collective-permute-done((bf16[256,512]{1,0:T(8,128)(2,1)S(1)}, bf16[256,512]{1,0:T(8,128)(2,1)S(1)}, u32[]{:S(2)}, u32[]{:S(2)}) %collective-permute-start.2) | collective-permute-done | bytes 262176 | tf_op jit(solution)/shard_map/ppermute | solution.py:1077
  27.5 2.3 %back_stage.4 = (f32[256,2048]{1,0:T(8,128)S(1)}, f32[256,512]{1,0:T(8,128)S(1)}, bf16[256,512]{1,0:T(8,128)(2,1)S(1)}, bf16[256,1024]{1,0:T(8,128)(2,1)S(1)}, b...) custom-call(s32[4]{0:T(128)S(4)} %get-tuple-element.206.place_ref, ...), custom_call_target="tpu_custom_call", output_to_operand_aliasing={{0}: (11, {}), {1}: (12, {}), {2}: (13, {}), {3}: (14, {}),... | custom-call | flops 900000000 | tf_op jit(solution)/shard_map/back_stage/pallas_call | solution.py:239
  29.8 0.5 collective-permute-done.3.refs_6_
  30.3 0.3 back_stage.5
  30.6 1.9 %collective-permute-done.4.refs_6_ = bf16[128,512]{1,0:T(8,128)(2,1)S(1)} collective-permute-done((bf16[128,512]{1,0:T(8,128)(2,1)S(1)}, bf16[128,512]{1,0:T(8,128)(2,1)S(1)}, u32[]{:S(2)}, u32[]{:S(2)}) %collective-permute-start.4) | collective-permute-done | bytes 131104 | tf_op jit(solution)/shard_map/ppermute | solution.py:1077
  32.5 0.8 back_stage.6
  33.3 2.1 %back_stage.7 = (f32[256,2048]{1,0:T(8,128)S(1)}, f32[256,512]{1,0:T(8,128)S(1)}, bf16[256,512]{1,0:T(8,128)(2,1)S(1)}, bf16[256,1024]{1,0:T(8,128)(2,1)S(1)}, b...) custom-call(s32[4]{0:T(128)S(4)} %get-tuple-element.206.place_ref, ...), custom_call_target="tpu_custom_call", output_to_operand_aliasing={{0}: (11, {}), {1}: (12, {}), {2}: (13, {}), {3}: (14, {}),... | custom-call | flops 1000000000 | tf_op jit(solution)/shard_map/back_stage/pallas_call | solution.py:239
  35.4 0.5 collective-permute-start.6
  36.0 0.6 sum_0.4
  36.5 1.8 %collective-permute-start.8 = (bf16[448,512]{1,0:T(8,128)(2,1)S(1)}, bf16[448,512]{1,0:T(8,128)(2,1)S(1)}, u32[]{:S(2)}, u32[]{:S(2)}) collective-permute-start(bf16[448,512]{1,0:T(8,128)(2,1)S(1)} %get-tuple-element.319), channel_id=1, source_target_pairs={{0,2},{1,5},{2,0},{3,7},{4,6},{5,1},{6,4},{7,3},{8,10},{9,13},{10,... | collective-permute-start | bytes 1376264 | tf_op jit(solution)/shard_map/ppermute | solution.py:895
  38.3 0.5 product.1
  38.9 0.6 sum_0.5
  39.5 1.4 %collective-permute-start.11 = (bf16[448,512]{1,0:T(8,128)(2,1)S(1)}, bf16[448,512]{1,0:T(8,128)(2,1)S(1)}, u32[]{:S(2)}, u32[]{:S(2)}) collective-permute-start(bf16[448,512]{1,0:T(8,128)(2,1)S(1)} %get-tuple-element.327), channel_id=1, source_target_pairs={{0,2},{1,5},{2,0},{3,7},{4,6},{5,1},{6,4},{7,3},{8,10},{9,13},{10,... | collective-permute-start | bytes 1376264 | tf_op jit(solution)/shard_map/ppermute | solution.py:895
  40.8 3.2 %late_stage.1 = (bf16[256,1536]{1,0:T(8,128)(2,1)S(1)}, bf16[256,1536]{1,0:T(8,128)(2,1)S(1)}, bf16[896,512]{1,0:T(8,128)(2,1)S(1)}, bf16[896,512]{1,0:T(8,128)(2,1)S(1)}, f32[8,128]{1,0:T(8,128)S(1)}) custom-call(s32[4]{0:T(128)S(4)} %get-tuple-element.206.place_ref, f32[8,128]{1,0:T(8,128)S(1)} %get-tuple-element.310.token_in, ...), custom_call_target="tpu_custom_call" | custom-call | flops 8000000000 | tf_op jit(solution)/shard_map/late_stage/pallas_call | solution.py:239
  44.0 0.6 collective-permute-start.9
  44.6 0.5 sum_0.6
  45.2 0.9 collective-permute-start.13
  46.2 1.5 %collective-permute-start.12 = (bf16[224,512]{1,0:T(8,128)(2,1)S(1)}, bf16[224,512]{1,0:T(8,128)(2,1)S(1)}, u32[]{:S(2)}, u32[]{:S(2)}) collective-permute-start(bf16[224,512]{1,0:T(8,128)(2,1)S(1)} %get-tuple-element.330), channel_id=1, source_target_pairs={{0,4},{1,3},{2,6},{3,1},{4,0},{5,7},{6,2},{7,5},{8,12},{9,11},{10,... | collective-permute-start | bytes 688136 | tf_op jit(solution)/shard_map/ppermute | solution.py:895
  47.7 0.3 collective-permute-done.10.refs_1_
  48.0 0.7 sum_0.7
  48.7 1.2 collective-permute-start.15
  49.9 1.1 collective-permute-done.11.refs_1_
  51.1 2.4 %collective-permute-start.14 = (bf16[224,512]{1,0:T(8,128)(2,1)S(1)}, bf16[224,512]{1,0:T(8,128)(2,1)S(1)}, u32[]{:S(2)}, u32[]{:S(2)}) collective-permute-start(bf16[224,512]{1,0:T(8,128)(2,1)S(1)} %get-tuple-element.343), channel_id=1, source_target_pairs={{0,4},{1,3},{2,6},{3,1},{4,0},{5,7},{6,2},{7,5},{8,12},{9,11},{10,... | collective-permute-start | bytes 688136 | tf_op jit(solution)/shard_map/ppermute | solution.py:895
  53.5 1.3 %collective-permute-done.12.refs_1_ = bf16[224,512]{1,0:T(8,128)(2,1)S(1)} collective-permute-done((bf16[224,512]{1,0:T(8,128)(2,1)S(1)}, bf16[224,512]{1,0:T(8,128)(2,1)S(1)}, u32[]{:S(2)}, u32[]{:S(2)}) %collective-permute-start.12) | collective-permute-done | bytes 229408 | tf_op jit(solution)/shard_map/ppermute | solution.py:895
  54.8 2.7 %collective-permute-start.16 = (bf16[224,512]{1,0:T(8,128)(2,1)S(1)}, bf16[224,512]{1,0:T(8,128)(2,1)S(1)}, u32[]{:S(2)}, u32[]{:S(2)}) collective-permute-start(bf16[224,512]{1,0:T(8,128)(2,1)S(1)} %get-tuple-element.348.refs_0_), channel_id=1, source_target_pairs={{0,8},{1,9},{2,10},{3,11},{4,12},{5,13},{6,14},{7,15},{8,0},{9,1},... | collective-permute-start | bytes 688136 | tf_op jit(solution)/shard_map/ppermute | solution.py:895
  57.5 3.3 %collective-permute-done.13.refs_1_ = bf16[448,512]{1,0:T(8,128)(2,1)S(1)} collective-permute-done((bf16[448,512]{1,0:T(8,128)(2,1)S(1)}, bf16[448,512]{1,0:T(8,128)(2,1)S(1)}, u32[]{:S(2)}, u32[]{:S(2)}) %collective-permute-start.13) | collective-permute-done | bytes 458784 | tf_op jit(solution)/shard_map/ppermute | solution.py:895
  60.9 2.4 %collective-permute-start.17 = (bf16[224,512]{1,0:T(8,128)(2,1)S(1)}, bf16[224,512]{1,0:T(8,128)(2,1)S(1)}, u32[]{:S(2)}, u32[]{:S(2)}) collective-permute-start(bf16[224,512]{1,0:T(8,128)(2,1)S(1)} %get-tuple-element.351), channel_id=1, source_target_pairs={{0,4},{1,3},{2,6},{3,1},{4,0},{5,7},{6,2},{7,5},{8,12},{9,11},{10,... | collective-permute-start | bytes 688136 | tf_op jit(solution)/shard_map/ppermute | solution.py:895
  63.3 1.6 %final_stage.1 = (f32[8,128]{1,0:T(8,128)S(1)}, bf16[1,256,512]{2,1,0:T(8,128)(2,1)}, bf16[1,256,512]{2,1,0:T(8,128)(2,1)}) custom-call(s32[4]{0:T(128)S(4)} %get-tuple-element.206.place_ref, f32[8,128]{1,0:T(8,128)S(1)} %get-tuple-element.334.token_in, f32[256,512]{1,0:T(8,128)S(1)} %get-tuple-element.335.refs_0_, ...), custom_call_target="tpu_custom_call" | custom-call | flops 1000000000 | tf_op jit(solution)/shard_map/final_stage/pallas_call | solution.py:239
  64.9 3.9 %collective-permute-done.14.refs_1_ = bf16[224,512]{1,0:T(8,128)(2,1)S(1)} collective-permute-done((bf16[224,512]{1,0:T(8,128)(2,1)S(1)}, bf16[224,512]{1,0:T(8,128)(2,1)S(1)}, u32[]{:S(2)}, u32[]{:S(2)}) %collective-permute-start.14) | collective-permute-done | bytes 229408 | tf_op jit(solution)/shard_map/ppermute | solution.py:895
  68.8 1.9 %collective-permute-start.18 = (bf16[224,512]{1,0:T(8,128)(2,1)S(1)}, bf16[224,512]{1,0:T(8,128)(2,1)S(1)}, u32[]{:S(2)}, u32[]{:S(2)}) collective-permute-start(bf16[224,512]{1,0:T(8,128)(2,1)S(1)} %get-tuple-element.353.refs_0_), channel_id=1, source_target_pairs={{0,8},{1,9},{2,10},{3,11},{4,12},{5,13},{6,14},{7,15},{8,0},{9,1},... | collective-permute-start | bytes 688136 | tf_op jit(solution)/shard_map/ppermute | solution.py:895
  70.8 1.6 %collective-permute-start.19 = (bf16[224,512]{1,0:T(8,128)(2,1)S(1)}, bf16[224,512]{1,0:T(8,128)(2,1)S(1)}, u32[]{:S(2)}, u32[]{:S(2)}) collective-permute-start(bf16[224,512]{1,0:T(8,128)(2,1)S(1)} %get-tuple-element.356), channel_id=1, source_target_pairs={{0,2},{1,5},{2,0},{3,7},{4,6},{5,1},{6,4},{7,3},{8,10},{9,13},{10,... | collective-permute-start | bytes 688136 | tf_op jit(solution)/shard_map/ppermute | solution.py:895
  72.5 2.5 %collective-permute-start.20 = (bf16[224,512]{1,0:T(8,128)(2,1)S(1)}, bf16[224,512]{1,0:T(8,128)(2,1)S(1)}, u32[]{:S(2)}, u32[]{:S(2)}) collective-permute-start(bf16[224,512]{1,0:T(8,128)(2,1)S(1)} %get-tuple-element.358.refs_0_), channel_id=1, source_target_pairs={{0,4},{1,3},{2,6},{3,1},{4,0},{5,7},{6,2},{7,5},{8,12},{9,11},{10,... | collective-permute-start | bytes 688136 | tf_op jit(solution)/shard_map/ppermute | solution.py:895
  75.1 0.5 collective-permute-start.21
  75.7 7.7 %collective-permute-done.18.refs_1_ = bf16[224,512]{1,0:T(8,128)(2,1)S(1)} collective-permute-done((bf16[224,512]{1,0:T(8,128)(2,1)S(1)}, bf16[224,512]{1,0:T(8,128)(2,1)S(1)}, u32[]{:S(2)}, u32[]{:S(2)}) %collective-permute-start.18) | collective-permute-done | bytes 229408 | tf_op jit(solution)/shard_map/ppermute | solution.py:895
  83.5 1.7 %collective-permute-start.24 = (bf16[448,512]{1,0:T(8,128)(2,1)S(1)}, bf16[448,512]{1,0:T(8,128)(2,1)S(1)}, u32[]{:S(2)}, u32[]{:S(2)}) collective-permute-start(bf16[448,512]{1,0:T(8,128)(2,1)S(1)} %get-tuple-element.366.refs_0_), channel_id=1, source_target_pairs={{0,2},{1,5},{2,0},{3,7},{4,6},{5,1},{6,4},{7,3},{8,10},{9,13},{10,... | collective-permute-start | bytes 1376264 | tf_op jit(solution)/shard_map/ppermute | solution.py:895
  85.2 1.7 %collective-permute-start.22 = (bf16[224,512]{1,0:T(8,128)(2,1)S(1)}, bf16[224,512]{1,0:T(8,128)(2,1)S(1)}, u32[]{:S(2)}, u32[]{:S(2)}) collective-permute-start(bf16[224,512]{1,0:T(8,128)(2,1)S(1)} %get-tuple-element.362.refs_0_), channel_id=1, source_target_pairs={{0,4},{1,3},{2,6},{3,1},{4,0},{5,7},{6,2},{7,5},{8,12},{9,11},{10,... | collective-permute-start | bytes 688136 | tf_op jit(solution)/shard_map/ppermute | solution.py:895
  86.9 3.6 %collective-permute-start.23 = (bf16[224,512]{1,0:T(8,128)(2,1)S(1)}, bf16[224,512]{1,0:T(8,128)(2,1)S(1)}, u32[]{:S(2)}, u32[]{:S(2)}) collective-permute-start(bf16[224,512]{1,0:T(8,128)(2,1)S(1)} %get-tuple-element.364.refs_0_), channel_id=1, source_target_pairs={{0,8},{1,9},{2,10},{3,11},{4,12},{5,13},{6,14},{7,15},{8,0},{9,1},... | collective-permute-start | bytes 688136 | tf_op jit(solution)/shard_map/ppermute | solution.py:895
  90.6 1.9 %collective-permute-done.21.refs_1_ = bf16[224,512]{1,0:T(8,128)(2,1)S(1)} collective-permute-done((bf16[224,512]{1,0:T(8,128)(2,1)S(1)}, bf16[224,512]{1,0:T(8,128)(2,1)S(1)}, u32[]{:S(2)}, u32[]{:S(2)}) %collective-permute-start.21) | collective-permute-done | bytes 229408 | tf_op jit(solution)/shard_map/ppermute | solution.py:895
  92.7 6.0 %collective-permute-done.22.refs_1_ = bf16[224,512]{1,0:T(8,128)(2,1)S(1)} collective-permute-done((bf16[224,512]{1,0:T(8,128)(2,1)S(1)}, bf16[224,512]{1,0:T(8,128)(2,1)S(1)}, u32[]{:S(2)}, u32[]{:S(2)}) %collective-permute-start.22) | collective-permute-done | bytes 229408 | tf_op jit(solution)/shard_map/ppermute | solution.py:895
  98.8 1.4 %collective-permute-start.27 = (bf16[224,512]{1,0:T(8,128)(2,1)S(1)}, bf16[224,512]{1,0:T(8,128)(2,1)S(1)}, u32[]{:S(2)}, u32[]{:S(2)}) collective-permute-start(bf16[224,512]{1,0:T(8,128)(2,1)S(1)} %get-tuple-element.377.refs_0_), channel_id=1, source_target_pairs={{0,2},{1,5},{2,0},{3,7},{4,6},{5,1},{6,4},{7,3},{8,10},{9,13},{10,... | collective-permute-start | bytes 688136 | tf_op jit(solution)/shard_map/ppermute | solution.py:895
  100.1 0.7 collective-permute-start.26
  101.1 1.4 %collective-permute-start.29 = (bf16[448,512]{1,0:T(8,128)(2,1)S(1)}, bf16[448,512]{1,0:T(8,128)(2,1)S(1)}, u32[]{:S(2)}, u32[]{:S(2)}) collective-permute-start(bf16[448,512]{1,0:T(8,128)(2,1)S(1)} %get-tuple-element.381.refs_0_), channel_id=1, source_target_pairs={{0,2},{1,5},{2,0},{3,7},{4,6},{5,1},{6,4},{7,3},{8,10},{9,13},{10,... | collective-permute-start | bytes 1376264 | tf_op jit(solution)/shard_map/ppermute | solution.py:895
  102.5 1.3 %unpack_1.4 = (f32[8,128]{1,0:T(8,128)S(1)}, f32[1,2048,512]{2,1,0:T(8,128)}) custom-call(s32[4]{0:T(128)S(4)} %get-tuple-element.206.place_ref, f32[8,128]{1,0:T(8,128)S(1)} %get-tuple-element.369.token_in, bf16[896,512]{1,0:T(8,128)(2,1)S(1)} %get-tuple-element.370.refs_0_), custom_call_target="tpu_custom_call" | custom-call | flops 8000000000 | tf_op jit(solution)/shard_map/unpack_1/pallas_call | solution.py:239
  103.8 5.9 %collective-permute-done.26.refs_1_ = bf16[448,512]{1,0:T(8,128)(2,1)S(1)} collective-permute-done((bf16[448,512]{1,0:T(8,128)(2,1)S(1)}, bf16[448,512]{1,0:T(8,128)(2,1)S(1)}, u32[]{:S(2)}, u32[]{:S(2)}) %collective-permute-start.26) | collective-permute-done | bytes 458784 | tf_op jit(solution)/shard_map/ppermute | solution.py:895
  109.9 1.3 %unpack_1.5 = (f32[8,128]{1,0:T(8,128)S(1)}, f32[1,512,1024]{2,1,0:T(8,128)}, f32[1,512,512]{2,1,0:T(8,128)}, f32[1,512,2048]{2,1,0:T(8,128)}, f32[1,2048,512]{2,1,0:T(8,128)}) custom-call(s32[4]{0:T(128)S(4)} %get-tuple-element.206.place_ref, f32[8,128]{1,0:T(8,128)S(1)} %get-tuple-element.373.token_in, ...), custom_call_target="tpu_custom_call", output_to_operand_aliasing={{4}: (3, {})} | custom-call | flops 8000000000 | tf_op jit(solution)/shard_map/unpack_1/pallas_call | solution.py:239
  111.3 2.5 %collective-permute-start.31 = (bf16[448,512]{1,0:T(8,128)(2,1)S(1)}, bf16[448,512]{1,0:T(8,128)(2,1)S(1)}, u32[]{:S(2)}, u32[]{:S(2)}) collective-permute-start(bf16[448,512]{1,0:T(8,128)(2,1)S(1)} %get-tuple-element.391.refs_0_), channel_id=1, source_target_pairs={{0,4},{1,3},{2,6},{3,1},{4,0},{5,7},{6,2},{7,5},{8,12},{9,11},{10,... | collective-permute-start | bytes 1376264 | tf_op jit(solution)/shard_map/ppermute | solution.py:895
  113.8 1.3 %unpack_0.4 = (f32[8,128]{1,0:T(8,128)S(1)}, f32[1,2048,512]{2,1,0:T(8,128)}) custom-call(s32[4]{0:T(128)S(4)} %get-tuple-element.206.place_ref, f32[8,128]{1,0:T(8,128)S(1)} %get-tuple-element.378.token_in, bf16[896,512]{1,0:T(8,128)(2,1)S(1)} %collective-permute-done.28.refs_0_, ...), custom_call_target="tpu_custom_call", output_to_operand_aliasing={{1}: (3, {})} | custom-call | flops 1000000000 | tf_op jit(solution)/shard_map/unpack_0/pallas_call | solution.py:239
  115.3 1.3 %unpack_0.5 = (f32[8,128]{1,0:T(8,128)S(1)}, f32[1,512,1024]{2,1,0:T(8,128)}, f32[1,512,512]{2,1,0:T(8,128)}, f32[1,2048,512]{2,1,0:T(8,128)}, f32[1,512,2048]{2,1,0:T(8,128)}) custom-call(s32[4]{0:T(128)S(4)} %get-tuple-element.206.place_ref, ...), custom_call_target="tpu_custom_call", output_to_operand_aliasing={{1}: (3, {}), {2}: (4, {}), {3}: (5, {}), {4}: (6, {})} | custom-call | flops 1000000000 | tf_op jit(solution)/shard_map/unpack_0/pallas_call | solution.py:239
  116.6 1.3 %unpack_1.6 = (f32[8,128]{1,0:T(8,128)S(1)}, f32[1,512,2048]{2,1,0:T(8,128)}) custom-call(s32[4]{0:T(128)S(4)} %get-tuple-element.206.place_ref, f32[8,128]{1,0:T(8,128)S(1)} %get-tuple-element.387.token_in, bf16[896,512]{1,0:T(8,128)(2,1)S(1)} %get-tuple-element.388.refs_0_, f32[1,512,2048]{2,1,0:T(8,128)} %get-tuple-element.389.refs_1_), custom_call_target="tpu_custom_call", output_to_operand_aliasing={{1}: (3, {})} | custom-call | flops 1000000000 | tf_op jit(solution)/shard_map/unpack_1/pallas_call | solution.py:239
  117.9 2.4 %collective-permute-done.31.refs_1_ = bf16[448,512]{1,0:T(8,128)(2,1)S(1)} collective-permute-done((bf16[448,512]{1,0:T(8,128)(2,1)S(1)}, bf16[448,512]{1,0:T(8,128)(2,1)S(1)}, u32[]{:S(2)}, u32[]{:S(2)}) %collective-permute-start.31) | collective-permute-done | bytes 458784 | tf_op jit(solution)/shard_map/ppermute | solution.py:895
  120.4 1.3 %unpack_0.6 = (f32[8,128]{1,0:T(8,128)S(1)}, f32[1,512,2048]{2,1,0:T(8,128)}) custom-call(s32[4]{0:T(128)S(4)} %get-tuple-element.206.place_ref, f32[8,128]{1,0:T(8,128)S(1)} %get-tuple-element.392.token_in, bf16[896,512]{1,0:T(8,128)(2,1)S(1)} %collective-permute-done.32.refs_0_, ...), custom_call_target="tpu_custom_call", output_to_operand_aliasing={{1}: (3, {})} | custom-call | flops 3000000000 | tf_op jit(solution)/shard_map/unpack_0/pallas_call | solution.py:239
  121.7 1.3 %unpack_1.7 = (f32[8,128]{1,0:T(8,128)S(1)}, f32[1,512,1536]{2,1,0:T(8,128)}, f32[1,512,512]{2,1,0:T(8,128)}) custom-call(s32[4]{0:T(128)S(4)} %get-tuple-element.206.place_ref, f32[8,128]{1,0:T(8,128)S(1)} %get-tuple-element.394.token_in, bf16[896,512]{1,0:T(8,128)(2,1)S(1)} %get-tuple-element.395.refs_0_, ...), custom_call_target="tpu_custom_call", output_to_operand_aliasing={{2}: (3, {})} | custom-call | flops 1000000000 | tf_op jit(solution)/shard_map/unpack_1/pallas_call | solution.py:239
  123.0 1.9 %unpack_0.7 = (f32[8,128]{1,0:T(8,128)}, f32[1,512,1536]{2,1,0:T(8,128)}, f32[1,512,512]{2,1,0:T(8,128)}) custom-call(s32[4]{0:T(128)S(4)} %get-tuple-element.206.place_ref, f32[8,128]{1,0:T(8,128)S(1)} %get-tuple-element.397.token_in, bf16[896,512]{1,0:T(8,128)(2,1)S(1)} %collective-permute-done.33.refs_0_, ...), custom_call_target="tpu_custom_call", output_to_operand_aliasing={{1}: (3, {}), {2}: (4, {})} | custom-call | flops 1000000000 | tf_op jit(solution)/shard_map/unpack_0/pallas_call | solution.py:239
  (48 shorter events, 2.0 us)
Async XLA Ops:
  5.0 8.0 %collective-permute-start = (bf16[128,1024]{1,0:T(8,128)(2,1)S(1)}, bf16[128,1024]{1,0:T(8,128)(2,1)S(1)}, u32[]{:S(2)}, u32[]{:S(2)}) collective-permute-start(bf16[128,1024]{1,0:T(8,128)(2,1)S(1)} %get-tuple-element.232), channel_id=1, source_target_pairs={{0,16},{1,17},{2,18},{3,19},{4,20},{5,21},{6,22},{7,23},{8,24},{9,... | collective-permute-start | bytes 786440 | tf_op jit(solution)/shard_map/ppermute | solution.py:1072
  9.3 9.0 %collective-permute-start.1 = (bf16[128,1024]{1,0:T(8,128)(2,1)S(1)}, bf16[128,1024]{1,0:T(8,128)(2,1)S(1)}, u32[]{:S(2)}, u32[]{:S(2)}) collective-permute-start(bf16[128,1024]{1,0:T(8,128)(2,1)S(1)} %get-tuple-element.236), channel_id=1, source_target_pairs={{0,16},{1,17},{2,18},{3,19},{4,20},{5,21},{6,22},{7,23},{8,24},{9,... | collective-permute-start | bytes 786440 | tf_op jit(solution)/shard_map/ppermute | solution.py:1074
  13.6 13.9 %collective-permute-start.2 = (bf16[256,512]{1,0:T(8,128)(2,1)S(1)}, bf16[256,512]{1,0:T(8,128)(2,1)S(1)}, u32[]{:S(2)}, u32[]{:S(2)}) collective-permute-start(bf16[256,512]{1,0:T(8,128)(2,1)S(1)} %get-tuple-element.255), channel_id=1, source_target_pairs={{16,0},{17,1},{18,2},{19,3},{20,4},{21,5},{22,6},{23,7},{24,8},{25... | collective-permute-start | bytes 786440 | tf_op jit(solution)/shard_map/ppermute | solution.py:1077
  19.0 11.4 %collective-permute-start.3 = (bf16[128,512]{1,0:T(8,128)(2,1)S(1)}, bf16[128,512]{1,0:T(8,128)(2,1)S(1)}, u32[]{:S(2)}, u32[]{:S(2)}) collective-permute-start(bf16[128,512]{1,0:T(8,128)(2,1)S(1)} %get-tuple-element.268), channel_id=1, source_target_pairs={{16,0},{17,1},{18,2},{19,3},{20,4},{21,5},{22,6},{23,7},{24,8},{25... | collective-permute-start | bytes 393224 | tf_op jit(solution)/shard_map/ppermute | solution.py:1077
  20.3 12.2 %collective-permute-start.4 = (bf16[128,512]{1,0:T(8,128)(2,1)S(1)}, bf16[128,512]{1,0:T(8,128)(2,1)S(1)}, u32[]{:S(2)}, u32[]{:S(2)}) collective-permute-start(bf16[128,512]{1,0:T(8,128)(2,1)S(1)} %get-tuple-element.279), channel_id=1, source_target_pairs={{16,0},{17,1},{18,2},{19,3},{20,4},{21,5},{22,6},{23,7},{24,8},{25... | collective-permute-start | bytes 393224 | tf_op jit(solution)/shard_map/ppermute | solution.py:1077
  33.3 2.7 %collective-permute-start.5 = (bf16[896,512]{1,0:T(8,128)(2,1)S(1)}, bf16[896,512]{1,0:T(8,128)(2,1)S(1)}, u32[]{:S(2)}, u32[]{:S(2)}) collective-permute-start(bf16[896,512]{1,0:T(8,128)(2,1)S(1)} %get-tuple-element.300), channel_id=1, source_target_pairs={{0,1},{1,0},{2,3},{3,2},{4,5},{5,4},{6,7},{7,6},{8,9},{9,8},{10,11... | collective-permute-start | bytes 2752520 | tf_op jit(solution)/shard_map/ppermute | solution.py:895
  35.4 3.5 %collective-permute-start.6 = (bf16[896,512]{1,0:T(8,128)(2,1)S(1)}, bf16[896,512]{1,0:T(8,128)(2,1)S(1)}, u32[]{:S(2)}, u32[]{:S(2)}) collective-permute-start(bf16[896,512]{1,0:T(8,128)(2,1)S(1)} %get-tuple-element.306), channel_id=1, source_target_pairs={{0,1},{1,0},{2,3},{3,2},{4,5},{5,4},{6,7},{7,6},{8,9},{9,8},{10,11... | collective-permute-start | bytes 2752520 | tf_op jit(solution)/shard_map/ppermute | solution.py:895
  36.5 9.5 %collective-permute-start.8 = (bf16[448,512]{1,0:T(8,128)(2,1)S(1)}, bf16[448,512]{1,0:T(8,128)(2,1)S(1)}, u32[]{:S(2)}, u32[]{:S(2)}) collective-permute-start(bf16[448,512]{1,0:T(8,128)(2,1)S(1)} %get-tuple-element.319), channel_id=1, source_target_pairs={{0,2},{1,5},{2,0},{3,7},{4,6},{5,1},{6,4},{7,3},{8,10},{9,13},{10,... | collective-permute-start | bytes 1376264 | tf_op jit(solution)/shard_map/ppermute | solution.py:895
  38.8 5.8 %collective-permute-start.7 = (bf16[896,512]{1,0:T(8,128)(2,1)S(1)}, bf16[896,512]{1,0:T(8,128)(2,1)S(1)}, u32[]{:S(2)}, u32[]{:S(2)}) collective-permute-start(bf16[896,512]{1,0:T(8,128)(2,1)S(1)} %get-tuple-element.316), channel_id=1, source_target_pairs={{0,1},{1,0},{2,3},{3,2},{4,5},{5,4},{6,7},{7,6},{8,9},{9,8},{10,11... | collective-permute-start | bytes 2752520 | tf_op jit(solution)/shard_map/ppermute | solution.py:895
  39.5 11.5 %collective-permute-start.11 = (bf16[448,512]{1,0:T(8,128)(2,1)S(1)}, bf16[448,512]{1,0:T(8,128)(2,1)S(1)}, u32[]{:S(2)}, u32[]{:S(2)}) collective-permute-start(bf16[448,512]{1,0:T(8,128)(2,1)S(1)} %get-tuple-element.327), channel_id=1, source_target_pairs={{0,2},{1,5},{2,0},{3,7},{4,6},{5,1},{6,4},{7,3},{8,10},{9,13},{10,... | collective-permute-start | bytes 1376264 | tf_op jit(solution)/shard_map/ppermute | solution.py:895
  44.0 3.7 %collective-permute-start.9 = (bf16[896,512]{1,0:T(8,128)(2,1)S(1)}, bf16[896,512]{1,0:T(8,128)(2,1)S(1)}, u32[]{:S(2)}, u32[]{:S(2)}) collective-permute-start(bf16[896,512]{1,0:T(8,128)(2,1)S(1)} %get-tuple-element.321), channel_id=1, source_target_pairs={{0,1},{1,0},{2,3},{3,2},{4,5},{5,4},{6,7},{7,6},{8,9},{9,8},{10,11... | collective-permute-start | bytes 2752520 | tf_op jit(solution)/shard_map/ppermute | solution.py:895
  44.5 3.4 %collective-permute-start.10 = (bf16[896,512]{1,0:T(8,128)(2,1)S(1)}, bf16[896,512]{1,0:T(8,128)(2,1)S(1)}, u32[]{:S(2)}, u32[]{:S(2)}) collective-permute-start(bf16[896,512]{1,0:T(8,128)(2,1)S(1)} %get-tuple-element.322), channel_id=1, source_target_pairs={{0,1},{1,0},{2,3},{3,2},{4,5},{5,4},{6,7},{7,6},{8,9},{9,8},{10,11... | collective-permute-start | bytes 2752520 | tf_op jit(solution)/shard_map/ppermute | solution.py:895
  45.2 15.6 %collective-permute-start.13 = (bf16[448,512]{1,0:T(8,128)(2,1)S(1)}, bf16[448,512]{1,0:T(8,128)(2,1)S(1)}, u32[]{:S(2)}, u32[]{:S(2)}) collective-permute-start(bf16[448,512]{1,0:T(8,128)(2,1)S(1)} %get-tuple-element.333), channel_id=1, source_target_pairs={{0,2},{1,5},{2,0},{3,7},{4,6},{5,1},{6,4},{7,3},{8,10},{9,13},{10,... | collective-permute-start | bytes 1376264 | tf_op jit(solution)/shard_map/ppermute | solution.py:895
  46.2 8.6 %collective-permute-start.12 = (bf16[224,512]{1,0:T(8,128)(2,1)S(1)}, bf16[224,512]{1,0:T(8,128)(2,1)S(1)}, u32[]{:S(2)}, u32[]{:S(2)}) collective-permute-start(bf16[224,512]{1,0:T(8,128)(2,1)S(1)} %get-tuple-element.330), channel_id=1, source_target_pairs={{0,4},{1,3},{2,6},{3,1},{4,0},{5,7},{6,2},{7,5},{8,12},{9,11},{10,... | collective-permute-start | bytes 688136 | tf_op jit(solution)/shard_map/ppermute | solution.py:895
  48.7 22.0 %collective-permute-start.15 = (bf16[448,512]{1,0:T(8,128)(2,1)S(1)}, bf16[448,512]{1,0:T(8,128)(2,1)S(1)}, u32[]{:S(2)}, u32[]{:S(2)}) collective-permute-start(bf16[448,512]{1,0:T(8,128)(2,1)S(1)} %get-tuple-element.346), channel_id=1, source_target_pairs={{0,4},{1,3},{2,6},{3,1},{4,0},{5,7},{6,2},{7,5},{8,12},{9,11},{10,... | collective-permute-start | bytes 1376264 | tf_op jit(solution)/shard_map/ppermute | solution.py:895
  51.1 17.7 %collective-permute-start.14 = (bf16[224,512]{1,0:T(8,128)(2,1)S(1)}, bf16[224,512]{1,0:T(8,128)(2,1)S(1)}, u32[]{:S(2)}, u32[]{:S(2)}) collective-permute-start(bf16[224,512]{1,0:T(8,128)(2,1)S(1)} %get-tuple-element.343), channel_id=1, source_target_pairs={{0,4},{1,3},{2,6},{3,1},{4,0},{5,7},{6,2},{7,5},{8,12},{9,11},{10,... | collective-permute-start | bytes 688136 | tf_op jit(solution)/shard_map/ppermute | solution.py:895
  54.8 17.6 %collective-permute-start.16 = (bf16[224,512]{1,0:T(8,128)(2,1)S(1)}, bf16[224,512]{1,0:T(8,128)(2,1)S(1)}, u32[]{:S(2)}, u32[]{:S(2)}) collective-permute-start(bf16[224,512]{1,0:T(8,128)(2,1)S(1)} %get-tuple-element.348.refs_0_), channel_id=1, source_target_pairs={{0,8},{1,9},{2,10},{3,11},{4,12},{5,13},{6,14},{7,15},{8,0},{9,1},... | collective-permute-start | bytes 688136 | tf_op jit(solution)/shard_map/ppermute | solution.py:895
  60.9 14.2 %collective-permute-start.17 = (bf16[224,512]{1,0:T(8,128)(2,1)S(1)}, bf16[224,512]{1,0:T(8,128)(2,1)S(1)}, u32[]{:S(2)}, u32[]{:S(2)}) collective-permute-start(bf16[224,512]{1,0:T(8,128)(2,1)S(1)} %get-tuple-element.351), channel_id=1, source_target_pairs={{0,4},{1,3},{2,6},{3,1},{4,0},{5,7},{6,2},{7,5},{8,12},{9,11},{10,... | collective-permute-start | bytes 688136 | tf_op jit(solution)/shard_map/ppermute | solution.py:895
  68.8 14.5 %collective-permute-start.18 = (bf16[224,512]{1,0:T(8,128)(2,1)S(1)}, bf16[224,512]{1,0:T(8,128)(2,1)S(1)}, u32[]{:S(2)}, u32[]{:S(2)}) collective-permute-start(bf16[224,512]{1,0:T(8,128)(2,1)S(1)} %get-tuple-element.353.refs_0_), channel_id=1, source_target_pairs={{0,8},{1,9},{2,10},{3,11},{4,12},{5,13},{6,14},{7,15},{8,0},{9,1},... | collective-permute-start | bytes 688136 | tf_op jit(solution)/shard_map/ppermute | solution.py:895
  70.8 12.6 %collective-permute-start.19 = (bf16[224,512]{1,0:T(8,128)(2,1)S(1)}, bf16[224,512]{1,0:T(8,128)(2,1)S(1)}, u32[]{:S(2)}, u32[]{:S(2)}) collective-permute-start(bf16[224,512]{1,0:T(8,128)(2,1)S(1)} %get-tuple-element.356), channel_id=1, source_target_pairs={{0,2},{1,5},{2,0},{3,7},{4,6},{5,1},{6,4},{7,3},{8,10},{9,13},{10,... | collective-permute-start | bytes 688136 | tf_op jit(solution)/shard_map/ppermute | solution.py:895
  72.5 11.0 %collective-permute-start.20 = (bf16[224,512]{1,0:T(8,128)(2,1)S(1)}, bf16[224,512]{1,0:T(8,128)(2,1)S(1)}, u32[]{:S(2)}, u32[]{:S(2)}) collective-permute-start(bf16[224,512]{1,0:T(8,128)(2,1)S(1)} %get-tuple-element.358.refs_0_), channel_id=1, source_target_pairs={{0,4},{1,3},{2,6},{3,1},{4,0},{5,7},{6,2},{7,5},{8,12},{9,11},{10,... | collective-permute-start | bytes 688136 | tf_op jit(solution)/shard_map/ppermute | solution.py:895
  75.1 17.4 %collective-permute-start.21 = (bf16[224,512]{1,0:T(8,128)(2,1)S(1)}, bf16[224,512]{1,0:T(8,128)(2,1)S(1)}, u32[]{:S(2)}, u32[]{:S(2)}) collective-permute-start(bf16[224,512]{1,0:T(8,128)(2,1)S(1)} %get-tuple-element.360.refs_0_), channel_id=1, source_target_pairs={{0,8},{1,9},{2,10},{3,11},{4,12},{5,13},{6,14},{7,15},{8,0},{9,1},... | collective-permute-start | bytes 688136 | tf_op jit(solution)/shard_map/ppermute | solution.py:895
  83.5 17.3 %collective-permute-start.24 = (bf16[448,512]{1,0:T(8,128)(2,1)S(1)}, bf16[448,512]{1,0:T(8,128)(2,1)S(1)}, u32[]{:S(2)}, u32[]{:S(2)}) collective-permute-start(bf16[448,512]{1,0:T(8,128)(2,1)S(1)} %get-tuple-element.366.refs_0_), channel_id=1, source_target_pairs={{0,2},{1,5},{2,0},{3,7},{4,6},{5,1},{6,4},{7,3},{8,10},{9,13},{10,... | collective-permute-start | bytes 1376264 | tf_op jit(solution)/shard_map/ppermute | solution.py:895
  85.2 13.4 %collective-permute-start.22 = (bf16[224,512]{1,0:T(8,128)(2,1)S(1)}, bf16[224,512]{1,0:T(8,128)(2,1)S(1)}, u32[]{:S(2)}, u32[]{:S(2)}) collective-permute-start(bf16[224,512]{1,0:T(8,128)(2,1)S(1)} %get-tuple-element.362.refs_0_), channel_id=1, source_target_pairs={{0,4},{1,3},{2,6},{3,1},{4,0},{5,7},{6,2},{7,5},{8,12},{9,11},{10,... | collective-permute-start | bytes 688136 | tf_op jit(solution)/shard_map/ppermute | solution.py:895
  86.9 11.7 %collective-permute-start.23 = (bf16[224,512]{1,0:T(8,128)(2,1)S(1)}, bf16[224,512]{1,0:T(8,128)(2,1)S(1)}, u32[]{:S(2)}, u32[]{:S(2)}) collective-permute-start(bf16[224,512]{1,0:T(8,128)(2,1)S(1)} %get-tuple-element.364.refs_0_), channel_id=1, source_target_pairs={{0,8},{1,9},{2,10},{3,11},{4,12},{5,13},{6,14},{7,15},{8,0},{9,1},... | collective-permute-start | bytes 688136 | tf_op jit(solution)/shard_map/ppermute | solution.py:895
  92.6 8.5 %collective-permute-start.25 = (bf16[224,512]{1,0:T(8,128)(2,1)S(1)}, bf16[224,512]{1,0:T(8,128)(2,1)S(1)}, u32[]{:S(2)}, u32[]{:S(2)}) collective-permute-start(bf16[224,512]{1,0:T(8,128)(2,1)S(1)} %get-tuple-element.368.refs_0_), channel_id=1, source_target_pairs={{0,4},{1,3},{2,6},{3,1},{4,0},{5,7},{6,2},{7,5},{8,12},{9,11},{10,... | collective-permute-start | bytes 688136 | tf_op jit(solution)/shard_map/ppermute | solution.py:895
  98.8 12.5 %collective-permute-start.27 = (bf16[224,512]{1,0:T(8,128)(2,1)S(1)}, bf16[224,512]{1,0:T(8,128)(2,1)S(1)}, u32[]{:S(2)}, u32[]{:S(2)}) collective-permute-start(bf16[224,512]{1,0:T(8,128)(2,1)S(1)} %get-tuple-element.377.refs_0_), channel_id=1, source_target_pairs={{0,2},{1,5},{2,0},{3,7},{4,6},{5,1},{6,4},{7,3},{8,10},{9,13},{10,... | collective-permute-start | bytes 688136 | tf_op jit(solution)/shard_map/ppermute | solution.py:895
  100.1 9.6 %collective-permute-start.26 = (bf16[448,512]{1,0:T(8,128)(2,1)S(1)}, bf16[448,512]{1,0:T(8,128)(2,1)S(1)}, u32[]{:S(2)}, u32[]{:S(2)}) collective-permute-start(bf16[448,512]{1,0:T(8,128)(2,1)S(1)} %get-tuple-element.372.refs_0_), channel_id=1, source_target_pairs={{0,2},{1,5},{2,0},{3,7},{4,6},{5,1},{6,4},{7,3},{8,10},{9,13},{10,... | collective-permute-start | bytes 1376264 | tf_op jit(solution)/shard_map/ppermute | solution.py:895
  101.1 14.0 %collective-permute-start.29 = (bf16[448,512]{1,0:T(8,128)(2,1)S(1)}, bf16[448,512]{1,0:T(8,128)(2,1)S(1)}, u32[]{:S(2)}, u32[]{:S(2)}) collective-permute-start(bf16[448,512]{1,0:T(8,128)(2,1)S(1)} %get-tuple-element.381.refs_0_), channel_id=1, source_target_pairs={{0,2},{1,5},{2,0},{3,7},{4,6},{5,1},{6,4},{7,3},{8,10},{9,13},{10,... | collective-permute-start | bytes 1376264 | tf_op jit(solution)/shard_map/ppermute | solution.py:895
  102.5 11.3 %collective-permute-start.28 = (bf16[896,512]{1,0:T(8,128)(2,1)S(1)}, bf16[896,512]{1,0:T(8,128)(2,1)S(1)}, u32[]{:S(2)}, u32[]{:S(2)}) collective-permute-start(bf16[896,512]{1,0:T(8,128)(2,1)S(1)} %get-tuple-element.370.refs_0_), channel_id=1, source_target_pairs={{0,1},{1,0},{2,3},{3,2},{4,5},{5,4},{6,7},{7,6},{8,9},{9,8},{10,11... | collective-permute-start | bytes 2752520 | tf_op jit(solution)/shard_map/ppermute | solution.py:895
  109.8 5.5 %collective-permute-start.30 = (bf16[896,512]{1,0:T(8,128)(2,1)S(1)}, bf16[896,512]{1,0:T(8,128)(2,1)S(1)}, u32[]{:S(2)}, u32[]{:S(2)}) collective-permute-start(bf16[896,512]{1,0:T(8,128)(2,1)S(1)} %get-tuple-element.374.refs_0_), channel_id=1, source_target_pairs={{0,1},{1,0},{2,3},{3,2},{4,5},{5,4},{6,7},{7,6},{8,9},{9,8},{10,11... | collective-permute-start | bytes 2752520 | tf_op jit(solution)/shard_map/ppermute | solution.py:895
  111.3 9.0 %collective-permute-start.31 = (bf16[448,512]{1,0:T(8,128)(2,1)S(1)}, bf16[448,512]{1,0:T(8,128)(2,1)S(1)}, u32[]{:S(2)}, u32[]{:S(2)}) collective-permute-start(bf16[448,512]{1,0:T(8,128)(2,1)S(1)} %get-tuple-element.391.refs_0_), channel_id=1, source_target_pairs={{0,4},{1,3},{2,6},{3,1},{4,0},{5,7},{6,2},{7,5},{8,12},{9,11},{10,... | collective-permute-start | bytes 1376264 | tf_op jit(solution)/shard_map/ppermute | solution.py:895
  115.2 5.2 %collective-permute-start.32 = (bf16[896,512]{1,0:T(8,128)(2,1)S(1)}, bf16[896,512]{1,0:T(8,128)(2,1)S(1)}, u32[]{:S(2)}, u32[]{:S(2)}) collective-permute-start(bf16[896,512]{1,0:T(8,128)(2,1)S(1)} %get-tuple-element.388.refs_0_), channel_id=1, source_target_pairs={{0,1},{1,0},{2,3},{3,2},{4,5},{5,4},{6,7},{7,6},{8,9},{9,8},{10,11... | collective-permute-start | bytes 2752520 | tf_op jit(solution)/shard_map/ppermute | solution.py:895
  120.3 2.7 %collective-permute-start.33 = (bf16[896,512]{1,0:T(8,128)(2,1)S(1)}, bf16[896,512]{1,0:T(8,128)(2,1)S(1)}, u32[]{:S(2)}, u32[]{:S(2)}) collective-permute-start(bf16[896,512]{1,0:T(8,128)(2,1)S(1)} %get-tuple-element.395.refs_0_), channel_id=1, source_target_pairs={{0,1},{1,0},{2,3},{3,2},{4,5},{5,4},{6,7},{7,6},{8,9},{9,8},{10,11... | collective-permute-start | bytes 2752520 | tf_op jit(solution)/shard_map/ppermute | solution.py:895
